TPU v7x, 128 devices: a whole 4x4x4 slice. The times are simulated.
128 devices in a mesh: ctx: 8 (over y_lo, x), shard: 16 (over z, y_hi, core).
Axes of the slice: x: 4, y: 4 (y_hi: 2, y_lo: 2; y = y_hi * 2 + y_lo), z: 4, core: 2. Of those that a mesh axis runs over, the one named last changes fastest.
Arguments:
- tokens: bfloat16 [16, 1152, 2048], P('shard', 'ctx'), may hold values from -6 to 6
- cotangent: bfloat16 [16, 1152, 2048], P('shard', 'ctx'), may hold values from -6 to 6
- query_matrix: bfloat16 [2048, 2048], P('shard'), may hold values from -0.125 to 0.125
- key_matrix: bfloat16 [2048, 2048], P('shard'), may hold values from -0.125 to 0.125
- value_matrix: bfloat16 [2048, 2048], P('shard'), may hold values from -0.125 to 0.125
- output_matrix: bfloat16 [2048, 2048], P('shard'), may hold values from -0.125 to 0.125
- gate_matrix: bfloat16 [2048, 8192], P('shard'), may hold values from -0.125 to 0.125
- upward_matrix: bfloat16 [2048, 8192], P('shard'), may hold values from -0.125 to 0.125
- down_matrix: bfloat16 [8192, 2048], P('shard'), may hold values from -0.0625 to 0.0625
- norm_gain_vectors: float32 [4, 2048], replicated, may hold values from 0.1 to 1.9
- adapter_down_inputs: bfloat16 [8, 6, 16, 2048], replicated, may hold values from -0.125 to 0.125
- adapter_down_feedforward: bfloat16 [8, 16, 8192], replicated, may hold values from -0.0625 to 0.0625
- adapter_up_model_maps: bfloat16 [8, 5, 16, 2048], replicated, may hold values from -0.375 to 0.375
- adapter_up_hidden_maps: bfloat16 [8, 2, 16, 8192], replicated, may hold values from -0.375 to 0.375
- group_adapter_index: int32 [16, 1], P('shard'), may hold values from 0 to 7
- continuation_lengths: int32 [16, 2], P('shard'), may hold values from 32 to 96, as said below
Outputs:
- output: bfloat16 [16, 1152, 2048], P('shard', 'ctx')
- grad_tokens: bfloat16 [16, 1152, 2048], P('shard', 'ctx')
- grad_down_in: float32 [8, 6, 16, 2048], replicated
- grad_down_ff: float32 [8, 16, 8192], replicated
- grad_up_model: float32 [8, 5, 16, 2048], replicated
- grad_up_hidden: float32 [8, 2, 16, 8192], replicated
Inputs may be any that keep to these rules, and one draw needn't show every extreme that they name: `group_adapter_index`: every adapter is used by some group. `continuation_lengths`: each group's two lengths sum to 128; the longer one lies between 64 and 96, and in group 0 it is exactly 96.
All inputs are finite; a program needn't handle non-finite values.
Results may differ from a plain program's by a relative error of at most 0.035.
Values may be sent and summed in bfloat16 or wider, within the bound.
No kernel may reach another device: no remote copies, remote signals or barrier semaphores. Data moves between devices by JAX's collectives and lax.ppermute only.
A program may use at most 448 MiB of HBM per device.

v0:
```python
import jax
import jax.numpy as jnp
from jax import lax
from jax.sharding import PartitionSpec as P

H = 16
HD = 128
ADAPTER_TOTAL = 8
PROMPT = 1024


adapter_scale = 2.0
norm_eps = 1e-06
rope_base = 500000.0
masked_score = -1e30


def layout(lengths, prompt, total):
    csum = jnp.cumsum(lengths, axis=1, dtype=jnp.int32)
    bounds = prompt + csum - lengths
    places = jnp.arange(total, dtype=jnp.int32)
    after = places[None, :, None] >= bounds[:, None, :]
    segment = jnp.sum(after.astype(jnp.int32), axis=2, dtype=jnp.int32)
    begin = jnp.max(jnp.where(after, bounds[:, None, :], 0), axis=2)
    position = jnp.where(segment == 0, places[None, :], prompt + places[None, :] - begin)
    return (segment, position)


def rope_tables(position, head_dim):
    half = head_dim // 2
    freq = rope_base ** (-(jnp.arange(half, dtype=jnp.float32) * 2.0 / head_dim))
    angle = position.astype(jnp.float32)[..., None] * freq
    return (jnp.cos(angle), jnp.sin(angle))


def rotate(field, cosine, sine, heads):
    shape = field.shape
    split = field.reshape(shape[:-1] + (heads, 2, shape[-1] // heads // 2))
    first = split[..., 0, :]
    second = split[..., 1, :]
    cos_part = cosine[..., None, :]
    sin_part = sine[..., None, :]
    turned = jnp.stack(
        [first * cos_part - second * sin_part, second * cos_part + first * sin_part], axis=-2
    )
    return turned.reshape(shape)


def normalize(field, gain):
    inverse = lax.rsqrt(jnp.mean(field * field, axis=-1, keepdims=True) + norm_eps)
    return (field * inverse * gain, inverse)


def normalize_back(field, inverse, gain, grad):
    weighted = grad * gain
    return inverse * weighted - field * inverse**3 * jnp.mean(
        weighted * field, axis=-1, keepdims=True
    )


def visible(query_segment, query_place, key_segment, key_place):
    causal = key_place[None, None, :] <= query_place[None, :, None]
    shared = (key_segment[:, None, :] == 0) | (key_segment[:, None, :] == query_segment[:, :, None])
    return (causal & shared)[:, None]


def project(inputs, weight, adapter_down, adapter_lift_map):
    frozen_output = jnp.einsum("gtd,de->gte", inputs, weight, preferred_element_type=jnp.float32)
    reduced_rank_output = jnp.einsum(
        "gtd,grd->gtr", inputs, adapter_down, preferred_element_type=jnp.float32
    ).astype(jnp.bfloat16)
    raised_output = jnp.einsum(
        "gtr,gre->gte", reduced_rank_output, adapter_lift_map, preferred_element_type=jnp.float32
    )
    return (frozen_output + adapter_scale * raised_output, reduced_rank_output)


def project_back(inputs, reduced_rank_output, weight, adapter_down, adapter_lift_map, grad):
    low_grad = (
        adapter_scale
        * jnp.einsum("gte,gre->gtr", grad, adapter_lift_map, preferred_element_type=jnp.float32)
    ).astype(jnp.bfloat16)
    back = jnp.einsum("gte,de->gtd", grad, weight, preferred_element_type=jnp.float32)
    back = back + jnp.einsum(
        "gtr,grd->gtd", low_grad, adapter_down, preferred_element_type=jnp.float32
    )
    grad_down = jnp.einsum("gtr,gtd->grd", low_grad, inputs, preferred_element_type=jnp.float32)
    gradient_upward_map = adapter_scale * jnp.einsum(
        "gtr,gte->gre", reduced_rank_output, grad, preferred_element_type=jnp.float32
    )
    return (back, grad_down, gradient_upward_map)


def on_device(
    tokens,
    cotangent,
    query_matrix,
    key_matrix,
    value_matrix,
    output_matrix,
    gate_matrix,
    upward_matrix,
    down_matrix,
    norm_gain_vectors,
    adapter_down_inputs,
    adapter_down_feedforward,
    adapter_up_model_maps,
    adapter_up_hidden_maps,
    group_adapter_index,
    continuation_lengths,
):
    groups, rows, width = tokens.shape
    total = rows * lax.axis_size("ctx")
    offset = lax.axis_index("ctx") * rows
    score_scale = HD ** (-0.5)
    highest_precision = lax.Precision.HIGHEST
    segment, position = layout(continuation_lengths, PROMPT, total)
    local_segment = lax.dynamic_slice_in_dim(segment, offset, rows, 1)
    local_position = lax.dynamic_slice_in_dim(position, offset, rows, 1)
    local_place = offset + jnp.arange(rows, dtype=jnp.int32)
    cosine, sine = rope_tables(local_position, HD)
    picks = group_adapter_index == jnp.arange(ADAPTER_TOTAL, dtype=jnp.int32)[None, :]
    adapter_picker = picks.astype(jnp.bfloat16)
    chosen_in = jnp.einsum(
        "ms,sxni->mxni", adapter_picker, adapter_down_inputs, preferred_element_type=jnp.float32
    ).astype(jnp.bfloat16)
    chosen_ff = jnp.einsum(
        "tz,zwh->twh", adapter_picker, adapter_down_feedforward, preferred_element_type=jnp.float32
    ).astype(jnp.bfloat16)
    chosen_model = jnp.einsum(
        "ms,sxni->mxni", adapter_picker, adapter_up_model_maps, preferred_element_type=jnp.float32
    ).astype(jnp.bfloat16)
    chosen_hidden = jnp.einsum(
        "ms,sxni->mxni", adapter_picker, adapter_up_hidden_maps, preferred_element_type=jnp.float32
    ).astype(jnp.bfloat16)
    full = (
        lax.all_gather(query_matrix, "shard", axis=0, tiled=True),
        lax.all_gather(key_matrix, "shard", axis=0, tiled=True),
        lax.all_gather(value_matrix, "shard", axis=0, tiled=True),
        lax.all_gather(output_matrix, "shard", axis=0, tiled=True),
        lax.all_gather(gate_matrix, "shard", axis=0, tiled=True),
        lax.all_gather(upward_matrix, "shard", axis=0, tiled=True),
        lax.all_gather(down_matrix, "shard", axis=0, tiled=True),
    )
    query_full, key_full, value_full, out_full, gate_full, up_full, down_full = full
    query_pre, query_low = project(tokens, query_full, chosen_in[:, 0], chosen_model[:, 0])
    key_pre, key_low = project(tokens, key_full, chosen_in[:, 1], chosen_model[:, 1])
    value_pre, value_low = project(tokens, value_full, chosen_in[:, 2], chosen_model[:, 2])
    query_normed, query_inverse = normalize(query_pre, norm_gain_vectors[0])
    key_normed, key_inverse = normalize(key_pre, norm_gain_vectors[1])
    query = rotate(query_normed, cosine, sine, H).astype(jnp.bfloat16)
    keyed = rotate(key_normed, cosine, sine, H).astype(jnp.bfloat16)
    valued = value_pre.astype(jnp.bfloat16)
    query_heads = query.reshape(groups, rows, H, HD)

    def piece_scores(key_piece):
        count = key_piece.shape[1]
        key_heads = key_piece.reshape(groups, count, H, HD)
        key_place = jnp.arange(count, dtype=jnp.int32)
        allowed = visible(local_segment, local_place, segment, key_place)
        scores = (
            jnp.einsum(
                "gqhe,gkhe->ghqk", query_heads, key_heads, preferred_element_type=jnp.float32
            )
            * score_scale
        )
        return (key_heads, allowed, scores)

    start_top = jnp.full((groups, H, rows), masked_score, jnp.float32)
    top = start_top
    key_piece = lax.all_gather(keyed, "ctx", axis=1, tiled=True)
    value_piece = lax.all_gather(valued, "ctx", axis=1, tiled=True)
    count = key_piece.shape[1]
    value_heads = value_piece.reshape(groups, count, H, HD)
    key_heads, allowed, scores = piece_scores(key_piece)
    masked = jnp.where(allowed, scores, masked_score)
    new_top = jnp.maximum(top, jnp.max(masked, axis=-1))
    weights = jnp.where(allowed, jnp.exp(masked - new_top[..., None]), 0.0)
    denom = jnp.sum(weights, axis=-1)
    added = jnp.einsum(
        "ghqk,gkhe->gqhe",
        weights.astype(jnp.bfloat16),
        value_heads,
        preferred_element_type=jnp.float32,
    )
    accum = added
    top, denom, accum = (new_top, denom, accum)
    attended_heads = accum / jnp.transpose(denom, (0, 2, 1))[..., None]
    log_total = top + jnp.log(denom)
    attended = attended_heads.reshape(groups, rows, width)
    attended_low = attended.astype(jnp.bfloat16)
    attn_pre, out_low = project(attended_low, out_full, chosen_in[:, 3], chosen_model[:, 3])
    attn_normed, attn_inverse = normalize(attn_pre, norm_gain_vectors[2])
    hidden = tokens.astype(jnp.float32) + attn_normed
    hidden_low = hidden.astype(jnp.bfloat16)
    gate, gate_low = project(hidden_low, gate_full, chosen_in[:, 4], chosen_hidden[:, 0])
    upward, upward_low = project(hidden_low, up_full, chosen_in[:, 5], chosen_hidden[:, 1])
    sigmoid_gate = jax.nn.sigmoid(gate)
    activated = gate * sigmoid_gate
    mixed = (activated * upward).astype(jnp.bfloat16)
    mlp_pre, down_low = project(mixed, down_full, chosen_ff, chosen_model[:, 4])
    mlp_normed, mlp_inverse = normalize(mlp_pre, norm_gain_vectors[3])
    output = (hidden + mlp_normed).astype(jnp.bfloat16)
    back_weights = (
        lax.all_gather(query_matrix, "shard", axis=0, tiled=True),
        lax.all_gather(key_matrix, "shard", axis=0, tiled=True),
        lax.all_gather(value_matrix, "shard", axis=0, tiled=True),
        lax.all_gather(output_matrix, "shard", axis=0, tiled=True),
        lax.all_gather(gate_matrix, "shard", axis=0, tiled=True),
        lax.all_gather(upward_matrix, "shard", axis=0, tiled=True),
        lax.all_gather(down_matrix, "shard", axis=0, tiled=True),
    )
    query_back, key_back, value_back, out_back, gate_back, up_back, down_back = back_weights
    grad_output = cotangent.astype(jnp.float32)
    grad_mlp = normalize_back(mlp_pre, mlp_inverse, norm_gain_vectors[3], grad_output).astype(
        jnp.bfloat16
    )
    grad_mixed, down_grad_ff, down_grad_up = project_back(
        mixed, down_low, down_back, chosen_ff, chosen_model[:, 4], grad_mlp
    )
    grad_gate = (grad_mixed * upward * sigmoid_gate * (1.0 + gate * (1.0 - sigmoid_gate))).astype(
        jnp.bfloat16
    )
    grad_upward = (grad_mixed * activated).astype(jnp.bfloat16)
    gate_back_in, gate_grad_down, gate_grad_up = project_back(
        hidden_low, gate_low, gate_back, chosen_in[:, 4], chosen_hidden[:, 0], grad_gate
    )
    up_back_in, up_grad_down, up_grad_up = project_back(
        hidden_low, upward_low, up_back, chosen_in[:, 5], chosen_hidden[:, 1], grad_upward
    )
    grad_hidden = grad_output + gate_back_in + up_back_in
    grad_attn = normalize_back(attn_pre, attn_inverse, norm_gain_vectors[2], grad_hidden).astype(
        jnp.bfloat16
    )
    out_back_in, out_grad_down, out_grad_up = project_back(
        attended_low, out_low, out_back, chosen_in[:, 3], chosen_model[:, 3], grad_attn
    )
    grad_attended = out_back_in.astype(jnp.bfloat16)
    grad_heads = grad_attended.reshape(groups, rows, H, HD)
    delta = jnp.transpose(
        jnp.sum(grad_heads.astype(jnp.float32) * attended_heads, axis=-1), (0, 2, 1)
    )
    key_piece = lax.all_gather(keyed, "ctx", axis=1, tiled=True)
    value_piece = lax.all_gather(valued, "ctx", axis=1, tiled=True)
    count = key_piece.shape[1]
    value_heads = value_piece.reshape(groups, count, H, HD)
    key_heads, allowed, scores = piece_scores(key_piece)
    probs = jnp.exp(jnp.where(allowed, scores - log_total[..., None], masked_score))
    upstream = jnp.einsum(
        "gqhe,gkhe->ghqk", grad_heads, value_heads, preferred_element_type=jnp.float32
    )
    grad_scores = (probs * (upstream - delta[..., None])).astype(jnp.bfloat16)
    grad_query = score_scale * jnp.einsum(
        "ghqk,gkhe->gqhe", grad_scores, key_heads, preferred_element_type=jnp.float32
    )
    key_term = score_scale * jnp.einsum(
        "ghqk,gqhe->gkhe", grad_scores, query_heads, preferred_element_type=jnp.float32
    )
    value_term = jnp.einsum(
        "ghqk,gqhe->gkhe",
        probs.astype(jnp.bfloat16),
        grad_heads,
        preferred_element_type=jnp.float32,
    )
    key_slice = key_term.reshape(groups, count, width)
    value_slice = value_term.reshape(groups, count, width)
    key_grads = key_slice
    value_grads = value_slice
    grad_query, key_grads, value_grads = (grad_query, key_grads, value_grads)
    grad_key, grad_value = (
        lax.psum_scatter(
            key_grads.astype(jnp.bfloat16), "ctx", scatter_dimension=1, tiled=True
        ).astype(jnp.float32),
        lax.psum_scatter(
            value_grads.astype(jnp.bfloat16), "ctx", scatter_dimension=1, tiled=True
        ).astype(jnp.float32),
    )
    turned_query = rotate(grad_query.reshape(groups, rows, width), cosine, -sine, H)
    turned_key = rotate(grad_key, cosine, -sine, H)
    grad_query_pre = normalize_back(
        query_pre, query_inverse, norm_gain_vectors[0], turned_query
    ).astype(jnp.bfloat16)
    grad_key_pre = normalize_back(key_pre, key_inverse, norm_gain_vectors[1], turned_key).astype(
        jnp.bfloat16
    )
    grad_value_pre = grad_value.astype(jnp.bfloat16)
    query_back_in, query_grad_down, query_grad_up = project_back(
        tokens, query_low, query_back, chosen_in[:, 0], chosen_model[:, 0], grad_query_pre
    )
    key_back_in, key_grad_down, key_grad_up = project_back(
        tokens, key_low, key_back, chosen_in[:, 1], chosen_model[:, 1], grad_key_pre
    )
    value_back_in, value_grad_down, value_grad_up = project_back(
        tokens, value_low, value_back, chosen_in[:, 2], chosen_model[:, 2], grad_value_pre
    )
    grad_tokens = (grad_hidden + query_back_in + key_back_in + value_back_in).astype(jnp.bfloat16)
    pick_float = picks.astype(jnp.float32)
    stack_down_in = jnp.stack(
        [
            query_grad_down,
            key_grad_down,
            value_grad_down,
            out_grad_down,
            gate_grad_down,
            up_grad_down,
        ],
        axis=1,
    )
    stack_up_model = jnp.stack(
        [query_grad_up, key_grad_up, value_grad_up, out_grad_up, down_grad_up], axis=1
    )
    stack_up_hidden = jnp.stack([gate_grad_up, up_grad_up], axis=1)
    local_down_in = jnp.einsum(
        "ga,gjrd->ajrd", pick_float, stack_down_in, precision=highest_precision
    )
    local_down_ff = jnp.einsum("ga,grd->ard", pick_float, down_grad_ff, precision=highest_precision)
    local_up_model = jnp.einsum(
        "ga,gjrd->ajrd", pick_float, stack_up_model, precision=highest_precision
    )
    local_up_hidden = jnp.einsum(
        "ga,gjrd->ajrd", pick_float, stack_up_hidden, precision=highest_precision
    )
    summed = lax.psum(
        (local_down_in, local_down_ff, local_up_model, local_up_hidden), ("ctx", "shard")
    )
    return (output, grad_tokens, summed[0], summed[1], summed[2], summed[3])


def solution(mesh):
    return jax.shard_map(
        on_device,
        mesh=mesh,
        in_specs=(
            P("shard", "ctx", None),
            P("shard", "ctx", None),
            P("shard", None),
            P("shard", None),
            P("shard", None),
            P("shard", None),
            P("shard", None),
            P("shard", None),
            P("shard", None),
            P(),
            P(),
            P(),
            P(),
            P(),
            P("shard", None),
            P("shard", None),
        ),
        out_specs=(P("shard", "ctx", None), P("shard", "ctx", None), P(), P(), P(), P()),
        check_vma=False,
    )
```

profile of v0, /device:TPU:7, one launch (start us, length us, event | category | flops | bytes accessed | tf_op | source)
XLA Modules:
  0.0 1481.7 jit_solution(10391894801641569954)
XLA Ops:
  12.3 3.7 fusion.24
  24.2 62.2 %all-gather.15.cloned.1.call-done = bf16[2048,2048]{1,0:T(8,128)(2,1)} async-done(((bf16[128,2048]{1,0:T(8,128)(2,1)}), bf16[2048,2048]{1,0:T(8,128)(2,1)}) %all-gather.15.cloned.1.call-update) | async-done | bytes 8388624 | tf_op jit(solution)/shard_map/all_gather | solution.py:138
  86.4 4.8 fusion.108
  93.3 3.1 reshape.1191
  96.4 63.3 %all-gather.13.cloned.1.call-done = bf16[2048,2048]{1,0:T(8,128)(2,1)} async-done(((bf16[128,2048]{1,0:T(8,128)(2,1)}), bf16[2048,2048]{1,0:T(8,128)(2,1)}) %all-gather.13.cloned.1.call-update) | async-done | bytes 8388624 | tf_op jit(solution)/shard_map/all_gather | solution.py:137
  159.7 4.8 fusion.111
  166.6 3.3 reshape.1188
  169.9 8.9 subtract_convert_fusion.3
  178.8 4.1 pad_maximum_fusion.3
  182.9 4.2 convert_element_type.264
  187.4 45.6 %all-gather.11.cloned.1.call-done = bf16[2048,2048]{1,0:T(8,128)(2,1)} async-done(((bf16[128,2048]{1,0:T(8,128)(2,1)}), bf16[2048,2048]{1,0:T(8,128)(2,1)}) %all-gather.11.cloned.1.call-update) | async-done | bytes 8388624 | tf_op jit(solution)/shard_map/all_gather | solution.py:139
  233.0 4.8 fusion.114
  243.0 7.3 fusion.18
  251.7 3.3 fusion.60
  255.3 4.5 pad_maximum_fusion.2
  262.4 25.2 %all-gather.17.cloned.1.call-done = bf16[1,1152,2048]{2,1,0:T(8,128)(2,1)} async-done(((bf16[1,144,2048]{2,1,0:T(8,128)(2,1)}), bf16[1,1152,2048]{2,1,0:T(8,128)(2,1)}) %all-gather.17.cloned.1.call-update) | async-done | bytes 4718608 | tf_op jit(solution)/shard_map/all_gather | solution.py:171
  287.7 6.6 copy.56
  294.3 4.8 select_reduce_fusion
  299.1 3.9 copy-done.3
  303.0 3.4 fusion.5
  306.4 39.7 %all-gather.27.cloned.1.call-done = bf16[1152,2048]{1,0:T(8,128)(2,1)} async-done(((bf16[144,2048]{1,0:T(8,128)(2,1)}), bf16[1152,2048]{1,0:T(8,128)(2,1)}) %all-gather.27.cloned.1.call-update) | async-done | bytes 4718608 | tf_op jit(solution)/shard_map/all_gather | solution.py:172
  346.0 10.0 fusion.147
  356.5 66.5 %all-gather.19.cloned.1.call-done = bf16[2048,2048]{1,0:T(8,128)(2,1)} async-done(((bf16[128,2048]{1,0:T(8,128)(2,1)}), bf16[2048,2048]{1,0:T(8,128)(2,1)}) %all-gather.19.cloned.1.call-update) | async-done | bytes 8388624 | tf_op jit(solution)/shard_map/all_gather | solution.py:140
  422.9 4.8 fusion.100
  431.0 178.3 %all-gather.21.cloned.1.call-done = bf16[2048,8192]{1,0:T(8,128)(2,1)} async-done(((bf16[128,8192]{1,0:T(8,128)(2,1)}), bf16[2048,8192]{1,0:T(8,128)(2,1)}) %all-gather.21.cloned.1.call-update) | async-done | bytes 33554448 | tf_op jit(solution)/shard_map/all_gather | solution.py:141
  609.3 14.3 fusion.148
  623.6 3.0 fusion
  626.6 168.8 %all-gather.23.cloned.1.call-done = bf16[2048,8192]{1,0:T(8,128)(2,1)} async-done(((bf16[128,8192]{1,0:T(8,128)(2,1)}), bf16[2048,8192]{1,0:T(8,128)(2,1)}) %all-gather.23.cloned.1.call-update) | async-done | bytes 33554448 | tf_op jit(solution)/shard_map/all_gather | solution.py:142
  795.4 14.3 fusion.149
  809.7 3.2 multiply_convert_fusion.4
  815.0 166.5 %all-gather.25.cloned.1.call-done = bf16[8192,2048]{1,0:T(8,128)(2,1)} async-done(((bf16[512,2048]{1,0:T(8,128)(2,1)}), bf16[8192,2048]{1,0:T(8,128)(2,1)}) %all-gather.25.cloned.1.call-update) | async-done | bytes 33554448 | tf_op jit(solution)/shard_map/all_gather | solution.py:143
  981.5 14.0 fusion.150
  998.5 17.9 %fusion.151 = f32[144,8192]{1,0:T(8,128)} fusion(bf16[144,2048]{1,0:T(8,128)(2,1)S(1)} %fusion.97, bf16[8192,2048]{1,0:T(8,128)(2,1)} %all-gather.25.cloned.1.call-done), kind=kOutput, calls=%fused_computation.274 | convolution fusion | flops 4831838208 | bytes 38862848 | tf_op jit(solution)/shard_map/gte,de->gtd/dot_general | solution.py:83
  1016.4 8.0 multiply_convert_fusion.3
  1025.9 17.1 %fusion.153 = f32[144,2048]{1,0:T(8,128)} fusion(bf16[144,8192]{1,0:T(8,128)(2,1)S(1)} %get-tuple-element.13, bf16[2048,8192]{1,0:T(8,128)(2,1)} %all-gather.23.cloned.1.call-done), kind=kOutput, calls=%fused_computation.276 | convolution fusion | flops 4831838208 | bytes 37093376 | tf_op jit(solution)/shard_map/gte,de->gtd/dot_general | solution.py:83
  1045.6 17.5 %fusion.152 = f32[144,2048]{1,0:T(8,128)} fusion(bf16[144,8192]{1,0:T(8,128)(2,1)S(1)} %get-tuple-element.12, bf16[2048,8192]{1,0:T(8,128)(2,1)} %all-gather.21.cloned.1.call-done), kind=kOutput, calls=%fused_computation.275 | convolution fusion | flops 4831838208 | bytes 37093376 | tf_op jit(solution)/shard_map/gte,de->gtd/dot_general | solution.py:83
  1068.7 6.4 fusion.154
  1077.9 8.7 multiply_convert_fusion
  1086.7 3.9 multiply_convert_fusion.1
  1090.6 6.7 copy.67
  1097.6 5.7 fusion.64
  1103.7 2.7 reshape_reshape.3
  1106.4 9.7 convolution_convert_fusion
  1116.1 21.6 %copy.82 = bf16[1,1152,2048]{2,0,1:T(2,128)(2,1)} copy(bf16[1,1152,2048]{1,2,0:T(8,128)(2,1)} %bitcast.430) | data formatting | bytes 9437184
  1137.7 9.1 copy.155
  1152.5 3.5 broadcast_multiply_fusion.3
  1156.0 4.4 broadcast_multiply_fusion
  1160.4 4.3 reshape.1215
  1164.7 9.1 multiply_subtract_fusion.1
  1173.8 4.0 pad_maximum_fusion
  1177.8 4.4 reshape.1204
  1182.2 5.3 pad_maximum_fusion.1
  1187.5 4.7 reshape.1207
  1197.6 12.6 reduce-scatter.7.cloned.1.call-done
  1210.2 2.8 reshape_bitcast_fusion
  1219.6 3.1 broadcast_multiply_fusion.2
  1222.6 3.5 broadcast_multiply_fusion.1
  1227.3 6.4 fusion.156
  1234.1 7.6 fusion.86
  1242.7 2.9 fusion.155
  1247.0 209.7 %all-reduce.3.cloned.1.call-done = (f32[8,6,16,2048]{3,2,1,0:T(8,128)}, f32[8,16,8192]{2,1,0:T(8,128)}, f32[8,5,16,2048]{3,2,1,0:T(8,128)}, f32[8,2,16,8192]{3,2,1,0:T(8,128)}) async-done(((f32[8,6,16,2048]{3,2,1,0:T(8,128)}, f32[8,16,8192]{2,1,0:T(8,128)}, f32[8,5,16,2048]{3,2,1,0:T(8,128)}, f32[8,2,16,8192]{3,2,1,0:T(8,128)}), (f32[8,6,16,2048]{3,2,1,0:T(8,128)}, f32[8,16,8192]{2,1,0:T(8,128)}, ...) | async-done | bytes 24117264 | tf_op jit(solution)/shard_map/psum | solution.py:323
  1456.7 6.8 copy.173
  1465.7 2.7 copy.175
  1470.4 3.9 copy.176
  (289 shorter events, 73.8 us)
Async XLA Ops:
  7.2 9.8 copy-start
  7.2 79.2 %all-gather.15.cloned.1.call-start = ((), (), s32[]{:S(2)}) async-start(), calls=%async_computation.4 | async-start | bytes 8912896 | tf_op jit(solution)/shard_map/all_gather | solution.py:138
  7.9 151.8 %all-gather.13.cloned.1.call-start = ((), (), s32[]{:S(2)}) async-start(), calls=%async_computation.3 | async-start | bytes 8912896 | tf_op jit(solution)/shard_map/all_gather | solution.py:137
  8.7 224.4 %all-gather.11.cloned.1.call-start = ((), (), s32[]{:S(2)}) async-start(), calls=%async_computation.2 | async-start | bytes 8912896 | tf_op jit(solution)/shard_map/all_gather | solution.py:139
  9.4 278.3 %all-gather.17.cloned.1.call-start = ((), (), s32[]{:S(2)}) async-start(), calls=%async_computation.5 | async-start | bytes 5308416 | tf_op jit(solution)/shard_map/all_gather | solution.py:171
  19.3 4.8 copy-start.70
  19.3 67.1 %copy-start.2 = (bf16[1,144,2048]{2,1,0:T(8,128)(2,1)S(1)}, bf16[1,144,2048]{2,1,0:T(8,128)(2,1)}, u32[]{:S(2)}) copy-start(bf16[1,144,2048]{2,1,0:T(8,128)(2,1)} %param.16) | copy-start | bytes 1769476
  19.6 1055.5 %copy-start.39 = (bf16[1,6,16,2048]{3,2,1,0:T(8,128)(2,1)}, bf16[1,6,16,2048]{3,2,1,0:T(8,128)(2,1)S(1)}, u32[]{:S(2)}) copy-start(bf16[1,6,16,2048]{3,2,1,0:T(8,128)(2,1)S(1)} %copy.157) | copy-start | bytes 1179652
  21.4 148.5 %copy-start.49 = (f32[144,64]{1,0:T(8,128)}, f32[144,64]{1,0:T(8,128)S(1)}, u32[]{:S(2)}) copy-start(f32[144,64]{1,0:T(8,128)S(1)} %get-tuple-element.34) | copy-start | bytes 110596
  22.7 68.4 %copy-start.56 = (bf16[16,144]{1,0:T(8,128)(2,1)}, bf16[16,144]{1,0:T(8,128)(2,1)S(1)}, u32[]{:S(2)}) copy-start(bf16[16,144]{1,0:T(8,128)(2,1)S(1)} %convolution_convert_fusion.4) | copy-start | bytes 13828
  24.1 140.4 %copy-start.58 = (bf16[16,144]{1,0:T(8,128)(2,1)}, bf16[16,144]{1,0:T(8,128)(2,1)S(1)}, u32[]{:S(2)}) copy-start(bf16[16,144]{1,0:T(8,128)(2,1)S(1)} %convolution_convert_fusion.5) | copy-start | bytes 13828
  24.2 68.9 %copy-start.52 = (f32[1,2048]{1,0:T(1,128)}, f32[1,2048]{1,0:T(1,128)S(1)}, u32[]{:S(2)}) copy-start(f32[1,2048]{1,0:T(1,128)S(1)} %get-tuple-element.29) | copy-start | bytes 24580
  24.2 142.2 %copy-start.54 = (f32[1,2048]{1,0:T(1,128)}, f32[1,2048]{1,0:T(1,128)S(1)}, u32[]{:S(2)}) copy-start(f32[1,2048]{1,0:T(1,128)S(1)} %get-tuple-element.30) | copy-start | bytes 24580
  92.5 3.9 copy-start.11
  165.8 4.1 copy-start.13
  187.1 158.9 %all-gather.27.cloned.1.call-start = ((), (), s32[]{:S(2)}) async-start(), calls=%async_computation.11 | async-start | bytes 5308416 | tf_op jit(solution)/shard_map/all_gather | solution.py:172
  187.4 50.4 %copy-start.60 = (bf16[16,144]{1,0:T(8,128)(2,1)}, bf16[16,144]{1,0:T(8,128)(2,1)S(1)}, u32[]{:S(2)}) copy-start(bf16[16,144]{1,0:T(8,128)(2,1)S(1)} %convolution_convert_fusion.6) | copy-start | bytes 13828
  239.8 183.1 %all-gather.19.cloned.1.call-start = ((), (), s32[]{:S(2)}) async-start(), calls=%async_computation.6 | async-start | bytes 8912896 | tf_op jit(solution)/shard_map/all_gather | solution.py:140
  240.4 368.9 %all-gather.21.cloned.1.call-start = ((), (), s32[]{:S(2)}) async-start(), calls=%async_computation.7 | async-start | bytes 35651584 | tf_op jit(solution)/shard_map/all_gather | solution.py:141
  241.2 554.2 %all-gather.23.cloned.1.call-start = ((), (), s32[]{:S(2)}) async-start(), calls=%async_computation.8 | async-start | bytes 35651584 | tf_op jit(solution)/shard_map/all_gather | solution.py:142
  241.9 739.6 %all-gather.25.cloned.1.call-start = ((), (), s32[]{:S(2)}) async-start(), calls=%async_computation.9 | async-start | bytes 35651584 | tf_op jit(solution)/shard_map/all_gather | solution.py:143
  242.7 917.7 %reduce-scatter.5.cloned.1.call-start = ((), (), s32[]{:S(2)}) async-start(), calls=%async_computation.10 | async-start | bytes 5308416 | tf_op jit(solution)/shard_map/reduce_scatter | solution.py:271
  243.0 8.7 copy-start.43
  250.3 4.7 copy-start.72
  262.4 31.9 %copy-start.27 = (bf16[144,16,128]{2,1,0:T(8,128)(2,1)}, bf16[144,16,128]{2,1,0:T(8,128)(2,1)S(1)}, u32[]{:S(2)}) copy-start(bf16[144,16,128]{2,1,0:T(8,128)(2,1)S(1)} %convert_element_type.262) | copy-start | bytes 1769476
  299.1 3.9 copy-start.3
  356.2 71.5 %copy-start.29 = (bf16[1,144,16,128]{3,2,1,0:T(8,128)(2,1)}, bf16[1,144,16,128]{3,2,1,0:T(8,128)(2,1)S(1)}, u32[]{:S(2)}) copy-start(bf16[1,144,16,128]{3,2,1,0:T(8,128)(2,1)S(1)} %copy.60) | copy-start | bytes 1769476
  356.5 71.3 %copy-start.64 = (bf16[144,16]{0,1:T(8,128)(2,1)}, bf16[144,16]{0,1:T(8,128)(2,1)S(1)}, u32[]{:S(2)}) copy-start(bf16[144,16]{0,1:T(8,128)(2,1)S(1)} %convolution_convert_fusion.3) | copy-start | bytes 13828
  429.0 194.6 %copy-start.15 = (f32[144,2048]{1,0:T(8,128)}, f32[144,2048]{1,0:T(8,128)S(1)}, u32[]{:S(2)}) copy-start(f32[144,2048]{1,0:T(8,128)S(1)} %get-tuple-element.52) | copy-start | bytes 3538948
  430.8 378.9 %copy-start.66 = (bf16[144,16]{0,1:T(8,128)(2,1)}, bf16[144,16]{0,1:T(8,128)(2,1)S(1)}, u32[]{:S(2)}) copy-start(bf16[144,16]{0,1:T(8,128)(2,1)S(1)} %convolution_convert_fusion.1) | copy-start | bytes 13828
  431.0 192.6 %copy-start.62 = (bf16[144,16]{0,1:T(8,128)(2,1)}, bf16[144,16]{0,1:T(8,128)(2,1)S(1)}, u32[]{:S(2)}) copy-start(bf16[144,16]{0,1:T(8,128)(2,1)S(1)} %convolution_convert_fusion.2) | copy-start | bytes 13828
  431.0 192.6 %copy-start.37 = (bf16[1,2,16,8192]{3,2,1,0:T(8,128)(2,1)S(1)}, bf16[1,2,16,8192]{3,2,1,0:T(8,128)(2,1)}, u32[]{:S(2)}) copy-start(bf16[1,2,16,8192]{3,2,1,0:T(8,128)(2,1)} %copy.156) | copy-start | bytes 1572868
  795.4 14.3 copy-start.35
  809.7 4.6 copy-start.45
  815.0 180.5 %copy-start.31 = (bf16[1,144,2048]{2,1,0:T(8,128)(2,1)S(1)}, bf16[1,144,2048]{2,1,0:T(8,128)(2,1)}, u32[]{:S(2)}) copy-start(bf16[1,144,2048]{2,1,0:T(8,128)(2,1)} %param.17) | copy-start | bytes 1769476
  998.5 17.9 %copy-start.68 = (bf16[144,16]{0,1:T(8,128)(2,1)}, bf16[144,16]{0,1:T(8,128)(2,1)S(1)}, u32[]{:S(2)}) copy-start(bf16[144,16]{0,1:T(8,128)(2,1)S(1)} %fusion.77) | copy-start | bytes 13828
  1016.3 8.1 copy-start.38
  1024.4 21.2 %copy-start.6 = (bf16[144,8192]{1,0:T(8,128)(2,1)}, bf16[144,8192]{1,0:T(8,128)(2,1)S(1)}, u32[]{:S(2)}) copy-start(bf16[144,8192]{1,0:T(8,128)(2,1)S(1)} %get-tuple-element.12) | copy-start | bytes 7077892
  1045.6 17.5 %copy-start.16 = (f32[144,2048]{1,0:T(8,128)S(1)}, f32[144,2048]{1,0:T(8,128)}, u32[]{:S(2)}) copy-start(f32[144,2048]{1,0:T(8,128)} %copy-done.15) | copy-start | bytes 3538948
  1045.6 17.5 %copy-start.33 = (bf16[1,144,2048]{2,1,0:T(8,128)(2,1)S(1)}, bf16[1,144,2048]{2,1,0:T(8,128)(2,1)}, u32[]{:S(2)}) copy-start(bf16[1,144,2048]{2,1,0:T(8,128)(2,1)} %param.17) | copy-start | bytes 1769476
  1065.4 12.5 slice-start
  1068.6 9.3 slice-start.1
  1077.9 8.7 copy-start.28
  1086.7 3.9 copy-start.10
  1097.4 112.8 %reduce-scatter.7.cloned.1.call-start = ((), (), s32[]{:S(2)}) async-start(), calls=%async_computation.12 | async-start | bytes 5308416
  1137.7 9.1 copy-start.7
  1137.7 9.1 copy-start.63
  1137.7 10.3 copy-start.67
  1151.1 305.6 %all-reduce.3.cloned.1.call-start = ((), (), s32[]{:S(2)}) async-start(), calls=%async_computation.13 | async-start | bytes 48234496 | tf_op jit(solution)/shard_map/psum | solution.py:323
  1160.4 4.3 copy-start.50
  1160.4 4.3 copy-start.51
  1187.5 4.7 copy-start.55
  1187.5 6.8 copy-start.12
  1187.5 6.8 copy-start.53
  1197.6 12.6 copy-start.47
  1197.6 18.2 %copy-start.61 = (bf16[16,144]{1,0:T(8,128)(2,1)S(1)}, bf16[16,144]{1,0:T(8,128)(2,1)}, u32[]{:S(2)}) copy-start(bf16[16,144]{1,0:T(8,128)(2,1)} %copy-done.60) | copy-start | bytes 13828
  1227.3 6.4 copy-start.40
  1227.3 14.7 slice-start.3
  1234.0 8.0 slice-start.4
  1456.7 6.8 copy-start.36
  1456.7 9.0 copy-start.34
  1463.5 5.3 slice-start.5
  1465.7 4.8 slice-start.6
  1470.4 4.2 copy-start.1
  (36 other events, 73.5 us)
Sparse Core Ops, SparseCore 0:
  10.5 75.8 all-gather.14
  88.9 70.7 all-gather.12
  162.2 70.7 all-gather.10
  235.1 52.5 all-gather.16
  289.7 56.2 all-gather.26
  348.4 74.5 all-gather.18
  425.4 183.8 all-gather.20
  611.8 183.5 all-gather.22
  797.9 183.5 all-gather.24
  1097.5 52.8 reduce-scatter.4
  1153.4 56.8 reduce-scatter.6
  1226.3 230.3 all-reduce.2
where the time goes:
time: 1490 us; the launch traced here: 1480 us
  waiting for transfers between devices  1040 us (70%)
  matrix products  244 us (16%)
  local copies, waits for them, and re-layouts  111 us (7%)
  other arithmetic  67.6 us (5%)
  between operations  16.1 us (1%)
    psum x1, waiting for transfers between devices, on_device(): lax.psum((local_down_in, local_down_ff, local_up_model, local_up_hidden),...  210 us
    all_gather x1, waiting for transfers between devices, on_device(): lax.all_gather(gate_matrix, 'shard', axis=0, tiled=True)  178 us
    all_gather x1, waiting for transfers between devices, on_device(): lax.all_gather(upward_matrix, 'shard', axis=0, tiled=True)  169 us
    all_gather x1, waiting for transfers between devices, on_device(): lax.all_gather(down_matrix, 'shard', axis=0, tiled=True)  166 us
    dot_general x7, matrix products, project_back(): jnp.einsum('gte,de->gtd', grad, weight, preferred_element_type=jnp.float32)  75.8 us
    all_gather x1, waiting for transfers between devices, on_device(): lax.all_gather(output_matrix, 'shard', axis=0, tiled=True)  66.5 us
    unnamed x185, local copies, waits for them, and re-layouts  64.2 us
    all_gather x1, waiting for transfers between devices, on_device(): lax.all_gather(query_matrix, 'shard', axis=0, tiled=True)  63.3 us
  transfers between devices with their start and end apart: 12, of which 11 were waited for; matrix products, arithmetic and copies ran while one was open for 18% of the time, Pallas kernels for 0%

commit v1 on v0

v1 whole, which is shorter than its diff:
```python
import jax
import jax.numpy as jnp
from jax import lax
from jax.experimental import pallas as pl
from jax.experimental.pallas import tpu as pltpu
from jax.sharding import Mesh, PartitionSpec as P

HD = 128
PROMPT = 1024
ROWS = 144
TOTAL = 1152
D = 2048
HALF = 1024
FF = 4096
RANK = 16
SCALE = HD**-0.5
EPS = 1e-06
BASE = 500000.0
ALL = ("yl", "x", "z", "yh", "c")
CTX = ("yl", "x")
BF = jnp.bfloat16
F32 = jnp.float32
CUT_A = (1536, 512)
CUT_G = (3072, 2560)
CUT_D = (512, 512)
EARLY, LATE = 2176, 768


DEPTH = 4
ORDER = (
    "sA0", "czA", "sM0", "sA1", "czD", "sA2", "pzA", "sM1", "cxA", "y0A0",
    "pxA", "sM2", "czG", "y1A0", "z0A0", "z0G0", "pzG", "cxG", "z1A0", "y1A1",
    "z0A1", "pxG", "cxD", "z1A1", "y0A1", "pzD", "z0A2", "y0A2", "z1A2", "y1A2",
    "y1D0", "z1G0", "pxD", "y0G0", "z0G1", "y1G0", "z0D0", "y0G1", "z1G1", "y1G1",
    "z0G2", "z1G2", "y0G2", "z1D0", "y1G2", "y0D0", "z0D1", "z1D1", "y0D1", "y1D1",
    "z0D2", "z1D2", "y1D2", "y0D2",
)


def _place(yl, x, z, yh, c):
    return (((yl * 4 + x) * 4 + z) * 2 + yh) * 2 + c


def _permutation(move):
    pairs = []
    for yl in range(2):
        for x in range(4):
            for z in range(4):
                for yh in range(2):
                    for c in range(2):
                        nx, ny, nz, nc = move(x, 2 * yh + yl, z, c)
                        pairs.append(
                            (_place(yl, x, z, yh, c), _place(ny % 2, nx % 4, nz % 4, (ny % 4) // 2, nc))
                        )
    return pairs


STEPS = {
    "y": _permutation(lambda x, y, z, c: (x, (y + 1 - 2 * c) % 4, z, c)),
    "z": _permutation(lambda x, y, z, c: (x, y, z + 1 - 2 * c, c)),
    "cross": _permutation(lambda x, y, z, c: (x, 3 - y, z, c)),
    "pair": _permutation(lambda x, y, z, c: (x, y ^ 1, z, c)),
    "core": _permutation(lambda x, y, z, c: (x, y, z, 1 - c)),
}


def swap(value):
    return lax.ppermute(value, ALL, STEPS["core"])


class Queue:
    def __init__(self, depth):
        self.depth = depth
        self.sent = []

    def send(self, value, how):
        if len(self.sent) >= self.depth:
            value, _ = lax.optimization_barrier((value, self.sent[-self.depth]))
        got = lax.ppermute(value, ALL, STEPS[how])
        self.sent.append(got)
        return got


def _smem():
    return pl.BlockSpec(memory_space=pltpu.SMEM)


def _vmem():
    return pl.BlockSpec(memory_space=pltpu.VMEM)


def _plain(body, name, outs, ins, scalars, scratch=(), limit=48):
    size = sum(v.size * v.dtype.itemsize for v in list(ins) + list(outs))
    return pl.pallas_call(
        body,
        out_shape=outs,
        in_specs=[_smem()] * len(scalars) + [_vmem()] * len(ins),
        out_specs=[_vmem()] * len(outs),
        scratch_shapes=list(scratch),
        compiler_params=pltpu.CompilerParams(vmem_limit_bytes=limit * 2**20),
        cost_estimate=pl.CostEstimate(flops=0, bytes_accessed=size, transcendentals=0),
        name=name,
    )(*scalars, *ins)


def bf(*shape):
    return jax.ShapeDtypeStruct(shape, BF)


def split_a(core, q, k, v):
    def body(core, q, k, v, keep, give):
        for n, w in enumerate((q, k, v)):
            for h in range(8):
                here = slice(n * HALF + HD * h, n * HALF + HD * (h + 1))
                keep[:, here] = w[:, pl.ds(pl.multiple_of((2 * h + core[0]) * HD, HD), HD)]
                give[:, here] = w[:, pl.ds(pl.multiple_of((2 * h + 1 - core[0]) * HD, HD), HD)]

    return _plain(body, "split_a", [bf(HD, 3 * HALF)] * 2, [q, k, v], [core])


def split_g(core, gate, upward):
    def body(core, gate, upward, keep, give):
        for m in range(FF // 128):
            for n, w in enumerate((gate, upward)):
                here = slice(256 * m + 128 * n, 256 * m + 128 * (n + 1))
                for side, out in ((core[0], keep), (1 - core[0], give)):
                    start = (2 * (m // 4) + side) * 512 + (m % 4) * 128
                    out[:, here] = w[:, pl.ds(pl.multiple_of(start, 128), 128)]

    return _plain(body, "split_g", [bf(HD, 2 * FF)] * 2, [gate, upward], [core])


def parts_a(me, keep, got, out):
    cx, cy = CUT_A
    cz = 4 * HALF - cx - cy
    first = 3 * HALF - cx - cy

    def body(me, keep, got, out, zpart, small):
        for side, w in ((me[CORE], keep), (1 - me[CORE], got)):
            rows = pl.ds(pl.multiple_of(side * HD, HD), HD)
            zpart[rows, :first] = w[:, cx + cy :]
            small[rows, : cx // 4] = w[:, pl.ds(pl.multiple_of(me[X] * (cx // 4), 128), cx // 4)]
            small[rows, cx // 4 :] = w[:, pl.ds(pl.multiple_of(cx + me[YL] * (cy // 2), 128), cy // 2)]
        zpart[:HD, first:] = out[:, :HALF]
        zpart[HD:, first:] = out[:, HALF:]

    return _plain(body, "parts_a", [bf(256, cz), bf(256, cx // 4 + cy // 2)], [keep, got, out], [me])


def parts_m(me, keep, got, down):
    gx, gy = CUT_G
    dx, dy = CUT_D
    gz, dz = 2 * FF - gx - gy, D - dx - dy
    widths = [gx // 4, gy // 2, dx // 4, dx // 4, dy // 2, dy // 2]
    starts = [sum(widths[:n]) for n in range(7)]

    def body(me, keep, got, down, zg, zd, small):
        for side, w in ((me[CORE], keep), (1 - me[CORE], got)):
            rows = pl.ds(pl.multiple_of(side * HD, HD), HD)
            zg[rows, :] = w[:, gx + gy :]
            small[rows, : starts[1]] = w[:, pl.ds(pl.multiple_of(me[X] * (gx // 4), 128), gx // 4)]
            small[rows, starts[1] : starts[2]] = w[:, pl.ds(pl.multiple_of(gx + me[YL] * (gy // 2), 128), gy // 2)]
        zd[...] = down[:, dx + dy :]
        for n in range(2):
            rows = slice(256 * n, 256 * (n + 1))
            small[:, starts[2 + n] : starts[3 + n]] = down[rows, pl.ds(pl.multiple_of(me[X] * (dx // 4), 128), dx // 4)]
            small[:, starts[4 + n] : starts[5 + n]] = down[
                rows, pl.ds(pl.multiple_of(dx + me[YL] * (dy // 2), 128), dy // 2)
            ]

    return _plain(body, "parts_m", [bf(256, gz), bf(512, dz), bf(256, starts[6])], [keep, got, down], [me])


def spread(me, got, column, rows, cut):
    wx, wy, fold = cut[0] // 4, cut[1] // 2, rows // 256

    def body(me, *refs):
        chunks, (xs, y0, y1) = refs[:4], refs[4:]
        for k in range(4):
            z = me[Z0 + k]
            for n in range(fold):
                start = column + n * wx
                at = pl.multiple_of(z * rows + 256 * n, 256)
                xs[pl.ds(at, 256), :] = chunks[k][:, start : start + wx]
                start = column + fold * wx + n * wy
                for half, out in ((0, y0), (1, y1)):

                    @pl.when(z // 2 == half)
                    def _():
                        here = pl.ds(pl.multiple_of((z - 2 * half) * rows + 256 * n, 256), 256)
                        out[here, :] = chunks[k][:, start : start + wy]

    outs = [bf(4 * rows, wx), bf(2 * rows, wy), bf(2 * rows, wy)]
    return _plain(body, "spread", outs, list(got), [me]), column + fold * (wx + wy)


def join_x(me, own, near, far):
    rows = own.shape[0] // 4

    def body(me, own, near, far, out):
        for z in range(4):
            out[pl.ds(pl.multiple_of((2 * z + me[YH]) * rows, rows), rows), :] = own[z * rows : (z + 1) * rows]
        for z in range(2):
            for half, piece in ((me[YL], near), (1 - me[YL], far)):
                at = pl.multiple_of((2 * (2 * half + z) + 1 - me[YH]) * rows, rows)
                out[pl.ds(at, rows), :] = piece[z * rows : (z + 1) * rows]

    return _plain(body, "join_x", [bf(8 * rows, own.shape[1])], [own, near, far], [me])[0]


class Chunks:
    def __init__(self, rows, cut, width, places, xg, y, z):
        self.rows, self.cx, self.cy = rows, cut[0], cut[1]
        self.cz = width - sum(cut)
        self.depth = 8 * rows
        self.places = places
        self.arrays = [xg] + y[0] + y[1] + z[0] + z[1]


def _y_rows(places, rows, half, j, k):
    return pl.multiple_of((2 * half + j) * 2 * rows + places[0, k] * rows, rows)


def _z_rows(places, rows, half, k):
    return pl.multiple_of(places[2, k] * 2 * rows + places[3, half] * rows, rows)


def _assemble_body(w, places, *refs):
    rows, cx, cy, cz = w.rows, w.cx, w.cy, w.cz
    xg, y, z, out, sems = refs[0], refs[1:9], refs[9:17], refs[17], refs[18]
    copies = []
    for k in range(4):
        copies.append((xg.at[k], out.at[:, pl.ds(k * (cx // 4), cx // 4)]))
        column = pl.multiple_of(cx + places[1, k] * (cy // 2), 128)
        for half in range(2):
            for j in range(2):
                row = _y_rows(places, rows, half, j, k)
                copies.append(
                    (
                        y[4 * half + k].at[pl.ds(j * rows, rows)],
                        out.at[pl.ds(row, rows), pl.ds(column, cy // 2)],
                    )
                )
            row = _z_rows(places, rows, half, k)
            copies.append((z[4 * half + k], out.at[pl.ds(row, rows), pl.ds(cx + cy, cz)]))
    started = [pltpu.make_async_copy(s, d, sems.at[n]) for n, (s, d) in enumerate(copies)]
    for copy in started:
        copy.start()
    for copy in started:
        copy.wait()


def assemble(w):
    anywhere = pl.BlockSpec(memory_space=pl.ANY)
    width = w.cx + w.cy + w.cz

    def body(*refs):
        _assemble_body(w, *refs)

    return pl.pallas_call(
        body,
        out_shape=jax.ShapeDtypeStruct((w.depth, width), BF),
        in_specs=[pl.BlockSpec(memory_space=pltpu.SMEM)] + [anywhere] * 17,
        out_specs=pl.BlockSpec(memory_space=pltpu.VMEM),
        scratch_shapes=[pltpu.SemaphoreType.DMA((28,))],
        compiler_params=pltpu.CompilerParams(vmem_limit_bytes=48 * 2**20),
        cost_estimate=pl.CostEstimate(flops=0, bytes_accessed=4 * w.depth * width, transcendentals=0),
        name="assemble",
    )(w.places, *w.arrays)


class Resident:
    def __init__(self, w, panels, zcuts):
        self.w = w
        cx, cy, cz = w.cx, w.cy, w.cz
        self.panels, self.zcuts = panels, zcuts
        step = cx // 4 * panels
        self.pieces = [(n * step, step) for n in range(4 // panels)] + [(cx, cy)]
        self.pieces += [(cx + cy + n * (cz // zcuts), cz // zcuts) for n in range(zcuts)]

    def scratch(self):
        w = self.w
        return [pltpu.VMEM((w.depth, w.cx + w.cy + w.cz), BF), pltpu.SemaphoreType.DMA((20 + 8 * self.zcuts,))]

    def start(self, places, refs, whole, sems):
        w = self.w
        rows, cx, cy, cz = w.rows, w.cx, w.cy, w.cz
        xg, y, z = refs[0], refs[1:9], refs[9:17]
        pieces = [[] for _ in self.pieces]
        for k in range(4):
            pieces[k // self.panels].append((xg.at[k], whole.at[:, pl.ds(k * (cx // 4), cx // 4)]))
        first = 4 // self.panels
        part = cz // self.zcuts
        for k in range(4):
            column = pl.multiple_of(cx + places[1, k] * (cy // 2), 128)
            for half in range(2):
                for j in range(2):
                    row = _y_rows(places, rows, half, j, k)
                    pieces[first].append(
                        (
                            y[4 * half + k].at[pl.ds(j * rows, rows)],
                            whole.at[pl.ds(row, rows), pl.ds(column, cy // 2)],
                        )
                    )
                row = _z_rows(places, rows, half, k)
                for n in range(self.zcuts):
                    pieces[first + 1 + n].append(
                        (
                            z[4 * half + k].at[:, pl.ds(n * part, part)],
                            whole.at[pl.ds(row, rows), pl.ds(cx + cy + n * part, part)],
                        )
                    )
        numbers = [sum(len(p) for p in pieces[:n]) for n in range(len(pieces))]
        copies = [
            [pltpu.make_async_copy(a, b, sems.at[first + m]) for m, (a, b) in enumerate(piece)]
            for first, piece in zip(numbers, pieces)
        ]

        def begin(n):
            if n < len(copies):
                for copy in copies[n]:
                    copy.start()

        def arrive(n):
            for copy in copies[n]:
                copy.wait()

        begin(0)
        begin(1)
        return begin, arrive

    def forward(self, places, refs, whole, sems, x, tile, finish):
        begin, arrive = self.start(places, refs, whole, sems)
        for n, (start, width) in enumerate(self.pieces):
            arrive(n)
            begin(n + 2)
            for column in range(start, start + width, tile):
                size = min(tile, start + width - column)
                finish(jnp.dot(x[...], whole[:, column : column + size], preferred_element_type=F32), column)

    def backward(self, places, refs, whole, sems, dy, tile, finish):
        begin, arrive = self.start(places, refs, whole, sems)
        for n, (start, width) in enumerate(self.pieces):
            arrive(n)
            begin(n + 2)
            left = dy[:, start : start + width]
            for row in range(0, self.w.depth, tile):
                finish(lax.dot_general(left, whole[row : row + tile, start : start + width], **NT), row, n)

    def call(self, body, name, ins, outs, flops):
        w = self.w
        anywhere = pl.BlockSpec(memory_space=pl.ANY)
        size = 2 * w.depth * (w.cx + w.cy + w.cz) + sum(v.size * v.dtype.itemsize for v in ins)
        return pl.pallas_call(
            body,
            out_shape=outs,
            in_specs=[_smem()] + [anywhere] * 17 + [_vmem()] * len(ins),
            out_specs=[_vmem()] * len(outs),
            scratch_shapes=self.scratch(),
            compiler_params=pltpu.CompilerParams(vmem_limit_bytes=60 * 2**20),
            cost_estimate=pl.CostEstimate(flops=flops, bytes_accessed=size, transcendentals=0),
            name=name,
        )(w.places, *w.arrays, *ins)


def gate_and_up(w, x, low, up):
    rows = x.shape[0]
    plan = Resident(w, 1, 2)

    def body(places, *refs):
        weights, (x_ref, low_ref, up_ref, gu, mixed, whole, sems) = refs[:17], refs[17:]

        def finish(total, column):
            width = total.shape[1]
            total = total + jnp.dot(low_ref[...], up_ref[:, column : column + width], preferred_element_type=F32)
            gu[:, column : column + width] = total.astype(BF)
            unit = column // 2
            for m in range(width // 256):
                g, u = total[:, 256 * m : 256 * m + 128], total[:, 256 * m + 128 : 256 * m + 256]
                mixed[:, unit + 128 * m : unit + 128 * (m + 1)] = (g * jax.nn.sigmoid(g) * u).astype(BF)

        plan.forward(places, weights, whole, sems, x_ref, 768, finish)

    outs = [jax.ShapeDtypeStruct((rows, 2 * FF), BF), jax.ShapeDtypeStruct((rows, FF), BF)]
    return plan.call(body, "gate_and_up", [x, low, up], outs, 2 * rows * D * 2 * FF)


def down(w, x):
    rows = x.shape[0]
    plan = Resident(w, 2, 2)

    def body(places, *refs):
        weights, (x_ref, out, whole, sems) = refs[:17], refs[17:]

        def finish(total, column):
            out[:, column : column + total.shape[1]] = total

        plan.forward(places, weights, whole, sems, x_ref, 512, finish)

    return plan.call(body, "down", [x], [jax.ShapeDtypeStruct((rows, D), F32)], 2 * rows * D * FF)[0]


def down_back(w, dy, low, ff_down, gu):
    rows = dy.shape[0]
    plan = Resident(w, 4, 1)

    def body(places, *refs):
        weights, (dy_ref, low_ref, ff_ref, gu_ref, out, whole, sems, sums) = refs[:17], refs[17:]

        def finish(part_sum, row, part):
            units = slice(row, row + part_sum.shape[1])
            if part == 0:
                sums[:, units] = part_sum + jnp.dot(low_ref[...], ff_ref[:, units], preferred_element_type=F32)
            elif part == 1:
                sums[:, units] += part_sum
            else:
                d_mixed = sums[:, units] + part_sum
                column = 2 * row
                for m in range(part_sum.shape[1] // 128):
                    g = gu_ref[:, column + 256 * m : column + 256 * m + 128].astype(F32)
                    u = gu_ref[:, column + 256 * m + 128 : column + 256 * (m + 1)].astype(F32)
                    d = d_mixed[:, 128 * m : 128 * (m + 1)]
                    s = jax.nn.sigmoid(g)
                    out[:, column + 256 * m : column + 256 * m + 128] = (d * u * s * (1.0 + g * (1.0 - s))).astype(BF)
                    out[:, column + 256 * m + 128 : column + 256 * (m + 1)] = (d * g * s).astype(BF)

        plan.backward(places, weights, whole, sems, dy_ref, 1024, finish)

    outs = [jax.ShapeDtypeStruct((rows, 2 * FF), BF)]
    plan_scratch = plan.scratch
    plan.scratch = lambda: plan_scratch() + [pltpu.VMEM((rows, FF), F32)]
    return plan.call(body, "down_back", [dy, low, ff_down, gu], outs, 2 * rows * D * FF)[0]


def gate_and_up_back(w, dy):
    rows = dy.shape[0]
    plan = Resident(w, 2, 1)

    def body(places, *refs):
        weights, (dy_ref, out, whole, sems) = refs[:17], refs[17:]

        def finish(part_sum, row, part):
            units = slice(row, row + part_sum.shape[1])
            if part == 0:
                out[:, units] = part_sum
            else:
                out[:, units] += part_sum

        plan.backward(places, weights, whole, sems, dy_ref, 1024, finish)

    outs = [jax.ShapeDtypeStruct((rows, D), F32)]
    return plan.call(body, "gate_and_up_back", [dy], outs, 2 * rows * D * 2 * FF)[0]


CORE, X, YL, YH, Z0 = 0, 1, 2, 3, 4


class Gather:
    def __init__(self):
        core = lax.axis_index("c")
        x, z = lax.axis_index("x"), lax.axis_index("z")
        yl, yh = lax.axis_index("yl"), lax.axis_index("yh")
        y = 2 * yh + yl
        sign = 1 - 2 * core
        ys = [lax.rem(y - sign * k + 8, 4) for k in range(4)]
        zs = [lax.rem(z - sign * k + 8, 4) for k in range(4)]
        self.yl = yl
        self.me = jnp.stack([core, x, yl, yh] + zs).astype(jnp.int32)
        self.places = jnp.stack(
            [
                jnp.stack([v // 2 for v in ys]),
                jnp.stack([v % 2 for v in ys]),
                jnp.stack(zs),
                jnp.stack([yh, 1 - yh, yh, yh]),
            ]
        ).astype(jnp.int32)

    def halves(self, value):
        n = value.shape[0] // 2
        upper, lower = value[:n], value[n:]
        return jnp.where(self.yl == 0, upper, lower), jnp.where(self.yl == 0, lower, upper)


def gather_weights(plan, split, out_shard, split_m, down_shard):
    me = plan.me
    queue = Queue(DEPTH)
    state = {}
    shapes = {"A": (256, CUT_A, 4 * HALF), "G": (256, CUT_G, 2 * FF), "D": (512, CUT_D, D)}
    zpart = {}
    zpart["A"], small_a = parts_a(me, *split, out_shard)
    zpart["G"], zpart["D"], small_m = parts_m(me, *split_m, down_shard)
    ring = {"sA": [small_a], "sM": [small_m]}
    for g in "AGD":
        ring["z0" + g] = [zpart[g]]
    cross = {}

    def need(key):
        if key in ring or key in cross:
            return
        kind, g = key[:-1], key[-1]
        rows, cut, _ = shapes[g]
        if kind in ("y0", "y1", "x"):
            if g == "A":
                (xs, y0, y1), _ = spread(me, ring["sA"], 0, rows, cut)
                values = {"A": (xs, y0, y1)}
            else:
                values = {}
                values["G"], column = spread(me, ring["sM"], 0, *shapes["G"][:2])
                values["D"], _ = spread(me, ring["sM"], column, *shapes["D"][:2])
            for n, (xs, y0, y1) in values.items():
                cross["x" + n], ring["y0" + n], ring["y1" + n] = xs, [y0], [y1]
        elif kind == "z1":
            near, far = cross["near_z" + g], cross["far_z" + g]
            ring[key] = [
                jnp.where(plan.yl == 0, jnp.concatenate([near, far]), jnp.concatenate([far, near]))
            ]

    panels = {}
    for entry in ORDER:
        if entry[0] == "c":
            kind, g = entry[1], entry[2]
            if kind == "x":
                need("x" + g)
            source = cross["x" + g] if kind == "x" else zpart[g]
            cross["near_" + kind + g] = queue.send(plan.halves(source)[1], "cross")
        elif entry[0] == "p":
            kind, g = entry[1], entry[2]
            cross["far_" + kind + g] = queue.send(cross["near_" + kind + g], "pair")
            if kind == "x":
                full = join_x(me, cross["x" + g], cross["near_x" + g], cross["far_x" + g])
                panels[g] = lax.all_gather(full, "x")
        else:
            key = entry[:-1]
            need(key)
            ring[key].append(queue.send(ring[key][-1], "y" if key[0] == "y" else "z"))
    chunks = []
    for g in "AGD":
        rows, cut, width = shapes[g]
        y, z = (ring["y0" + g], ring["y1" + g]), (ring["z0" + g], ring["z1" + g])
        chunks.append(Chunks(rows, cut, width, plan.places, panels[g], y, z))
    return chunks


def turn(value, cosine, sine):
    return value * cosine + pltpu.roll(value, 64, 1) * sine


def _pack_body(me, q, k, v, scales, gains, cosine, sine, out):
    c, s = cosine[...], sine[...]
    out[0, :, 0:HD] = turn(q[...] * scales[:, 0:1] * gains[0:1], c, s).astype(BF)
    out[0, :, HD : 2 * HD] = turn(k[...] * scales[:, 1:2] * gains[1:2], c, s).astype(BF)
    out[0, :, 2 * HD :] = v[...].astype(BF)


def pack_heads(me, qkv, scales, gains, cosine, sine):
    rows = qkv.shape[0]
    whole = lambda shape: pl.BlockSpec(shape, lambda i, me: (0, 0))
    return pl.pallas_call(
        _pack_body,
        out_shape=jax.ShapeDtypeStruct((8, rows, 3 * HD), BF),
        grid_spec=pltpu.PrefetchScalarGridSpec(
            num_scalar_prefetch=1,
            grid=(8,),
            in_specs=[
            pl.BlockSpec((rows, HD), lambda i, me: (0, i)),
            pl.BlockSpec((rows, HD), lambda i, me: (0, 8 + i)),
            pl.BlockSpec((rows, HD), lambda i, me: (0, 16 + i)),
            whole((rows, 2)),
            pl.BlockSpec((4, HD), lambda i, me: (0, 2 * i + me[CORE])),
            whole((rows, HD)),
            whole((rows, HD)),
        ],
            out_specs=pl.BlockSpec((1, rows, 3 * HD), lambda i, me: (i, 0, 0)),
        ),
        name="pack_heads",
    )(me, qkv, qkv, qkv, scales, gains, cosine, sine)


def _unpack_body(me, d, q, k, gains, cosine, sine, wq, wk, dv, sums):
    c, s = cosine[...], -sine[...]
    i = pl.program_id(0)
    gq = turn(d[0, :, 0:HD].astype(F32), c, s) * gains[0:1]
    gk = turn(d[0, :, HD : 2 * HD].astype(F32), c, s) * gains[1:2]
    wq[...] = gq
    wk[...] = gk
    dv[...] = d[0, :, 2 * HD :]

    @pl.when(i == 0)
    def _():
        sums[...] = jnp.zeros_like(sums)

    sums[:, 0:HD] += gq * q[...]
    sums[:, HD:] += gk * k[...]


def unpack_heads(me, d, qkv, gains, cosine, sine):
    rows = qkv.shape[0]
    whole = lambda shape: pl.BlockSpec(shape, lambda i, me: (0, 0))
    column = pl.BlockSpec((rows, HD), lambda i, me: (0, i))
    return pl.pallas_call(
        _unpack_body,
        out_shape=[
            jax.ShapeDtypeStruct((rows, HALF), F32),
            jax.ShapeDtypeStruct((rows, HALF), F32),
            jax.ShapeDtypeStruct((rows, HALF), BF),
            jax.ShapeDtypeStruct((rows, 2 * HD), F32),
        ],
        grid_spec=pltpu.PrefetchScalarGridSpec(
            num_scalar_prefetch=1,
            grid=(8,),
            in_specs=[
            pl.BlockSpec((1, rows, 3 * HD), lambda i, me: (i, 0, 0)),
            pl.BlockSpec((rows, HD), lambda i, me: (0, i)),
            pl.BlockSpec((rows, HD), lambda i, me: (0, 8 + i)),
            pl.BlockSpec((4, HD), lambda i, me: (0, 2 * i + me[CORE])),
            whole((rows, HD)),
            whole((rows, HD)),
        ],
            out_specs=[column, column, column, whole((rows, 2 * HD))],
        ),
        name="unpack_heads",
    )(me, d, qkv, qkv, gains, cosine, sine)


TILE = 128
NT = dict(dimension_numbers=(((1,), (1,)), ((), ())), preferred_element_type=F32)
TN = dict(dimension_numbers=(((0,), (0,)), ((), ())), preferred_element_type=F32)


def hidden_pairs(t, bound):
    query = t * TILE + lax.broadcasted_iota(jnp.int32, (TILE, TILE), 0)
    key = t * TILE + lax.broadcasted_iota(jnp.int32, (TILE, TILE), 1)
    hidden = key > query
    if t * TILE >= PROMPT:
        hidden = hidden | ((query >= bound) & (key < bound))
    return hidden


def tile_scores(q, k, t, bound):
    n = (t + 1) * TILE
    s = lax.dot_general(q[t * TILE : n], k[:n], **NT) * SCALE
    last = jnp.where(hidden_pairs(t, bound), -1e30, s[:, n - TILE :])
    return last if t == 0 else jnp.concatenate([s[:, : n - TILE], last], axis=1)


def _attend_body(bounds, qkv, out, exact, total):
    bound = bounds[pl.program_id(0)]
    q = qkv[:, 0, :, 0:HD].reshape(TOTAL, HD)
    k = qkv[:, 0, :, HD : 2 * HD].reshape(TOTAL, HD)
    v = qkv[:, 0, :, 2 * HD :].reshape(TOTAL, HD)
    for t in range(TOTAL // TILE):
        n = (t + 1) * TILE
        s = tile_scores(q, k, t, bound)
        top = jnp.max(s, axis=1, keepdims=True)
        p = jnp.exp(s - top)
        denom = jnp.sum(p, axis=1, keepdims=True)
        o = jnp.dot(p.astype(BF), v[:n], preferred_element_type=F32) / denom
        exact[0, t * TILE : n] = o
        total[0, t * TILE : n] = top + jnp.log(denom)
    out[:, 0] = exact[0].reshape(8, ROWS, HD).astype(BF)


def attend(bounds, qkv):
    return pl.pallas_call(
        _attend_body,
        grid=(2,),
        out_shape=[
            jax.ShapeDtypeStruct((8, 2, ROWS, HD), BF),
            jax.ShapeDtypeStruct((2, TOTAL, HD), F32),
            jax.ShapeDtypeStruct((2, TOTAL, 1), F32),
        ],
        in_specs=[
            pl.BlockSpec(memory_space=pltpu.SMEM),
            pl.BlockSpec((8, 1, ROWS, 3 * HD), lambda g: (0, g, 0, 0)),
        ],
        out_specs=[
            pl.BlockSpec((8, 1, ROWS, HD), lambda g: (0, g, 0, 0)),
            pl.BlockSpec((1, TOTAL, HD), lambda g: (g, 0, 0)),
            pl.BlockSpec((1, TOTAL, 1), lambda g: (g, 0, 0)),
        ],
        compiler_params=pltpu.CompilerParams(vmem_limit_bytes=40 * 2**20),
        cost_estimate=pl.CostEstimate(flops=900_000_000, bytes_accessed=5_000_000, transcendentals=1_500_000),
        name="attend",
    )(bounds, qkv)


def _attend_back_body(bounds, qkv, grad, exact, total, out, dk, dv, dq):
    bound = bounds[pl.program_id(0)]
    q = qkv[:, 0, :, 0:HD].reshape(TOTAL, HD)
    k = qkv[:, 0, :, HD : 2 * HD].reshape(TOTAL, HD)
    v = qkv[:, 0, :, 2 * HD :].reshape(TOTAL, HD)
    g = grad[:, 0].reshape(TOTAL, HD)
    dk[...] = jnp.zeros_like(dk)
    dv[...] = jnp.zeros_like(dv)
    for t in range(TOTAL // TILE):
        n = (t + 1) * TILE
        here = slice(t * TILE, n)
        s = tile_scores(q, k, t, bound)
        p = jnp.exp(s - total[0, here])
        delta = jnp.sum(g[here].astype(F32) * exact[0, here], axis=1, keepdims=True)
        dp = lax.dot_general(g[here], v[:n], **NT)
        ds = (p * (dp - delta)).astype(BF)
        dq[here] = jnp.dot(ds, k[:n], preferred_element_type=F32) * SCALE
        dk[:n] += lax.dot_general(ds, q[here], **TN) * SCALE
        dv[:n] += lax.dot_general(p.astype(BF), g[here], **TN)
    out[:, 0, :, 0:HD] = dq[...].reshape(8, ROWS, HD).astype(BF)
    out[:, 0, :, HD : 2 * HD] = dk[...].reshape(8, ROWS, HD).astype(BF)
    out[:, 0, :, 2 * HD :] = dv[...].reshape(8, ROWS, HD).astype(BF)


def attend_back(bounds, qkv, grad, exact, total):
    return pl.pallas_call(
        _attend_back_body,
        grid=(2,),
        out_shape=jax.ShapeDtypeStruct((8, 2, ROWS, 3 * HD), BF),
        in_specs=[
            pl.BlockSpec(memory_space=pltpu.SMEM),
            pl.BlockSpec((8, 1, ROWS, 3 * HD), lambda g: (0, g, 0, 0)),
            pl.BlockSpec((8, 1, ROWS, HD), lambda g: (0, g, 0, 0)),
            pl.BlockSpec((1, TOTAL, HD), lambda g: (g, 0, 0)),
            pl.BlockSpec((1, TOTAL, 1), lambda g: (g, 0, 0)),
        ],
        out_specs=pl.BlockSpec((8, 1, ROWS, 3 * HD), lambda g: (0, g, 0, 0)),
        scratch_shapes=[pltpu.VMEM((TOTAL, HD), F32)] * 3,
        compiler_params=pltpu.CompilerParams(vmem_limit_bytes=40 * 2**20),
        cost_estimate=pl.CostEstimate(flops=2_300_000_000, bytes_accessed=8_000_000, transcendentals=1_500_000),
        name="attend_back",
    )(bounds, qkv, grad, exact, total)


def dot(a, b):
    return jnp.dot(a, b, preferred_element_type=F32)


def dot_nt(a, b):
    return lax.dot_general(a, b, **NT)


def dot_tn(a, b):
    return lax.dot_general(a, b, **TN)


def normalize_back(field, inverse, gain, grad):
    weighted = grad * gain
    return inverse * weighted - field * inverse**3 * jnp.mean(weighted * field, axis=-1, keepdims=True)


def choose_adapters(slots, down_in, down_ff, up_model, up_hidden):
    def body(slots, down_in, down_ff, up_model, up_hidden, qkv_down, gu_down, out_down, ff_down, qkv_up, out_up, ff_up, gu_up):
        core = slots[2]
        qkv_down[...] = down_in[0, :3].reshape(3 * RANK, D)
        gu_down[...] = down_in[0, 4:].reshape(2 * RANK, D)
        out_up[...] = up_model[0, 3]
        ff_up[...] = up_model[0, 4]
        qkv_up[...] = jnp.zeros_like(qkv_up)
        gu_up[...] = jnp.zeros_like(gu_up)
        for h in range(8):
            head = pl.ds(pl.multiple_of((2 * h + core) * HD, HD), HD)
            out_down[:, HD * h : HD * (h + 1)] = down_in[0, 3, :, head]
            for n in range(3):
                here = slice(n * HALF + HD * h, n * HALF + HD * (h + 1))
                qkv_up[n * RANK : (n + 1) * RANK, here] = up_model[0, n, :, head]
        for m in range(FF // 128):
            start = (2 * (m // 4) + core) * 512 + (m % 4) * 128
            units = pl.ds(pl.multiple_of(start, 128), 128)
            ff_down[:, 128 * m : 128 * (m + 1)] = down_ff[0, :, units]
            for n in range(2):
                here = slice(256 * m + 128 * n, 256 * m + 128 * (n + 1))
                gu_up[n * RANK : (n + 1) * RANK, here] = up_hidden[0, n, :, units]

    def chosen(shape):
        return pl.BlockSpec((1,) + shape[1:], lambda g, slots: (slots[g],) + (0,) * (len(shape) - 1))

    shapes = [(48, D), (32, D), (16, HALF), (16, FF), (48, 3 * HALF), (16, D), (16, D), (32, 2 * FF)]
    maps = [down_in, down_ff, up_model, up_hidden]
    return pl.pallas_call(
        body,
        out_shape=[bf(2 * r, c) for r, c in shapes],
        grid_spec=pltpu.PrefetchScalarGridSpec(
            num_scalar_prefetch=1,
            grid=(2,),
            in_specs=[chosen(m.shape) for m in maps],
            out_specs=[pl.BlockSpec(shape, lambda g, slots: (g, 0)) for shape in shapes],
        ),
        cost_estimate=pl.CostEstimate(flops=0, bytes_accessed=7_000_000, transcendentals=0),
        name="choose_adapters",
    )(slots, *maps)


def rank_gradients(lows, acts, core, name, plan, width):
    def body(core, *refs):
        lows, acts, out = refs[: len(lows_)], refs[len(lows_) : -1], refs[-1]
        at = 0
        for low, act, column, stride, starts in plan:
            picked = jnp.concatenate(
                [lows[low][:, g * stride + column : g * stride + column + RANK] for g in range(2)], axis=1
            )
            for start in starts(core[0]):
                right = acts[act][:, start if isinstance(start, slice) else pl.ds(pl.multiple_of(start, 128), 128)]
                n = right.shape[1]
                grad = lax.dot_general(picked, right, **TN).astype(BF)
                for b in range(n // 128):
                    block, slot = divmod(at, width // 128)
                    out[block, :, 128 * slot : 128 * (slot + 1)] = grad[:, 128 * b : 128 * (b + 1)]
                    at += 1

    lows_ = lows
    return _plain(body, name, [bf(8, 2 * RANK, width)], list(lows) + list(acts), [core])[0]


def adapter_outputs(core, early, early_other, late, late_other):
    shapes = [(8, 6, RANK, D), (8, RANK, 2 * FF), (8, 5, RANK, D), (8, 2, RANK, 2 * FF)]

    def body(core, early, early_other, late, late_other, down_in, down_ff, up_model, up_hidden):
        for side, e, l in ((core[0], early, late), (1 - core[0], early_other, late_other)):

            def piece(half, at):
                block, slot = divmod(at, half.shape[3] // 128)
                return half[block, 0, :, 128 * slot : 128 * (slot + 1)].astype(F32)

            def place(start):
                return pl.ds(pl.multiple_of(start, 128), 128)

            for m in range(FF // 128):
                units = place((2 * (m // 4) + side) * 512 + (m % 4) * 128)
                up_hidden[0, 0, :, units] = piece(e, m)
                up_hidden[0, 1, :, units] = piece(e, 32 + m)
                down_ff[0, :, units] = piece(e, 64 + m)
            for m in range(8):
                whole, head = place(side * HALF + 128 * m), place((2 * m + side) * HD)
                down_in[0, 4, :, whole] = piece(e, 96 + m)
                down_in[0, 5, :, whole] = piece(e, 104 + m)
                down_in[0, 3, :, head] = piece(e, 112 + m)
                up_model[0, 3, :, whole] = piece(e, 120 + m)
                up_model[0, 4, :, whole] = piece(e, 128 + m)
                for n in range(3):
                    down_in[0, n, :, whole] = piece(l, 8 * n + m)
                    up_model[0, n, :, head] = piece(l, 24 + 8 * n + m)

    halves = [early, early_other, late, late_other]
    return pl.pallas_call(
        body,
        grid=(8,),
        out_shape=[jax.ShapeDtypeStruct(s, F32) for s in shapes],
        in_specs=[_smem()] + [pl.BlockSpec((8, 1) + v.shape[2:], lambda i: (0, i, 0, 0)) for v in halves],
        out_specs=[pl.BlockSpec((1,) + s[1:], lambda i, n=len(s): (i,) + (0,) * (n - 1)) for s in shapes],
        compiler_params=pltpu.CompilerParams(vmem_limit_bytes=40 * 2**20),
        cost_estimate=pl.CostEstimate(flops=0, bytes_accessed=37_000_000, transcendentals=0),
        name="adapter_outputs",
    )(core, *halves)


def on_device(
    tokens,
    cotangent,
    query_matrix,
    key_matrix,
    value_matrix,
    output_matrix,
    gate_matrix,
    upward_matrix,
    down_matrix,
    gains,
    adapter_down_inputs,
    adapter_down_feedforward,
    adapter_up_model_maps,
    adapter_up_hidden_maps,
    group_adapter_index,
    continuation_lengths,
):
    core = lax.axis_index("c")
    first = core == 0
    ctx = lax.axis_index("yl") * 4 + lax.axis_index("x")
    tokens, cotangent = tokens[0], cotangent[0]

    def both(own, other):
        return jnp.where(first, jnp.stack([own, other]), jnp.stack([other, own]))

    def rows_of_both(own):
        return both(own, swap(own)).reshape(2 * own.shape[0], own.shape[1])

    def mine(pair):
        return jnp.where(first, pair[0], pair[1])

    def exchange_sum(part):
        upper, lower = part[:ROWS], part[ROWS:]
        sent = jnp.where(first, lower, upper)
        kept = jnp.where(first, upper, lower)
        return kept.astype(F32) + swap(sent.astype(BF)).astype(F32)

    plan = Gather()
    keep_a, give_a = split_a(plan.me, query_matrix, key_matrix, value_matrix)
    keep_g, give_g = split_g(plan.me, gate_matrix, upward_matrix)
    got_a, got_g = swap(give_a), swap(give_g)
    wa, wg, wd = gather_weights(plan, (keep_a, got_a), output_matrix, (keep_g, got_g), down_matrix)
    wa = assemble(wa)
    w_qkv = wa[:, : 3 * HALF]
    w_out = wa[:, 3 * HALF :].reshape(8, 2, HD, HALF).transpose(0, 2, 1, 3).reshape(HALF, D)

    facts = jnp.concatenate([group_adapter_index[0], continuation_lengths[0]]).astype(F32)
    facts = jnp.broadcast_to(jnp.pad(facts, (0, 125))[None], (8, 128))
    pair_facts = both(facts, swap(facts))[:, 0, :2].astype(jnp.int32)
    slots = pair_facts[:, 0]
    bounds = PROMPT + pair_facts[:, 1]
    (qkv_down, gu_down, out_down, ff_down, qkv_up, out_up2, ff_up2, gu_up) = choose_adapters(
        jnp.concatenate([slots, plan.me[:1]]),
        adapter_down_inputs,
        adapter_down_feedforward,
        adapter_up_model_maps,
        adapter_up_hidden_maps,
    )

    def of_own(maps):
        n = maps.shape[0] // 2
        return lax.dynamic_slice_in_dim(maps, core * n, n, 0)

    group_row = lax.broadcasted_iota(jnp.int32, (2 * ROWS, 1), 0) // ROWS

    def own_columns(low, count):
        group_column = lax.broadcasted_iota(jnp.int32, (1, 2 * count), 1) // count
        return jnp.where(group_row == group_column, low, jnp.zeros_like(low))

    place = ctx * ROWS + lax.broadcasted_iota(jnp.int32, (2, ROWS), 1)
    position = jnp.where(place >= bounds[:, None], PROMPT + place - bounds[:, None], place)
    freq = BASE ** (-(jnp.arange(HD // 2, dtype=F32) * 2.0 / HD))
    angle = position.reshape(2 * ROWS, 1).astype(F32) * freq[None]
    cosine = jnp.concatenate([jnp.cos(angle)] * 2, axis=1)
    sine = jnp.concatenate([-jnp.sin(angle), jnp.sin(angle)], axis=1)

    x2 = rows_of_both(tokens)
    qkv_low = own_columns((2.0 * dot_nt(x2, qkv_down).astype(BF)).astype(BF), 3 * RANK)
    qkv = dot(x2, w_qkv) + dot(qkv_low, qkv_up)
    q_pre, k_pre = qkv[:, :HALF], qkv[:, HALF : 2 * HALF]
    squares = jnp.stack([jnp.sum(q_pre * q_pre, axis=1), jnp.sum(k_pre * k_pre, axis=1)])
    squares = squares + swap(squares)
    inverse = lax.rsqrt(squares.T / D + EPS)
    packed = pack_heads(plan.me, qkv, inverse, gains, cosine, sine)
    heads = lax.all_to_all(packed, CTX, 0, 0, tiled=True).reshape(8, 2, ROWS, 3 * HD)
    out_heads, exact, log_total = attend(bounds, heads)
    attended = lax.all_to_all(out_heads, CTX, 0, 0, tiled=True).reshape(8, 2 * ROWS, HD)
    attended = jnp.swapaxes(attended, 0, 1).reshape(2 * ROWS, HALF)

    def fold_groups(low, count):
        return low[:, :count] + low[:, count:]

    part = dot(attended, w_out)
    part_low = fold_groups(own_columns(dot_nt(attended, out_down), RANK), RANK)
    summed = exchange_sum(jnp.concatenate([part, jnp.pad(part_low, ((0, 0), (0, 112)))], axis=1))
    out_low = summed[:, D : D + RANK].astype(BF)
    out_up = of_own(out_up2)
    attn_pre = summed[:, :D] + 2.0 * dot(out_low, out_up)
    attn_inverse = lax.rsqrt(jnp.mean(attn_pre * attn_pre, axis=1, keepdims=True) + EPS)
    hidden = tokens.astype(F32) + attn_pre * attn_inverse * gains[2]

    h2 = rows_of_both(hidden.astype(BF))
    gu_low = own_columns((2.0 * dot_nt(h2, gu_down).astype(BF)).astype(BF), 2 * RANK)
    gu, mixed = gate_and_up(wg, h2, gu_low, gu_up)
    part = down(wd, mixed)
    part_low = fold_groups(own_columns(dot_nt(mixed, ff_down), RANK), RANK)
    summed = exchange_sum(jnp.concatenate([part, jnp.pad(part_low, ((0, 0), (0, 112)))], axis=1))
    ff_low = summed[:, D : D + RANK].astype(BF)
    ff_up = of_own(ff_up2)
    mlp_pre = summed[:, :D] + 2.0 * dot(ff_low, ff_up)
    mlp_inverse = lax.rsqrt(jnp.mean(mlp_pre * mlp_pre, axis=1, keepdims=True) + EPS)
    output = (hidden + mlp_pre * mlp_inverse * gains[3]).astype(BF)

    cot = cotangent.astype(F32)
    d_mlp = rows_of_both(normalize_back(mlp_pre, mlp_inverse, gains[3], cot).astype(BF))
    ff_grad_low = own_columns((2.0 * dot_nt(d_mlp, ff_up2)).astype(BF), RANK)
    d_gu = down_back(wd, d_mlp, ff_grad_low, ff_down, gu)
    part = gate_and_up_back(wg, d_gu)
    part_low = own_columns(dot_nt(d_gu, gu_up), 2 * RANK)
    part_low = fold_groups(part_low, 2 * RANK)
    summed = exchange_sum(jnp.concatenate([part, jnp.pad(part_low, ((0, 0), (0, 96)))], axis=1))
    gu_grad_low = (2.0 * summed[:, D : D + 2 * RANK]).astype(BF)
    gu_down_own = of_own(gu_down)
    d_hidden = cot + summed[:, :D] + dot(gu_grad_low, gu_down_own)

    d_attn = rows_of_both(normalize_back(attn_pre, attn_inverse, gains[2], d_hidden).astype(BF))
    out_grad_low = own_columns((2.0 * dot_nt(d_attn, out_up2)).astype(BF), RANK)
    d_attended = (dot_nt(d_attn, w_out) + dot(out_grad_low, out_down)).astype(BF)
    d_out_heads = jnp.swapaxes(d_attended.reshape(2 * ROWS, 8, HD), 0, 1)
    d_out_heads = lax.all_to_all(d_out_heads, CTX, 0, 0, tiled=True).reshape(8, 2, ROWS, HD)
    d_heads = attend_back(bounds, heads, d_out_heads, exact, log_total)
    d_heads = lax.all_to_all(d_heads, CTX, 0, 0, tiled=True).reshape(8, 2 * ROWS, 3 * HD)
    w_q, w_k, d_v, sums = unpack_heads(plan.me, d_heads, qkv, gains, cosine, sine)
    sums = jnp.stack([jnp.sum(sums[:, :HD], axis=1), jnp.sum(sums[:, HD:], axis=1)])
    sums = ((sums + swap(sums)) / D).T
    d_q = inverse[:, :1] * w_q - q_pre * (inverse[:, :1] ** 3 * sums[:, :1])
    d_k = inverse[:, 1:] * w_k - k_pre * (inverse[:, 1:] ** 3 * sums[:, 1:])
    d_qkv = jnp.concatenate([d_q.astype(BF), d_k.astype(BF), d_v], axis=1)
    part = dot_nt(d_qkv, w_qkv)
    part_low = fold_groups(own_columns(dot_nt(d_qkv, qkv_up), 3 * RANK), 3 * RANK)
    summed = exchange_sum(jnp.concatenate([part, jnp.pad(part_low, ((0, 0), (0, 80)))], axis=1))
    qkv_grad_low = (2.0 * summed[:, D : D + 3 * RANK]).astype(BF)
    qkv_down_own = of_own(qkv_down)
    grad_tokens = (d_hidden + summed[:, :D] + dot(qkv_grad_low, qkv_down_own)).astype(BF)

    def low_of_both(own, count):
        pair = rows_of_both(jnp.pad(own, ((0, 0), (0, 128 - count))))[:, :count]
        return own_columns(jnp.concatenate([pair, pair], axis=1), count)

    def whole(n):
        return lambda core: [slice(0, n)]

    def half(core):
        return [core * HALF + 128 * m for m in range(8)]

    def turns(n):
        return lambda core: [slice(256 * m + 128 * n, 256 * m + 128 * (n + 1)) for m in range(FF // 128)]

    def third(n):
        return lambda core: [slice(n * HALF, (n + 1) * HALF)]

    shard = ("z", "yh")
    early = rank_gradients(
        [gu_low, ff_grad_low, low_of_both(gu_grad_low, 2 * RANK), out_grad_low]
        + [2 * low_of_both(out_low, RANK), 2 * low_of_both(ff_low, RANK)],
        [d_gu, mixed, h2, attended, d_attn, d_mlp],
        plan.me,
        "early_gradients",
        [
            (0, 0, 0, 2 * RANK, turns(0)),
            (0, 0, RANK, 2 * RANK, turns(1)),
            (1, 1, 0, RANK, whole(FF)),
            (2, 2, 0, 2 * RANK, half),
            (2, 2, RANK, 2 * RANK, half),
            (3, 3, 0, RANK, whole(HALF)),
            (4, 4, 0, RANK, half),
            (5, 5, 0, RANK, half),
        ],
        EARLY,
    )
    own = lax.psum_scatter(early.reshape(8 * 2 * RANK, EARLY), CTX, scatter_dimension=0, tiled=True)
    own_slot = jnp.repeat(slots, RANK)[:, None] == lax.broadcasted_iota(jnp.int32, (1, 128), 1)
    own = jnp.concatenate([own, own_slot.astype(BF)], axis=1)
    groups = lax.all_gather(own, shard).reshape(16, RANK, EARLY + 128)
    picker = groups[:, 0, EARLY : EARLY + 8]

    def by_slot(groups):
        flat = groups.reshape(16, -1)
        return lax.dot_general(picker, flat, **TN).astype(BF).reshape(8 * RANK, -1)

    early = lax.all_gather(by_slot(groups[:, :, :EARLY]), CTX)
    early_other = swap(early)
    qkv_grad_low2 = low_of_both(qkv_grad_low, 3 * RANK)
    late = rank_gradients(
        [qkv_grad_low2, qkv_low],
        [x2, d_qkv],
        plan.me,
        "late_gradients",
        [(0, 0, n * RANK, 3 * RANK, half) for n in range(3)] + [(1, 1, n * RANK, 3 * RANK, third(n)) for n in range(3)],
        LATE,
    )

    def spread_over(value, axes):
        return lax.all_to_all(jnp.broadcast_to(value[None], (8,) + value.shape), axes, 0, 0, tiled=True)

    late = lax.all_to_all(late, CTX, 0, 0, tiled=True)
    late = jnp.sum(late.astype(F32), axis=0).astype(BF)
    late = by_slot(spread_over(late, shard).reshape(16, RANK, LATE))
    late = spread_over(late, CTX)
    late_other = swap(late)
    grads = adapter_outputs(
        plan.me,
        early.reshape(8, 8, RANK, EARLY),
        early_other.reshape(8, 8, RANK, EARLY),
        late.reshape(8, 8, RANK, LATE),
        late_other.reshape(8, 8, RANK, LATE),
    )
    return (output[None], grad_tokens[None], *grads)


def solution(mesh):
    fine = Mesh(mesh.devices.reshape(2, 4, 4, 2, 2), ALL)
    shard = ("z", "yh", "c")
    rows = P(shard, None)
    per_token = P(shard, CTX, None)
    return jax.shard_map(
        on_device,
        mesh=fine,
        in_specs=(per_token, per_token) + (rows,) * 7 + (P(),) * 5 + (rows, rows),
        out_specs=(per_token, per_token, P(), P(), P(), P()),
        check_vma=False,
    )
```

time: 1490 us -> 816 us (0.55)
  waiting for transfers between devices: 1040 us -> 285 us
  matrix products: 244 us -> 39.7 us
  Pallas kernels: 0 us -> 157 us
  starting transfers between devices: 0.86 us -> 118 us
  blocking collectives: 0 us -> 88.3 us
  local copies, waits for them, and re-layouts: 111 us -> 58.7 us
  other arithmetic: 67.6 us -> 38.7 us
    all_gather x9 -> x5, waiting for transfers between devices: 816 us -> 45.3 us  [the longest x1 45.3 us: on_device(): groups = lax.all_gather(own, shard).reshape(16, RANK, EARLY + 128)]
    psum x1 -> x0, waiting for transfers between devices: 210 us -> none  [on_device(): lax.psum((local_down_in, local_down_ff, local_up_model, local_up_hidden),...]
    ppermute x0 -> x73, waiting for transfers between devices: none -> 204 us  [the longest x54 192 us: send(): got = lax.ppermute(value, ALL, STEPS[how])]
    dot_general x66 -> x20, matrix products: 244 us -> 39.7 us  [the longest x10 20.8 us: dot_nt(): return lax.dot_general(a, b, **NT)]
    pallas_call x0 -> x23, Pallas kernels: none -> 157 us  [the longest x4 70 us: call(): pl.pallas_call(body, out_shape=outs, in_specs=[_smem()] + [anywhere] * 17...]
    ppermute x0 -> x73, starting transfers between devices: none -> 104 us  [the longest x54 80.1 us: send(): got = lax.ppermute(value, ALL, STEPS[how])]
    all_to_all x0 -> x4, blocking collectives: none -> 88.3 us  [the longest x1 43.8 us: on_device(): lax.all_to_all(d_heads, CTX, 0, 0, tiled=True).reshape(8, 2 * ROWS, 3 * HD)]
    reduce_scatter x1, waiting for transfers between devices: 0.01 us -> 35.1 us  [on_device(): lax.psum_scatter(early.reshape(8 * 2 * RANK, EARLY), CTX, scatter_dimensi...]
  transfers between devices with their start and end apart: 12 -> 82, of which waited for: 11 -> 39; matrix products, arithmetic and copies ran while one was open for 18% -> 11% of each run, Pallas kernels for 0% -> 11%
where the time goes in v1:
time: 816 us; the launch traced here: 802 us
  waiting for transfers between devices  285 us (35%)
  Pallas kernels  157 us (19%)
  starting transfers between devices  118 us (14%)
  blocking collectives  88.3 us (11%)
  local copies, waits for them, and re-layouts  58.7 us (7%)
  matrix products  39.7 us (5%)
  other arithmetic  38.7 us (5%)
  between operations  16.6 us (2%)
    ppermute x54, waiting for transfers between devices, send(): got = lax.ppermute(value, ALL, STEPS[how])  192 us
    ppermute x54, starting transfers between devices, send(): got = lax.ppermute(value, ALL, STEPS[how])  80.1 us
    pallas_call x4, Pallas kernels, call(): pl.pallas_call(body, out_shape=outs, in_specs=[_smem()] + [anywhere] * 17...  70 us
    all_gather x1, waiting for transfers between devices, on_device(): groups = lax.all_gather(own, shard).reshape(16, RANK, EARLY + 128)  45.3 us
    all_to_all x1, blocking collectives, on_device(): lax.all_to_all(d_heads, CTX, 0, 0, tiled=True).reshape(8, 2 * ROWS, 3 * HD)  43.8 us
    unnamed x214, local copies, waits for them, and re-layouts  36.7 us
    reduce_scatter x1, waiting for transfers between devices, on_device(): lax.psum_scatter(early.reshape(8 * 2 * RANK, EARLY), CTX, scatter_dimensi...  35.1 us
    all_to_all x2, blocking collectives, spread_over(): lax.all_to_all(jnp.broadcast_to(value[None], (8,) + value.shape), axes, 0...  33.8 us
  transfers between devices with their start and end apart: 82, of which 39 were waited for; matrix products, arithmetic and copies ran while one was open for 11% of the time, Pallas kernels for 11%

profile of v1, /device:TPU:7, one launch (start us, length us, event | category | flops | bytes accessed | tf_op | source)
XLA Modules:
  0.0 801.9 jit_solution(5041086450595135494)
XLA Ops:
  7.3 4.8 split_g.1
  16.0 3.3 collective-permute-done.2.got
  19.9 3.8 collective-permute-start.3
  29.4 2.8 collective-permute-start.5
  32.2 12.0 %collective-permute-done.5 = bf16[128,2048]{1,0:T(8,128)(2,1)S(1)} collective-permute-done((bf16[128,2048]{1,0:T(8,128)(2,1)S(1)}, bf16[128,2048]{1,0:T(8,128)(2,1)S(1)}, u32[]{:S(2)}, u32[]{:S(2)}) %collective-permute-start.5) | collective-permute-done | bytes 524320 | tf_op jit(solution)/shard_map/ppermute | solution.py:79
  44.2 5.4 collective-permute-done.4.refs_2_
  50.7 2.8 collective-permute-start.8
  58.0 7.4 collective-permute-done.8
  68.0 8.2 %collective-permute-done.9.near = bf16[512,384]{1,0:T(8,128)(2,1)S(1)} collective-permute-done((bf16[512,384]{1,0:T(8,128)(2,1)S(1)}, bf16[512,384]{1,0:T(8,128)(2,1)S(1)}, u32[]{:S(2)}, u32[]{:S(2)}) %collective-permute-start.9) | collective-permute-done | bytes 393248 | tf_op jit(solution)/shard_map/ppermute | solution.py:79
  76.2 8.7 %collective-permute-done.12.far = bf16[512,384]{1,0:T(8,128)(2,1)S(1)} collective-permute-done((bf16[512,384]{1,0:T(8,128)(2,1)S(1)}, bf16[512,384]{1,0:T(8,128)(2,1)S(1)}, u32[]{:S(2)}, u32[]{:S(2)}) %collective-permute-start.12) | collective-permute-done | bytes 393248 | tf_op jit(solution)/shard_map/ppermute | solution.py:79
  86.9 18.5 %collective-permute-done.21.refs_2_ = bf16[256,2816]{1,0:T(8,128)(2,1)S(1)} collective-permute-done((bf16[256,2816]{1,0:T(8,128)(2,1)}, bf16[256,2816]{1,0:T(8,128)(2,1)S(1)}, u32[]{:S(2)}, u32[]{:S(2)}) %collective-permute-start.21) | collective-permute-done | bytes 1441824 | tf_op jit(solution)/shard_map/ppermute | solution.py:79
  109.0 3.6 collective-permute-done.13.refs_3_
  112.7 3.4 collective-permute-start.20
  116.1 7.5 collective-permute-done.22.refs_3_
  127.5 3.8 spread.4
  136.5 11.1 %collective-permute-done.27.near = bf16[512,768]{1,0:T(8,128)(2,1)S(1)} collective-permute-done((bf16[512,768]{1,0:T(8,128)(2,1)S(1)}, bf16[512,768]{1,0:T(8,128)(2,1)S(1)}, u32[]{:S(2)}, u32[]{:S(2)}) %collective-permute-start.27) | collective-permute-done | bytes 786464 | tf_op jit(solution)/shard_map/ppermute | solution.py:79
  147.7 11.5 %collective-permute-done.28.far = bf16[512,768]{1,0:T(8,128)(2,1)S(1)} collective-permute-done((bf16[512,768]{1,0:T(8,128)(2,1)S(1)}, bf16[512,768]{1,0:T(8,128)(2,1)S(1)}, u32[]{:S(2)}, u32[]{:S(2)}) %collective-permute-start.28) | collective-permute-done | bytes 786464 | tf_op jit(solution)/shard_map/ppermute | solution.py:79
  161.6 8.8 %collective-permute-start.14 = (bf16[256,2048]{1,0:T(8,128)(2,1)S(1)}, bf16[256,2048]{1,0:T(8,128)(2,1)S(1)}, u32[]{:S(2)}, u32[]{:S(2)}) collective-permute-start(bf16[256,2048]{1,0:T(8,128)(2,1)S(1)} %get-tuple-element.111.refs_10_), channel_id=1, source_target_pairs={{0,4},{1,13},{2,6},{3,15},{4,8},{5,1},{6,10},{7,3},{8,12},{9,5},{1... | collective-permute-start | bytes 3145736 | tf_op jit(solution)/shard_map/ppermute | solution.py:79
  174.1 8.0 collective-permute-done.14.refs_11_
  183.1 3.5 collective-permute-start.19
  191.3 12.0 %collective-permute-done.16 = bf16[128,2560]{1,0:T(8,128)(2,1)} collective-permute-done((bf16[128,2560]{1,0:T(8,128)(2,1)}, bf16[128,2560]{1,0:T(8,128)(2,1)}, u32[]{:S(2)}, u32[]{:S(2)}) %collective-permute-start.16) | collective-permute-done | bytes 655392 | tf_op jit(solution)/shard_map/ppermute | solution.py:79
  222.5 6.4 collective-permute-done.31.near
  234.2 3.2 maximum_select_fusion.refs_13_
  242.2 3.8 choose_adapters.1
  248.0 3.1 collective-permute-start.38
  256.8 4.3 collective-permute-done.38.refs_6_
  261.1 4.0 collective-permute-done.30.refs_9_
  277.0 11.7 %assemble.1 = bf16[2048,4096]{1,0:T(8,128)(2,1)} custom-call(s32[4,4]{1,0:T(4,128)S(1)} %pad_add_fusion.refs_0_.places, bf16[4,2048,384]{2,1,0:T(8,128)(2,1)} %bitcast.171, bf16[512,256]{1,0:T(8,128)(2,1)S(1)} %copy-done.37, bf16[512,256]{1,0:T(8,128)(2,1)S(1)} %copy-done.42, bf16[512,256]{1,0:T(8,128)(2,1)S(1)} %copy-done.46, ...), custom_call_target="tpu_custom_call" | custom-call | bytes 33554432 | tf_op jit(solution)/shard_map/assemble/pallas_call | solution.py:260
  288.6 6.8 fusion.8.q.k.v
  297.5 8.4 %collective-permute-start.34 = (f32[2,288]{1,0:T(2,128)S(1)}, f32[2,288]{1,0:T(2,128)S(1)}, u32[]{:S(2)}, u32[]{:S(2)}) collective-permute-start(f32[2,288]{1,0:T(2,128)S(1)} %pad_maximum_fusion.6), channel_id=1, source_target_pairs={{0,1},{1,0},{2,3},{3,2},{4,5},{5,4},{6,7},{7,6},{8,9},{9,8},{10,11... | collective-permute-start | bytes 6920 | tf_op jit(solution)/shard_map/ppermute | solution.py:68
  307.6 7.9 pack_heads.1
  315.5 4.5 all-to-all-start
  323.2 24.1 %collective-permute-done.36.far = bf16[1024,128]{1,0:T(8,128)(2,1)S(1)} collective-permute-done((bf16[1024,128]{1,0:T(8,128)(2,1)S(1)}, bf16[1024,128]{1,0:T(8,128)(2,1)S(1)}, u32[]{:S(2)}, u32[]{:S(2)}) %collective-permute-start.36) | collective-permute-done | bytes 262176 | tf_op jit(solution)/shard_map/ppermute | solution.py:79
  347.8 7.8 attend.1
  357.8 4.2 all-to-all-start.1
  362.1 3.0 maximum_select_fusion.6.refs_13_
  368.6 12.4 %collective-permute-done.46.refs_7_ = bf16[512,1280]{1,0:T(8,128)(2,1)} collective-permute-done((bf16[512,1280]{1,0:T(8,128)(2,1)}, bf16[512,1280]{1,0:T(8,128)(2,1)}, u32[]{:S(2)}, u32[]{:S(2)}) %collective-permute-start.46) | collective-permute-done | bytes 1310752 | tf_op jit(solution)/shard_map/ppermute | solution.py:79
  381.6 4.6 slice.237
  386.2 6.8 copy.69
  394.3 3.9 fusion.6
  400.0 2.9 collective-permute-start.55
  402.9 6.3 collective-permute-done.57.refs_14_
  417.4 5.0 collective-permute-done.49.refs_8_
  428.0 5.6 collective-permute-done.50.refs_3_
  438.8 23.6 %gate_and_up.1 = (bf16[288,8192]{1,0:T(8,128)(2,1)}, bf16[288,4096]{1,0:T(8,128)(2,1)}) custom-call(s32[4,4]{1,0:T(4,128)} %copy-done.56, bf16[4,2048,768]{2,1,0:T(8,128)(2,1)} %bitcast.165, bf16[512,1280]{1,0:T(8,128)(2,1)} %copy-done.16, bf16[512,1280]{1,0:T(8,128)(2,1)} %collective-permute-done.41.refs_2_, ...), custom_call_target="tpu_custom_call" | custom-call | flops 9663676416 | bytes 35819520 | tf_op jit(solution)/shard_map/gate_and_up/pallas_call | solution.py:354
  466.2 11.9 %down.3 = f32[288,2048]{1,0:T(8,128)} custom-call(s32[4,4]{1,0:T(4,128)} %copy-done.56, bf16[4,4096,128]{2,1,0:T(8,128)(2,1)} %bitcast.168, bf16[1024,256]{1,0:T(8,128)(2,1)} %copy-done.26, bf16[1024,256]{1,0:T(8,128)(2,1)} %copy-done.79, bf16[1024,256]{1,0:T(8,128)(2,1)} %collective-permute-done.50.refs_3_, ...), custom_call_target="tpu_custom_call" | custom-call | flops 4831838208 | bytes 19136512 | tf_op jit(solution)/shard_map/down/pallas_call | solution.py:354
  486.8 15.9 %down_back.1.refs_17_.refs_6_ = bf16[288,8192]{1,0:T(8,128)(2,1)} custom-call(s32[4,4]{1,0:T(4,128)} %copy-done.56, bf16[4,4096,128]{2,1,0:T(8,128)(2,1)} %bitcast.169, bf16[1024,256]{1,0:T(8,128)(2,1)} %copy-done.26, bf16[1024,256]{1,0:T(8,128)(2,1)} %copy-done.79, bf16[1024,256]{1,0:T(8,128)(2,1)} %collective-permute-done.50.refs_3_, ...), custom_call_target="tpu_custom_call" | custom-call | flops 4831838208 | bytes 22956032 | tf_op jit(solution)/shard_map/down_back/pallas_call | solution.py:354
  502.8 3.7 convolution_select_fusion.3
  506.6 18.6 %gate_and_up_back.1 = f32[288,2048]{1,0:T(8,128)} custom-call(s32[4,4]{1,0:T(4,128)} %copy-done.56, bf16[4,2048,768]{2,1,0:T(8,128)(2,1)} %bitcast.166, bf16[512,1280]{1,0:T(8,128)(2,1)} %copy-done.16, bf16[512,1280]{1,0:T(8,128)(2,1)} %collective-permute-done.41.refs_2_, bf16[512,1280]{1,0:T(8,128)(2,1)} %collective-permute-done.42.refs_3_, ...), custom_call_target="tpu_custom_call" | custom-call | flops 9663676416 | bytes 38273024 | tf_op jit(solution)/shard_map/gate_and_up_back/pallas_call | solution.py:354
  542.0 6.3 early_gradients.1
  548.8 35.1 %reduce-scatter.2.cloned.1.call-done = bf16[32,2176]{1,0:T(8,128)(2,1)} async-done(((bf16[256,2176]{1,0:T(8,128)(2,1)}), bf16[32,2176]{1,0:T(8,128)(2,1)}) %reduce-scatter.2.cloned.1.call-update) | async-done | bytes 139280 | tf_op jit(solution)/shard_map/reduce_scatter | solution.py:1034
  585.5 3.6 fusion.4
  590.3 4.9 all-to-all-start.2
  595.2 45.3 %all-gather.18.cloned.1.call-done = bf16[256,2304]{1,0:T(8,128)(2,1)} async-done(((bf16[32,2304]{1,0:T(8,128)(2,1)}), bf16[256,2304]{1,0:T(8,128)(2,1)}) %all-gather.18.cloned.1.call-update) | async-done | bytes 1179664 | tf_op jit(solution)/shard_map/all_gather | solution.py:1037
  646.1 7.8 attend_back.1
  653.9 43.8 %all_to_all.35 = bf16[8,2,144,384]{3,2,1,0:T(8,128)(2,1)} all-to-all(bf16[8,2,144,384]{3,2,1,0:T(8,128)(2,1)S(1)} %attend_back.1), channel_id=1, replica_groups=mesh['yl'=2,'x'=4,'z'=4,'yh'=2,'c'=2] {'yl','x'}, dimensions={0} | all-to-all | bytes 3538944 | tf_op jit(solution)/shard_map/all_to_all | solution.py:985
  697.7 8.1 %unpack_heads.1 = (f32[288,1024]{1,0:T(8,128)}, f32[288,1024]{1,0:T(8,128)}, bf16[288,1024]{1,0:T(8,128)(2,1)}, f32[288,256]{1,0:T(8,128)}) custom-call(s32[8]{0:T(128)} %copy-done.53, bf16[8,288,384]{2,1,0:T(8,128)(2,1)} %bitcast.170, f32[288,3072]{1,0:T(8,128)} %copy-done.61, f32[288,3072]{1,0:T(8,128)} %copy-done.61, f32[4,2048]{1,0:T(4,128)} %gains.3, ...), custom_call_target="tpu_custom_call" | custom-call | tf_op jit(solution)/shard_map/unpack_heads/pallas_call | solution.py:600
  707.1 3.4 collective-permute-start.65
  715.4 6.9 fusion
  729.5 10.6 %all_to_all.36 = bf16[8,32,768]{2,1,0:T(8,128)(2,1)S(1)} all-to-all(bf16[8,32,768]{2,1,0:T(8,128)(2,1)S(1)} %late_gradients.1), channel_id=1, replica_groups=mesh['yl'=2,'x'=4,'z'=4,'yh'=2,'c'=2] {'yl','x'}, dimensions={0} | all-to-all | bytes 786432 | tf_op jit(solution)/shard_map/all_to_all | solution.py:1059
  740.1 13.0 %all_to_all.37 = bf16[8,32,768]{2,1,0:T(8,128)(2,1)S(1)} all-to-all(bf16[8,32,768]{2,1,0:T(8,128)(2,1)S(1)} %broadcast_in_dim.47), channel_id=1, replica_groups=mesh['yl'=2,'x'=4,'z'=4,'yh'=2,'c'=2] {'z','yh'}, dimensions={0} | all-to-all | bytes 786432 | tf_op jit(solution)/shard_map/all_to_all | solution.py:1057
  753.7 20.9 %all_to_all.38 = bf16[8,128,768]{2,1,0:T(8,128)(2,1)S(1)} all-to-all(bf16[8,128,768]{2,1,0:T(8,128)(2,1)S(1)} %broadcast_in_dim.49), channel_id=1, replica_groups=mesh['yl'=2,'x'=4,'z'=4,'yh'=2,'c'=2] {'yl','x'}, dimensions={0} | all-to-all | bytes 3145728 | tf_op jit(solution)/shard_map/all_to_all | solution.py:1057
  774.6 4.1 collective-permute-start.72
  784.0 10.9 %adapter_outputs.1 = (f32[8,6,16,2048]{3,2,1,0:T(8,128)}, f32[8,16,8192]{2,1,0:T(8,128)}, f32[8,5,16,2048]{3,2,1,0:T(8,128)}, f32[8,2,16,8192]{3,2,1,0:T(8,128)}) custom-call(s32[8]{0:T(128)S(1)} %copy-done.55, bf16[8,8,16,2176]{3,2,1,0:T(8,128)(2,1)S(1)} %bitcast.161, bf16[8,8,16,2176]{3,2,1,0:T(8,128)(2,1)} %bitcast.69.early_other, ...), custom_call_target="tpu_custom_call" | custom-call | bytes 37000000 | tf_op jit(solution)/shard_map/adapter_outputs/pallas_call | solution.py:841
  (482 shorter events, 185.1 us)
Async XLA Ops:
  7.2 261.9 %all-gather.12.cloned.1.call-start = ((), (), s32[]{:S(2)}) async-start(), calls=%async_computation.10 | async-start | bytes 7864320 | tf_op jit(solution)/shard_map/all_gather | solution.py:531
  13.5 10.3 %collective-permute-start.7 = (bf16[128,8192]{1,0:T(8,128)(2,1)}, bf16[128,8192]{1,0:T(8,128)(2,1)}, u32[]{:S(2)}, u32[]{:S(2)}) collective-permute-start(bf16[128,8192]{1,0:T(8,128)(2,1)} %get-tuple-element.102), channel_id=1, source_target_pairs={{0,1},{1,0},{2,3},{3,2},{4,5},{5,4},{6,7},{7,6},{8,9},{9,8},{10,11... | collective-permute-start | bytes 6291464 | tf_op jit(solution)/shard_map/ppermute | solution.py:68
  19.9 12.3 %collective-permute-start.3 = (bf16[256,640]{1,0:T(8,128)(2,1)S(1)}, bf16[256,640]{1,0:T(8,128)(2,1)S(1)}, u32[]{:S(2)}, u32[]{:S(2)}) collective-permute-start(bf16[256,640]{1,0:T(8,128)(2,1)S(1)} %get-tuple-element.97.refs_0_), channel_id=1, source_target_pairs={{0,4},{1,13},{2,6},{3,15},{4,8},{5,1},{6,10},{7,3},{8,12},{9,5},{1... | collective-permute-start | bytes 983048 | tf_op jit(solution)/shard_map/ppermute | solution.py:79
  27.9 28.7 %collective-permute-start.10 = (bf16[256,2816]{1,0:T(8,128)(2,1)S(1)}, bf16[256,2816]{1,0:T(8,128)(2,1)S(1)}, u32[]{:S(2)}, u32[]{:S(2)}) collective-permute-start(bf16[256,2816]{1,0:T(8,128)(2,1)S(1)} %get-tuple-element.106.refs_0_), channel_id=1, source_target_pairs={{0,4},{1,13},{2,6},{3,15},{4,8},{5,1},{6,10},{7,3},{8,12},{9,5},{1... | collective-permute-start | bytes 4325384 | tf_op jit(solution)/shard_map/ppermute | solution.py:79
  29.4 14.8 %collective-permute-start.5 = (bf16[128,2048]{1,0:T(8,128)(2,1)S(1)}, bf16[128,2048]{1,0:T(8,128)(2,1)S(1)}, u32[]{:S(2)}, u32[]{:S(2)}) collective-permute-start(bf16[128,2048]{1,0:T(8,128)(2,1)S(1)} %slice_select_fusion.3), channel_id=1, source_target_pairs={{0,66},{1,67},{2,64},{3,65},{4,70},{5,71},{6,68},{7,69},{8,74},{9,... | collective-permute-start | bytes 1572872 | tf_op jit(solution)/shard_map/ppermute | solution.py:79
  32.2 17.4 %collective-permute-start.4 = (bf16[256,640]{1,0:T(8,128)(2,1)S(1)}, bf16[256,640]{1,0:T(8,128)(2,1)S(1)}, u32[]{:S(2)}, u32[]{:S(2)}) collective-permute-start(bf16[256,640]{1,0:T(8,128)(2,1)S(1)} %collective-permute-done.3.refs_1_), channel_id=1, source_target_pairs={{0,4},{1,13},{2,6},{3,15},{4,8},{5,1},{6,10},{7,3},{8,12},{9,5},{1... | collective-permute-start | bytes 983048 | tf_op jit(solution)/shard_map/ppermute | solution.py:79
  50.7 14.7 %collective-permute-start.8 = (bf16[256,1024]{1,0:T(8,128)(2,1)S(1)}, bf16[256,1024]{1,0:T(8,128)(2,1)S(1)}, u32[]{:S(2)}, u32[]{:S(2)}) collective-permute-start(bf16[256,1024]{1,0:T(8,128)(2,1)S(1)} %slice_select_fusion.2), channel_id=1, source_target_pairs={{0,66},{1,67},{2,64},{3,65},{4,70},{5,71},{6,68},{7,69},{8,74},{9,... | collective-permute-start | bytes 1572872 | tf_op jit(solution)/shard_map/ppermute | solution.py:79
  56.6 19.6 %collective-permute-start.11 = (bf16[128,2048]{1,0:T(8,128)(2,1)S(1)}, bf16[128,2048]{1,0:T(8,128)(2,1)S(1)}, u32[]{:S(2)}, u32[]{:S(2)}) collective-permute-start(bf16[128,2048]{1,0:T(8,128)(2,1)S(1)} %collective-permute-done.5), channel_id=1, source_target_pairs={{0,64},{1,65},{2,66},{3,67},{4,68},{5,69},{6,70},{7,71},{8,72},{9,... | collective-permute-start | bytes 1572872 | tf_op jit(solution)/shard_map/ppermute | solution.py:79
  65.4 10.8 %collective-permute-start.9 = (bf16[512,384]{1,0:T(8,128)(2,1)S(1)}, bf16[512,384]{1,0:T(8,128)(2,1)S(1)}, u32[]{:S(2)}, u32[]{:S(2)}) collective-permute-start(bf16[512,384]{1,0:T(8,128)(2,1)S(1)} %slice_select_fusion.4), channel_id=1, source_target_pairs={{0,66},{1,67},{2,64},{3,65},{4,70},{5,71},{6,68},{7,69},{8,74},{9,... | collective-permute-start | bytes 1179656 | tf_op jit(solution)/shard_map/ppermute | solution.py:79
  86.8 352.1 %all-gather.16.cloned.1.call-start = ((), (), s32[]{:S(2)}) async-start(), calls=%async_computation.12 | async-start | bytes 15728640 | tf_op jit(solution)/shard_map/all_gather | solution.py:531
  86.8 18.5 %collective-permute-start.21 = (bf16[256,2816]{1,0:T(8,128)(2,1)}, bf16[256,2816]{1,0:T(8,128)(2,1)S(1)}, u32[]{:S(2)}, u32[]{:S(2)}) collective-permute-start(bf16[256,2816]{1,0:T(8,128)(2,1)} %copy-done.11), channel_id=1, source_target_pairs={{0,4},{1,13},{2,6},{3,15},{4,8},{5,1},{6,10},{7,3},{8,12},{9,5},{1... | collective-permute-start | bytes 4325384 | tf_op jit(solution)/shard_map/ppermute | solution.py:79
  105.4 18.3 %collective-permute-start.22 = (bf16[256,2816]{1,0:T(8,128)(2,1)S(1)}, bf16[256,2816]{1,0:T(8,128)(2,1)S(1)}, u32[]{:S(2)}, u32[]{:S(2)}) collective-permute-start(bf16[256,2816]{1,0:T(8,128)(2,1)S(1)} %collective-permute-done.21.refs_2_), channel_id=1, source_target_pairs={{0,4},{1,13},{2,6},{3,15},{4,8},{5,1},{6,10},{7,3},{8,12},{9,5},{1... | collective-permute-start | bytes 4325384 | tf_op jit(solution)/shard_map/ppermute | solution.py:79
  112.7 21.3 %collective-permute-start.20 = (bf16[512,256]{1,0:T(8,128)(2,1)}, bf16[512,256]{1,0:T(8,128)(2,1)S(1)}, u32[]{:S(2)}, u32[]{:S(2)}) collective-permute-start(bf16[512,256]{1,0:T(8,128)(2,1)} %copy-done.38), channel_id=1, source_target_pairs={{0,64},{1,67},{2,66},{3,65},{4,68},{5,71},{6,70},{7,69},{8,72},{9,... | collective-permute-start | bytes 786440 | tf_op jit(solution)/shard_map/ppermute | solution.py:79
  134.0 13.7 %collective-permute-start.27 = (bf16[512,768]{1,0:T(8,128)(2,1)S(1)}, bf16[512,768]{1,0:T(8,128)(2,1)S(1)}, u32[]{:S(2)}, u32[]{:S(2)}) collective-permute-start(bf16[512,768]{1,0:T(8,128)(2,1)S(1)} %slice_select_fusion), channel_id=1, source_target_pairs={{0,66},{1,67},{2,64},{3,65},{4,70},{5,71},{6,68},{7,69},{8,74},{9,... | collective-permute-start | bytes 2359304 | tf_op jit(solution)/shard_map/ppermute | solution.py:79
  147.7 11.5 %collective-permute-start.28 = (bf16[512,768]{1,0:T(8,128)(2,1)S(1)}, bf16[512,768]{1,0:T(8,128)(2,1)S(1)}, u32[]{:S(2)}, u32[]{:S(2)}) collective-permute-start(bf16[512,768]{1,0:T(8,128)(2,1)S(1)} %collective-permute-done.27.near), channel_id=1, source_target_pairs={{0,64},{1,65},{2,66},{3,67},{4,68},{5,69},{6,70},{7,71},{8,72},{9,... | collective-permute-start | bytes 2359304 | tf_op jit(solution)/shard_map/ppermute | solution.py:79
  161.6 20.5 %collective-permute-start.14 = (bf16[256,2048]{1,0:T(8,128)(2,1)S(1)}, bf16[256,2048]{1,0:T(8,128)(2,1)S(1)}, u32[]{:S(2)}, u32[]{:S(2)}) collective-permute-start(bf16[256,2048]{1,0:T(8,128)(2,1)S(1)} %get-tuple-element.111.refs_10_), channel_id=1, source_target_pairs={{0,4},{1,13},{2,6},{3,15},{4,8},{5,1},{6,10},{7,3},{8,12},{9,5},{1... | collective-permute-start | bytes 3145736 | tf_op jit(solution)/shard_map/ppermute | solution.py:79
  170.5 17.8 %collective-permute-start.15 = (bf16[128,2560]{1,0:T(8,128)(2,1)S(1)}, bf16[128,2560]{1,0:T(8,128)(2,1)}, u32[]{:S(2)}, u32[]{:S(2)}) collective-permute-start(bf16[128,2560]{1,0:T(8,128)(2,1)S(1)} %slice_select_fusion.1), channel_id=1, source_target_pairs={{0,66},{1,67},{2,64},{3,65},{4,70},{5,71},{6,68},{7,69},{8,74},{9,... | collective-permute-start | bytes 1966088 | tf_op jit(solution)/shard_map/ppermute | solution.py:79
  172.9 30.4 %collective-permute-start.23 = (bf16[256,2560]{1,0:T(8,128)(2,1)S(1)}, bf16[256,2560]{1,0:T(8,128)(2,1)}, u32[]{:S(2)}, u32[]{:S(2)}) collective-permute-start(bf16[256,2560]{1,0:T(8,128)(2,1)S(1)} %get-tuple-element.122.refs_9_), channel_id=1, source_target_pairs={{0,4},{1,13},{2,6},{3,15},{4,8},{5,1},{6,10},{7,3},{8,12},{9,5},{1... | collective-permute-start | bytes 3932168 | tf_op jit(solution)/shard_map/ppermute | solution.py:79
  183.1 24.4 %collective-permute-start.19 = (bf16[256,2048]{1,0:T(8,128)(2,1)}, bf16[256,2048]{1,0:T(8,128)(2,1)}, u32[]{:S(2)}, u32[]{:S(2)}) collective-permute-start(bf16[256,2048]{1,0:T(8,128)(2,1)} %maximum_select_fusion.5.refs_14_), channel_id=1, source_target_pairs={{0,4},{1,13},{2,6},{3,15},{4,8},{5,1},{6,10},{7,3},{8,12},{9,5},{1... | collective-permute-start | bytes 3145736 | tf_op jit(solution)/shard_map/ppermute | solution.py:79
  188.3 15.0 %collective-permute-start.16 = (bf16[128,2560]{1,0:T(8,128)(2,1)}, bf16[128,2560]{1,0:T(8,128)(2,1)}, u32[]{:S(2)}, u32[]{:S(2)}) collective-permute-start(bf16[128,2560]{1,0:T(8,128)(2,1)} %collective-permute-done.15), channel_id=1, source_target_pairs={{0,64},{1,65},{2,66},{3,67},{4,68},{5,69},{6,70},{7,71},{8,72},{9,... | collective-permute-start | bytes 1966088 | tf_op jit(solution)/shard_map/ppermute | solution.py:79
  189.0 22.2 %collective-permute-start = (f32[8,128]{1,0:T(8,128)S(1)}, f32[8,128]{1,0:T(8,128)S(1)}, u32[]{:S(2)}, u32[]{:S(2)}) collective-permute-start(f32[8,128]{1,0:T(8,128)S(1)} %broadcast_in_dim.18), channel_id=1, source_target_pairs={{0,1},{1,0},{2,3},{3,2},{4,5},{5,4},{6,7},{7,6},{8,9},{9,8},{10,11... | collective-permute-start | bytes 12296 | tf_op jit(solution)/shard_map/ppermute | solution.py:68
  190.8 55.3 %collective-permute-start.1 = (bf16[144,2048]{1,0:T(8,128)(2,1)}, bf16[144,2048]{1,0:T(8,128)(2,1)}, u32[]{:S(2)}, u32[]{:S(2)}) collective-permute-start(bf16[144,2048]{1,0:T(8,128)(2,1)} %bitcast), channel_id=1, source_target_pairs={{0,1},{1,0},{2,3},{3,2},{4,5},{5,4},{6,7},{7,6},{8,9},{9,8},{10,11... | collective-permute-start | bytes 1769480 | tf_op jit(solution)/shard_map/ppermute | solution.py:68
  203.3 16.2 %collective-permute-start.17 = (bf16[256,2048]{1,0:T(8,128)(2,1)}, bf16[256,2048]{1,0:T(8,128)(2,1)}, u32[]{:S(2)}, u32[]{:S(2)}) collective-permute-start(bf16[256,2048]{1,0:T(8,128)(2,1)} %copy-done.28), channel_id=1, source_target_pairs={{0,4},{1,13},{2,6},{3,15},{4,8},{5,1},{6,10},{7,3},{8,12},{9,5},{1... | collective-permute-start | bytes 3145736 | tf_op jit(solution)/shard_map/ppermute | solution.py:79
  209.1 22.4 %collective-permute-start.25 = (bf16[256,2048]{1,0:T(8,128)(2,1)}, bf16[256,2048]{1,0:T(8,128)(2,1)}, u32[]{:S(2)}, u32[]{:S(2)}) collective-permute-start(bf16[256,2048]{1,0:T(8,128)(2,1)} %collective-permute-done.19.refs_15_), channel_id=1, source_target_pairs={{0,4},{1,13},{2,6},{3,15},{4,8},{5,1},{6,10},{7,3},{8,12},{9,5},{1... | collective-permute-start | bytes 3145736 | tf_op jit(solution)/shard_map/ppermute | solution.py:79
  219.5 12.0 %collective-permute-start.18 = (bf16[512,256]{1,0:T(8,128)(2,1)S(1)}, bf16[512,256]{1,0:T(8,128)(2,1)S(1)}, u32[]{:S(2)}, u32[]{:S(2)}) collective-permute-start(bf16[512,256]{1,0:T(8,128)(2,1)S(1)} %copy-done.41), channel_id=1, source_target_pairs={{0,64},{1,67},{2,66},{3,65},{4,68},{5,71},{6,70},{7,69},{8,72},{9,... | collective-permute-start | bytes 786440 | tf_op jit(solution)/shard_map/ppermute | solution.py:79
  228.9 19.1 %collective-permute-start.32 = (bf16[256,2048]{1,0:T(8,128)(2,1)}, bf16[256,2048]{1,0:T(8,128)(2,1)}, u32[]{:S(2)}, u32[]{:S(2)}) collective-permute-start(bf16[256,2048]{1,0:T(8,128)(2,1)} %collective-permute-done.17.refs_12_), channel_id=1, source_target_pairs={{0,4},{1,13},{2,6},{3,15},{4,8},{5,1},{6,10},{7,3},{8,12},{9,5},{1... | collective-permute-start | bytes 3145736 | tf_op jit(solution)/shard_map/ppermute | solution.py:79
  237.5 28.3 %collective-permute-start.37 = (bf16[256,2560]{1,0:T(8,128)(2,1)}, bf16[256,2560]{1,0:T(8,128)(2,1)}, u32[]{:S(2)}, u32[]{:S(2)}) collective-permute-start(bf16[256,2560]{1,0:T(8,128)(2,1)} %maximum_select_fusion.refs_13_), channel_id=1, source_target_pairs={{0,4},{1,13},{2,6},{3,15},{4,8},{5,1},{6,10},{7,3},{8,12},{9,5},{1... | collective-permute-start | bytes 3932168 | tf_op jit(solution)/shard_map/ppermute | solution.py:79
  240.4 28.7 %collective-permute-start.33 = (bf16[256,2048]{1,0:T(8,128)(2,1)}, bf16[256,2048]{1,0:T(8,128)(2,1)}, u32[]{:S(2)}, u32[]{:S(2)}) collective-permute-start(bf16[256,2048]{1,0:T(8,128)(2,1)} %collective-permute-done.25.refs_16_), channel_id=1, source_target_pairs={{0,4},{1,13},{2,6},{3,15},{4,8},{5,1},{6,10},{7,3},{8,12},{9,5},{1... | collective-permute-start | bytes 3145736 | tf_op jit(solution)/shard_map/ppermute | solution.py:79
  241.2 10.4 %collective-permute-start.29 = (bf16[256,1024]{1,0:T(8,128)(2,1)S(1)}, bf16[256,1024]{1,0:T(8,128)(2,1)S(1)}, u32[]{:S(2)}, u32[]{:S(2)}) collective-permute-start(bf16[256,1024]{1,0:T(8,128)(2,1)S(1)} %copy-done.89), channel_id=1, source_target_pairs={{0,64},{1,65},{2,66},{3,67},{4,68},{5,69},{6,70},{7,71},{8,72},{9,... | collective-permute-start | bytes 1572872 | tf_op jit(solution)/shard_map/ppermute | solution.py:79
  248.0 13.1 %collective-permute-start.38 = (bf16[1024,256]{1,0:T(8,128)(2,1)}, bf16[1024,256]{1,0:T(8,128)(2,1)S(1)}, u32[]{:S(2)}, u32[]{:S(2)}) collective-permute-start(bf16[1024,256]{1,0:T(8,128)(2,1)} %get-tuple-element.144.refs_5_), channel_id=1, source_target_pairs={{0,64},{1,67},{2,66},{3,65},{4,68},{5,71},{6,70},{7,69},{8,72},{9,... | collective-permute-start | bytes 1572872 | tf_op jit(solution)/shard_map/ppermute | solution.py:79
  251.6 13.6 %collective-permute-start.30 = (bf16[512,256]{1,0:T(8,128)(2,1)}, bf16[512,256]{1,0:T(8,128)(2,1)S(1)}, u32[]{:S(2)}, u32[]{:S(2)}) collective-permute-start(bf16[512,256]{1,0:T(8,128)(2,1)} %collective-permute-done.24.refs_8_), channel_id=1, source_target_pairs={{0,64},{1,67},{2,66},{3,65},{4,68},{5,71},{6,70},{7,69},{8,72},{9,... | collective-permute-start | bytes 786440 | tf_op jit(solution)/shard_map/ppermute | solution.py:79
  261.1 60.4 %collective-permute-start.39 = (bf16[256,2560]{1,0:T(8,128)(2,1)}, bf16[256,2560]{1,0:T(8,128)(2,1)}, u32[]{:S(2)}, u32[]{:S(2)}) collective-permute-start(bf16[256,2560]{1,0:T(8,128)(2,1)} %collective-permute-done.23.refs_10_), channel_id=1, source_target_pairs={{0,4},{1,13},{2,6},{3,15},{4,8},{5,1},{6,10},{7,3},{8,12},{9,5},{1... | collective-permute-start | bytes 3932168 | tf_op jit(solution)/shard_map/ppermute | solution.py:79
  265.8 55.5 %collective-permute-start.41 = (bf16[512,1280]{1,0:T(8,128)(2,1)S(1)}, bf16[512,1280]{1,0:T(8,128)(2,1)}, u32[]{:S(2)}, u32[]{:S(2)}) collective-permute-start(bf16[512,1280]{1,0:T(8,128)(2,1)S(1)} %copy-done.17), channel_id=1, source_target_pairs={{0,64},{1,67},{2,66},{3,65},{4,68},{5,71},{6,70},{7,69},{8,72},{9,... | collective-permute-start | bytes 3932168 | tf_op jit(solution)/shard_map/ppermute | solution.py:79
  265.9 56.3 %collective-permute-start.45 = (bf16[512,1280]{1,0:T(8,128)(2,1)}, bf16[512,1280]{1,0:T(8,128)(2,1)}, u32[]{:S(2)}, u32[]{:S(2)}) collective-permute-start(bf16[512,1280]{1,0:T(8,128)(2,1)} %get-tuple-element.153.refs_5_), channel_id=1, source_target_pairs={{0,64},{1,67},{2,66},{3,65},{4,68},{5,71},{6,70},{7,69},{8,72},{9,... | collective-permute-start | bytes 3932168 | tf_op jit(solution)/shard_map/ppermute | solution.py:79
  297.5 9.3 %collective-permute-start.34 = (f32[2,288]{1,0:T(2,128)S(1)}, f32[2,288]{1,0:T(2,128)S(1)}, u32[]{:S(2)}, u32[]{:S(2)}) collective-permute-start(f32[2,288]{1,0:T(2,128)S(1)} %pad_maximum_fusion.6), channel_id=1, source_target_pairs={{0,1},{1,0},{2,3},{3,2},{4,5},{5,4},{6,7},{7,6},{8,9},{9,8},{10,11... | collective-permute-start | bytes 6920 | tf_op jit(solution)/shard_map/ppermute | solution.py:68
  315.5 32.3 %all-to-all-start = ((bf16[8,288,384]{2,1,0:T(8,128)(2,1)}), bf16[8,288,384]{2,1,0:T(8,128)(2,1)}, u32[]{:S(2)}, u32[]{:S(2)}) async-start(bf16[8,288,384]{2,1,0:T(8,128)(2,1)} %pack_heads.1), calls=%async_computation | async-start | bytes 3538944 | tf_op jit(solution)/shard_map/all_to_all | solution.py:938
  320.1 27.2 %collective-permute-start.36 = (bf16[1024,128]{1,0:T(8,128)(2,1)S(1)}, bf16[1024,128]{1,0:T(8,128)(2,1)S(1)}, u32[]{:S(2)}, u32[]{:S(2)}) collective-permute-start(bf16[1024,128]{1,0:T(8,128)(2,1)S(1)} %copy-done.52), channel_id=1, source_target_pairs={{0,64},{1,65},{2,66},{3,67},{4,68},{5,69},{6,70},{7,71},{8,72},{9,... | collective-permute-start | bytes 786440 | tf_op jit(solution)/shard_map/ppermute | solution.py:79
  321.3 45.6 %collective-permute-start.42 = (bf16[512,1280]{1,0:T(8,128)(2,1)}, bf16[512,1280]{1,0:T(8,128)(2,1)}, u32[]{:S(2)}, u32[]{:S(2)}) collective-permute-start(bf16[512,1280]{1,0:T(8,128)(2,1)} %collective-permute-done.41.refs_2_), channel_id=1, source_target_pairs={{0,64},{1,67},{2,66},{3,65},{4,68},{5,71},{6,70},{7,69},{8,72},{9,... | collective-permute-start | bytes 3932168 | tf_op jit(solution)/shard_map/ppermute | solution.py:79
  321.5 45.4 %collective-permute-start.40 = (bf16[256,2560]{1,0:T(8,128)(2,1)}, bf16[256,2560]{1,0:T(8,128)(2,1)}, u32[]{:S(2)}, u32[]{:S(2)}) collective-permute-start(bf16[256,2560]{1,0:T(8,128)(2,1)} %collective-permute-done.37.refs_14_), channel_id=1, source_target_pairs={{0,4},{1,13},{2,6},{3,15},{4,8},{5,1},{6,10},{7,3},{8,12},{9,5},{1... | collective-permute-start | bytes 3932168 | tf_op jit(solution)/shard_map/ppermute | solution.py:79
  322.1 58.9 %collective-permute-start.46 = (bf16[512,1280]{1,0:T(8,128)(2,1)}, bf16[512,1280]{1,0:T(8,128)(2,1)}, u32[]{:S(2)}, u32[]{:S(2)}) collective-permute-start(bf16[512,1280]{1,0:T(8,128)(2,1)} %collective-permute-done.45.refs_6_), channel_id=1, source_target_pairs={{0,64},{1,67},{2,66},{3,65},{4,68},{5,71},{6,70},{7,69},{8,72},{9,... | collective-permute-start | bytes 3932168 | tf_op jit(solution)/shard_map/ppermute | solution.py:79
  347.3 19.5 %collective-permute-start.47 = (bf16[512,1024]{1,0:T(8,128)(2,1)S(1)}, bf16[512,1024]{1,0:T(8,128)(2,1)S(1)}, u32[]{:S(2)}, u32[]{:S(2)}) collective-permute-start(bf16[512,1024]{1,0:T(8,128)(2,1)S(1)} %get-tuple-element.155.refs_9_), channel_id=1, source_target_pairs={{0,4},{1,13},{2,6},{3,15},{4,8},{5,1},{6,10},{7,3},{8,12},{9,5},{1... | collective-permute-start | bytes 3145736 | tf_op jit(solution)/shard_map/ppermute | solution.py:79
  357.8 35.2 %all-to-all-start.1 = ((bf16[8,2,144,128]{3,2,1,0:T(8,128)(2,1)}), bf16[8,2,144,128]{3,2,1,0:T(8,128)(2,1)}, u32[]{:S(2)}, u32[]{:S(2)}) async-start(bf16[8,2,144,128]{3,2,1,0:T(8,128)(2,1)} %get-tuple-element.137), calls=%async_computation.1 | async-start | bytes 1179648 | tf_op jit(solution)/shard_map/all_to_all | solution.py:940
  362.0 103.3 %all-gather.14.cloned.1.call-start = ((), (), s32[]{:S(2)}) async-start(), calls=%async_computation.11 | async-start | bytes 5242880 | tf_op jit(solution)/shard_map/all_gather | solution.py:531
  366.7 217.2 %reduce-scatter.2.cloned.1.call-start = ((), (), s32[]{:S(2)}) async-start(), calls=%async_computation.8 | async-start | bytes 1253376 | tf_op jit(solution)/shard_map/reduce_scatter | solution.py:1034
  366.8 36.0 %collective-permute-start.48 = (bf16[256,2560]{1,0:T(8,128)(2,1)}, bf16[256,2560]{1,0:T(8,128)(2,1)}, u32[]{:S(2)}, u32[]{:S(2)}) collective-permute-start(bf16[256,2560]{1,0:T(8,128)(2,1)} %collective-permute-done.39.refs_11_), channel_id=1, source_target_pairs={{0,4},{1,13},{2,6},{3,15},{4,8},{5,1},{6,10},{7,3},{8,12},{9,5},{1... | collective-permute-start | bytes 3932168 | tf_op jit(solution)/shard_map/ppermute | solution.py:79
  366.9 32.9 %collective-permute-start.43 = (bf16[256,2560]{1,0:T(8,128)(2,1)}, bf16[256,2560]{1,0:T(8,128)(2,1)}, u32[]{:S(2)}, u32[]{:S(2)}) collective-permute-start(bf16[256,2560]{1,0:T(8,128)(2,1)} %collective-permute-done.40.refs_15_), channel_id=1, source_target_pairs={{0,4},{1,13},{2,6},{3,15},{4,8},{5,1},{6,10},{7,3},{8,12},{9,5},{1... | collective-permute-start | bytes 3932168 | tf_op jit(solution)/shard_map/ppermute | solution.py:79
  367.0 32.9 %collective-permute-start.54 = (bf16[512,1280]{1,0:T(8,128)(2,1)}, bf16[512,1280]{1,0:T(8,128)(2,1)}, u32[]{:S(2)}, u32[]{:S(2)}) collective-permute-start(bf16[512,1280]{1,0:T(8,128)(2,1)} %collective-permute-done.42.refs_3_), channel_id=1, source_target_pairs={{0,64},{1,67},{2,66},{3,65},{4,68},{5,71},{6,70},{7,69},{8,72},{9,... | collective-permute-start | bytes 3932168 | tf_op jit(solution)/shard_map/ppermute | solution.py:79
  381.0 28.2 %collective-permute-start.57 = (bf16[512,1024]{1,0:T(8,128)(2,1)}, bf16[512,1024]{1,0:T(8,128)(2,1)}, u32[]{:S(2)}, u32[]{:S(2)}) collective-permute-start(bf16[512,1024]{1,0:T(8,128)(2,1)} %maximum_select_fusion.6.refs_13_), channel_id=1, source_target_pairs={{0,4},{1,13},{2,6},{3,15},{4,8},{5,1},{6,10},{7,3},{8,12},{9,5},{1... | collective-permute-start | bytes 3145736 | tf_op jit(solution)/shard_map/ppermute | solution.py:79
  399.8 10.7 %collective-permute-start.35 = (bf16[144,2176]{1,0:T(8,128)(2,1)}, bf16[144,2176]{1,0:T(8,128)(2,1)}, u32[]{:S(2)}, u32[]{:S(2)}) collective-permute-start(bf16[144,2176]{1,0:T(8,128)(2,1)} %select_convert_fusion.3), channel_id=1, source_target_pairs={{0,1},{1,0},{2,3},{3,2},{4,5},{5,4},{6,7},{7,6},{8,9},{9,8},{10,11... | collective-permute-start | bytes 1880072 | tf_op jit(solution)/shard_map/ppermute | solution.py:68
  399.9 16.2 %collective-permute-start.44 = (bf16[1024,256]{1,0:T(8,128)(2,1)S(1)}, bf16[1024,256]{1,0:T(8,128)(2,1)S(1)}, u32[]{:S(2)}, u32[]{:S(2)}) collective-permute-start(bf16[1024,256]{1,0:T(8,128)(2,1)S(1)} %copy-done.27), channel_id=1, source_target_pairs={{0,64},{1,67},{2,66},{3,65},{4,68},{5,71},{6,70},{7,69},{8,72},{9,... | collective-permute-start | bytes 1572872 | tf_op jit(solution)/shard_map/ppermute | solution.py:79
  400.0 24.1 %collective-permute-start.55 = (bf16[512,1024]{1,0:T(8,128)(2,1)}, bf16[512,1024]{1,0:T(8,128)(2,1)}, u32[]{:S(2)}, u32[]{:S(2)}) collective-permute-start(bf16[512,1024]{1,0:T(8,128)(2,1)} %copy-done.71), channel_id=1, source_target_pairs={{0,4},{1,13},{2,6},{3,15},{4,8},{5,1},{6,10},{7,3},{8,12},{9,5},{1... | collective-permute-start | bytes 3145736 | tf_op jit(solution)/shard_map/ppermute | solution.py:79
  402.8 19.6 %collective-permute-start.49 = (bf16[512,1280]{1,0:T(8,128)(2,1)}, bf16[512,1280]{1,0:T(8,128)(2,1)S(1)}, u32[]{:S(2)}, u32[]{:S(2)}) collective-permute-start(bf16[512,1280]{1,0:T(8,128)(2,1)} %collective-permute-done.46.refs_7_), channel_id=1, source_target_pairs={{0,64},{1,67},{2,66},{3,65},{4,68},{5,71},{6,70},{7,69},{8,72},{9,... | collective-permute-start | bytes 3932168 | tf_op jit(solution)/shard_map/ppermute | solution.py:79
  409.2 25.7 %collective-permute-start.58 = (bf16[512,1024]{1,0:T(8,128)(2,1)}, bf16[512,1024]{1,0:T(8,128)(2,1)}, u32[]{:S(2)}, u32[]{:S(2)}) collective-permute-start(bf16[512,1024]{1,0:T(8,128)(2,1)} %collective-permute-done.57.refs_14_), channel_id=1, source_target_pairs={{0,4},{1,13},{2,6},{3,15},{4,8},{5,1},{6,10},{7,3},{8,12},{9,5},{1... | collective-permute-start | bytes 3145736 | tf_op jit(solution)/shard_map/ppermute | solution.py:79
  413.9 23.6 %collective-permute-start.60 = (bf16[144,2048]{1,0:T(8,128)(2,1)S(1)}, bf16[144,2048]{1,0:T(8,128)(2,1)S(1)}, u32[]{:S(2)}, u32[]{:S(2)}) collective-permute-start(bf16[144,2048]{1,0:T(8,128)(2,1)S(1)} %fusion.31), channel_id=1, source_target_pairs={{0,1},{1,0},{2,3},{3,2},{4,5},{5,4},{6,7},{7,6},{8,9},{9,8},{10,11... | collective-permute-start | bytes 1769480 | tf_op jit(solution)/shard_map/ppermute | solution.py:68
  416.2 11.8 %collective-permute-start.51 = (bf16[1024,256]{1,0:T(8,128)(2,1)S(1)}, bf16[1024,256]{1,0:T(8,128)(2,1)}, u32[]{:S(2)}, u32[]{:S(2)}) collective-permute-start(bf16[1024,256]{1,0:T(8,128)(2,1)S(1)} %copy-done.78), channel_id=1, source_target_pairs={{0,64},{1,67},{2,66},{3,65},{4,68},{5,71},{6,70},{7,69},{8,72},{9,... | collective-permute-start | bytes 1572872 | tf_op jit(solution)/shard_map/ppermute | solution.py:79
  422.4 11.2 %collective-permute-start.50 = (bf16[1024,256]{1,0:T(8,128)(2,1)S(1)}, bf16[1024,256]{1,0:T(8,128)(2,1)}, u32[]{:S(2)}, u32[]{:S(2)}) collective-permute-start(bf16[1024,256]{1,0:T(8,128)(2,1)S(1)} %collective-permute-done.44.refs_2_), channel_id=1, source_target_pairs={{0,64},{1,67},{2,66},{3,65},{4,68},{5,71},{6,70},{7,69},{8,72},{9,... | collective-permute-start | bytes 1572872 | tf_op jit(solution)/shard_map/ppermute | solution.py:79
  424.0 41.2 %collective-permute-start.56 = (bf16[512,1024]{1,0:T(8,128)(2,1)}, bf16[512,1024]{1,0:T(8,128)(2,1)S(1)}, u32[]{:S(2)}, u32[]{:S(2)}) collective-permute-start(bf16[512,1024]{1,0:T(8,128)(2,1)} %collective-permute-done.55.refs_11_), channel_id=1, source_target_pairs={{0,4},{1,13},{2,6},{3,15},{4,8},{5,1},{6,10},{7,3},{8,12},{9,5},{1... | collective-permute-start | bytes 3145736 | tf_op jit(solution)/shard_map/ppermute | solution.py:79
  433.7 31.6 %collective-permute-start.52 = (bf16[1024,256]{1,0:T(8,128)(2,1)}, bf16[1024,256]{1,0:T(8,128)(2,1)}, u32[]{:S(2)}, u32[]{:S(2)}) collective-permute-start(bf16[1024,256]{1,0:T(8,128)(2,1)} %collective-permute-done.50.refs_3_), channel_id=1, source_target_pairs={{0,64},{1,67},{2,66},{3,65},{4,68},{5,71},{6,70},{7,69},{8,72},{9,... | collective-permute-start | bytes 1572872 | tf_op jit(solution)/shard_map/ppermute | solution.py:79
  434.9 30.4 %collective-permute-start.53 = (bf16[1024,256]{1,0:T(8,128)(2,1)}, bf16[1024,256]{1,0:T(8,128)(2,1)}, u32[]{:S(2)}, u32[]{:S(2)}) collective-permute-start(bf16[1024,256]{1,0:T(8,128)(2,1)} %collective-permute-done.51.refs_7_), channel_id=1, source_target_pairs={{0,64},{1,67},{2,66},{3,65},{4,68},{5,71},{6,70},{7,69},{8,72},{9,... | collective-permute-start | bytes 1572872 | tf_op jit(solution)/shard_map/ppermute | solution.py:79
  434.9 30.4 %collective-permute-start.59 = (bf16[512,1024]{1,0:T(8,128)(2,1)}, bf16[512,1024]{1,0:T(8,128)(2,1)}, u32[]{:S(2)}, u32[]{:S(2)}) collective-permute-start(bf16[512,1024]{1,0:T(8,128)(2,1)} %collective-permute-done.58.refs_15_), channel_id=1, source_target_pairs={{0,4},{1,13},{2,6},{3,15},{4,8},{5,1},{6,10},{7,3},{8,12},{9,5},{1... | collective-permute-start | bytes 3145736 | tf_op jit(solution)/shard_map/ppermute | solution.py:79
  548.3 92.1 %all-gather.18.cloned.1.call-start = ((), (), s32[]{:S(2)}) async-start(), calls=%async_computation.13 | async-start | bytes 1327104 | tf_op jit(solution)/shard_map/all_gather | solution.py:1037
  590.3 55.8 %all-to-all-start.2 = ((bf16[8,288,128]{2,1,0:T(8,128)(2,1)}), bf16[8,288,128]{2,1,0:T(8,128)(2,1)S(1)}, u32[]{:S(2)}, u32[]{:S(2)}) async-start(bf16[8,288,128]{2,1,0:T(8,128)(2,1)} %bitcast.142), calls=%async_computation.2 | async-start | bytes 1179648 | tf_op jit(solution)/shard_map/all_to_all | solution.py:983
  595.2 131.2 %all-gather.10.cloned.1.call-start = ((), (), s32[]{:S(2)}) async-start(), calls=%async_computation.9 | async-start | bytes 5013504 | tf_op jit(solution)/shard_map/all_gather | solution.py:1044
  726.4 55.4 %collective-permute-start.70 = (bf16[8,128,2176]{2,1,0:T(8,128)(2,1)}, bf16[8,128,2176]{2,1,0:T(8,128)(2,1)}, u32[]{:S(2)}, u32[]{:S(2)}) collective-permute-start(bf16[8,128,2176]{2,1,0:T(8,128)(2,1)} %all-gather.10.cloned.1.call-done), channel_id=1, source_target_pairs={{0,1},{1,0},{2,3},{3,2},{4,5},{5,4},{6,7},{7,6},{8,9},{9,8},{10,11... | collective-permute-start | bytes 13369352 | tf_op jit(solution)/shard_map/ppermute | solution.py:68
  (123 other events, 1458.1 us)
Sparse Core Ops, SparseCore 0:
  86.9 64.6 all-gather.11
  161.7 128.4 all-gather.15
  366.9 46.8 all-gather.13
  548.5 35.3 reduce-scatter.1
  586.9 53.5 all-gather.17
  646.2 71.4 all-gather.9

commit v2 on v1

v2 whole, which is shorter than its diff:
```python
import jax
import jax.numpy as jnp
from jax import lax
from jax.experimental import pallas as pl
from jax.experimental.pallas import tpu as pltpu
from jax.sharding import Mesh, PartitionSpec as P

HD = 128
PROMPT = 1024
ROWS = 144
TOTAL = 1152
D = 2048
HALF = 1024
FF = 4096
RANK = 16
SCALE = HD**-0.5
EPS = 1e-06
BASE = 500000.0
ALL = ("yl", "x", "z", "yh", "c")
CTX = ("yl", "x")
BF = jnp.bfloat16
F32 = jnp.float32
CUT_A, CUT_G, CUT_D = 2048, 5120, 1536
EARLY, LATE = 1664, 1280


NT = dict(dimension_numbers=(((1,), (1,)), ((), ())), preferred_element_type=F32)
TN = dict(dimension_numbers=(((0,), (0,)), ((), ())), preferred_element_type=F32)


CORE, X, YL, YH, Z0 = 0, 1, 2, 3, 4


def _place(yl, x, z, yh, c):
    return (((yl * 4 + x) * 4 + z) * 2 + yh) * 2 + c


def _permutation(move):
    pairs = []
    for yl in range(2):
        for x in range(4):
            for z in range(4):
                for yh in range(2):
                    for c in range(2):
                        nx, ny, nz, nc = move(x, 2 * yh + yl, z, c)
                        pairs.append(
                            (_place(yl, x, z, yh, c), _place(ny % 2, nx % 4, nz % 4, (ny % 4) // 2, nc))
                        )
    return pairs


STEPS = {
    "y": _permutation(lambda x, y, z, c: (x, (y + 1 - 2 * c) % 4, z, c)),
    "z": _permutation(lambda x, y, z, c: (x, y, z + 1 - 2 * c, c)),
    "cross": _permutation(lambda x, y, z, c: (x, 3 - y, z, c)),
    "core": _permutation(lambda x, y, z, c: (x, y, z, 1 - c)),
}


def swap(value):
    return lax.ppermute(value, ALL, STEPS["core"])


class Lane:
    def __init__(self):
        self.last = None

    def send(self, value, how):
        if self.last is not None:
            value, _ = lax.optimization_barrier((value, self.last))
        self.last = lax.ppermute(value, ALL, STEPS[how])
        return self.last


def after(value, *others):
    return lax.optimization_barrier((value, *others))[0]


def _smem():
    return pl.BlockSpec(memory_space=pltpu.SMEM)


def _vmem():
    return pl.BlockSpec(memory_space=pltpu.VMEM)


def _plain(body, name, outs, ins, scalars, scratch=(), limit=48):
    size = sum(v.size * v.dtype.itemsize for v in list(ins) + list(outs))
    return pl.pallas_call(
        body,
        out_shape=outs,
        in_specs=[_smem()] * len(scalars) + [_vmem()] * len(ins),
        out_specs=[_vmem()] * len(outs),
        scratch_shapes=list(scratch),
        compiler_params=pltpu.CompilerParams(vmem_limit_bytes=limit * 2**20),
        cost_estimate=pl.CostEstimate(flops=0, bytes_accessed=size, transcendentals=0),
        name=name,
    )(*scalars, *ins)


def bf(*shape):
    return jax.ShapeDtypeStruct(shape, BF)


def split_a(core, q, k, v):
    def body(core, q, k, v, keep, give):
        for n, w in enumerate((q, k, v)):
            for h in range(8):
                here = slice(n * HALF + HD * h, n * HALF + HD * (h + 1))
                keep[:, here] = w[:, pl.ds(pl.multiple_of((2 * h + core[0]) * HD, HD), HD)]
                give[:, here] = w[:, pl.ds(pl.multiple_of((2 * h + 1 - core[0]) * HD, HD), HD)]

    return _plain(body, "split_a", [bf(HD, 3 * HALF)] * 2, [q, k, v], [core])


def split_g(core, gate, upward):
    def body(core, gate, upward, keep, give):
        for m in range(FF // 128):
            for n, w in enumerate((gate, upward)):
                here = slice(256 * m + 128 * n, 256 * m + 128 * (n + 1))
                for side, out in ((core[0], keep), (1 - core[0], give)):
                    start = (2 * (m // 4) + side) * 512 + (m % 4) * 128
                    out[:, here] = w[:, pl.ds(pl.multiple_of(start, 128), 128)]

    return _plain(body, "split_g", [bf(HD, 2 * FF)] * 2, [gate, upward], [core])


def parts_a(me, keep, got, out):
    quarter = CUT_A // 4

    def body(me, keep, got, out, xs, ys):
        for side, w in ((me[CORE], keep), (1 - me[CORE], got)):
            rows = pl.ds(pl.multiple_of(side * HD, HD), HD)
            xs[rows, :] = w[:, pl.ds(pl.multiple_of(me[X] * quarter, 128), quarter)]

            @pl.when(me[YL] == 0)
            def _():
                ys[rows, :] = w[:, 2 * HALF :]

        @pl.when(me[YL] == 1)
        def _():
            ys[:HD, :] = out[:, :HALF]
            ys[HD:, :] = out[:, HALF:]

    return _plain(body, "parts_a", [bf(256, quarter), bf(256, HALF)], [keep, got, out], [me])


def parts_m(me, keep, got, down):
    gx, dx = CUT_G // 4, CUT_D // 4
    gy, dy = FF - CUT_G // 2, HALF - CUT_D // 2

    def body(me, keep, got, down, xs, yg, yd):
        for side, w in ((me[CORE], keep), (1 - me[CORE], got)):
            rows = pl.ds(pl.multiple_of(side * HD, HD), HD)
            xs[rows, :gx] = w[:, pl.ds(pl.multiple_of(me[X] * gx, 128), gx)]
            yg[rows, :] = w[:, pl.ds(pl.multiple_of(CUT_G + me[YL] * gy, 128), gy)]
        for n in range(2):
            rows = slice(256 * n, 256 * (n + 1))
            xs[:, gx + n * dx : gx + (n + 1) * dx] = down[rows, pl.ds(pl.multiple_of(me[X] * dx, 128), dx)]
            yd[:, n * dy : (n + 1) * dy] = down[rows, pl.ds(pl.multiple_of(CUT_D + me[YL] * dy, 128), dy)]

    outs = [bf(256, gx + 2 * dx), bf(256, gy), bf(256, 2 * dy)]
    return _plain(body, "parts_m", outs, [keep, got, down], [me])


def spread(me, got, pieces, name):
    def body(me, *refs):
        chunks, outs = refs[:4], refs[4:]
        for k in range(4):
            z = me[Z0 + k]
            for p, (column, width, folds) in enumerate(pieces):
                for half in range(2):

                    @pl.when(z // 2 == half)
                    def _():
                        for n in range(folds):
                            at = pl.multiple_of(((z - 2 * half) * folds + n) * 256, 256)
                            start = column + n * width
                            outs[2 * p + half][pl.ds(at, 256), :] = chunks[k][:, start : start + width]

    outs = [bf(2 * folds * 256, width) for _, width, folds in pieces for _ in range(2)]
    return _plain(body, name, outs, list(got), [me])


class Chunks:
    def __init__(self, rows, cut, width, places, xs, column, y):
        self.rows, self.cx, self.cy = rows, cut, width - cut
        self.depth = 8 * rows
        self.places = places
        self.column = column
        self.arrays = [xs] + y[0] + y[1]


def _y_rows(places, rows, half, j, k):
    return pl.multiple_of((2 * half + j) * 2 * rows + places[0, k] * rows, rows)


def _copies(w, places, refs, whole):
    xs, y = refs[0], refs[1:9]
    quarter, half_width = w.cx // 4, w.cy // 2
    folds = w.rows // 256
    panels = []
    for k in range(4):
        panel = []
        for z in range(4):
            for yh in range(2):
                for n in range(folds):
                    target = whole.at[pl.ds((2 * z + yh) * w.rows + 256 * n, 256), pl.ds(k * quarter, quarter)]
                    panel.append((xs.at[k, z, yh, :, pl.ds(w.column + n * quarter, quarter)], target))
        panels.append(panel)
    chunks = []
    for k in range(4):
        column = pl.multiple_of(w.cx + places[1, k] * half_width, 128)
        for half in range(2):
            for j in range(2):
                row = _y_rows(places, w.rows, half, j, k)
                chunks.append(
                    (
                        y[4 * half + k].at[pl.ds(j * w.rows, w.rows)],
                        whole.at[pl.ds(row, w.rows), pl.ds(column, half_width)],
                    )
                )
    return panels, chunks


def assemble(w):
    anywhere = pl.BlockSpec(memory_space=pl.ANY)

    def body(places, *refs):
        out, out_matrix, sems = refs[9], refs[10], refs[11]
        panels, chunks = _copies(w, places, refs[:9], out)
        plain = [pltpu.make_async_copy(a, b, sems.at[n]) for n, (a, b) in enumerate(sum(panels, []))]
        for copy in plain:
            copy.start()

        def move(started):
            at = len(plain)
            for k in range(4):
                for half in range(2):
                    for j in range(2):
                        source = refs[1 + 4 * half + k].at[pl.ds(j * 256, 256)]
                        block = 2 * (2 * half + j) + places[0, k]

                        @pl.when(places[1, k] == 0)
                        def _():
                            row = pl.multiple_of(block * 256, 256)
                            target = out.at[pl.ds(row, 256), pl.ds(2 * HALF, HALF)]
                            copy = pltpu.make_async_copy(source, target, sems.at[at])
                            copy.wait() if started else copy.start()

                        @pl.when(places[1, k] == 1)
                        def _():
                            for n in range(2):
                                row = pl.multiple_of(block * HD, HD)
                                target = out_matrix.at[pl.ds(row, HD), pl.ds(n * HALF, HALF)]
                                copy = pltpu.make_async_copy(source.at[pl.ds(n * HD, HD)], target, sems.at[at + n])
                                copy.wait() if started else copy.start()

                        at += 2

        move(False)
        for copy in plain:
            copy.wait()
        move(True)

    return pl.pallas_call(
        body,
        out_shape=[bf(D, 3 * HALF), bf(HALF, D)],
        in_specs=[_smem()] + [anywhere] * 9,
        out_specs=[_vmem()] * 2,
        scratch_shapes=[pltpu.SemaphoreType.DMA((64,))],
        compiler_params=pltpu.CompilerParams(vmem_limit_bytes=48 * 2**20),
        cost_estimate=pl.CostEstimate(flops=0, bytes_accessed=64 * 2**20, transcendentals=0),
        name="assemble",
    )(w.places, *w.arrays)


class Resident:
    def __init__(self, w, panels):
        self.w = w
        self.panels = panels
        step = w.cx // 4 * panels
        self.pieces = [(n * step, step) for n in range(4 // panels)] + [(w.cx, w.cy)]

    def scratch(self):
        w = self.w
        return [pltpu.VMEM((w.depth, w.cx + w.cy), BF), pltpu.SemaphoreType.DMA((80,))]

    def start(self, places, refs, whole, sems):
        panels, chunks = _copies(self.w, places, refs, whole)
        n = self.panels
        pieces = [sum(panels[k : k + n], []) for k in range(0, 4, n)] + [chunks]
        numbers = [sum(len(p) for p in pieces[:n]) for n in range(len(pieces))]
        copies = [
            [pltpu.make_async_copy(a, b, sems.at[first + m]) for m, (a, b) in enumerate(piece)]
            for first, piece in zip(numbers, pieces)
        ]

        def begin(n):
            if n < len(copies):
                for copy in copies[n]:
                    copy.start()

        def arrive(n):
            for copy in copies[n]:
                copy.wait()

        begin(0)
        begin(1)
        return begin, arrive

    def forward(self, places, refs, whole, sems, first, x, tile, finish):
        begin, arrive = self.start(places, refs, whole, sems)
        first()
        for n, (start, width) in enumerate(self.pieces):
            arrive(n)
            begin(n + 2)
            for column in range(start, start + width, tile):
                size = min(tile, start + width - column)
                finish(jnp.dot(x[...], whole[:, column : column + size], preferred_element_type=F32), column)

    def backward(self, places, refs, whole, sems, first, dy, tile, finish):
        begin, arrive = self.start(places, refs, whole, sems)
        first()
        for n, (start, width) in enumerate(self.pieces):
            arrive(n)
            begin(n + 2)
            left = dy[:, start : start + width]
            for row in range(0, self.w.depth, tile):
                finish(lax.dot_general(left, whole[row : row + tile, start : start + width], **NT), row, n)

    def call(self, body, name, ins, outs, flops, scratch=()):
        w = self.w
        anywhere = pl.BlockSpec(memory_space=pl.ANY)
        size = 2 * w.depth * (w.cx + w.cy) + sum(v.size * v.dtype.itemsize for v in ins)
        return pl.pallas_call(
            body,
            out_shape=outs,
            in_specs=[_smem()] + [anywhere] * 9 + [_vmem()] * len(ins),
            out_specs=[_vmem()] * len(outs),
            scratch_shapes=self.scratch() + list(scratch),
            compiler_params=pltpu.CompilerParams(vmem_limit_bytes=60 * 2**20),
            cost_estimate=pl.CostEstimate(flops=flops, bytes_accessed=size, transcendentals=0),
            name=name,
        )(w.places, *w.arrays, *ins)


WIDE = D + 128


def _f32(*shape):
    return jax.ShapeDtypeStruct(shape, F32)


def _pair_up(core, own, other, pair):
    pair[pl.ds(pl.multiple_of(core * ROWS, ROWS), ROWS), :] = own[...]
    pair[pl.ds(pl.multiple_of((1 - core) * ROWS, ROWS), ROWS), :] = other[...]


def _split(core, sums, keep, give):
    keep[...] = sums[pl.ds(pl.multiple_of(core * ROWS, ROWS), ROWS), :]
    give[...] = sums[pl.ds(pl.multiple_of((1 - core) * ROWS, ROWS), ROWS), :].astype(BF)


def _in_group(rows, columns, count):
    row = lax.broadcasted_iota(jnp.int32, (rows, columns), 0) >= ROWS
    column = lax.broadcasted_iota(jnp.int32, (rows, columns), 1) >= count
    return row == column


def _own_group(low, count):
    row = lax.broadcasted_iota(jnp.int32, (low.shape[0], count), 0)
    return jnp.where(row >= ROWS, low[:, count:], low[:, :count])


def _put_low(sums, low):
    count = low.shape[1]
    sums[:, D:] = jnp.zeros((sums.shape[0], WIDE - D), F32)
    sums[:, D : D + count] = low


def gate_and_up(w, own, other, maps_down, maps_up):
    rows = 2 * ROWS
    plan = Resident(w, 1)

    def body(places, *refs):
        weights, (own_ref, other_ref, down_ref, up_ref, gu, mixed, pair, low_ref, whole, sems) = refs[:9], refs[9:]

        def first():
            _pair_up(places[2, 0], own_ref, other_ref, pair)
            low = 2.0 * lax.dot_general(pair[:, :D], down_ref[...], **NT).astype(BF).astype(F32)
            low_ref[...] = jnp.where(_in_group(rows, 4 * RANK, 2 * RANK), low, 0.0).astype(BF)

        def finish(total, column):
            width = total.shape[1]
            total = total + jnp.dot(low_ref[...], up_ref[:, column : column + width], preferred_element_type=F32)
            gu[:, column : column + width] = total.astype(BF)
            unit = column // 2
            for m in range(width // 256):
                g, u = total[:, 256 * m : 256 * m + 128], total[:, 256 * m + 128 : 256 * m + 256]
                mixed[:, unit + 128 * m : unit + 128 * (m + 1)] = (g * jax.nn.sigmoid(g) * u).astype(BF)

        plan.forward(places, weights, whole, sems, first, pair.at[:, pl.ds(0, D)], 768, finish)

    outs = [bf(rows, 2 * FF), bf(rows, FF), bf(rows, WIDE), bf(rows, 4 * RANK)]
    return plan.call(body, "gate_and_up", [own, other, maps_down, maps_up], outs, 2 * rows * D * 2 * FF)


def down(w, x, maps_down):
    rows = x.shape[0]
    plan = Resident(w, 2)

    def body(places, *refs):
        weights, (x_ref, down_ref, keep, give, whole, sems, sums) = refs[:9], refs[9:]

        def first():
            _put_low(sums, _own_group(lax.dot_general(x_ref[...], down_ref[...], **NT), RANK))

        def finish(total, column):
            sums[:, column : column + total.shape[1]] = total

        plan.forward(places, weights, whole, sems, first, x_ref, 512, finish)
        _split(places[2, 0], sums, keep, give)

    outs = [_f32(ROWS, WIDE), bf(ROWS, WIDE)]
    return plan.call(body, "down", [x, maps_down], outs, 2 * rows * D * FF, [pltpu.VMEM((rows, WIDE), F32)])


def down_back(w, own, other, maps_up, maps_down, gu):
    rows = 2 * ROWS
    plan = Resident(w, 4)

    def body(places, *refs):
        weights, (own_ref, other_ref, up_ref, down_ref, gu_ref, out, pair, low_ref, whole, sems, sums) = refs[:9], refs[9:]

        def first():
            _pair_up(places[2, 0], own_ref, other_ref, pair)
            low = 2.0 * lax.dot_general(pair[:, :D], up_ref[...], **NT)
            low_ref[...] = jnp.where(_in_group(rows, 2 * RANK, RANK), low, 0.0).astype(BF)

        def finish(part_sum, row, part):
            units = slice(row, row + part_sum.shape[1])
            if part == 0:
                sums[:, units] = part_sum + jnp.dot(low_ref[...], down_ref[:, units], preferred_element_type=F32)
            else:
                d_mixed = sums[:, units] + part_sum
                column = 2 * row
                for m in range(part_sum.shape[1] // 128):
                    g = gu_ref[:, column + 256 * m : column + 256 * m + 128].astype(F32)
                    u = gu_ref[:, column + 256 * m + 128 : column + 256 * (m + 1)].astype(F32)
                    d = d_mixed[:, 128 * m : 128 * (m + 1)]
                    s = jax.nn.sigmoid(g)
                    out[:, column + 256 * m : column + 256 * m + 128] = (d * u * s * (1.0 + g * (1.0 - s))).astype(BF)
                    out[:, column + 256 * m + 128 : column + 256 * (m + 1)] = (d * g * s).astype(BF)

        plan.backward(places, weights, whole, sems, first, pair, 1024, finish)

    outs = [bf(rows, 2 * FF), bf(rows, WIDE), bf(rows, 2 * RANK)]
    scratch = [pltpu.VMEM((rows, FF), F32)]
    return plan.call(body, "down_back", [own, other, maps_up, maps_down, gu], outs, 2 * rows * D * FF, scratch)


def gate_and_up_back(w, dy, maps_up):
    rows = dy.shape[0]
    plan = Resident(w, 2)

    def body(places, *refs):
        weights, (dy_ref, up_ref, keep, give, whole, sems, sums) = refs[:9], refs[9:]

        def first():
            _put_low(sums, _own_group(lax.dot_general(dy_ref[...], up_ref[...], **NT), 2 * RANK))

        def finish(part_sum, row, part):
            units = slice(row, row + part_sum.shape[1])
            if part == 0:
                sums[:, units] = part_sum
            else:
                sums[:, units] += part_sum

        plan.backward(places, weights, whole, sems, first, dy_ref, 1024, finish)
        _split(places[2, 0], sums, keep, give)

    outs = [_f32(ROWS, WIDE), bf(ROWS, WIDE)]
    return plan.call(
        body, "gate_and_up_back", [dy, maps_up], outs, 2 * rows * D * 2 * FF, [pltpu.VMEM((rows, WIDE), F32)]
    )


def project_qkv(x, w, low, maps_up):
    rows, tile = x.shape[0], 512

    def body(x, w, low, up, out, squares):
        i = pl.program_id(0)

        @pl.when(i == 0)
        def _():
            squares[...] = jnp.zeros_like(squares)

        total = jnp.dot(x[...], w[...], preferred_element_type=F32)
        total = total + jnp.dot(low[...], up[...], preferred_element_type=F32)
        out[...] = total
        here = lax.broadcasted_iota(jnp.int32, squares.shape, 1) == i // 2
        squares[...] += jnp.where(here, jnp.sum(total * total, axis=1, keepdims=True), 0.0)

    whole = lambda v: pl.BlockSpec(v.shape, lambda i: (0, 0))
    column = lambda n: pl.BlockSpec((n, tile), lambda i: (0, i))
    return pl.pallas_call(
        body,
        grid=(3 * HALF // tile,),
        out_shape=[_f32(rows, 3 * HALF), _f32(rows, 128)],
        in_specs=[whole(x), column(D), whole(low), column(maps_up.shape[0])],
        out_specs=[column(rows), pl.BlockSpec((rows, 128), lambda i: (0, 0))],
        compiler_params=pltpu.CompilerParams(vmem_limit_bytes=32 * 2**20),
        cost_estimate=pl.CostEstimate(flops=2 * rows * D * 3 * HALF, bytes_accessed=18_000_000, transcendentals=0),
        name="project_qkv",
    )(x, w, low, maps_up)


def project_out(me, heads, w, maps_down):
    rows = 2 * ROWS

    def body(me, heads, w, down, keep, give, flat, sums):
        flat[...] = jnp.concatenate([heads[h] for h in range(8)], axis=1)
        for n in range(0, D, 512):
            sums[:, n : n + 512] = jnp.dot(flat[...], w[:, n : n + 512], preferred_element_type=F32)
        _put_low(sums, _own_group(lax.dot_general(flat[...], down[...], **NT), RANK))
        _split(me[CORE], sums, keep, give)

    outs = [_f32(ROWS, WIDE), bf(ROWS, WIDE), bf(rows, HALF)]
    return _plain(body, "project_out", outs, [heads, w, maps_down], [me], [pltpu.VMEM((rows, WIDE), F32)])


def _low_and_sum(me, keep, got, maps, count, factor):
    total = keep[...] + got[...].astype(F32)
    low = (factor * total[:, D : D + count]).astype(BF)
    start = pl.multiple_of(me[CORE] * count, count)
    return total[:, :D], low, jnp.dot(low, maps[pl.ds(start, count), :], preferred_element_type=F32)


def _send(out, value, low):
    out[:, :D] = value.astype(BF)
    out[:, D:] = jnp.zeros((ROWS, WIDE - D), BF)
    out[:, D : D + low.shape[1]] = low


def _inverse(field):
    return lax.rsqrt(jnp.mean(field * field, axis=1, keepdims=True) + EPS)


def combine_attention(me, keep, got, tokens, gains, maps_up):
    def body(me, keep, got, tokens, gains, up, pre, hidden, out):
        total, low, raised = _low_and_sum(me, keep, got, up, RANK, 1.0)
        field = total + 2.0 * raised
        pre[...] = field
        value = tokens[...].astype(F32) + field * _inverse(field) * gains[2:3]
        hidden[...] = value
        _send(out, value, low)

    outs = [_f32(ROWS, D), _f32(ROWS, D), bf(ROWS, WIDE)]
    return _plain(body, "combine_attention", outs, [keep, got, tokens, gains, maps_up], [me])


def combine_output(me, keep, got, hidden, cotangent, gains, maps_up):
    def body(me, keep, got, hidden, cotangent, gains, up, output, out):
        total, low, raised = _low_and_sum(me, keep, got, up, RANK, 1.0)
        field = total + 2.0 * raised
        inverse = _inverse(field)
        output[...] = (hidden[...] + field * inverse * gains[3:4]).astype(BF)
        _send(out, normalize_back(field, inverse, gains[3:4], cotangent[...].astype(F32)), low)

    outs = [bf(ROWS, D), bf(ROWS, WIDE)]
    return _plain(body, "combine_output", outs, [keep, got, hidden, cotangent, gains, maps_up], [me])


def combine_hidden(me, keep, got, cotangent, pre, gains, maps_down):
    def body(me, keep, got, cotangent, pre, gains, down, hidden, out):
        total, low, lowered = _low_and_sum(me, keep, got, down, 2 * RANK, 2.0)
        value = cotangent[...].astype(F32) + total + lowered
        hidden[...] = value
        field = pre[...]
        _send(out, normalize_back(field, _inverse(field), gains[2:3], value), low)

    outs = [_f32(ROWS, D), bf(ROWS, WIDE)]
    return _plain(body, "combine_hidden", outs, [keep, got, cotangent, pre, gains, maps_down], [me])


def combine_tokens(me, keep, got, hidden, maps_down):
    def body(me, keep, got, hidden, down, out, low_out):
        total, low, lowered = _low_and_sum(me, keep, got, down, 3 * RANK, 2.0)
        out[...] = (hidden[...] + total + lowered).astype(BF)
        low_out[...] = jnp.zeros_like(low_out)
        low_out[:, : 3 * RANK] = low

    outs = [bf(ROWS, D), bf(ROWS, 128)]
    return _plain(body, "combine_tokens", outs, [keep, got, hidden, maps_down], [me])


def project_out_back(me, own, other, w, maps_up, maps_down):
    rows = 2 * ROWS

    def body(me, own, other, w, up, down, heads, pair, low_ref):
        _pair_up(me[CORE], own, other, pair)
        low = 2.0 * lax.dot_general(pair[:, :D], up[...], **NT)
        low_ref[...] = jnp.where(_in_group(rows, 2 * RANK, RANK), low, 0.0).astype(BF)
        for n in range(0, HALF, 512):
            total = lax.dot_general(pair[:, :D], w[n : n + 512, :], **NT)
            total = total + jnp.dot(low_ref[...], down[:, n : n + 512], preferred_element_type=F32)
            for h in range(4):
                heads[n // HD + h] = total[:, h * HD : (h + 1) * HD].astype(BF)

    outs = [bf(8, rows, HD), bf(rows, WIDE), bf(rows, 2 * RANK)]
    return _plain(body, "project_out_back", outs, [own, other, w, maps_up, maps_down], [me])


def project_qkv_back(me, weighted, value_grad, qkv, squares, sums, w, maps_up):
    rows, tile = 2 * ROWS, 512

    def body(me, wq, wk, dv, q, k, sq, sq_other, su, su_other, w, up, d_qkv, keep, give, acc):
        i = pl.program_id(0)

        @pl.when(i == 0)
        def _():
            inverse = lax.rsqrt((sq[...] + sq_other[...]) / D + EPS)
            mean = (su[...] + su_other[...]) / D
            for n, (weight, field) in enumerate(((wq, q), (wk, k))):
                r, m = inverse[:, n : n + 1], mean[:, n : n + 1]
                d_qkv[:, n * HALF : (n + 1) * HALF] = (r * weight[...] - field[...] * (r * r * r * m)).astype(BF)
            d_qkv[:, 2 * HALF :] = dv[...]
            _put_low(acc, _own_group(lax.dot_general(d_qkv[...], up[...], **NT), 3 * RANK))

        acc[:, pl.ds(pl.multiple_of(i * tile, tile), tile)] = lax.dot_general(d_qkv[...], w[...], **NT)

        @pl.when(i == D // tile - 1)
        def _():
            _split(me[CORE], acc, keep, give)

    once = lambda v: pl.BlockSpec(v.shape, lambda i: (0, 0), pipeline_mode=pl.Buffered(1))
    third = lambda n: pl.BlockSpec((rows, HALF), lambda i: (0, n), pipeline_mode=pl.Buffered(1))
    ins = [*weighted, value_grad]
    return pl.pallas_call(
        body,
        grid=(D // tile,),
        out_shape=[bf(rows, 3 * HALF), _f32(ROWS, WIDE), bf(ROWS, WIDE)],
        in_specs=[_smem()]
        + [once(v) for v in ins]
        + [third(0), third(1)]
        + [once(v) for v in (*squares, *sums)]
        + [pl.BlockSpec((tile, 3 * HALF), lambda i: (i, 0)), once(maps_up)],
        out_specs=[once(jax.ShapeDtypeStruct((rows, 3 * HALF), BF))] + [once(_f32(ROWS, WIDE))] * 2,
        scratch_shapes=[pltpu.VMEM((rows, WIDE), F32)],
        compiler_params=pltpu.CompilerParams(vmem_limit_bytes=48 * 2**20),
        cost_estimate=pl.CostEstimate(flops=2 * rows * D * 3 * HALF, bytes_accessed=22_000_000, transcendentals=0),
        name="project_qkv_back",
    )(me, *ins, qkv, qkv, *squares, *sums, w, maps_up)


class Gather:
    def __init__(self):
        core = lax.axis_index("c")
        x, z = lax.axis_index("x"), lax.axis_index("z")
        yl, yh = lax.axis_index("yl"), lax.axis_index("yh")
        y = 2 * yh + yl
        sign = 1 - 2 * core
        ys = [lax.rem(y - sign * k + 8, 4) for k in range(4)]
        zs = [lax.rem(z - sign * k + 8, 4) for k in range(4)]
        self.yh = yh
        self.me = jnp.stack([core, x, yl, yh] + zs).astype(jnp.int32)
        self.places = jnp.stack([jnp.stack([v // 2 for v in ys]), jnp.stack([v % 2 for v in ys]), self.me[:4]]).astype(jnp.int32)
        self.lanes = {"y0": Lane(), "y1": Lane(), "z": Lane(), "cross": Lane()}

    def across(self, own):
        return self.lanes["cross"].send(own, "cross")

    def over_xz(self, own, other, *before):
        other = after(other, *before)
        both = jnp.where(self.yh == 0, jnp.stack([own, other]), jnp.stack([other, own]))
        return lax.all_gather(both, ("x", "z")).reshape(4, 4, 2, *own.shape)

    def small(self, own):
        got = [own]
        for _ in range(3):
            got.append(self.lanes["z"].send(got[-1], "z"))
        return got

    def round(self, rings, *before):
        for n in range(2):
            value = after(rings[n][-1], *before) if before else rings[n][-1]
            rings[n].append(self.lanes["y%d" % n].send(value, "y"))


def turn(value, cosine, sine):
    return value * cosine + pltpu.roll(value, 64, 1) * sine


def _pack_body(me, q, k, v, squares, other, gains, cosine, sine, out):
    scales = lax.rsqrt((squares[...] + other[...]) / D + EPS)
    c, s = cosine[...], sine[...]
    out[0, :, 0:HD] = turn(q[...] * scales[:, 0:1] * gains[0:1], c, s).astype(BF)
    out[0, :, HD : 2 * HD] = turn(k[...] * scales[:, 1:2] * gains[1:2], c, s).astype(BF)
    out[0, :, 2 * HD :] = v[...].astype(BF)


def pack_heads(me, qkv, squares, other, gains, cosine, sine):
    rows = qkv.shape[0]
    whole = lambda shape: pl.BlockSpec(shape, lambda i, me: (0, 0))
    return pl.pallas_call(
        _pack_body,
        out_shape=jax.ShapeDtypeStruct((8, rows, 3 * HD), BF),
        grid_spec=pltpu.PrefetchScalarGridSpec(
            num_scalar_prefetch=1,
            grid=(8,),
            in_specs=[
            pl.BlockSpec((rows, HD), lambda i, me: (0, i)),
            pl.BlockSpec((rows, HD), lambda i, me: (0, 8 + i)),
            pl.BlockSpec((rows, HD), lambda i, me: (0, 16 + i)),
            whole((rows, 128)),
            whole((rows, 128)),
            pl.BlockSpec((4, HD), lambda i, me: (0, 2 * i + me[CORE])),
            whole((rows, HD)),
            whole((rows, HD)),
        ],
            out_specs=pl.BlockSpec((1, rows, 3 * HD), lambda i, me: (i, 0, 0)),
        ),
        name="pack_heads",
    )(me, qkv, qkv, qkv, squares, other, gains, cosine, sine)


def _unpack_body(me, d, q, k, gains, cosine, sine, wq, wk, dv, sums):
    c, s = cosine[...], -sine[...]
    i = pl.program_id(0)
    gq = turn(d[0, :, 0:HD].astype(F32), c, s) * gains[0:1]
    gk = turn(d[0, :, HD : 2 * HD].astype(F32), c, s) * gains[1:2]
    wq[...] = gq
    wk[...] = gk
    dv[...] = d[0, :, 2 * HD :]

    @pl.when(i == 0)
    def _():
        sums[...] = jnp.zeros_like(sums)

    lane = lax.broadcasted_iota(jnp.int32, sums.shape, 1)
    of_q = jnp.sum(gq * q[...], axis=1, keepdims=True)
    of_k = jnp.sum(gk * k[...], axis=1, keepdims=True)
    sums[...] += jnp.where(lane == 0, of_q, jnp.where(lane == 1, of_k, 0.0))


def unpack_heads(me, d, qkv, gains, cosine, sine):
    rows = qkv.shape[0]
    whole = lambda shape: pl.BlockSpec(shape, lambda i, me: (0, 0))
    column = pl.BlockSpec((rows, HD), lambda i, me: (0, i))
    return pl.pallas_call(
        _unpack_body,
        out_shape=[
            jax.ShapeDtypeStruct((rows, HALF), F32),
            jax.ShapeDtypeStruct((rows, HALF), F32),
            jax.ShapeDtypeStruct((rows, HALF), BF),
            jax.ShapeDtypeStruct((rows, HD), F32),
        ],
        grid_spec=pltpu.PrefetchScalarGridSpec(
            num_scalar_prefetch=1,
            grid=(8,),
            in_specs=[
            pl.BlockSpec((1, rows, 3 * HD), lambda i, me: (i, 0, 0)),
            pl.BlockSpec((rows, HD), lambda i, me: (0, i)),
            pl.BlockSpec((rows, HD), lambda i, me: (0, 8 + i)),
            pl.BlockSpec((4, HD), lambda i, me: (0, 2 * i + me[CORE])),
            whole((rows, HD)),
            whole((rows, HD)),
        ],
            out_specs=[column, column, column, whole((rows, HD))],
        ),
        name="unpack_heads",
    )(me, d, qkv, qkv, gains, cosine, sine)


TILE = 128
def hidden_pairs(t, bound):
    query = t * TILE + lax.broadcasted_iota(jnp.int32, (TILE, TILE), 0)
    key = t * TILE + lax.broadcasted_iota(jnp.int32, (TILE, TILE), 1)
    hidden = key > query
    if t * TILE >= PROMPT:
        hidden = hidden | ((query >= bound) & (key < bound))
    return hidden


def tile_scores(q, k, t, bound):
    n = (t + 1) * TILE
    s = lax.dot_general(q[t * TILE : n], k[:n], **NT) * SCALE
    last = jnp.where(hidden_pairs(t, bound), -1e30, s[:, n - TILE :])
    return last if t == 0 else jnp.concatenate([s[:, : n - TILE], last], axis=1)


def _attend_body(bounds, qkv, out, exact, total):
    bound = bounds[pl.program_id(0)]
    q = qkv[:, 0, :, 0:HD].reshape(TOTAL, HD)
    k = qkv[:, 0, :, HD : 2 * HD].reshape(TOTAL, HD)
    v = qkv[:, 0, :, 2 * HD :].reshape(TOTAL, HD)
    for t in range(TOTAL // TILE):
        n = (t + 1) * TILE
        s = tile_scores(q, k, t, bound)
        top = jnp.max(s, axis=1, keepdims=True)
        p = jnp.exp(s - top)
        denom = jnp.sum(p, axis=1, keepdims=True)
        o = jnp.dot(p.astype(BF), v[:n], preferred_element_type=F32) / denom
        exact[0, t * TILE : n] = o
        total[0, t * TILE : n] = top + jnp.log(denom)
    out[:, 0] = exact[0].reshape(8, ROWS, HD).astype(BF)


def attend(bounds, qkv):
    return pl.pallas_call(
        _attend_body,
        grid=(2,),
        out_shape=[
            jax.ShapeDtypeStruct((8, 2, ROWS, HD), BF),
            jax.ShapeDtypeStruct((2, TOTAL, HD), F32),
            jax.ShapeDtypeStruct((2, TOTAL, 1), F32),
        ],
        in_specs=[
            pl.BlockSpec(memory_space=pltpu.SMEM),
            pl.BlockSpec((8, 1, ROWS, 3 * HD), lambda g: (0, g, 0, 0)),
        ],
        out_specs=[
            pl.BlockSpec((8, 1, ROWS, HD), lambda g: (0, g, 0, 0)),
            pl.BlockSpec((1, TOTAL, HD), lambda g: (g, 0, 0)),
            pl.BlockSpec((1, TOTAL, 1), lambda g: (g, 0, 0)),
        ],
        compiler_params=pltpu.CompilerParams(vmem_limit_bytes=40 * 2**20),
        cost_estimate=pl.CostEstimate(flops=900_000_000, bytes_accessed=5_000_000, transcendentals=1_500_000),
        name="attend",
    )(bounds, qkv)


def _attend_back_body(bounds, qkv, grad, exact, total, out, dk, dv, dq):
    bound = bounds[pl.program_id(0)]
    q = qkv[:, 0, :, 0:HD].reshape(TOTAL, HD)
    k = qkv[:, 0, :, HD : 2 * HD].reshape(TOTAL, HD)
    v = qkv[:, 0, :, 2 * HD :].reshape(TOTAL, HD)
    g = grad[:, 0].reshape(TOTAL, HD)
    dk[...] = jnp.zeros_like(dk)
    dv[...] = jnp.zeros_like(dv)
    for t in range(TOTAL // TILE):
        n = (t + 1) * TILE
        here = slice(t * TILE, n)
        s = tile_scores(q, k, t, bound)
        p = jnp.exp(s - total[0, here])
        delta = jnp.sum(g[here].astype(F32) * exact[0, here], axis=1, keepdims=True)
        dp = lax.dot_general(g[here], v[:n], **NT)
        ds = (p * (dp - delta)).astype(BF)
        dq[here] = jnp.dot(ds, k[:n], preferred_element_type=F32) * SCALE
        dk[:n] += lax.dot_general(ds, q[here], **TN) * SCALE
        dv[:n] += lax.dot_general(p.astype(BF), g[here], **TN)
    out[:, 0, :, 0:HD] = dq[...].reshape(8, ROWS, HD).astype(BF)
    out[:, 0, :, HD : 2 * HD] = dk[...].reshape(8, ROWS, HD).astype(BF)
    out[:, 0, :, 2 * HD :] = dv[...].reshape(8, ROWS, HD).astype(BF)


def attend_back(bounds, qkv, grad, exact, total):
    return pl.pallas_call(
        _attend_back_body,
        grid=(2,),
        out_shape=jax.ShapeDtypeStruct((8, 2, ROWS, 3 * HD), BF),
        in_specs=[
            pl.BlockSpec(memory_space=pltpu.SMEM),
            pl.BlockSpec((8, 1, ROWS, 3 * HD), lambda g: (0, g, 0, 0)),
            pl.BlockSpec((8, 1, ROWS, HD), lambda g: (0, g, 0, 0)),
            pl.BlockSpec((1, TOTAL, HD), lambda g: (g, 0, 0)),
            pl.BlockSpec((1, TOTAL, 1), lambda g: (g, 0, 0)),
        ],
        out_specs=pl.BlockSpec((8, 1, ROWS, 3 * HD), lambda g: (0, g, 0, 0)),
        scratch_shapes=[pltpu.VMEM((TOTAL, HD), F32)] * 3,
        compiler_params=pltpu.CompilerParams(vmem_limit_bytes=40 * 2**20),
        cost_estimate=pl.CostEstimate(flops=2_300_000_000, bytes_accessed=8_000_000, transcendentals=1_500_000),
        name="attend_back",
    )(bounds, qkv, grad, exact, total)


def dot(a, b):
    return jnp.dot(a, b, preferred_element_type=F32)


def dot_nt(a, b):
    return lax.dot_general(a, b, **NT)


def dot_tn(a, b):
    return lax.dot_general(a, b, **TN)


def normalize_back(field, inverse, gain, grad):
    weighted = grad * gain
    return inverse * weighted - field * inverse**3 * jnp.mean(weighted * field, axis=-1, keepdims=True)


def choose_adapters(slots, down_in, down_ff, up_model, up_hidden):
    def body(slots, down_in, down_ff, up_model, up_hidden, qkv_down, gu_down, out_down, ff_down, qkv_up, out_up, ff_up, gu_up):
        core = slots[2]
        qkv_down[...] = down_in[0, :3].reshape(3 * RANK, D)
        gu_down[...] = down_in[0, 4:].reshape(2 * RANK, D)
        out_up[...] = up_model[0, 3]
        ff_up[...] = up_model[0, 4]
        qkv_up[...] = jnp.zeros_like(qkv_up)
        gu_up[...] = jnp.zeros_like(gu_up)
        for h in range(8):
            head = pl.ds(pl.multiple_of((2 * h + core) * HD, HD), HD)
            out_down[:, HD * h : HD * (h + 1)] = down_in[0, 3, :, head]
            for n in range(3):
                here = slice(n * HALF + HD * h, n * HALF + HD * (h + 1))
                qkv_up[n * RANK : (n + 1) * RANK, here] = up_model[0, n, :, head]
        for m in range(FF // 128):
            start = (2 * (m // 4) + core) * 512 + (m % 4) * 128
            units = pl.ds(pl.multiple_of(start, 128), 128)
            ff_down[:, 128 * m : 128 * (m + 1)] = down_ff[0, :, units]
            for n in range(2):
                here = slice(256 * m + 128 * n, 256 * m + 128 * (n + 1))
                gu_up[n * RANK : (n + 1) * RANK, here] = up_hidden[0, n, :, units]

    def chosen(shape):
        return pl.BlockSpec((1,) + shape[1:], lambda g, slots: (slots[g],) + (0,) * (len(shape) - 1))

    shapes = [(48, D), (32, D), (16, HALF), (16, FF), (48, 3 * HALF), (16, D), (16, D), (32, 2 * FF)]
    maps = [down_in, down_ff, up_model, up_hidden]
    return pl.pallas_call(
        body,
        out_shape=[bf(2 * r, c) for r, c in shapes],
        grid_spec=pltpu.PrefetchScalarGridSpec(
            num_scalar_prefetch=1,
            grid=(2,),
            in_specs=[chosen(m.shape) for m in maps],
            out_specs=[pl.BlockSpec(shape, lambda g, slots: (g, 0)) for shape in shapes],
        ),
        cost_estimate=pl.CostEstimate(flops=0, bytes_accessed=7_000_000, transcendentals=0),
        name="choose_adapters",
    )(slots, *maps)


def rank_gradients(lows, acts, core, name, plan, width):
    count = len(lows)

    def body(core, *refs):
        lows, acts, out = refs[:count], refs[count:-1], refs[-1]
        at = 0
        for low, act, columns, factor, starts in plan:
            picked = [lows[low][:, c : c + RANK] for c in columns]
            picked = jnp.concatenate(picked, axis=1)
            if columns[0] == columns[1]:
                picked = jnp.where(_in_group(2 * ROWS, 2 * RANK, RANK), picked, jnp.zeros_like(picked))
            if factor != 1:
                picked = picked * factor
            for start in starts(core[0]):
                right = acts[act][:, start if isinstance(start, slice) else pl.ds(pl.multiple_of(start, 128), 128)]
                n = right.shape[1]
                grad = lax.dot_general(picked, right, **TN).astype(BF)
                for b in range(n // 128):
                    block, slot = divmod(at, width // 128)
                    out[block, :, 128 * slot : 128 * (slot + 1)] = grad[:, 128 * b : 128 * (b + 1)]
                    at += 1

    return _plain(body, name, [bf(8, 2 * RANK, width)], list(lows) + list(acts), [core])[0]


def adapter_outputs(core, halves, others, count, shapes, name, write):
    def body(core, *refs):
        own, other, outs = refs[:count], refs[count : 2 * count], refs[2 * count :]

        def place(start):
            return pl.ds(pl.multiple_of(start, 128), 128)

        for side, group in ((core[0], own), (1 - core[0], other)):

            def piece(n, at):
                block, slot = divmod(at, group[n].shape[3] // 128)
                return group[n][block, 0, :, 128 * slot : 128 * (slot + 1)].astype(F32)

            write(side, piece, place, outs)

    arrays = halves + others
    size = sum(v.size * 2 for v in arrays)
    return pl.pallas_call(
        body,
        grid=(8,),
        out_shape=[jax.ShapeDtypeStruct(s, F32) for s in shapes],
        in_specs=[_smem()] + [pl.BlockSpec((v.shape[0], 1) + v.shape[2:], lambda i: (0, i, 0, 0)) for v in arrays],
        out_specs=[pl.BlockSpec((1,) + s[1:], lambda i, n=len(s): (i,) + (0,) * (n - 1)) for s in shapes],
        compiler_params=pltpu.CompilerParams(vmem_limit_bytes=40 * 2**20),
        cost_estimate=pl.CostEstimate(flops=0, bytes_accessed=size, transcendentals=0),
        name=name,
    )(core, *arrays)


def write_early(side, piece, place, outs):
    up_hidden, down_ff = outs
    for m in range(FF // 128):
        units = place((2 * (m // 4) + side) * 512 + (m % 4) * 128)
        up_hidden[0, 0, :, units] = piece(0, m)
        up_hidden[0, 1, :, units] = piece(0, 32 + m)
        down_ff[0, :, units] = piece(0, 64 + m)


def write_late(side, piece, place, outs):
    down_in, up_model = outs
    for m in range(8):
        whole, head = place(side * HALF + 128 * m), place((2 * m + side) * HD)
        for n in range(3):
            down_in[0, n, :, whole] = piece(0, 8 * n + m)
            up_model[0, n, :, head] = piece(0, 24 + 8 * n + m)
        down_in[0, 4, :, whole] = piece(0, 48 + m)
        down_in[0, 5, :, whole] = piece(0, 56 + m)
        down_in[0, 3, :, head] = piece(0, 64 + m)
        up_model[0, 3, :, whole] = piece(0, 72 + m)
        up_model[0, 4, :, whole] = piece(1, EARLY // 128 - 8 + m)


def on_device(
    tokens,
    cotangent,
    query_matrix,
    key_matrix,
    value_matrix,
    output_matrix,
    gate_matrix,
    upward_matrix,
    down_matrix,
    gains,
    adapter_down_inputs,
    adapter_down_feedforward,
    adapter_up_model_maps,
    adapter_up_hidden_maps,
    group_adapter_index,
    continuation_lengths,
):
    core = lax.axis_index("c")
    first = core == 0
    ctx = lax.axis_index("yl") * 4 + lax.axis_index("x")
    tokens, cotangent = tokens[0], cotangent[0]

    def both(own, other):
        return jnp.where(first, jnp.stack([own, other]), jnp.stack([other, own]))

    def rows_of_both(own):
        return both(own, swap(own)).reshape(2 * own.shape[0], own.shape[1])

    plan = Gather()
    me, places = plan.me, plan.places
    keep_a, give_a = split_a(me, query_matrix, key_matrix, value_matrix)
    keep_g, give_g = split_g(me, gate_matrix, upward_matrix)
    got_a, got_g = swap(give_a), swap(give_g)
    xs_a, ys_a = parts_a(me, keep_a, got_a, output_matrix)
    xs_m, ys_g, ys_d = parts_m(me, keep_g, got_g, down_matrix)
    crossed = plan.across(xs_a)
    small_a = plan.small(ys_a)
    small_g = plan.small(ys_g)
    xs_a = plan.over_xz(xs_a, crossed, small_a[1])
    crossed = plan.across(after(xs_m, small_a[2]))
    y_a = spread(me, small_a, [(0, HALF, 1)], "spread_a")
    rings_a = [[v] for v in y_a]
    for _ in range(3):
        plan.round(rings_a)
    xs_m = plan.over_xz(xs_m, crossed, rings_a[0][1], rings_a[1][1])
    small_d = plan.small(ys_d)
    y_g = spread(me, small_g, [(0, FF - CUT_G // 2, 1)], "spread_g")
    rings_g = [[v] for v in y_g]
    plan.round(rings_g)
    w_qkv, w_out = assemble(Chunks(256, CUT_A, 4 * HALF, places, xs_a, 0, rings_a))

    facts = jnp.concatenate([group_adapter_index[0], continuation_lengths[0]]).astype(F32)
    facts = jnp.broadcast_to(jnp.pad(facts, (0, 125))[None], (8, 128))
    pair_facts = both(facts, swap(facts))[:, 0, :2].astype(jnp.int32)
    slots = pair_facts[:, 0]
    bounds = PROMPT + pair_facts[:, 1]
    (qkv_down, gu_down, out_down, ff_down, qkv_up, out_up2, ff_up2, gu_up) = choose_adapters(
        jnp.concatenate([slots, me[:1]]),
        adapter_down_inputs,
        adapter_down_feedforward,
        adapter_up_model_maps,
        adapter_up_hidden_maps,
    )

    group_row = lax.broadcasted_iota(jnp.int32, (2 * ROWS, 1), 0) // ROWS

    def own_columns(low, count):
        group_column = lax.broadcasted_iota(jnp.int32, (1, 2 * count), 1) // count
        return jnp.where(group_row == group_column, low, jnp.zeros_like(low))

    shard = ("z", "yh")

    def spread_over(value, axes):
        return lax.all_to_all(jnp.broadcast_to(value[None], (8,) + value.shape), axes, 0, 0, tiled=True)

    place = ctx * ROWS + lax.broadcasted_iota(jnp.int32, (2, ROWS), 1)
    position = jnp.where(place >= bounds[:, None], PROMPT + place - bounds[:, None], place)
    freq = BASE ** (-(jnp.arange(HD // 2, dtype=F32) * 2.0 / HD))
    angle = position.reshape(2 * ROWS, 1).astype(F32) * freq[None]
    cosine = jnp.concatenate([jnp.cos(angle)] * 2, axis=1)
    sine = jnp.concatenate([-jnp.sin(angle), jnp.sin(angle)], axis=1)

    def whole(n):
        return lambda core: [slice(0, n)]

    def half(core):
        return [core * HALF + 128 * m for m in range(8)]

    def turns(n):
        return lambda core: [slice(256 * m + 128 * n, 256 * m + 128 * (n + 1)) for m in range(FF // 128)]

    def third(n):
        return lambda core: [slice(n * HALF, (n + 1) * HALF)]

    x2 = rows_of_both(tokens)
    qkv_low = own_columns((2.0 * dot_nt(x2, qkv_down).astype(BF)).astype(BF), 3 * RANK)
    qkv, squares = project_qkv(x2, w_qkv, qkv_low, qkv_up)
    squares = (squares, swap(squares))
    qkv = after(qkv, small_d[1])
    packed = pack_heads(me, qkv, *squares, gains, cosine, sine)
    heads = lax.all_to_all(packed, CTX, 0, 0, tiled=True).reshape(8, 2, ROWS, 3 * HD)
    heads = after(heads, rings_g[0][-1], rings_g[1][-1], small_d[2])
    plan.round(rings_g, qkv)
    out_heads, exact, log_total = attend(bounds, heads)
    attended = lax.all_to_all(out_heads, CTX, 0, 0, tiled=True).reshape(8, 2 * ROWS, HD)
    y_d = spread(me, small_d, [(0, HALF - CUT_D // 2, 2)], "spread_d")
    attended = after(attended, rings_g[0][-1], rings_g[1][-1], y_d[0])
    keep, give, attended = project_out(me, attended, w_out, out_down)
    attn_pre, hidden, sent = combine_attention(me, keep, swap(give), tokens, gains, out_up2)

    plan.round(rings_g, out_heads)
    wg = Chunks(256, CUT_G, 2 * FF, places, xs_m, 0, rings_g)
    rings_d = [[v] for v in y_d]
    plan.round(rings_d)
    gu, mixed, h2, gu_low = gate_and_up(wg, sent, swap(sent), gu_down, gu_up)
    plan.round(rings_d)
    plan.round(rings_d)
    wd = Chunks(512, CUT_D, D, places, xs_m, CUT_G // 4, rings_d)
    keep, give = down(wd, mixed, ff_down)
    output, sent = combine_output(me, keep, swap(give), hidden, cotangent, gains, ff_up2)

    d_gu, d_mlp, ff_grad_low = down_back(wd, sent, swap(sent), ff_up2, ff_down, gu)
    early = rank_gradients(
        [gu_low, ff_grad_low, d_mlp],
        [d_gu, mixed, d_mlp],
        me,
        "early_gradients",
        [
            (0, 0, (0, 2 * RANK), 1, turns(0)),
            (0, 0, (RANK, 3 * RANK), 1, turns(1)),
            (1, 1, (0, RANK), 1, whole(FF)),
            (2, 2, (D, D), 2, half),
        ],
        EARLY,
    )
    d_gu, early = lax.optimization_barrier((d_gu, early))
    early = lax.all_to_all(early, CTX, 0, 0, tiled=True)
    keep, give = gate_and_up_back(wg, d_gu, gu_up)
    give, early = lax.optimization_barrier((give, early))
    d_hidden, sent = combine_hidden(me, keep, swap(give), cotangent, attn_pre, gains, gu_down)

    d_out_heads, d_attn, out_grad_low = project_out_back(me, sent, swap(sent), w_out, out_up2, out_down)
    d_out_heads = lax.all_to_all(d_out_heads, CTX, 0, 0, tiled=True).reshape(8, 2, ROWS, HD)
    own = jnp.sum(early.astype(F32), axis=0).astype(BF)
    own_slot = jnp.repeat(slots, RANK)[:, None] == lax.broadcasted_iota(jnp.int32, (1, 128), 1)
    own = jnp.concatenate([own, own_slot.astype(BF)], axis=1)
    d_out_heads, own = lax.optimization_barrier((d_out_heads, own))
    groups = spread_over(own, shard).reshape(16, RANK, EARLY + 128)
    d_heads = attend_back(bounds, heads, d_out_heads, exact, log_total)
    d_heads, groups = lax.optimization_barrier((d_heads, groups))
    picker = groups[:, 0, EARLY : EARLY + 8]
    d_heads = lax.all_to_all(d_heads, CTX, 0, 0, tiled=True).reshape(8, 2 * ROWS, 3 * HD)
    w_q, w_k, d_v, sums = unpack_heads(me, d_heads, qkv, gains, cosine, sine)

    def by_slot(groups):
        flat = groups.reshape(16, -1)
        return lax.dot_general(picker, flat, **TN).astype(BF).reshape(8 * RANK, -1)

    early, w_q = lax.optimization_barrier((by_slot(groups[:, :, :EARLY]), w_q))
    early = lax.all_gather(early, CTX)
    d_qkv, keep, give = project_qkv_back(me, (w_q, w_k), d_v, qkv, squares, (sums, swap(sums)), w_qkv, qkv_up)
    grad_tokens, low = combine_tokens(me, keep, swap(give), d_hidden, qkv_down)
    low = both(low, swap(low)).reshape(2 * ROWS, 128)

    late = rank_gradients(
        [low, qkv_low, d_attn, out_grad_low, h2],
        [x2, d_qkv, h2, attended, d_attn],
        me,
        "late_gradients",
        [(0, 0, (n * RANK, n * RANK), 1, half) for n in range(3)]
        + [(1, 1, (n * RANK, (3 + n) * RANK), 1, third(n)) for n in range(3)]
        + [
            (2, 2, (D, D), 1, half),
            (2, 2, (D + RANK, D + RANK), 1, half),
            (3, 3, (0, RANK), 1, whole(HALF)),
            (4, 4, (D, D), 2, half),
        ],
        LATE,
    )
    late = lax.all_to_all(late, CTX, 0, 0, tiled=True)
    late = jnp.sum(late.astype(F32), axis=0).astype(BF)
    late = spread_over(late, shard)
    early, late = lax.optimization_barrier((early, late))
    late = spread_over(by_slot(late.reshape(16, RANK, LATE)), CTX)
    shape = (8, 8, RANK, -1)
    early = early.reshape(shape)
    early_other = swap(early)
    grad_up_hidden, grad_down_ff = adapter_outputs(
        me,
        [early],
        [early_other],
        1,
        [(8, 2, RANK, 2 * FF), (8, RANK, 2 * FF)],
        "early_outputs",
        write_early,
    )
    late, grad_up_hidden = lax.optimization_barrier((late, grad_up_hidden))
    late_other = swap(late)
    late, late_other = late.reshape(shape), late_other.reshape(shape)
    grad_down_in, grad_up_model = adapter_outputs(
        me,
        [late, early[7:]],
        [late_other, early_other[7:]],
        2,
        [(8, 6, RANK, D), (8, 5, RANK, D)],
        "late_outputs",
        write_late,
    )
    return (output[None], grad_tokens[None], grad_down_in, grad_down_ff, grad_up_model, grad_up_hidden)


def solution(mesh):
    fine = Mesh(mesh.devices.reshape(2, 4, 4, 2, 2), ALL)
    shard = ("z", "yh", "c")
    rows = P(shard, None)
    per_token = P(shard, CTX, None)
    return jax.shard_map(
        on_device,
        mesh=fine,
        in_specs=(per_token, per_token) + (rows,) * 7 + (P(),) * 5 + (rows, rows),
        out_specs=(per_token, per_token, P(), P(), P(), P()),
        check_vma=False,
    )
```

time: 816 us -> 686 us (0.84)
  waiting for transfers between devices: 285 us -> 231 us
  blocking collectives: 88.3 us -> 37 us
  Pallas kernels: 157 us -> 194 us
  matrix products: 39.7 us -> 2.74 us
  other arithmetic: 38.7 us -> 9.46 us
  starting transfers between devices: 118 us -> 127 us
    ppermute x54 -> x29, waiting for transfers between devices: 192 us -> 117 us  [send(): self.last = lax.ppermute(value, ALL, STEPS[how])]
    all_to_all x0 -> x4, waiting for transfers between devices: none -> 47 us  [the longest x2 31.3 us: spread_over(): lax.all_to_all(jnp.broadcast_to(value[None], (8,) + value.shape), axes, 0...]
    all_gather x5 -> x3, waiting for transfers between devices: 45.3 us -> 0.01 us  [the longest x2 0.01 us: over_xz(): return lax.all_gather(both, ('x', 'z')).reshape(4, 4, 2, *own.shape)]
    all_to_all x1 -> x0, blocking collectives: 43.8 us -> none  [on_device(): lax.all_to_all(d_heads, CTX, 0, 0, tiled=True).reshape(8, 2 * ROWS, 3 * HD)]
    reduce_scatter x1 -> x0, waiting for transfers between devices: 35.1 us -> none  [on_device(): lax.psum_scatter(early.reshape(8 * 2 * RANK, EARLY), CTX, scatter_dimensi...]
    pallas_call x5 -> x7, Pallas kernels: 81.7 us -> 110 us  [the longest x4 81 us: call(): pl.pallas_call(body, out_shape=outs, in_specs=[_smem()] + [anywhere] * 9...]
    all_to_all x1, waiting for transfers between devices: 0.01 us -> 24.1 us  [on_device(): lax.all_to_all(packed, CTX, 0, 0, tiled=True).reshape(8, 2, ROWS, 3 * HD)]
    all_to_all x0 -> x4, starting transfers between devices: none -> 22.1 us  [the longest x2 9.63 us: spread_over(): lax.all_to_all(jnp.broadcast_to(value[None], (8,) + value.shape), axes, 0...]
  transfers between devices with their start and end apart: 82 -> 55, of which waited for: 39 -> 32; matrix products, arithmetic and copies ran while one was open for 11% -> 3% of each run, Pallas kernels for 11% -> 20%
where the time goes in v2:
time: 686 us; the launch traced here: 676 us
  waiting for transfers between devices  231 us (34%)
  Pallas kernels  194 us (28%)
  starting transfers between devices  127 us (19%)
  local copies, waits for them, and re-layouts  59.8 us (9%)
  blocking collectives  37 us (5%)
  between operations  15.6 us (2%)
  other arithmetic  9.46 us (1%)
    ppermute x29, waiting for transfers between devices, send(): self.last = lax.ppermute(value, ALL, STEPS[how])  117 us
    pallas_call x4, Pallas kernels, call(): pl.pallas_call(body, out_shape=outs, in_specs=[_smem()] + [anywhere] * 9...  81 us
    ppermute x29, starting transfers between devices, send(): self.last = lax.ppermute(value, ALL, STEPS[how])  79.1 us
    unnamed x177, local copies, waits for them, and re-layouts  51 us
    pallas_call x15, Pallas kernels, _plain(): pl.pallas_call(body, out_shape=outs, in_specs=[_smem()] * len(scalars) +...  33.9 us
    all_to_all x2, waiting for transfers between devices, spread_over(): lax.all_to_all(jnp.broadcast_to(value[None], (8,) + value.shape), axes, 0...  31.3 us
    all_to_all x1, waiting for transfers between devices, on_device(): lax.all_to_all(packed, CTX, 0, 0, tiled=True).reshape(8, 2, ROWS, 3 * HD)  24.1 us
    all_to_all x1, blocking collectives, on_device(): late = lax.all_to_all(late, CTX, 0, 0, tiled=True)  21.1 us
  transfers between devices with their start and end apart: 55, of which 32 were waited for; matrix products, arithmetic and copies ran while one was open for 3% of the time, Pallas kernels for 20%

profile of v2, /device:TPU:7, one launch (start us, length us, event | category | flops | bytes accessed | tf_op | source)
XLA Modules:
  0.0 675.8 jit_solution(11307384879926520329)
XLA Ops:
  14.7 3.8 collective-permute-start.2
  18.5 2.7 collective-permute-start.4
  21.3 5.5 collective-permute-done.4
  27.7 3.4 split_g.1
  33.1 6.7 collective-permute-done.3.refs_2_
  39.8 3.5 collective-permute-start.6
  44.6 3.2 parts_m.1
  47.8 3.1 collective-permute-start.5
  50.9 4.0 collective-permute-done.6.refs_3_
  55.6 2.7 collective-permute-start.7
  60.7 14.0 %collective-permute-done.5 = bf16[256,2048]{1,0:T(8,128)(2,1)S(1)} collective-permute-done((bf16[256,2048]{1,0:T(8,128)(2,1)S(1)}, bf16[256,2048]{1,0:T(8,128)(2,1)S(1)}, u32[]{:S(2)}, u32[]{:S(2)}) %collective-permute-start.5) | collective-permute-done | bytes 1048608 | tf_op jit(solution)/shard_map/ppermute | solution.py:71
  74.7 9.3 %collective-permute-done.7.refs_2_ = bf16[512,1024]{1,0:T(8,128)(2,1)S(1)} collective-permute-done((bf16[512,1024]{1,0:T(8,128)(2,1)S(1)}, bf16[512,1024]{1,0:T(8,128)(2,1)S(1)}, u32[]{:S(2)}, u32[]{:S(2)}) %collective-permute-start.7) | collective-permute-done | bytes 1048608 | tf_op jit(solution)/shard_map/ppermute | solution.py:71
  84.0 11.2 %collective-permute-done.8.refs_6_ = bf16[512,1024]{1,0:T(8,128)(2,1)S(1)} collective-permute-done((bf16[512,1024]{1,0:T(8,128)(2,1)S(1)}, bf16[512,1024]{1,0:T(8,128)(2,1)S(1)}, u32[]{:S(2)}, u32[]{:S(2)}) %collective-permute-start.8) | collective-permute-done | bytes 1048608 | tf_op jit(solution)/shard_map/ppermute | solution.py:71
  99.1 3.5 collective-permute-start.15
  102.6 6.6 collective-permute-done.9.refs_1_
  114.3 3.4 collective-permute-start.16
  117.7 7.9 %collective-permute-done.19.refs_7_ = bf16[512,1024]{1,0:T(8,128)(2,1)} collective-permute-done((bf16[512,1024]{1,0:T(8,128)(2,1)}, bf16[512,1024]{1,0:T(8,128)(2,1)}, u32[]{:S(2)}, u32[]{:S(2)}) %collective-permute-start.19) | collective-permute-done | bytes 1048608 | tf_op jit(solution)/shard_map/ppermute | solution.py:71
  125.7 3.4 collective-permute-start.20
  130.7 3.8 choose_adapters.1
  134.6 22.8 %collective-permute-done.11.refs_3_ = bf16[256,1536]{1,0:T(8,128)(2,1)} collective-permute-done((bf16[256,1536]{1,0:T(8,128)(2,1)S(1)}, bf16[256,1536]{1,0:T(8,128)(2,1)}, u32[]{:S(2)}, u32[]{:S(2)}) %collective-permute-start.11) | collective-permute-done | bytes 786464 | tf_op jit(solution)/shard_map/ppermute | solution.py:71
  160.8 2.6 spread_g.1
  169.8 3.5 collective-permute-start.12
  179.4 11.7 %assemble.1 = (bf16[2048,3072]{1,0:T(8,128)(2,1)}, bf16[1024,2048]{1,0:T(8,128)(2,1)}) custom-call(s32[3,4]{1,0:T(4,128)S(1)} %pad_add_fusion.places, bf16[4,4,2,256,512]{4,3,2,1,0:T(8,128)(2,1)} %bitcast.87, bf16[512,1024]{1,0:T(8,128)(2,1)S(1)} %copy-done.29, bf16[512,1024]{1,0:T(8,128)(2,1)S(1)} %copy-done.33, ...), custom_call_target="tpu_custom_call" | custom-call | bytes 67108864 | tf_op jit(solution)/shard_map/assemble/pallas_call | solution.py:266
  191.1 5.1 copy-done.1
  196.2 6.5 project_qkv.1
  207.5 8.0 %pack_heads.1 = bf16[8,288,384]{2,1,0:T(8,128)(2,1)} custom-call(s32[8]{0:T(128)} %copy-done.65, f32[288,3072]{1,0:T(8,128)} %copy-done, f32[288,3072]{1,0:T(8,128)} %copy-done, f32[288,3072]{1,0:T(8,128)} %copy-done, f32[288,128]{1,0:T(8,128)} %copy-done.49, f32[288,128]{1,0:T(8,128)} %collective-permute-done.23.other.sq_other, f32[4,2048]{1,0:T(4,128)} %gains.9, ...), custom_call_target="tpu_custom_call" | custom-call | tf_op jit(solution)/shard_map/pack_heads/pallas_call | solution.py:706
  215.5 4.4 all-to-all-start
  219.9 4.2 collective-permute-start.22
  226.9 9.2 %collective-permute-done.13.refs_2_ = bf16[256,512]{1,0:T(8,128)(2,1)S(1)} collective-permute-done((bf16[256,512]{1,0:T(8,128)(2,1)}, bf16[256,512]{1,0:T(8,128)(2,1)S(1)}, u32[]{:S(2)}, u32[]{:S(2)}) %collective-permute-start.13) | collective-permute-done | bytes 262176 | tf_op jit(solution)/shard_map/ppermute | solution.py:71
  236.1 24.1 %all-to-all-done = bf16[8,288,384]{2,1,0:T(8,128)(2,1)} async-done(((bf16[8,288,384]{2,1,0:T(8,128)(2,1)}), bf16[8,288,384]{2,1,0:T(8,128)(2,1)}, u32[]{:S(2)}, u32[]{:S(2)}) %all-to-all-start) | async-done | bytes 1769504 | tf_op jit(solution)/shard_map/all_to_all | solution.py:1115
  260.3 7.8 %attend.1 = (bf16[8,2,144,128]{3,2,1,0:T(8,128)(2,1)}, f32[2,1152,128]{2,1,0:T(8,128)S(1)}, f32[2,1152,1]{2,1,0:T(8,128)S(1)}) custom-call(s32[2]{0:T(128)S(1)} %get-tuple-element.238.bounds, bf16[8,2,144,384]{3,2,1,0:T(8,128)(2,1)} %bitcast.32.qkv), custom_call_target="tpu_custom_call" | custom-call | flops 900000000 | bytes 5000000 | tf_op jit(solution)/shard_map/attend/pallas_call | solution.py:811
  270.2 4.3 collective-permute-start.25
  277.6 4.2 all-to-all-start.1
  284.3 8.9 %collective-permute-done.14.refs_3_ = bf16[256,512]{1,0:T(8,128)(2,1)S(1)} collective-permute-done((bf16[256,512]{1,0:T(8,128)(2,1)S(1)}, bf16[256,512]{1,0:T(8,128)(2,1)S(1)}, u32[]{:S(2)}, u32[]{:S(2)}) %collective-permute-start.14) | collective-permute-done | bytes 262176 | tf_op jit(solution)/shard_map/ppermute | solution.py:71
  295.2 20.1 %all-to-all-done.1 = bf16[8,2,144,128]{3,2,1,0:T(8,128)(2,1)S(1)} async-done(((bf16[8,2,144,128]{3,2,1,0:T(8,128)(2,1)}), bf16[8,2,144,128]{3,2,1,0:T(8,128)(2,1)S(1)}, u32[]{:S(2)}, u32[]{:S(2)}) %all-to-all-start.1) | async-done | bytes 589856 | tf_op jit(solution)/shard_map/all_to_all | solution.py:1119
  315.3 4.1 project_out.1
  320.3 3.8 collective-permute-start.26
  330.2 3.5 collective-permute-start.27
  335.9 3.1 collective-permute-start.32
  341.5 3.1 collective-permute-start.28
  347.1 11.6 %collective-permute-start.33 = (bf16[1024,256]{1,0:T(8,128)(2,1)S(1)}, bf16[1024,256]{1,0:T(8,128)(2,1)}, u32[]{:S(2)}, u32[]{:S(2)}) collective-permute-start(bf16[1024,256]{1,0:T(8,128)(2,1)S(1)} %collective-permute-done.32.refs_7_), channel_id=1, source_target_pairs={{0,64},{1,67},{2,66},{3,65},{4,68},{5,71},{6,70},{7,69},{8,72},{9,... | collective-permute-start | bytes 1572872 | tf_op jit(solution)/shard_map/ppermute | solution.py:71
  358.7 21.4 %gate_and_up.1 = (bf16[288,8192]{1,0:T(8,128)(2,1)}, bf16[288,4096]{1,0:T(8,128)(2,1)}, bf16[288,2176]{1,0:T(8,128)(2,1)}, bf16[288,64]{1,0:T(8,128)(2,1)}) custom-call(s32[3,4]{1,0:T(4,128)} %copy-done.69, bf16[4,4,2,256,2048]{4,3,2,1,0:T(8,128)(2,1)} %bitcast.83, bf16[512,1536]{1,0:T(8,128)(2,1)} %copy-done.3, ...), custom_call_target="tpu_custom_call" | custom-call | flops 9663676416 | bytes 36118528 | tf_op jit(solution)/shard_map/gate_and_up/pallas_call | solution.py:336
  381.0 14.6 %down.3 = (f32[144,2176]{1,0:T(8,128)}, bf16[144,2176]{1,0:T(8,128)(2,1)}) custom-call(s32[3,4]{1,0:T(4,128)} %copy-done.69, bf16[4,4,2,256,2048]{4,3,2,1,0:T(8,128)(2,1)} %bitcast.84, bf16[1024,256]{1,0:T(8,128)(2,1)} %copy-done.13, bf16[1024,256]{1,0:T(8,128)(2,1)} %copy-done.76, bf16[1024,256]{1,0:T(8,128)(2,1)} %copy-done.78, ...), custom_call_target="tpu_custom_call" | custom-call | flops 4831838208 | bytes 19398656 | tf_op jit(solution)/shard_map/down/pallas_call | solution.py:336
  404.3 18.2 %down_back.1 = (bf16[288,8192]{1,0:T(8,128)(2,1)}, bf16[288,2176]{1,0:T(8,128)(2,1)}, bf16[288,32]{1,0:T(8,128)(2,1)}) custom-call(s32[3,4]{1,0:T(4,128)} %copy-done.69, bf16[4,4,2,256,2048]{4,3,2,1,0:T(8,128)(2,1)} %bitcast.85, bf16[1024,256]{1,0:T(8,128)(2,1)} %copy-done.13, bf16[1024,256]{1,0:T(8,128)(2,1)} %copy-done.76, bf16[1024,256]{1,0:T(8,128)(2,1)} %copy-done.78, ...), custom_call_target="tpu_custom_call" | custom-call | flops 4831838208 | bytes 23142400 | tf_op jit(solution)/shard_map/down_back/pallas_call | solution.py:336
  424.7 3.9 early_gradients.1
  429.5 4.6 all-to-all-start.2
  434.2 26.8 %gate_and_up_back.1 = (f32[144,2176]{1,0:T(8,128)}, bf16[144,2176]{1,0:T(8,128)(2,1)}) custom-call(s32[3,4]{1,0:T(4,128)} %copy-done.69, bf16[4,4,2,256,2048]{4,3,2,1,0:T(8,128)(2,1)} %bitcast.86, bf16[512,1536]{1,0:T(8,128)(2,1)} %copy-done.3, bf16[512,1536]{1,0:T(8,128)(2,1)} %collective-permute-done.17.refs_2_, ...), custom_call_target="tpu_custom_call" | custom-call | flops 9663676416 | bytes 39321600 | tf_op jit(solution)/shard_map/gate_and_up_back/pallas_call | solution.py:336
  469.7 4.2 project_out_back.1
  474.7 5.1 all-to-all-start.3
  481.4 6.3 all-to-all-done.3
  488.7 4.9 all-to-all-start.4
  496.1 7.7 %attend_back.1 = bf16[8,2,144,384]{3,2,1,0:T(8,128)(2,1)S(1)} custom-call(s32[2]{0:T(128)S(1)} %get-tuple-element.238.bounds, bf16[8,2,144,384]{3,2,1,0:T(8,128)(2,1)} %bitcast.32.qkv, bf16[8,2,144,128]{3,2,1,0:T(8,128)(2,1)S(1)} %bitcast.79, f32[2,1152,128]{2,1,0:T(8,128)S(1)} %copy-done.73, f32[2,1152,1]{2,1,0:T(8,128)S(1)} %copy-done.75), custom_call_target="tpu_custom_call" | custom-call | flops 2300000000 | bytes 8000000 | tf_op jit(solution)/shard_map/attend_back/pallas_call | solution.py:859
  507.6 7.9 %all-to-all-start.5 = ((bf16[8,2,144,384]{3,2,1,0:T(8,128)(2,1)}), bf16[8,2,144,384]{3,2,1,0:T(8,128)(2,1)}, u32[]{:S(2)}, u32[]{:S(2)}) async-start(bf16[8,2,144,384]{3,2,1,0:T(8,128)(2,1)} %copy-done.16), calls=%async_computation.5 | async-start | bytes 3538944 | tf_op jit(solution)/shard_map/all_to_all | solution.py:1166
  521.0 15.7 %all-to-all-done.5 = bf16[8,2,144,384]{3,2,1,0:T(8,128)(2,1)} async-done(((bf16[8,2,144,384]{3,2,1,0:T(8,128)(2,1)}), bf16[8,2,144,384]{3,2,1,0:T(8,128)(2,1)}, u32[]{:S(2)}, u32[]{:S(2)}) %all-to-all-start.5) | async-done | bytes 1769504 | tf_op jit(solution)/shard_map/all_to_all | solution.py:1166
  536.7 8.0 %unpack_heads.1 = (f32[288,1024]{1,0:T(8,128)}, f32[288,1024]{1,0:T(8,128)}, bf16[288,1024]{1,0:T(8,128)(2,1)}, f32[288,128]{1,0:T(8,128)}) custom-call(s32[8]{0:T(128)} %copy-done.65, bf16[8,288,384]{2,1,0:T(8,128)(2,1)} %bitcast.39.d, f32[288,3072]{1,0:T(8,128)} %copy-done, f32[288,3072]{1,0:T(8,128)} %copy-done, f32[4,2048]{1,0:T(4,128)} %gains.9, ...), custom_call_target="tpu_custom_call" | custom-call | tf_op jit(solution)/shard_map/unpack_heads/pallas_call | solution.py:751
  551.5 10.6 %project_qkv_back.1 = (bf16[288,3072]{1,0:T(8,128)(2,1)}, f32[144,2176]{1,0:T(8,128)S(1)}, bf16[144,2176]{1,0:T(8,128)(2,1)S(1)}) custom-call(s32[8]{0:T(128)S(1)} %copy-done.67, f32[288,1024]{1,0:T(8,128)S(1)} %copy-done.19, f32[288,1024]{1,0:T(8,128)S(1)} %copy-done.20, bf16[288,1024]{1,0:T(8,128)(2,1)S(1)} %copy-done.48, f32[288,3072]{1,0:T(8,128)} %copy-done, ...), custom_call_target="tpu_custom_call" | custom-call | flops 3623878656 | bytes 22000000 | tf_op jit(solution)/shard_map/project_qkv_back/pallas_call | solution.py:640
  567.1 3.0 late_gradients.1
  570.1 21.1 %all_to_all.45 = bf16[8,32,1280]{2,1,0:T(8,128)(2,1)S(1)} all-to-all(bf16[8,32,1280]{2,1,0:T(8,128)(2,1)S(1)} %late_gradients.1), channel_id=1, replica_groups=mesh['yl'=2,'x'=4,'z'=4,'yh'=2,'c'=2] {'yl','x'}, dimensions={0} | all-to-all | bytes 1310720 | tf_op jit(solution)/shard_map/all_to_all | solution.py:1194
  591.4 16.0 %all_to_all.46 = bf16[8,32,1280]{2,1,0:T(8,128)(2,1)S(1)} all-to-all(bf16[8,32,1280]{2,1,0:T(8,128)(2,1)S(1)} %broadcast_in_dim.46), channel_id=1, replica_groups=mesh['yl'=2,'x'=4,'z'=4,'yh'=2,'c'=2] {'z','yh'}, dimensions={0} | all-to-all | bytes 1310720 | tf_op jit(solution)/shard_map/all_to_all | solution.py:1088
  607.3 4.0 collective-permute-start.43
  613.7 4.7 all-to-all-start.8
  620.3 8.2 %early_outputs.1 = (f32[8,2,16,8192]{3,2,1,0:T(8,128)}, f32[8,16,8192]{2,1,0:T(8,128)}) custom-call(s32[8]{0:T(128)S(1)} %copy-done.67, bf16[8,8,16,1664]{3,2,1,0:T(8,128)(2,1)S(1)} %bitcast.70, bf16[8,8,16,1664]{3,2,1,0:T(8,128)(2,1)} %collective-permute-done.43.refs_1_), custom_call_target="tpu_custom_call" | custom-call | bytes 6815744 | tf_op jit(solution)/shard_map/early_outputs/pallas_call | solution.py:979
  628.6 28.8 %all-to-all-done.8 = bf16[8,128,1280]{2,1,0:T(8,128)(2,1)S(1)} async-done(((bf16[8,128,1280]{2,1,0:T(8,128)(2,1)}), bf16[8,128,1280]{2,1,0:T(8,128)(2,1)S(1)}, u32[]{:S(2)}, u32[]{:S(2)}) %all-to-all-start.8) | async-done | bytes 2621472 | tf_op jit(solution)/shard_map/all_to_all | solution.py:1088
  662.7 6.2 late_outputs.1
  (306 shorter events, 129.5 us)
Async XLA Ops:
  7.2 166.2 %all-gather.7.cloned.1.call-start = ((), (), s32[]{:S(2)}) async-start(), calls=%async_computation.10 | async-start | bytes 8912896 | tf_op jit(solution)/shard_map/all_gather | solution.py:677
  10.5 147.0 %copy-start.65 = (s32[8]{0:T(128)}, s32[8]{0:T(128)S(1)}, u32[]{:S(2)}) copy-start(s32[8]{0:T(128)S(1)} %stack.141.core.me) | copy-start | bytes 100
  11.4 2.7 collective-permute-start.1
  14.7 12.1 %collective-permute-start.2 = (bf16[256,1024]{1,0:T(8,128)(2,1)S(1)}, bf16[256,1024]{1,0:T(8,128)(2,1)S(1)}, u32[]{:S(2)}, u32[]{:S(2)}) collective-permute-start(bf16[256,1024]{1,0:T(8,128)(2,1)S(1)} %get-tuple-element.127.refs_0_), channel_id=1, source_target_pairs={{0,4},{1,13},{2,6},{3,15},{4,8},{5,1},{6,10},{7,3},{8,12},{9,5},{1... | collective-permute-start | bytes 1572872 | tf_op jit(solution)/shard_map/ppermute | solution.py:71
  18.5 8.2 %collective-permute-start.4 = (bf16[256,512]{1,0:T(8,128)(2,1)S(1)}, bf16[256,512]{1,0:T(8,128)(2,1)S(1)}, u32[]{:S(2)}, u32[]{:S(2)}) collective-permute-start(bf16[256,512]{1,0:T(8,128)(2,1)S(1)} %get-tuple-element.130), channel_id=1, source_target_pairs={{0,66},{1,67},{2,64},{3,65},{4,70},{5,71},{6,68},{7,69},{8,74},{9,... | collective-permute-start | bytes 786440 | tf_op jit(solution)/shard_map/ppermute | solution.py:71
  27.7 331.0 %all-gather.5.cloned.1.call-start = ((), (), s32[]{:S(2)}) async-start(), calls=%async_computation.9 | async-start | bytes 35651584 | tf_op jit(solution)/shard_map/all_gather | solution.py:677
  31.1 12.2 %collective-permute-start = (bf16[128,8192]{1,0:T(8,128)(2,1)S(1)}, bf16[128,8192]{1,0:T(8,128)(2,1)S(1)}, u32[]{:S(2)}, u32[]{:S(2)}) collective-permute-start(bf16[128,8192]{1,0:T(8,128)(2,1)S(1)} %get-tuple-element.123), channel_id=1, source_target_pairs={{0,1},{1,0},{2,3},{3,2},{4,5},{5,4},{6,7},{7,6},{8,9},{9,8},{10,11... | collective-permute-start | bytes 6291464 | tf_op jit(solution)/shard_map/ppermute | solution.py:61
  31.2 8.6 %collective-permute-start.3 = (bf16[256,1024]{1,0:T(8,128)(2,1)S(1)}, bf16[256,1024]{1,0:T(8,128)(2,1)S(1)}, u32[]{:S(2)}, u32[]{:S(2)}) collective-permute-start(bf16[256,1024]{1,0:T(8,128)(2,1)S(1)} %collective-permute-done.2.refs_1_), channel_id=1, source_target_pairs={{0,4},{1,13},{2,6},{3,15},{4,8},{5,1},{6,10},{7,3},{8,12},{9,5},{1... | collective-permute-start | bytes 1572872 | tf_op jit(solution)/shard_map/ppermute | solution.py:71
  39.8 15.1 %collective-permute-start.6 = (bf16[256,1024]{1,0:T(8,128)(2,1)S(1)}, bf16[256,1024]{1,0:T(8,128)(2,1)S(1)}, u32[]{:S(2)}, u32[]{:S(2)}) collective-permute-start(bf16[256,1024]{1,0:T(8,128)(2,1)S(1)} %collective-permute-done.3.refs_2_), channel_id=1, source_target_pairs={{0,4},{1,13},{2,6},{3,15},{4,8},{5,1},{6,10},{7,3},{8,12},{9,5},{1... | collective-permute-start | bytes 1572872 | tf_op jit(solution)/shard_map/ppermute | solution.py:71
  47.7 50.2 %copy-start.38 = (bf16[256,1536]{1,0:T(8,128)(2,1)}, bf16[256,1536]{1,0:T(8,128)(2,1)S(1)}, u32[]{:S(2)}) copy-start(bf16[256,1536]{1,0:T(8,128)(2,1)S(1)} %get-tuple-element.138.refs_0_) | copy-start | bytes 2359300
  47.8 26.9 %collective-permute-start.5 = (bf16[256,2048]{1,0:T(8,128)(2,1)S(1)}, bf16[256,2048]{1,0:T(8,128)(2,1)S(1)}, u32[]{:S(2)}, u32[]{:S(2)}) collective-permute-start(bf16[256,2048]{1,0:T(8,128)(2,1)S(1)} %get-tuple-element.131), channel_id=1, source_target_pairs={{0,66},{1,67},{2,64},{3,65},{4,70},{5,71},{6,68},{7,69},{8,74},{9,... | collective-permute-start | bytes 3145736 | tf_op jit(solution)/shard_map/ppermute | solution.py:71
  55.6 28.4 %collective-permute-start.7 = (bf16[512,1024]{1,0:T(8,128)(2,1)S(1)}, bf16[512,1024]{1,0:T(8,128)(2,1)S(1)}, u32[]{:S(2)}, u32[]{:S(2)}) collective-permute-start(bf16[512,1024]{1,0:T(8,128)(2,1)S(1)} %get-tuple-element.133.refs_1_), channel_id=1, source_target_pairs={{0,64},{1,67},{2,66},{3,65},{4,68},{5,71},{6,70},{7,69},{8,72},{9,... | collective-permute-start | bytes 3145736 | tf_op jit(solution)/shard_map/ppermute | solution.py:71
  59.3 35.9 %collective-permute-start.8 = (bf16[512,1024]{1,0:T(8,128)(2,1)S(1)}, bf16[512,1024]{1,0:T(8,128)(2,1)S(1)}, u32[]{:S(2)}, u32[]{:S(2)}) collective-permute-start(bf16[512,1024]{1,0:T(8,128)(2,1)S(1)} %get-tuple-element.134.refs_5_), channel_id=1, source_target_pairs={{0,64},{1,67},{2,66},{3,65},{4,68},{5,71},{6,70},{7,69},{8,72},{9,... | collective-permute-start | bytes 3145736 | tf_op jit(solution)/shard_map/ppermute | solution.py:71
  97.9 11.3 %collective-permute-start.9 = (bf16[256,1536]{1,0:T(8,128)(2,1)S(1)}, bf16[256,1536]{1,0:T(8,128)(2,1)S(1)}, u32[]{:S(2)}, u32[]{:S(2)}) collective-permute-start(bf16[256,1536]{1,0:T(8,128)(2,1)S(1)} %get-tuple-element.138.refs_0_), channel_id=1, source_target_pairs={{0,4},{1,13},{2,6},{3,15},{4,8},{5,1},{6,10},{7,3},{8,12},{9,5},{1... | collective-permute-start | bytes 2359304 | tf_op jit(solution)/shard_map/ppermute | solution.py:71
  99.1 15.3 %collective-permute-start.15 = (bf16[512,1024]{1,0:T(8,128)(2,1)S(1)}, bf16[512,1024]{1,0:T(8,128)(2,1)}, u32[]{:S(2)}, u32[]{:S(2)}) collective-permute-start(bf16[512,1024]{1,0:T(8,128)(2,1)S(1)} %collective-permute-done.7.refs_2_), channel_id=1, source_target_pairs={{0,64},{1,67},{2,66},{3,65},{4,68},{5,71},{6,70},{7,69},{8,72},{9,... | collective-permute-start | bytes 3145736 | tf_op jit(solution)/shard_map/ppermute | solution.py:71
  102.6 23.1 %collective-permute-start.19 = (bf16[512,1024]{1,0:T(8,128)(2,1)}, bf16[512,1024]{1,0:T(8,128)(2,1)}, u32[]{:S(2)}, u32[]{:S(2)}) collective-permute-start(bf16[512,1024]{1,0:T(8,128)(2,1)} %copy-done.82), channel_id=1, source_target_pairs={{0,64},{1,67},{2,66},{3,65},{4,68},{5,71},{6,70},{7,69},{8,72},{9,... | collective-permute-start | bytes 3145736 | tf_op jit(solution)/shard_map/ppermute | solution.py:71
  109.2 20.0 %collective-permute-start.10 = (bf16[256,1536]{1,0:T(8,128)(2,1)S(1)}, bf16[256,1536]{1,0:T(8,128)(2,1)S(1)}, u32[]{:S(2)}, u32[]{:S(2)}) collective-permute-start(bf16[256,1536]{1,0:T(8,128)(2,1)S(1)} %collective-permute-done.9.refs_1_), channel_id=1, source_target_pairs={{0,4},{1,13},{2,6},{3,15},{4,8},{5,1},{6,10},{7,3},{8,12},{9,5},{1... | collective-permute-start | bytes 2359304 | tf_op jit(solution)/shard_map/ppermute | solution.py:71
  111.5 55.8 %collective-permute-start.18 = (bf16[144,2048]{1,0:T(8,128)(2,1)S(1)}, bf16[144,2048]{1,0:T(8,128)(2,1)}, u32[]{:S(2)}, u32[]{:S(2)}) collective-permute-start(bf16[144,2048]{1,0:T(8,128)(2,1)S(1)} %bitcast.75), channel_id=1, source_target_pairs={{0,1},{1,0},{2,3},{3,2},{4,5},{5,4},{6,7},{7,6},{8,9},{9,8},{10,11... | collective-permute-start | bytes 1769480 | tf_op jit(solution)/shard_map/ppermute | solution.py:61
  113.1 16.6 %collective-permute-start.21 = (f32[8,128]{1,0:T(8,128)S(1)}, f32[8,128]{1,0:T(8,128)S(1)}, u32[]{:S(2)}, u32[]{:S(2)}) collective-permute-start(f32[8,128]{1,0:T(8,128)S(1)} %broadcast_in_dim.18), channel_id=1, source_target_pairs={{0,1},{1,0},{2,3},{3,2},{4,5},{5,4},{6,7},{7,6},{8,9},{9,8},{10,11... | collective-permute-start | bytes 12296 | tf_op jit(solution)/shard_map/ppermute | solution.py:61
  114.3 49.1 %collective-permute-start.16 = (bf16[512,1024]{1,0:T(8,128)(2,1)}, bf16[512,1024]{1,0:T(8,128)(2,1)S(1)}, u32[]{:S(2)}, u32[]{:S(2)}) collective-permute-start(bf16[512,1024]{1,0:T(8,128)(2,1)} %collective-permute-done.15.refs_3_), channel_id=1, source_target_pairs={{0,64},{1,67},{2,66},{3,65},{4,68},{5,71},{6,70},{7,69},{8,72},{9,... | collective-permute-start | bytes 3145736 | tf_op jit(solution)/shard_map/ppermute | solution.py:71
  125.7 40.0 %collective-permute-start.20 = (bf16[512,1024]{1,0:T(8,128)(2,1)}, bf16[512,1024]{1,0:T(8,128)(2,1)}, u32[]{:S(2)}, u32[]{:S(2)}) collective-permute-start(bf16[512,1024]{1,0:T(8,128)(2,1)} %collective-permute-done.19.refs_7_), channel_id=1, source_target_pairs={{0,64},{1,67},{2,66},{3,65},{4,68},{5,71},{6,70},{7,69},{8,72},{9,... | collective-permute-start | bytes 3145736 | tf_op jit(solution)/shard_map/ppermute | solution.py:71
  129.3 28.1 %collective-permute-start.11 = (bf16[256,1536]{1,0:T(8,128)(2,1)S(1)}, bf16[256,1536]{1,0:T(8,128)(2,1)}, u32[]{:S(2)}, u32[]{:S(2)}) collective-permute-start(bf16[256,1536]{1,0:T(8,128)(2,1)S(1)} %collective-permute-done.10.refs_2_), channel_id=1, source_target_pairs={{0,4},{1,13},{2,6},{3,15},{4,8},{5,1},{6,10},{7,3},{8,12},{9,5},{1... | collective-permute-start | bytes 2359304 | tf_op jit(solution)/shard_map/ppermute | solution.py:71
  129.5 43.9 %copy-start.69 = (s32[3,4]{1,0:T(4,128)}, s32[3,4]{1,0:T(4,128)S(1)}, u32[]{:S(2)}) copy-start(s32[3,4]{1,0:T(4,128)S(1)} %pad_add_fusion.places) | copy-start | bytes 148
  164.4 55.5 %collective-permute-start.17 = (bf16[512,1536]{1,0:T(8,128)(2,1)S(1)}, bf16[512,1536]{1,0:T(8,128)(2,1)}, u32[]{:S(2)}, u32[]{:S(2)}) collective-permute-start(bf16[512,1536]{1,0:T(8,128)(2,1)S(1)} %get-tuple-element.148.refs_1_), channel_id=1, source_target_pairs={{0,64},{1,67},{2,66},{3,65},{4,68},{5,71},{6,70},{7,69},{8,72},{9,... | collective-permute-start | bytes 4718600 | tf_op jit(solution)/shard_map/ppermute | solution.py:71
  165.6 58.5 %collective-permute-start.24 = (bf16[512,1536]{1,0:T(8,128)(2,1)}, bf16[512,1536]{1,0:T(8,128)(2,1)}, u32[]{:S(2)}, u32[]{:S(2)}) collective-permute-start(bf16[512,1536]{1,0:T(8,128)(2,1)} %get-tuple-element.161.refs_5_), channel_id=1, source_target_pairs={{0,64},{1,67},{2,66},{3,65},{4,68},{5,71},{6,70},{7,69},{8,72},{9,... | collective-permute-start | bytes 4718600 | tf_op jit(solution)/shard_map/ppermute | solution.py:71
  169.8 37.6 %collective-permute-start.12 = (bf16[256,512]{1,0:T(8,128)(2,1)}, bf16[256,512]{1,0:T(8,128)(2,1)}, u32[]{:S(2)}, u32[]{:S(2)}) collective-permute-start(bf16[256,512]{1,0:T(8,128)(2,1)} %get-tuple-element.141.refs_0_), channel_id=1, source_target_pairs={{0,4},{1,13},{2,6},{3,15},{4,8},{5,1},{6,10},{7,3},{8,12},{9,5},{1... | collective-permute-start | bytes 786440 | tf_op jit(solution)/shard_map/ppermute | solution.py:71
  204.5 2.9 collective-permute-start.23
  215.5 44.8 %all-to-all-start = ((bf16[8,288,384]{2,1,0:T(8,128)(2,1)}), bf16[8,288,384]{2,1,0:T(8,128)(2,1)}, u32[]{:S(2)}, u32[]{:S(2)}) async-start(bf16[8,288,384]{2,1,0:T(8,128)(2,1)} %pack_heads.1), calls=%async_computation | async-start | bytes 3538944 | tf_op jit(solution)/shard_map/all_to_all | solution.py:1115
  219.9 50.3 %collective-permute-start.22 = (bf16[512,1536]{1,0:T(8,128)(2,1)}, bf16[512,1536]{1,0:T(8,128)(2,1)}, u32[]{:S(2)}, u32[]{:S(2)}) collective-permute-start(bf16[512,1536]{1,0:T(8,128)(2,1)} %collective-permute-done.17.refs_2_), channel_id=1, source_target_pairs={{0,64},{1,67},{2,66},{3,65},{4,68},{5,71},{6,70},{7,69},{8,72},{9,... | collective-permute-start | bytes 4718600 | tf_op jit(solution)/shard_map/ppermute | solution.py:71
  224.1 51.2 %collective-permute-start.29 = (bf16[512,1536]{1,0:T(8,128)(2,1)}, bf16[512,1536]{1,0:T(8,128)(2,1)}, u32[]{:S(2)}, u32[]{:S(2)}) collective-permute-start(bf16[512,1536]{1,0:T(8,128)(2,1)} %collective-permute-done.24.refs_6_), channel_id=1, source_target_pairs={{0,64},{1,67},{2,66},{3,65},{4,68},{5,71},{6,70},{7,69},{8,72},{9,... | collective-permute-start | bytes 4718600 | tf_op jit(solution)/shard_map/ppermute | solution.py:71
  224.4 11.8 %collective-permute-start.13 = (bf16[256,512]{1,0:T(8,128)(2,1)}, bf16[256,512]{1,0:T(8,128)(2,1)S(1)}, u32[]{:S(2)}, u32[]{:S(2)}) collective-permute-start(bf16[256,512]{1,0:T(8,128)(2,1)} %collective-permute-done.12.refs_1_), channel_id=1, source_target_pairs={{0,4},{1,13},{2,6},{3,15},{4,8},{5,1},{6,10},{7,3},{8,12},{9,5},{1... | collective-permute-start | bytes 786440 | tf_op jit(solution)/shard_map/ppermute | solution.py:71
  260.2 33.0 %copy-start.66 = (s32[8]{0:T(128)S(1)}, s32[8]{0:T(128)}, u32[]{:S(2)}) copy-start(s32[8]{0:T(128)} %copy-done.65) | copy-start | bytes 100
  270.2 45.2 %copy-start.63 = (bf16[32,1024]{1,0:T(8,128)(2,1)S(1)}, bf16[32,1024]{1,0:T(8,128)(2,1)}, u32[]{:S(2)}) copy-start(bf16[32,1024]{1,0:T(8,128)(2,1)} %get-tuple-element.179.down) | copy-start | bytes 196612
  270.2 50.1 %collective-permute-start.25 = (bf16[512,1536]{1,0:T(8,128)(2,1)}, bf16[512,1536]{1,0:T(8,128)(2,1)}, u32[]{:S(2)}, u32[]{:S(2)}) collective-permute-start(bf16[512,1536]{1,0:T(8,128)(2,1)} %collective-permute-done.22.refs_3_), channel_id=1, source_target_pairs={{0,64},{1,67},{2,66},{3,65},{4,68},{5,71},{6,70},{7,69},{8,72},{9,... | collective-permute-start | bytes 4718600 | tf_op jit(solution)/shard_map/ppermute | solution.py:71
  275.3 48.8 %collective-permute-start.30 = (bf16[512,1536]{1,0:T(8,128)(2,1)}, bf16[512,1536]{1,0:T(8,128)(2,1)}, u32[]{:S(2)}, u32[]{:S(2)}) collective-permute-start(bf16[512,1536]{1,0:T(8,128)(2,1)} %collective-permute-done.29.refs_7_), channel_id=1, source_target_pairs={{0,64},{1,67},{2,66},{3,65},{4,68},{5,71},{6,70},{7,69},{8,72},{9,... | collective-permute-start | bytes 4718600 | tf_op jit(solution)/shard_map/ppermute | solution.py:71
  277.6 37.8 %all-to-all-start.1 = ((bf16[8,2,144,128]{3,2,1,0:T(8,128)(2,1)}), bf16[8,2,144,128]{3,2,1,0:T(8,128)(2,1)S(1)}, u32[]{:S(2)}, u32[]{:S(2)}) async-start(bf16[8,2,144,128]{3,2,1,0:T(8,128)(2,1)} %get-tuple-element.163), calls=%async_computation.1 | async-start | bytes 1179648 | tf_op jit(solution)/shard_map/all_to_all | solution.py:1119
  281.8 11.4 %collective-permute-start.14 = (bf16[256,512]{1,0:T(8,128)(2,1)S(1)}, bf16[256,512]{1,0:T(8,128)(2,1)S(1)}, u32[]{:S(2)}, u32[]{:S(2)}) collective-permute-start(bf16[256,512]{1,0:T(8,128)(2,1)S(1)} %collective-permute-done.13.refs_2_), channel_id=1, source_target_pairs={{0,4},{1,13},{2,6},{3,15},{4,8},{5,1},{6,10},{7,3},{8,12},{9,5},{1... | collective-permute-start | bytes 786440 | tf_op jit(solution)/shard_map/ppermute | solution.py:71
  320.2 4.6 collective-permute-start.34
  320.3 10.0 %collective-permute-start.26 = (bf16[1024,256]{1,0:T(8,128)(2,1)S(1)}, bf16[1024,256]{1,0:T(8,128)(2,1)S(1)}, u32[]{:S(2)}, u32[]{:S(2)}) collective-permute-start(bf16[1024,256]{1,0:T(8,128)(2,1)S(1)} %get-tuple-element.166.refs_1_), channel_id=1, source_target_pairs={{0,64},{1,67},{2,66},{3,65},{4,68},{5,71},{6,70},{7,69},{8,72},{9,... | collective-permute-start | bytes 1572872 | tf_op jit(solution)/shard_map/ppermute | solution.py:71
  324.1 11.7 %collective-permute-start.31 = (bf16[1024,256]{1,0:T(8,128)(2,1)S(1)}, bf16[1024,256]{1,0:T(8,128)(2,1)S(1)}, u32[]{:S(2)}, u32[]{:S(2)}) collective-permute-start(bf16[1024,256]{1,0:T(8,128)(2,1)S(1)} %copy-done.15), channel_id=1, source_target_pairs={{0,64},{1,67},{2,66},{3,65},{4,68},{5,71},{6,70},{7,69},{8,72},{9,... | collective-permute-start | bytes 1572872 | tf_op jit(solution)/shard_map/ppermute | solution.py:71
  328.0 30.7 %collective-permute-start.35 = (bf16[144,2176]{1,0:T(8,128)(2,1)S(1)}, bf16[144,2176]{1,0:T(8,128)(2,1)}, u32[]{:S(2)}, u32[]{:S(2)}) collective-permute-start(bf16[144,2176]{1,0:T(8,128)(2,1)S(1)} %get-tuple-element.183.refs_9_), channel_id=1, source_target_pairs={{0,1},{1,0},{2,3},{3,2},{4,5},{5,4},{6,7},{7,6},{8,9},{9,8},{10,11... | collective-permute-start | bytes 1880072 | tf_op jit(solution)/shard_map/ppermute | solution.py:61
  330.2 49.9 %copy-start.76 = (bf16[1024,256]{1,0:T(8,128)(2,1)}, bf16[1024,256]{1,0:T(8,128)(2,1)S(1)}, u32[]{:S(2)}) copy-start(bf16[1024,256]{1,0:T(8,128)(2,1)S(1)} %collective-permute-done.26.refs_2_) | copy-start | bytes 1572868
  330.2 11.2 %collective-permute-start.27 = (bf16[1024,256]{1,0:T(8,128)(2,1)S(1)}, bf16[1024,256]{1,0:T(8,128)(2,1)S(1)}, u32[]{:S(2)}, u32[]{:S(2)}) collective-permute-start(bf16[1024,256]{1,0:T(8,128)(2,1)S(1)} %collective-permute-done.26.refs_2_), channel_id=1, source_target_pairs={{0,64},{1,67},{2,66},{3,65},{4,68},{5,71},{6,70},{7,69},{8,72},{9,... | collective-permute-start | bytes 1572872 | tf_op jit(solution)/shard_map/ppermute | solution.py:71
  335.9 11.2 %collective-permute-start.32 = (bf16[1024,256]{1,0:T(8,128)(2,1)S(1)}, bf16[1024,256]{1,0:T(8,128)(2,1)S(1)}, u32[]{:S(2)}, u32[]{:S(2)}) collective-permute-start(bf16[1024,256]{1,0:T(8,128)(2,1)S(1)} %collective-permute-done.31.refs_6_), channel_id=1, source_target_pairs={{0,64},{1,67},{2,66},{3,65},{4,68},{5,71},{6,70},{7,69},{8,72},{9,... | collective-permute-start | bytes 1572872 | tf_op jit(solution)/shard_map/ppermute | solution.py:71
  341.5 38.7 %copy-start.78 = (bf16[1024,256]{1,0:T(8,128)(2,1)}, bf16[1024,256]{1,0:T(8,128)(2,1)S(1)}, u32[]{:S(2)}) copy-start(bf16[1024,256]{1,0:T(8,128)(2,1)S(1)} %collective-permute-done.27.refs_3_) | copy-start | bytes 1572868
  341.5 38.7 %collective-permute-start.28 = (bf16[1024,256]{1,0:T(8,128)(2,1)S(1)}, bf16[1024,256]{1,0:T(8,128)(2,1)S(1)}, u32[]{:S(2)}, u32[]{:S(2)}) collective-permute-start(bf16[1024,256]{1,0:T(8,128)(2,1)S(1)} %collective-permute-done.27.refs_3_), channel_id=1, source_target_pairs={{0,64},{1,67},{2,66},{3,65},{4,68},{5,71},{6,70},{7,69},{8,72},{9,... | collective-permute-start | bytes 1572872 | tf_op jit(solution)/shard_map/ppermute | solution.py:71
  347.1 33.1 %copy-start.79 = (bf16[1024,256]{1,0:T(8,128)(2,1)}, bf16[1024,256]{1,0:T(8,128)(2,1)S(1)}, u32[]{:S(2)}) copy-start(bf16[1024,256]{1,0:T(8,128)(2,1)S(1)} %collective-permute-done.32.refs_7_) | copy-start | bytes 1572868
  347.1 33.1 %collective-permute-start.33 = (bf16[1024,256]{1,0:T(8,128)(2,1)S(1)}, bf16[1024,256]{1,0:T(8,128)(2,1)}, u32[]{:S(2)}, u32[]{:S(2)}) collective-permute-start(bf16[1024,256]{1,0:T(8,128)(2,1)S(1)} %collective-permute-done.32.refs_7_), channel_id=1, source_target_pairs={{0,64},{1,67},{2,66},{3,65},{4,68},{5,71},{6,70},{7,69},{8,72},{9,... | collective-permute-start | bytes 1572872 | tf_op jit(solution)/shard_map/ppermute | solution.py:71
  395.6 2.3 collective-permute-start.36
  401.3 2.1 collective-permute-start.37
  429.5 31.5 %all-to-all-start.2 = ((bf16[8,32,1664]{2,1,0:T(8,128)(2,1)}), bf16[8,32,1664]{2,1,0:T(8,128)(2,1)}, u32[]{:S(2)}, u32[]{:S(2)}) async-start(bf16[8,32,1664]{2,1,0:T(8,128)(2,1)} %copy-done.7), calls=%async_computation.2 | async-start | bytes 1703936 | tf_op jit(solution)/shard_map/all_to_all | solution.py:1151
  434.1 30.0 %copy-start.11 = (bf16[1,144,2048]{2,1,0:T(8,128)(2,1)S(1)}, bf16[1,144,2048]{2,1,0:T(8,128)(2,1)}, u32[]{:S(2)}) copy-start(bf16[1,144,2048]{2,1,0:T(8,128)(2,1)} %param.17) | copy-start | bytes 1769476
  461.0 3.1 collective-permute-start.38
  467.6 2.1 collective-permute-start.39
  474.7 13.0 %all-to-all-start.3 = ((bf16[8,288,128]{2,1,0:T(8,128)(2,1)}), bf16[8,288,128]{2,1,0:T(8,128)(2,1)S(1)}, u32[]{:S(2)}, u32[]{:S(2)}) async-start(bf16[8,288,128]{2,1,0:T(8,128)(2,1)} %copy-done.51), calls=%async_computation.3 | async-start | bytes 1179648 | tf_op jit(solution)/shard_map/all_to_all | solution.py:1157
  488.7 18.9 %all-to-all-start.4 = ((bf16[8,32,1792]{2,1,0:T(8,128)(2,1)}), bf16[8,32,1792]{2,1,0:T(8,128)(2,1)}, u32[]{:S(2)}, u32[]{:S(2)}) async-start(bf16[8,32,1792]{2,1,0:T(8,128)(2,1)} %broadcast_in_dim.44), calls=%async_computation.4 | async-start | bytes 1835008 | tf_op jit(solution)/shard_map/all_to_all | solution.py:1088
  507.6 29.1 %all-to-all-start.5 = ((bf16[8,2,144,384]{3,2,1,0:T(8,128)(2,1)}), bf16[8,2,144,384]{3,2,1,0:T(8,128)(2,1)}, u32[]{:S(2)}, u32[]{:S(2)}) async-start(bf16[8,2,144,384]{3,2,1,0:T(8,128)(2,1)} %copy-done.16), calls=%async_computation.5 | async-start | bytes 3538944 | tf_op jit(solution)/shard_map/all_to_all | solution.py:1166
  515.5 91.8 %all-gather.9.cloned.1.call-start = ((), (), s32[]{:S(2)}) async-start(), calls=%async_computation.11 | async-start | bytes 3833856 | tf_op jit(solution)/shard_map/all_gather | solution.py:1174
  544.8 2.2 collective-permute-start.40
  562.1 2.1 collective-permute-start.41
  565.8 1.2 collective-permute-start.42
  607.3 11.0 %collective-permute-start.43 = (bf16[8,8,16,1664]{3,2,1,0:T(8,128)(2,1)}, bf16[8,8,16,1664]{3,2,1,0:T(8,128)(2,1)}, u32[]{:S(2)}, u32[]{:S(2)}) collective-permute-start(bf16[8,8,16,1664]{3,2,1,0:T(8,128)(2,1)} %bitcast.68), channel_id=1, source_target_pairs={{0,1},{1,0},{2,3},{3,2},{4,5},{5,4},{6,7},{7,6},{8,9},{9,8},{10,11... | collective-permute-start | bytes 10223624 | tf_op jit(solution)/shard_map/ppermute | solution.py:61
  613.7 43.7 %all-to-all-start.8 = ((bf16[8,128,1280]{2,1,0:T(8,128)(2,1)}), bf16[8,128,1280]{2,1,0:T(8,128)(2,1)S(1)}, u32[]{:S(2)}, u32[]{:S(2)}) async-start(bf16[8,128,1280]{2,1,0:T(8,128)(2,1)} %broadcast_in_dim.48), calls=%async_computation.8 | async-start | bytes 5242880 | tf_op jit(solution)/shard_map/all_to_all | solution.py:1088
  657.3 5.4 collective-permute-start.44
  (79 other events, 519.0 us)
Sparse Core Ops, SparseCore 0:
  27.8 72.1 all-gather.6
  102.7 231.9 all-gather.4
  544.9 51.2 all-gather.8

commit v3 on v2

--- a/solution.py
+++ b/solution.py
@@ -20,8 +20,8 @@
 CTX = ("yl", "x")
 BF = jnp.bfloat16
 F32 = jnp.float32
-CUT_A, CUT_G, CUT_D = 2048, 5120, 1536
-EARLY, LATE = 1664, 1280
+CUT_A, CUT_G = 2048, 4096
+EARLY, MIDDLE, LATE = 1664, 512, 768
 
 
 NT = dict(dimension_numbers=(((1,), (1,)), ((), ())), preferred_element_type=F32)
@@ -146,21 +146,18 @@
 
 
 def parts_m(me, keep, got, down):
-    gx, dx = CUT_G // 4, CUT_D // 4
-    gy, dy = FF - CUT_G // 2, HALF - CUT_D // 2
-
-    def body(me, keep, got, down, xs, yg, yd):
+    gx, dx, gy = CUT_G // 4, D // 4, FF - CUT_G // 2
+
+    def body(me, keep, got, down, xs, ys):
         for side, w in ((me[CORE], keep), (1 - me[CORE], got)):
             rows = pl.ds(pl.multiple_of(side * HD, HD), HD)
             xs[rows, :gx] = w[:, pl.ds(pl.multiple_of(me[X] * gx, 128), gx)]
-            yg[rows, :] = w[:, pl.ds(pl.multiple_of(CUT_G + me[YL] * gy, 128), gy)]
+            ys[rows, :] = w[:, pl.ds(pl.multiple_of(CUT_G + me[YL] * gy, 128), gy)]
         for n in range(2):
             rows = slice(256 * n, 256 * (n + 1))
             xs[:, gx + n * dx : gx + (n + 1) * dx] = down[rows, pl.ds(pl.multiple_of(me[X] * dx, 128), dx)]
-            yd[:, n * dy : (n + 1) * dy] = down[rows, pl.ds(pl.multiple_of(CUT_D + me[YL] * dy, 128), dy)]
-
-    outs = [bf(256, gx + 2 * dx), bf(256, gy), bf(256, 2 * dy)]
-    return _plain(body, "parts_m", outs, [keep, got, down], [me])
+
+    return _plain(body, "parts_m", [bf(256, gx + 2 * dx), bf(256, gy)], [keep, got, down], [me])
 
 
 def spread(me, got, pieces, name):
@@ -188,39 +185,31 @@
         self.depth = 8 * rows
         self.places = places
         self.column = column
-        self.arrays = [xs] + y[0] + y[1]
+        self.arrays = [xs] + (y[0] + y[1] if y else [])
 
 
 def _y_rows(places, rows, half, j, k):
     return pl.multiple_of((2 * half + j) * 2 * rows + places[0, k] * rows, rows)
 
 
-def _copies(w, places, refs, whole):
-    xs, y = refs[0], refs[1:9]
-    quarter, half_width = w.cx // 4, w.cy // 2
-    folds = w.rows // 256
-    panels = []
-    for k in range(4):
-        panel = []
+def _panel_copies(rows, width, column, xs, whole, panels):
+    copies = []
+    for at, k in enumerate(panels):
         for z in range(4):
             for yh in range(2):
-                for n in range(folds):
-                    target = whole.at[pl.ds((2 * z + yh) * w.rows + 256 * n, 256), pl.ds(k * quarter, quarter)]
-                    panel.append((xs.at[k, z, yh, :, pl.ds(w.column + n * quarter, quarter)], target))
-        panels.append(panel)
-    chunks = []
-    for k in range(4):
-        column = pl.multiple_of(w.cx + places[1, k] * half_width, 128)
-        for half in range(2):
-            for j in range(2):
-                row = _y_rows(places, w.rows, half, j, k)
-                chunks.append(
-                    (
-                        y[4 * half + k].at[pl.ds(j * w.rows, w.rows)],
-                        whole.at[pl.ds(row, w.rows), pl.ds(column, half_width)],
-                    )
-                )
-    return panels, chunks
+                for n in range(rows // 256):
+                    target = whole.at[pl.ds((2 * z + yh) * rows + 256 * n, 256), pl.ds(at * width, width)]
+                    copies.append((xs.at[k, z, yh, :, pl.ds(column + n * width, width)], target))
+    return copies
+
+
+def _y_copies(places, y, whole, k, column, width):
+    copies = []
+    for half in range(2):
+        for j in range(2):
+            row = _y_rows(places, 256, half, j, k)
+            copies.append((y[4 * half + k].at[pl.ds(j * 256, 256)], whole.at[pl.ds(row, 256), pl.ds(column, width)]))
+    return copies
 
 
 def assemble(w):
@@ -228,8 +217,8 @@
 
     def body(places, *refs):
         out, out_matrix, sems = refs[9], refs[10], refs[11]
-        panels, chunks = _copies(w, places, refs[:9], out)
-        plain = [pltpu.make_async_copy(a, b, sems.at[n]) for n, (a, b) in enumerate(sum(panels, []))]
+        panels = _panel_copies(256, w.cx // 4, 0, refs[0], out, range(4))
+        plain = [pltpu.make_async_copy(a, b, sems.at[n]) for n, (a, b) in enumerate(panels)]
         for copy in plain:
             copy.start()
 
@@ -275,215 +264,208 @@
     )(w.places, *w.arrays)
 
 
-class Resident:
-    def __init__(self, w, panels):
+WIDE = D + 128
+
+
+def _f32(*shape):
+    return jax.ShapeDtypeStruct(shape, F32)
+
+
+def _pair_up(core, own, other, pair):
+    pair[pl.ds(pl.multiple_of(core * ROWS, ROWS), ROWS), :] = own[...]
+    pair[pl.ds(pl.multiple_of((1 - core) * ROWS, ROWS), ROWS), :] = other[...]
+
+
+def _split(core, sums, keep, give):
+    keep[...] = sums[pl.ds(pl.multiple_of(core * ROWS, ROWS), ROWS), :]
+    give[...] = sums[pl.ds(pl.multiple_of((1 - core) * ROWS, ROWS), ROWS), :].astype(BF)
+
+
+def _in_group(rows, columns, count):
+    row = lax.broadcasted_iota(jnp.int32, (rows, columns), 0) >= ROWS
+    column = lax.broadcasted_iota(jnp.int32, (rows, columns), 1) >= count
+    return row == column
+
+
+def _own_group(low, count):
+    row = lax.broadcasted_iota(jnp.int32, (low.shape[0], count), 0)
+    return jnp.where(row >= ROWS, low[:, count:], low[:, :count])
+
+
+def _put_low(sums, low):
+    count = low.shape[1]
+    sums[:, D:] = jnp.zeros((sums.shape[0], WIDE - D), F32)
+    sums[:, D : D + count] = low
+
+
+SLOT = D
+SLOTS = 4
+
+
+class Stream:
+    def __init__(self, w):
         self.w = w
-        self.panels = panels
-        step = w.cx // 4 * panels
-        self.pieces = [(n * step, step) for n in range(4 // panels)] + [(w.cx, w.cy)]
-
-    def scratch(self):
-        w = self.w
-        return [pltpu.VMEM((w.depth, w.cx + w.cy), BF), pltpu.SemaphoreType.DMA((80,))]
-
-    def start(self, places, refs, whole, sems):
-        panels, chunks = _copies(self.w, places, refs, whole)
-        n = self.panels
-        pieces = [sum(panels[k : k + n], []) for k in range(0, 4, n)] + [chunks]
-        numbers = [sum(len(p) for p in pieces[:n]) for n in range(len(pieces))]
-        copies = [
-            [pltpu.make_async_copy(a, b, sems.at[first + m]) for m, (a, b) in enumerate(piece)]
-            for first, piece in zip(numbers, pieces)
+
+    def gate_up(self, places, refs, n):
+        xs, y, quarter = refs[0], refs[1:9], CUT_G // 4
+        if n < 2:
+            return n * SLOT, lambda slot: _panel_copies(256, quarter, 0, xs, slot, range(2 * n, 2 * n + 2))
+        column = pl.multiple_of(CUT_G + places[1, n - 2] * SLOT, SLOT)
+        return column, lambda slot: [
+            copy for k in (n - 2, n) for copy in _y_copies(places, y, slot, k, 0, SLOT)
         ]
+
+    def down(self, refs, n):
+        xs, quarter = refs[0], D // 4
+
+        def copies(slot):
+            made = []
+            for k in range(4):
+                for block in range(4 * n, 4 * n + 4):
+                    for m in range(2):
+                        source = xs.at[k, block // 2, block % 2, :, pl.ds(CUT_G // 4 + m * quarter, quarter)]
+                        row = (block - 4 * n) * 512 + 256 * m
+                        made.append((source, slot.at[pl.ds(row, 256), pl.ds(k * quarter, quarter)]))
+            return made
+
+        return n * SLOT, copies
+
+    def run(self, pieces, slots, sems, first, use):
+        copies = []
+        for n, (_, made) in enumerate(pieces):
+            slot = n % SLOTS
+            pairs = made(slots.at[slot])
+            copies.append([pltpu.make_async_copy(a, b, sems.at[slot, m]) for m, (a, b) in enumerate(pairs)])
 
         def begin(n):
             if n < len(copies):
                 for copy in copies[n]:
                     copy.start()
 
-        def arrive(n):
+        for n in range(SLOTS - 1):
+            begin(n)
+        first()
+        for n, (at, _) in enumerate(pieces):
             for copy in copies[n]:
                 copy.wait()
-
-        begin(0)
-        begin(1)
-        return begin, arrive
-
-    def forward(self, places, refs, whole, sems, first, x, tile, finish):
-        begin, arrive = self.start(places, refs, whole, sems)
-        first()
-        for n, (start, width) in enumerate(self.pieces):
-            arrive(n)
-            begin(n + 2)
-            for column in range(start, start + width, tile):
-                size = min(tile, start + width - column)
-                finish(jnp.dot(x[...], whole[:, column : column + size], preferred_element_type=F32), column)
-
-    def backward(self, places, refs, whole, sems, first, dy, tile, finish):
-        begin, arrive = self.start(places, refs, whole, sems)
-        first()
-        for n, (start, width) in enumerate(self.pieces):
-            arrive(n)
-            begin(n + 2)
-            left = dy[:, start : start + width]
-            for row in range(0, self.w.depth, tile):
-                finish(lax.dot_general(left, whole[row : row + tile, start : start + width], **NT), row, n)
-
-    def call(self, body, name, ins, outs, flops, scratch=()):
+            use(n, at, slots.at[n % SLOTS])
+            begin(n + SLOTS - 1)
+
+    def call(self, body, name, ins, outs, scratch=()):
         w = self.w
         anywhere = pl.BlockSpec(memory_space=pl.ANY)
-        size = 2 * w.depth * (w.cx + w.cy) + sum(v.size * v.dtype.itemsize for v in ins)
+        size = 6 * D * FF + sum(v.size * v.dtype.itemsize for v in ins)
         return pl.pallas_call(
             body,
             out_shape=outs,
             in_specs=[_smem()] + [anywhere] * 9 + [_vmem()] * len(ins),
             out_specs=[_vmem()] * len(outs),
-            scratch_shapes=self.scratch() + list(scratch),
+            scratch_shapes=[pltpu.VMEM((SLOTS, SLOT, SLOT), BF), pltpu.SemaphoreType.DMA((SLOTS, 32)), *scratch],
             compiler_params=pltpu.CompilerParams(vmem_limit_bytes=60 * 2**20),
-            cost_estimate=pl.CostEstimate(flops=flops, bytes_accessed=size, transcendentals=0),
+            cost_estimate=pl.CostEstimate(flops=4 * ROWS * D * 3 * FF, bytes_accessed=size, transcendentals=0),
             name=name,
         )(w.places, *w.arrays, *ins)
 
 
-WIDE = D + 128
-
-
-def _f32(*shape):
-    return jax.ShapeDtypeStruct(shape, F32)
-
-
-def _pair_up(core, own, other, pair):
-    pair[pl.ds(pl.multiple_of(core * ROWS, ROWS), ROWS), :] = own[...]
-    pair[pl.ds(pl.multiple_of((1 - core) * ROWS, ROWS), ROWS), :] = other[...]
-
-
-def _split(core, sums, keep, give):
-    keep[...] = sums[pl.ds(pl.multiple_of(core * ROWS, ROWS), ROWS), :]
-    give[...] = sums[pl.ds(pl.multiple_of((1 - core) * ROWS, ROWS), ROWS), :].astype(BF)
-
-
-def _in_group(rows, columns, count):
-    row = lax.broadcasted_iota(jnp.int32, (rows, columns), 0) >= ROWS
-    column = lax.broadcasted_iota(jnp.int32, (rows, columns), 1) >= count
-    return row == column
-
-
-def _own_group(low, count):
-    row = lax.broadcasted_iota(jnp.int32, (low.shape[0], count), 0)
-    return jnp.where(row >= ROWS, low[:, count:], low[:, :count])
-
-
-def _put_low(sums, low):
-    count = low.shape[1]
-    sums[:, D:] = jnp.zeros((sums.shape[0], WIDE - D), F32)
-    sums[:, D : D + count] = low
-
-
-def gate_and_up(w, own, other, maps_down, maps_up):
+def feed_forward(w, own, other, maps_down, maps_up, ff_down):
     rows = 2 * ROWS
-    plan = Resident(w, 1)
+    stream = Stream(w)
 
     def body(places, *refs):
-        weights, (own_ref, other_ref, down_ref, up_ref, gu, mixed, pair, low_ref, whole, sems) = refs[:9], refs[9:]
+        weights, (own_ref, other_ref, down_ref, up_ref, ff_ref) = refs[:9], refs[9:14]
+        gu, mixed, pair, low_ref, keep, give, slots, sems, sums = refs[14:]
 
         def first():
             _pair_up(places[2, 0], own_ref, other_ref, pair)
             low = 2.0 * lax.dot_general(pair[:, :D], down_ref[...], **NT).astype(BF).astype(F32)
             low_ref[...] = jnp.where(_in_group(rows, 4 * RANK, 2 * RANK), low, 0.0).astype(BF)
 
-        def finish(total, column):
-            width = total.shape[1]
-            total = total + jnp.dot(low_ref[...], up_ref[:, column : column + width], preferred_element_type=F32)
-            gu[:, column : column + width] = total.astype(BF)
-            unit = column // 2
-            for m in range(width // 256):
-                g, u = total[:, 256 * m : 256 * m + 128], total[:, 256 * m + 128 : 256 * m + 256]
-                mixed[:, unit + 128 * m : unit + 128 * (m + 1)] = (g * jax.nn.sigmoid(g) * u).astype(BF)
-
-        plan.forward(places, weights, whole, sems, first, pair.at[:, pl.ds(0, D)], 768, finish)
-
-    outs = [bf(rows, 2 * FF), bf(rows, FF), bf(rows, WIDE), bf(rows, 4 * RANK)]
-    return plan.call(body, "gate_and_up", [own, other, maps_down, maps_up], outs, 2 * rows * D * 2 * FF)
-
-
-def down(w, x, maps_down):
-    rows = x.shape[0]
-    plan = Resident(w, 2)
+        def use(n, at, slot):
+            tile = SLOT // 2
+            if n < 4:
+                for t in range(2):
+                    column = at + t * tile
+                    unit = column // 2
+                    if not isinstance(at, int):
+                        column, unit = pl.multiple_of(column, tile), pl.multiple_of(unit, tile // 2)
+                    total = jnp.dot(pair[:, :D], slot[:, t * tile : (t + 1) * tile], preferred_element_type=F32)
+                    total = total + jnp.dot(low_ref[...], up_ref[:, pl.ds(column, tile)], preferred_element_type=F32)
+                    gu[:, pl.ds(column, tile)] = total.astype(BF)
+                    for m in range(tile // 256):
+                        g, u = total[:, 256 * m : 256 * m + 128], total[:, 256 * m + 128 : 256 * m + 256]
+                        mixed[:, pl.ds(unit + 128 * m, 128)] = (g * jax.nn.sigmoid(g) * u).astype(BF)
+                return
+            left = mixed[:, at : at + SLOT]
+            for t in range(2):
+                here = slice(t * tile, (t + 1) * tile)
+                part = jnp.dot(left, slot[:, here], preferred_element_type=F32)
+                if n == 4:
+                    sums[:, here] = part
+                else:
+                    sums[:, here] += part
+
+        pieces = [stream.gate_up(places, weights, n) for n in range(4)] + [stream.down(weights, n) for n in range(2)]
+        stream.run(pieces, slots, sems, first, use)
+        _put_low(sums, _own_group(lax.dot_general(mixed[...], ff_ref[...], **NT), RANK))
+        _split(places[2, 0], sums, keep, give)
+
+    outs = [bf(rows, 2 * FF), bf(rows, FF), bf(rows, WIDE), bf(rows, 4 * RANK), _f32(ROWS, WIDE), bf(ROWS, WIDE)]
+    ins = [own, other, maps_down, maps_up, ff_down]
+    return stream.call(body, "feed_forward", ins, outs, [pltpu.VMEM((rows, WIDE), F32)])
+
+
+def feed_forward_back(w, own, other, ff_up, ff_down, gu, maps_up):
+    rows = 2 * ROWS
+    stream = Stream(w)
 
     def body(places, *refs):
-        weights, (x_ref, down_ref, keep, give, whole, sems, sums) = refs[:9], refs[9:]
-
-        def first():
-            _put_low(sums, _own_group(lax.dot_general(x_ref[...], down_ref[...], **NT), RANK))
-
-        def finish(total, column):
-            sums[:, column : column + total.shape[1]] = total
-
-        plan.forward(places, weights, whole, sems, first, x_ref, 512, finish)
-        _split(places[2, 0], sums, keep, give)
-
-    outs = [_f32(ROWS, WIDE), bf(ROWS, WIDE)]
-    return plan.call(body, "down", [x, maps_down], outs, 2 * rows * D * FF, [pltpu.VMEM((rows, WIDE), F32)])
-
-
-def down_back(w, own, other, maps_up, maps_down, gu):
-    rows = 2 * ROWS
-    plan = Resident(w, 4)
-
-    def body(places, *refs):
-        weights, (own_ref, other_ref, up_ref, down_ref, gu_ref, out, pair, low_ref, whole, sems, sums) = refs[:9], refs[9:]
+        weights, (own_ref, other_ref, ff_up_ref, ff_down_ref, gu_ref, up_ref) = refs[:9], refs[9:15]
+        out, pair, low_ref, keep, give, slots, sems, sums, lows = refs[15:]
 
         def first():
             _pair_up(places[2, 0], own_ref, other_ref, pair)
-            low = 2.0 * lax.dot_general(pair[:, :D], up_ref[...], **NT)
+            low = 2.0 * lax.dot_general(pair[:, :D], ff_up_ref[...], **NT)
             low_ref[...] = jnp.where(_in_group(rows, 2 * RANK, RANK), low, 0.0).astype(BF)
 
-        def finish(part_sum, row, part):
-            units = slice(row, row + part_sum.shape[1])
-            if part == 0:
-                sums[:, units] = part_sum + jnp.dot(low_ref[...], down_ref[:, units], preferred_element_type=F32)
+        def use(n, at, slot):
+            tile = SLOT // 2
+            if n < 2:
+                for t in range(2):
+                    units = slice(at + t * tile, at + (t + 1) * tile)
+                    d_mixed = lax.dot_general(pair[:, :D], slot[t * tile : (t + 1) * tile, :], **NT)
+                    d_mixed = d_mixed + jnp.dot(low_ref[...], ff_down_ref[:, units], preferred_element_type=F32)
+                    for m in range(tile // 128):
+                        column = 2 * (at + t * tile) + 256 * m
+                        g = gu_ref[:, column : column + 128].astype(F32)
+                        u = gu_ref[:, column + 128 : column + 256].astype(F32)
+                        d = d_mixed[:, 128 * m : 128 * (m + 1)]
+                        s = jax.nn.sigmoid(g)
+                        out[:, column : column + 128] = (d * u * s * (1.0 + g * (1.0 - s))).astype(BF)
+                        out[:, column + 128 : column + 256] = (d * g * s).astype(BF)
+                return
+            left = out[:, pl.ds(at, SLOT)]
+            low = lax.dot_general(left, up_ref[:, pl.ds(at, SLOT)], **NT)
+            for t in range(2):
+                here = slice(t * tile, (t + 1) * tile)
+                part = lax.dot_general(left, slot[here, :], **NT)
+                if n == 2:
+                    sums[:, here] = part
+                else:
+                    sums[:, here] += part
+            if n == 2:
+                lows[...] = low
             else:
-                d_mixed = sums[:, units] + part_sum
-                column = 2 * row
-                for m in range(part_sum.shape[1] // 128):
-                    g = gu_ref[:, column + 256 * m : column + 256 * m + 128].astype(F32)
-                    u = gu_ref[:, column + 256 * m + 128 : column + 256 * (m + 1)].astype(F32)
-                    d = d_mixed[:, 128 * m : 128 * (m + 1)]
-                    s = jax.nn.sigmoid(g)
-                    out[:, column + 256 * m : column + 256 * m + 128] = (d * u * s * (1.0 + g * (1.0 - s))).astype(BF)
-                    out[:, column + 256 * m + 128 : column + 256 * (m + 1)] = (d * g * s).astype(BF)
-
-        plan.backward(places, weights, whole, sems, first, pair, 1024, finish)
-
-    outs = [bf(rows, 2 * FF), bf(rows, WIDE), bf(rows, 2 * RANK)]
-    scratch = [pltpu.VMEM((rows, FF), F32)]
-    return plan.call(body, "down_back", [own, other, maps_up, maps_down, gu], outs, 2 * rows * D * FF, scratch)
-
-
-def gate_and_up_back(w, dy, maps_up):
-    rows = dy.shape[0]
-    plan = Resident(w, 2)
-
-    def body(places, *refs):
-        weights, (dy_ref, up_ref, keep, give, whole, sems, sums) = refs[:9], refs[9:]
-
-        def first():
-            _put_low(sums, _own_group(lax.dot_general(dy_ref[...], up_ref[...], **NT), 2 * RANK))
-
-        def finish(part_sum, row, part):
-            units = slice(row, row + part_sum.shape[1])
-            if part == 0:
-                sums[:, units] = part_sum
-            else:
-                sums[:, units] += part_sum
-
-        plan.backward(places, weights, whole, sems, first, dy_ref, 1024, finish)
+                lows[...] += low
+
+        pieces = [stream.down(weights, n) for n in range(2)] + [stream.gate_up(places, weights, n) for n in range(4)]
+        stream.run(pieces, slots, sems, first, use)
+        _put_low(sums, _own_group(lows[...], 2 * RANK))
         _split(places[2, 0], sums, keep, give)
 
-    outs = [_f32(ROWS, WIDE), bf(ROWS, WIDE)]
-    return plan.call(
-        body, "gate_and_up_back", [dy, maps_up], outs, 2 * rows * D * 2 * FF, [pltpu.VMEM((rows, WIDE), F32)]
-    )
+    outs = [bf(rows, 2 * FF), bf(rows, WIDE), bf(rows, 2 * RANK), _f32(ROWS, WIDE), bf(ROWS, WIDE)]
+    ins = [own, other, ff_up, ff_down, gu, maps_up]
+    scratch = [pltpu.VMEM((rows, WIDE), F32), pltpu.VMEM((rows, 4 * RANK), F32)]
+    return stream.call(body, "feed_forward_back", ins, outs, scratch)
 
 
 def project_qkv(x, w, low, maps_up):
@@ -595,10 +577,10 @@
     return _plain(body, "combine_tokens", outs, [keep, got, hidden, maps_down], [me])
 
 
-def project_out_back(me, own, other, w, maps_up, maps_down):
+def project_out_back(me, own, other, w, maps_up, maps_down, h2, attended):
     rows = 2 * ROWS
 
-    def body(me, own, other, w, up, down, heads, pair, low_ref):
+    def body(me, own, other, w, up, down, h2, attended, out, low_ref, pair):
         _pair_up(me[CORE], own, other, pair)
         low = 2.0 * lax.dot_general(pair[:, :D], up[...], **NT)
         low_ref[...] = jnp.where(_in_group(rows, 2 * RANK, RANK), low, 0.0).astype(BF)
@@ -606,10 +588,28 @@
             total = lax.dot_general(pair[:, :D], w[n : n + 512, :], **NT)
             total = total + jnp.dot(low_ref[...], down[:, n : n + 512], preferred_element_type=F32)
             for h in range(4):
-                heads[n // HD + h] = total[:, h * HD : (h + 1) * HD].astype(BF)
-
-    outs = [bf(8, rows, HD), bf(rows, WIDE), bf(rows, 2 * RANK)]
-    return _plain(body, "project_out_back", outs, [own, other, w, maps_up, maps_down], [me])
+                out[n // HD + h, :rows] = total[:, h * HD : (h + 1) * HD].astype(BF)
+
+        def shared(columns, start):
+            picked = jnp.concatenate([columns[:, start : start + RANK]] * 2, axis=1)
+            return jnp.where(_in_group(rows, 2 * RANK, RANK), picked, jnp.zeros_like(picked))
+
+        here = pl.ds(pl.multiple_of(me[CORE] * HALF, HALF), HALF)
+        pieces = [
+            (shared(pair, D), h2[:, here]),
+            (shared(pair, D + RANK), h2[:, here]),
+            (low_ref[...], attended[...]),
+            (2 * shared(h2, D), pair[:, here]),
+        ]
+        for p, (picked, act) in enumerate(pieces):
+            grad = lax.dot_general(picked, act, **TN).astype(BF)
+            at = slice(rows + 2 * RANK * p, rows + 2 * RANK * (p + 1))
+            for b in range(8):
+                out[b, at] = grad[:, HD * b : HD * (b + 1)]
+
+    outs = [bf(8, rows + 8 * RANK, HD), bf(rows, 2 * RANK)]
+    ins = [own, other, w, maps_up, maps_down, h2, attended]
+    return _plain(body, "project_out_back", outs, ins, [me], [pltpu.VMEM((rows, WIDE), BF)])
 
 
 def project_qkv_back(me, weighted, value_grad, qkv, squares, sums, w, maps_up):
@@ -692,83 +692,72 @@
     return value * cosine + pltpu.roll(value, 64, 1) * sine
 
 
+def _gain(gains, n, h, core):
+    return gains[n : n + 1, pl.ds(pl.multiple_of((2 * h + core) * HD, HD), HD)]
+
+
 def _pack_body(me, q, k, v, squares, other, gains, cosine, sine, out):
     scales = lax.rsqrt((squares[...] + other[...]) / D + EPS)
     c, s = cosine[...], sine[...]
-    out[0, :, 0:HD] = turn(q[...] * scales[:, 0:1] * gains[0:1], c, s).astype(BF)
-    out[0, :, HD : 2 * HD] = turn(k[...] * scales[:, 1:2] * gains[1:2], c, s).astype(BF)
-    out[0, :, 2 * HD :] = v[...].astype(BF)
+    for h in range(4):
+        here = slice(h * HD, (h + 1) * HD)
+        out[h, :, 0:HD] = turn(q[:, here] * scales[:, 0:1] * _gain(gains, 0, h, me[CORE]), c, s).astype(BF)
+        out[h, :, HD : 2 * HD] = turn(k[:, here] * scales[:, 1:2] * _gain(gains, 1, h, me[CORE]), c, s).astype(BF)
+        out[h, :, 2 * HD :] = v[:, here].astype(BF)
+
+
+def _head_specs(rows):
+    whole = pl.BlockSpec((rows, HD), lambda i: (0, 0))
+    columns = [pl.BlockSpec((rows, 4 * HD), lambda i, n=n: (0, 2 * n + i)) for n in range(3)]
+    heads = pl.BlockSpec((4, rows, 3 * HD), lambda i: (i, 0, 0))
+    gains = pl.BlockSpec((4, 8 * HD), lambda i: (0, i))
+    return whole, columns, heads, gains
 
 
 def pack_heads(me, qkv, squares, other, gains, cosine, sine):
     rows = qkv.shape[0]
-    whole = lambda shape: pl.BlockSpec(shape, lambda i, me: (0, 0))
+    whole, columns, heads, gain = _head_specs(rows)
     return pl.pallas_call(
         _pack_body,
-        out_shape=jax.ShapeDtypeStruct((8, rows, 3 * HD), BF),
-        grid_spec=pltpu.PrefetchScalarGridSpec(
-            num_scalar_prefetch=1,
-            grid=(8,),
-            in_specs=[
-            pl.BlockSpec((rows, HD), lambda i, me: (0, i)),
-            pl.BlockSpec((rows, HD), lambda i, me: (0, 8 + i)),
-            pl.BlockSpec((rows, HD), lambda i, me: (0, 16 + i)),
-            whole((rows, 128)),
-            whole((rows, 128)),
-            pl.BlockSpec((4, HD), lambda i, me: (0, 2 * i + me[CORE])),
-            whole((rows, HD)),
-            whole((rows, HD)),
-        ],
-            out_specs=pl.BlockSpec((1, rows, 3 * HD), lambda i, me: (i, 0, 0)),
-        ),
+        grid=(2,),
+        out_shape=bf(8, rows, 3 * HD),
+        in_specs=[_smem(), *columns, whole, whole, gain, whole, whole],
+        out_specs=heads,
         name="pack_heads",
     )(me, qkv, qkv, qkv, squares, other, gains, cosine, sine)
 
 
 def _unpack_body(me, d, q, k, gains, cosine, sine, wq, wk, dv, sums):
     c, s = cosine[...], -sine[...]
-    i = pl.program_id(0)
-    gq = turn(d[0, :, 0:HD].astype(F32), c, s) * gains[0:1]
-    gk = turn(d[0, :, HD : 2 * HD].astype(F32), c, s) * gains[1:2]
-    wq[...] = gq
-    wk[...] = gk
-    dv[...] = d[0, :, 2 * HD :]
-
-    @pl.when(i == 0)
+
+    @pl.when(pl.program_id(0) == 0)
     def _():
         sums[...] = jnp.zeros_like(sums)
 
     lane = lax.broadcasted_iota(jnp.int32, sums.shape, 1)
-    of_q = jnp.sum(gq * q[...], axis=1, keepdims=True)
-    of_k = jnp.sum(gk * k[...], axis=1, keepdims=True)
+    of_q, of_k = 0.0, 0.0
+    for h in range(4):
+        here = slice(h * HD, (h + 1) * HD)
+        gq = turn(d[h, :, 0:HD].astype(F32), c, s) * _gain(gains, 0, h, me[CORE])
+        gk = turn(d[h, :, HD : 2 * HD].astype(F32), c, s) * _gain(gains, 1, h, me[CORE])
+        wq[:, here] = gq
+        wk[:, here] = gk
+        dv[:, here] = d[h, :, 2 * HD :]
+        of_q += gq * q[:, here]
+        of_k += gk * k[:, here]
+    of_q, of_k = jnp.sum(of_q, axis=1, keepdims=True), jnp.sum(of_k, axis=1, keepdims=True)
     sums[...] += jnp.where(lane == 0, of_q, jnp.where(lane == 1, of_k, 0.0))
 
 
 def unpack_heads(me, d, qkv, gains, cosine, sine):
     rows = qkv.shape[0]
-    whole = lambda shape: pl.BlockSpec(shape, lambda i, me: (0, 0))
-    column = pl.BlockSpec((rows, HD), lambda i, me: (0, i))
+    whole, columns, heads, gain = _head_specs(rows)
     return pl.pallas_call(
         _unpack_body,
-        out_shape=[
-            jax.ShapeDtypeStruct((rows, HALF), F32),
-            jax.ShapeDtypeStruct((rows, HALF), F32),
-            jax.ShapeDtypeStruct((rows, HALF), BF),
-            jax.ShapeDtypeStruct((rows, HD), F32),
-        ],
-        grid_spec=pltpu.PrefetchScalarGridSpec(
-            num_scalar_prefetch=1,
-            grid=(8,),
-            in_specs=[
-            pl.BlockSpec((1, rows, 3 * HD), lambda i, me: (i, 0, 0)),
-            pl.BlockSpec((rows, HD), lambda i, me: (0, i)),
-            pl.BlockSpec((rows, HD), lambda i, me: (0, 8 + i)),
-            pl.BlockSpec((4, HD), lambda i, me: (0, 2 * i + me[CORE])),
-            whole((rows, HD)),
-            whole((rows, HD)),
-        ],
-            out_specs=[column, column, column, whole((rows, HD))],
-        ),
+        grid=(2,),
+        out_shape=[_f32(rows, HALF), _f32(rows, HALF), bf(rows, HALF), _f32(rows, HD)],
+        in_specs=[_smem(), heads, *columns[:2], gain, whole, whole],
+        out_specs=[columns[0], columns[0], columns[0], whole],
         name="unpack_heads",
     )(me, d, qkv, qkv, gains, cosine, sine)
 
@@ -836,7 +825,7 @@
     q = qkv[:, 0, :, 0:HD].reshape(TOTAL, HD)
     k = qkv[:, 0, :, HD : 2 * HD].reshape(TOTAL, HD)
     v = qkv[:, 0, :, 2 * HD :].reshape(TOTAL, HD)
-    g = grad[:, 0].reshape(TOTAL, HD)
+    g = grad[...].reshape(TOTAL, HD)
     dk[...] = jnp.zeros_like(dk)
     dv[...] = jnp.zeros_like(dv)
     for t in range(TOTAL // TILE):
@@ -863,7 +852,7 @@
         in_specs=[
             pl.BlockSpec(memory_space=pltpu.SMEM),
             pl.BlockSpec((8, 1, ROWS, 3 * HD), lambda g: (0, g, 0, 0)),
-            pl.BlockSpec((8, 1, ROWS, HD), lambda g: (0, g, 0, 0)),
+            pl.BlockSpec((8, ROWS, HD), lambda g: (0, g, 0)),
             pl.BlockSpec((1, TOTAL, HD), lambda g: (g, 0, 0)),
             pl.BlockSpec((1, TOTAL, 1), lambda g: (g, 0, 0)),
         ],
@@ -959,20 +948,22 @@
     return _plain(body, name, [bf(8, 2 * RANK, width)], list(lows) + list(acts), [core])[0]
 
 
-def adapter_outputs(core, halves, others, count, shapes, name, write):
+def adapter_outputs(core, halves, others, shapes, name, write, done=()):
+    count = len(halves)
+
     def body(core, *refs):
-        own, other, outs = refs[:count], refs[count : 2 * count], refs[2 * count :]
+        own, other = refs[:count], refs[count : 2 * count]
+        ready, outs = refs[2 * count : 2 * count + len(done)], refs[2 * count + len(done) :]
 
         def place(start):
             return pl.ds(pl.multiple_of(start, 128), 128)
 
         for side, group in ((core[0], own), (1 - core[0], other)):
 
-            def piece(n, at):
-                block, slot = divmod(at, group[n].shape[3] // 128)
-                return group[n][block, 0, :, 128 * slot : 128 * (slot + 1)].astype(F32)
-
-            write(side, piece, place, outs)
+            def block(n, b, t):
+                return group[n][b, 0, :, 128 * t : 128 * (t + 1)].astype(F32)
+
+            write(side, block, place, outs, *ready)
 
     arrays = halves + others
     size = sum(v.size * 2 for v in arrays)
@@ -980,35 +971,44 @@
         body,
         grid=(8,),
         out_shape=[jax.ShapeDtypeStruct(s, F32) for s in shapes],
-        in_specs=[_smem()] + [pl.BlockSpec((v.shape[0], 1) + v.shape[2:], lambda i: (0, i, 0, 0)) for v in arrays],
+        in_specs=[_smem()] + [pl.BlockSpec((8, 1) + v.shape[2:], lambda i: (0, i, 0, 0)) for v in arrays]
+        + [pl.BlockSpec((1,) + v.shape[1:], lambda i: (i, 0, 0, 0)) for v in done],
         out_specs=[pl.BlockSpec((1,) + s[1:], lambda i, n=len(s): (i,) + (0,) * (n - 1)) for s in shapes],
         compiler_params=pltpu.CompilerParams(vmem_limit_bytes=40 * 2**20),
         cost_estimate=pl.CostEstimate(flops=0, bytes_accessed=size, transcendentals=0),
         name=name,
-    )(core, *arrays)
-
-
-def write_early(side, piece, place, outs):
-    up_hidden, down_ff = outs
+    )(core, *arrays, *done)
+
+
+def write_early(side, block, place, outs):
+    up_hidden, down_ff, middle = outs
+    slots = EARLY // 128
     for m in range(FF // 128):
         units = place((2 * (m // 4) + side) * 512 + (m % 4) * 128)
-        up_hidden[0, 0, :, units] = piece(0, m)
-        up_hidden[0, 1, :, units] = piece(0, 32 + m)
-        down_ff[0, :, units] = piece(0, 64 + m)
-
-
-def write_late(side, piece, place, outs):
+        up_hidden[0, 0, :, units] = block(0, *divmod(m, slots))
+        up_hidden[0, 1, :, units] = block(0, *divmod(32 + m, slots))
+        down_ff[0, :, units] = block(0, *divmod(64 + m, slots))
+    for m in range(8):
+        whole, head = place(side * HALF + 128 * m), place((2 * m + side) * HD)
+        for n in range(2):
+            middle[0, n, :, whole] = block(0, m, slots + n)
+        middle[0, 2, :, head] = block(0, m, slots + 2)
+        middle[0, 3, :, whole] = block(0, m, slots + 3)
+        middle[0, 4, :, whole] = block(0, *divmod(96 + m, slots))
+
+
+def write_late(side, block, place, outs, middle):
     down_in, up_model = outs
+    for n, m in ((4, 0), (5, 1), (3, 2)):
+        down_in[0, n] = middle[0, m]
+    for n in (3, 4):
+        up_model[0, n] = middle[0, n]
+    slots = LATE // 128
     for m in range(8):
         whole, head = place(side * HALF + 128 * m), place((2 * m + side) * HD)
         for n in range(3):
-            down_in[0, n, :, whole] = piece(0, 8 * n + m)
-            up_model[0, n, :, head] = piece(0, 24 + 8 * n + m)
-        down_in[0, 4, :, whole] = piece(0, 48 + m)
-        down_in[0, 5, :, whole] = piece(0, 56 + m)
-        down_in[0, 3, :, head] = piece(0, 64 + m)
-        up_model[0, 3, :, whole] = piece(0, 72 + m)
-        up_model[0, 4, :, whole] = piece(1, EARLY // 128 - 8 + m)
+            down_in[0, n, :, whole] = block(0, *divmod(8 * n + m, slots))
+            up_model[0, n, :, head] = block(0, *divmod(24 + 8 * n + m, slots))
 
 
 def on_device(
@@ -1046,7 +1046,7 @@
     keep_g, give_g = split_g(me, gate_matrix, upward_matrix)
     got_a, got_g = swap(give_a), swap(give_g)
     xs_a, ys_a = parts_a(me, keep_a, got_a, output_matrix)
-    xs_m, ys_g, ys_d = parts_m(me, keep_g, got_g, down_matrix)
+    xs_m, ys_g = parts_m(me, keep_g, got_g, down_matrix)
     crossed = plan.across(xs_a)
     small_a = plan.small(ys_a)
     small_g = plan.small(ys_g)
@@ -1057,11 +1057,10 @@
     for _ in range(3):
         plan.round(rings_a)
     xs_m = plan.over_xz(xs_m, crossed, rings_a[0][1], rings_a[1][1])
-    small_d = plan.small(ys_d)
-    y_g = spread(me, small_g, [(0, FF - CUT_G // 2, 1)], "spread_g")
-    rings_g = [[v] for v in y_g]
+    w_qkv, w_out = assemble(Chunks(256, CUT_A, 4 * HALF, places, xs_a, 0, rings_a))
+    small_g[3] = after(small_g[3], w_qkv)
+    rings_g = [[v] for v in spread(me, small_g, [(0, FF - CUT_G // 2, 1)], "spread_g")]
     plan.round(rings_g)
-    w_qkv, w_out = assemble(Chunks(256, CUT_A, 4 * HALF, places, xs_a, 0, rings_a))
 
     facts = jnp.concatenate([group_adapter_index[0], continuation_lengths[0]]).astype(F32)
     facts = jnp.broadcast_to(jnp.pad(facts, (0, 125))[None], (8, 128))
@@ -1110,30 +1109,22 @@
     qkv_low = own_columns((2.0 * dot_nt(x2, qkv_down).astype(BF)).astype(BF), 3 * RANK)
     qkv, squares = project_qkv(x2, w_qkv, qkv_low, qkv_up)
     squares = (squares, swap(squares))
-    qkv = after(qkv, small_d[1])
     packed = pack_heads(me, qkv, *squares, gains, cosine, sine)
     heads = lax.all_to_all(packed, CTX, 0, 0, tiled=True).reshape(8, 2, ROWS, 3 * HD)
-    heads = after(heads, rings_g[0][-1], rings_g[1][-1], small_d[2])
-    plan.round(rings_g, qkv)
+    heads = after(heads, rings_g[0][-1], rings_g[1][-1])
+    plan.round(rings_g, heads)
     out_heads, exact, log_total = attend(bounds, heads)
     attended = lax.all_to_all(out_heads, CTX, 0, 0, tiled=True).reshape(8, 2 * ROWS, HD)
-    y_d = spread(me, small_d, [(0, HALF - CUT_D // 2, 2)], "spread_d")
-    attended = after(attended, rings_g[0][-1], rings_g[1][-1], y_d[0])
     keep, give, attended = project_out(me, attended, w_out, out_down)
     attn_pre, hidden, sent = combine_attention(me, keep, swap(give), tokens, gains, out_up2)
 
-    plan.round(rings_g, out_heads)
+    sent = after(sent, rings_g[0][-1], rings_g[1][-1])
+    plan.round(rings_g, attended)
     wg = Chunks(256, CUT_G, 2 * FF, places, xs_m, 0, rings_g)
-    rings_d = [[v] for v in y_d]
-    plan.round(rings_d)
-    gu, mixed, h2, gu_low = gate_and_up(wg, sent, swap(sent), gu_down, gu_up)
-    plan.round(rings_d)
-    plan.round(rings_d)
-    wd = Chunks(512, CUT_D, D, places, xs_m, CUT_G // 4, rings_d)
-    keep, give = down(wd, mixed, ff_down)
+    gu, mixed, h2, gu_low, keep, give = feed_forward(wg, sent, swap(sent), gu_down, gu_up, ff_down)
     output, sent = combine_output(me, keep, swap(give), hidden, cotangent, gains, ff_up2)
 
-    d_gu, d_mlp, ff_grad_low = down_back(wd, sent, swap(sent), ff_up2, ff_down, gu)
+    d_gu, d_mlp, ff_grad_low, keep, give = feed_forward_back(wg, sent, swap(sent), ff_up2, ff_down, gu, gu_up)
     early = rank_gradients(
         [gu_low, ff_grad_low, d_mlp],
         [d_gu, mixed, d_mlp],
@@ -1147,22 +1138,20 @@
         ],
         EARLY,
     )
-    d_gu, early = lax.optimization_barrier((d_gu, early))
+    d_hidden, sent = combine_hidden(me, keep, swap(give), cotangent, attn_pre, gains, gu_down)
+    sent, early = lax.optimization_barrier((sent, early))
     early = lax.all_to_all(early, CTX, 0, 0, tiled=True)
-    keep, give = gate_and_up_back(wg, d_gu, gu_up)
-    give, early = lax.optimization_barrier((give, early))
-    d_hidden, sent = combine_hidden(me, keep, swap(give), cotangent, attn_pre, gains, gu_down)
-
-    d_out_heads, d_attn, out_grad_low = project_out_back(me, sent, swap(sent), w_out, out_up2, out_down)
-    d_out_heads = lax.all_to_all(d_out_heads, CTX, 0, 0, tiled=True).reshape(8, 2, ROWS, HD)
+
+    d_out_heads, _ = project_out_back(me, sent, swap(sent), w_out, out_up2, out_down, h2, attended)
+    d_out_heads = lax.all_to_all(d_out_heads, CTX, 0, 0, tiled=True)
     own = jnp.sum(early.astype(F32), axis=0).astype(BF)
+    middle = jnp.sum(d_out_heads[:, 2 * ROWS :].astype(F32), axis=0).astype(BF).reshape(4, 2 * RANK, HD)
+    own = jnp.concatenate([own, *middle], axis=1)
     own_slot = jnp.repeat(slots, RANK)[:, None] == lax.broadcasted_iota(jnp.int32, (1, 128), 1)
     own = jnp.concatenate([own, own_slot.astype(BF)], axis=1)
     d_out_heads, own = lax.optimization_barrier((d_out_heads, own))
-    groups = spread_over(own, shard).reshape(16, RANK, EARLY + 128)
+    groups = spread_over(own, shard).reshape(16, RANK, EARLY + MIDDLE + 128)
     d_heads = attend_back(bounds, heads, d_out_heads, exact, log_total)
-    d_heads, groups = lax.optimization_barrier((d_heads, groups))
-    picker = groups[:, 0, EARLY : EARLY + 8]
     d_heads = lax.all_to_all(d_heads, CTX, 0, 0, tiled=True).reshape(8, 2 * ROWS, 3 * HD)
     w_q, w_k, d_v, sums = unpack_heads(me, d_heads, qkv, gains, cosine, sine)
 
@@ -1170,25 +1159,20 @@
         flat = groups.reshape(16, -1)
         return lax.dot_general(picker, flat, **TN).astype(BF).reshape(8 * RANK, -1)
 
-    early, w_q = lax.optimization_barrier((by_slot(groups[:, :, :EARLY]), w_q))
+    picker = groups[:, 0, EARLY + MIDDLE : EARLY + MIDDLE + 8]
+    early, w_q = lax.optimization_barrier((by_slot(groups[:, :, : EARLY + MIDDLE]), w_q))
     early = lax.all_gather(early, CTX)
     d_qkv, keep, give = project_qkv_back(me, (w_q, w_k), d_v, qkv, squares, (sums, swap(sums)), w_qkv, qkv_up)
     grad_tokens, low = combine_tokens(me, keep, swap(give), d_hidden, qkv_down)
     low = both(low, swap(low)).reshape(2 * ROWS, 128)
 
     late = rank_gradients(
-        [low, qkv_low, d_attn, out_grad_low, h2],
-        [x2, d_qkv, h2, attended, d_attn],
+        [low, qkv_low],
+        [x2, d_qkv],
         me,
         "late_gradients",
         [(0, 0, (n * RANK, n * RANK), 1, half) for n in range(3)]
-        + [(1, 1, (n * RANK, (3 + n) * RANK), 1, third(n)) for n in range(3)]
-        + [
-            (2, 2, (D, D), 1, half),
-            (2, 2, (D + RANK, D + RANK), 1, half),
-            (3, 3, (0, RANK), 1, whole(HALF)),
-            (4, 4, (D, D), 2, half),
-        ],
+        + [(1, 1, (n * RANK, (3 + n) * RANK), 1, third(n)) for n in range(3)],
         LATE,
     )
     late = lax.all_to_all(late, CTX, 0, 0, tiled=True)
@@ -1199,26 +1183,20 @@
     shape = (8, 8, RANK, -1)
     early = early.reshape(shape)
     early_other = swap(early)
-    grad_up_hidden, grad_down_ff = adapter_outputs(
+    grad_up_hidden, grad_down_ff, middle = adapter_outputs(
         me,
         [early],
         [early_other],
-        1,
-        [(8, 2, RANK, 2 * FF), (8, RANK, 2 * FF)],
+        [(8, 2, RANK, 2 * FF), (8, RANK, 2 * FF), (8, 5, RANK, D)],
         "early_outputs",
         write_early,
     )
-    late, grad_up_hidden = lax.optimization_barrier((late, grad_up_hidden))
+    late, middle = lax.optimization_barrier((late, middle))
     late_other = swap(late)
     late, late_other = late.reshape(shape), late_other.reshape(shape)
+    shapes = [(8, 6, RANK, D), (8, 5, RANK, D)]
     grad_down_in, grad_up_model = adapter_outputs(
-        me,
-        [late, early[7:]],
-        [late_other, early_other[7:]],
-        2,
-        [(8, 6, RANK, D), (8, 5, RANK, D)],
-        "late_outputs",
-        write_late,
+        me, [late], [late_other], shapes, "late_outputs", write_late, [middle]
     )
     return (output[None], grad_tokens[None], grad_down_in, grad_down_ff, grad_up_model, grad_up_hidden)
 

time: 686 us -> 658 us (0.959)
  blocking collectives: 37 us -> 131 us
  waiting for transfers between devices: 231 us -> 170 us
  starting transfers between devices: 127 us -> 83.7 us
  Pallas kernels: 194 us -> 160 us
  local copies, waits for them, and re-layouts: 59.8 us -> 73 us
    all_to_all x0 -> x2, blocking collectives: none -> 88 us  [the longest x1 44.8 us: on_device(): lax.all_to_all(packed, CTX, 0, 0, tiled=True).reshape(8, 2, ROWS, 3 * HD)]
    all_to_all x3 -> x1, waiting for transfers between devices: 50.5 us -> 7.99 us  [on_device(): d_out_heads = lax.all_to_all(d_out_heads, CTX, 0, 0, tiled=True)]
    ppermute x29 -> x20, starting transfers between devices: 79.1 us -> 45.2 us  [send(): self.last = lax.ppermute(value, ALL, STEPS[how])]
    pallas_call x4 -> x2, Pallas kernels: 81 us -> 55.5 us  [call(): pl.pallas_call(body, out_shape=outs, in_specs=[_smem()] + [anywhere] * 9...]
    all_to_all x2, waiting for transfers between devices: 31.3 us -> 14.8 us  [spread_over(): lax.all_to_all(jnp.broadcast_to(value[None], (8,) + value.shape), axes, 0...]
    unnamed x177 -> x166, local copies, waits for them, and re-layouts: 51 us -> 63.6 us
    all_to_all x1, blocking collectives: 16 us -> 27.5 us  [spread_over(): lax.all_to_all(jnp.broadcast_to(value[None], (8,) + value.shape), axes, 0...]
    all_to_all x3 -> x1, starting transfers between devices: 13.8 us -> 5.53 us  [on_device(): d_out_heads = lax.all_to_all(d_out_heads, CTX, 0, 0, tiled=True)]
  transfers between devices with their start and end apart: 55 -> 44, of which waited for: 32 -> 28; matrix products, arithmetic and copies ran while one was open for 3% -> 3% of each run, Pallas kernels for 20% -> 14%
where the time goes in v3:
time: 658 us; the launch traced here: 647 us
  waiting for transfers between devices  170 us (26%)
  Pallas kernels  160 us (24%)
  blocking collectives  131 us (20%)
  starting transfers between devices  83.7 us (13%)
  local copies, waits for them, and re-layouts  73 us (11%)
  between operations  15.2 us (2%)
  other arithmetic  11.6 us (2%)
    ppermute x20, waiting for transfers between devices, send(): self.last = lax.ppermute(value, ALL, STEPS[how])  116 us
    unnamed x166, local copies, waits for them, and re-layouts  63.6 us
    pallas_call x2, Pallas kernels, call(): pl.pallas_call(body, out_shape=outs, in_specs=[_smem()] + [anywhere] * 9...  55.5 us
    ppermute x20, starting transfers between devices, send(): self.last = lax.ppermute(value, ALL, STEPS[how])  45.2 us
    all_to_all x1, blocking collectives, on_device(): lax.all_to_all(packed, CTX, 0, 0, tiled=True).reshape(8, 2, ROWS, 3 * HD)  44.8 us
    all_to_all x1, blocking collectives, on_device(): lax.all_to_all(out_heads, CTX, 0, 0, tiled=True).reshape(8, 2 * ROWS, HD)  43.2 us
    pallas_call x14, Pallas kernels, _plain(): pl.pallas_call(body, out_shape=outs, in_specs=[_smem()] * len(scalars) +...  34.4 us
    all_to_all x1, blocking collectives, spread_over(): lax.all_to_all(jnp.broadcast_to(value[None], (8,) + value.shape), axes, 0...  27.5 us
  transfers between devices with their start and end apart: 44, of which 28 were waited for; matrix products, arithmetic and copies ran while one was open for 3% of the time, Pallas kernels for 14%

profile of v3, /device:TPU:7, one launch (start us, length us, event | category | flops | bytes accessed | tf_op | source)
XLA Modules:
  0.0 647.0 jit_solution(16074165312530502443)
XLA Ops:
  15.7 3.8 collective-permute-start.2
  19.6 2.7 collective-permute-start.4
  22.3 5.5 collective-permute-done.4
  28.8 3.4 split_g.1
  34.1 6.7 %collective-permute-done.3.refs_2_ = bf16[256,1024]{1,0:T(8,128)(2,1)S(1)} collective-permute-done((bf16[256,1024]{1,0:T(8,128)(2,1)S(1)}, bf16[256,1024]{1,0:T(8,128)(2,1)S(1)}, u32[]{:S(2)}, u32[]{:S(2)}) %collective-permute-start.3) | collective-permute-done | bytes 524320 | tf_op jit(solution)/shard_map/ppermute | solution.py:71
  40.8 3.5 collective-permute-start.6
  45.6 2.4 parts_m.1
  48.1 3.2 collective-permute-start.5
  51.2 4.7 collective-permute-done.6.refs_3_
  56.7 2.7 collective-permute-start.7
  61.7 13.4 %collective-permute-done.5 = bf16[256,2048]{1,0:T(8,128)(2,1)S(1)} collective-permute-done((bf16[256,2048]{1,0:T(8,128)(2,1)S(1)}, bf16[256,2048]{1,0:T(8,128)(2,1)S(1)}, u32[]{:S(2)}, u32[]{:S(2)}) %collective-permute-start.5) | collective-permute-done | bytes 1048608 | tf_op jit(solution)/shard_map/ppermute | solution.py:71
  75.1 9.3 %collective-permute-done.7.refs_2_ = bf16[512,1024]{1,0:T(8,128)(2,1)S(1)} collective-permute-done((bf16[512,1024]{1,0:T(8,128)(2,1)S(1)}, bf16[512,1024]{1,0:T(8,128)(2,1)S(1)}, u32[]{:S(2)}, u32[]{:S(2)}) %collective-permute-start.7) | collective-permute-done | bytes 1048608 | tf_op jit(solution)/shard_map/ppermute | solution.py:71
  84.4 11.2 %collective-permute-done.8.refs_6_ = bf16[512,1024]{1,0:T(8,128)(2,1)S(1)} collective-permute-done((bf16[512,1024]{1,0:T(8,128)(2,1)S(1)}, bf16[512,1024]{1,0:T(8,128)(2,1)S(1)}, u32[]{:S(2)}, u32[]{:S(2)}) %collective-permute-start.8) | collective-permute-done | bytes 1048608 | tf_op jit(solution)/shard_map/ppermute | solution.py:71
  100.1 3.6 collective-permute-start.12
  103.7 8.7 %collective-permute-done.9.refs_1_ = bf16[256,2048]{1,0:T(8,128)(2,1)} collective-permute-done((bf16[256,2048]{1,0:T(8,128)(2,1)S(1)}, bf16[256,2048]{1,0:T(8,128)(2,1)}, u32[]{:S(2)}, u32[]{:S(2)}) %collective-permute-start.9) | collective-permute-done | bytes 1048608 | tf_op jit(solution)/shard_map/ppermute | solution.py:71
  112.4 2.3 collective-permute-start.10
  116.8 2.7 collective-permute-start.13
  119.5 7.2 %collective-permute-done.14.refs_7_ = bf16[512,1024]{1,0:T(8,128)(2,1)} collective-permute-done((bf16[512,1024]{1,0:T(8,128)(2,1)}, bf16[512,1024]{1,0:T(8,128)(2,1)}, u32[]{:S(2)}, u32[]{:S(2)}) %collective-permute-start.14) | collective-permute-done | bytes 1048608 | tf_op jit(solution)/shard_map/ppermute | solution.py:71
  126.7 3.4 collective-permute-start.15
  130.1 10.6 %collective-permute-done.10.refs_2_ = bf16[256,2048]{1,0:T(8,128)(2,1)} collective-permute-done((bf16[256,2048]{1,0:T(8,128)(2,1)}, bf16[256,2048]{1,0:T(8,128)(2,1)}, u32[]{:S(2)}, u32[]{:S(2)}) %collective-permute-start.10) | collective-permute-done | bytes 1048608 | tf_op jit(solution)/shard_map/ppermute | solution.py:71
  140.8 3.4 collective-permute-start.11
  144.8 3.8 choose_adapters.1
  155.8 12.1 %assemble.1 = (bf16[2048,3072]{1,0:T(8,128)(2,1)}, bf16[1024,2048]{1,0:T(8,128)(2,1)}) custom-call(s32[3,4]{1,0:T(4,128)S(1)} %pad_add_fusion.places, bf16[4,4,2,256,512]{4,3,2,1,0:T(8,128)(2,1)} %bitcast.82, bf16[512,1024]{1,0:T(8,128)(2,1)S(1)} %copy-done.24, bf16[512,1024]{1,0:T(8,128)(2,1)S(1)} %copy-done.28, ...), custom_call_target="tpu_custom_call" | custom-call | bytes 67108864 | tf_op jit(solution)/shard_map/assemble/pallas_call | solution.py:255
  167.9 3.7 collective-permute-done.11.refs_3_
  171.7 4.3 spread_g.1
  176.0 3.4 collective-permute-start.20
  179.5 7.1 %copy-done.1 = bf16[2048,3072]{1,0:T(8,128)(2,1)S(1)} copy-done((bf16[2048,3072]{1,0:T(8,128)(2,1)S(1)}, bf16[2048,3072]{1,0:T(8,128)(2,1)}, u32[]{:S(2)}) %copy-start.1) | copy-done | bytes 12582936
  186.5 6.5 %project_qkv.1 = (f32[288,3072]{1,0:T(8,128)S(1)}, f32[288,128]{1,0:T(8,128)S(1)}) custom-call(bf16[288,2048]{1,0:T(8,128)(2,1)S(1)} %bitcast.63, bf16[2048,3072]{1,0:T(8,128)(2,1)S(1)} %copy-done.1, bf16[288,96]{1,0:T(8,128)(2,1)S(1)} %fusion.1.low.refs_1_, bf16[96,3072]{1,0:T(8,128)(2,1)S(1)} %copy-done.6), custom_call_target="tpu_custom_call" | custom-call | flops 3623878656 | bytes 18000000 | tf_op jit(solution)/shard_map/project_qkv/pallas_call | solution.py:489
  198.5 4.0 pack_heads.1
  202.6 44.8 %all_to_all.45 = bf16[8,288,384]{2,1,0:T(8,128)(2,1)S(1)} all-to-all(bf16[8,288,384]{2,1,0:T(8,128)(2,1)} %pack_heads.1), channel_id=1, replica_groups=mesh['yl'=2,'x'=4,'z'=4,'yh'=2,'c'=2] {'yl','x'}, dimensions={0} | all-to-all | bytes 3538944 | tf_op jit(solution)/shard_map/all_to_all | solution.py:1113
  247.4 3.2 collective-permute-start.23
  250.9 6.6 %attend.1 = (bf16[8,2,144,128]{3,2,1,0:T(8,128)(2,1)S(1)}, f32[2,1152,128]{2,1,0:T(8,128)S(1)}, f32[2,1152,1]{2,1,0:T(8,128)S(1)}) custom-call(s32[2]{0:T(128)S(1)} %get-tuple-element.204.bounds, bf16[8,2,144,384]{3,2,1,0:T(8,128)(2,1)S(1)} %bitcast.73), custom_call_target="tpu_custom_call" | custom-call | flops 900000000 | bytes 5000000 | tf_op jit(solution)/shard_map/attend/pallas_call | solution.py:800
  258.5 43.2 %all_to_all.46 = bf16[8,2,144,128]{3,2,1,0:T(8,128)(2,1)S(1)} all-to-all(bf16[8,2,144,128]{3,2,1,0:T(8,128)(2,1)S(1)} %get-tuple-element.141), channel_id=1, replica_groups=mesh['yl'=2,'x'=4,'z'=4,'yh'=2,'c'=2] {'yl','x'}, dimensions={0} | all-to-all | bytes 1179648 | tf_op jit(solution)/shard_map/all_to_all | solution.py:1117
  301.8 4.1 project_out.1
  307.9 2.2 collective-permute-start.24
  318.1 13.9 %collective-permute-done.22.refs_4_ = bf16[512,2048]{1,0:T(8,128)(2,1)S(1)} collective-permute-done((bf16[512,2048]{1,0:T(8,128)(2,1)S(1)}, bf16[512,2048]{1,0:T(8,128)(2,1)S(1)}, u32[]{:S(2)}, u32[]{:S(2)}) %collective-permute-start.22) | collective-permute-done | bytes 2097184 | tf_op jit(solution)/shard_map/ppermute | solution.py:71
  333.4 21.1 %collective-permute-done.24.refs_8_ = bf16[512,2048]{1,0:T(8,128)(2,1)} collective-permute-done((bf16[512,2048]{1,0:T(8,128)(2,1)S(1)}, bf16[512,2048]{1,0:T(8,128)(2,1)}, u32[]{:S(2)}, u32[]{:S(2)}) %collective-permute-start.24) | collective-permute-done | bytes 2097184 | tf_op jit(solution)/shard_map/ppermute | solution.py:71
  354.5 26.6 %feed_forward.1 = (bf16[288,8192]{1,0:T(8,128)(2,1)}, bf16[288,4096]{1,0:T(8,128)(2,1)}, bf16[288,2176]{1,0:T(8,128)(2,1)}, bf16[288,64]{1,0:T(8,128)(2,1)}, f32...) custom-call(s32[3,4]{1,0:T(4,128)} %copy-done.62, bf16[4,4,2,256,2048]{4,3,2,1,0:T(8,128)(2,1)} %bitcast.80, ...), custom_call_target="tpu_custom_call" | custom-call | flops 14495514624 | bytes 53157888 | tf_op jit(solution)/shard_map/feed_forward/pallas_call | solution.py:358
  381.1 4.2 collective-permute-start.27
  389.8 2.1 combine_output.1
  395.7 28.9 %feed_forward_back.1 = (bf16[288,8192]{1,0:T(8,128)(2,1)}, bf16[288,2176]{1,0:T(8,128)(2,1)}, bf16[288,32]{1,0:T(8,128)(2,1)}, f32[144,2176]{1,0:T(8,128)}, bf16[144,2176]{1,0:T(8,128)(2,1)}) custom-call(s32[3,4]{1,0:T(4,128)} %copy-done.62, bf16[4,4,2,256,2048]{4,3,2,1,0:T(8,128)(2,1)} %bitcast.81, bf16[512,2048]{1,0:T(8,128)(2,1)} %get-tuple-element.131.refs_1_, ...), custom_call_target="tpu_custom_call" | custom-call | flops 14495514624 | bytes 57745408 | tf_op jit(solution)/shard_map/feed_forward_back/pallas_call | solution.py:358
  428.9 4.9 early_gradients.1
  436.9 4.3 all-to-all-start.3
  447.5 5.2 project_out_back.1
  453.6 5.5 all-to-all-start.2
  463.0 8.0 %all-to-all-done.2.grad = bf16[8,416,128]{2,1,0:T(8,128)(2,1)} async-done(((bf16[8,416,128]{2,1,0:T(8,128)(2,1)}), bf16[8,416,128]{2,1,0:T(8,128)(2,1)}, u32[]{:S(2)}, u32[]{:S(2)}) %all-to-all-start.2) | async-done | bytes 852000 | tf_op jit(solution)/shard_map/all_to_all | solution.py:1146
  477.0 4.4 all-to-all-start.4
  484.0 7.6 %attend_back.1 = bf16[8,2,144,384]{3,2,1,0:T(8,128)(2,1)S(1)} custom-call(s32[2]{0:T(128)S(1)} %get-tuple-element.204.bounds, bf16[8,2,144,384]{3,2,1,0:T(8,128)(2,1)S(1)} %bitcast.74, bf16[8,416,128]{2,1,0:T(8,128)(2,1)} %all-to-all-done.2.grad, f32[2,1152,128]{2,1,0:T(8,128)S(1)} %copy-done.65, f32[2,1152,1]{2,1,0:T(8,128)S(1)} %copy-done.67), custom_call_target="tpu_custom_call" | custom-call | flops 2300000000 | bytes 8000000 | tf_op jit(solution)/shard_map/attend_back/pallas_call | solution.py:848
  492.9 6.5 %all-to-all-done.4 = bf16[8,32,2304]{2,1,0:T(8,128)(2,1)} async-done(((bf16[8,32,2304]{2,1,0:T(8,128)(2,1)}), bf16[8,32,2304]{2,1,0:T(8,128)(2,1)}, u32[]{:S(2)}, u32[]{:S(2)}) %all-to-all-start.4) | async-done | bytes 1179680 | tf_op jit(solution)/shard_map/all_to_all | solution.py:1087
  499.4 5.0 all-to-all-start.5
  505.1 2.3 slice.32
  512.2 13.3 %all-to-all-done.5 = bf16[8,2,144,384]{3,2,1,0:T(8,128)(2,1)S(1)} async-done(((bf16[8,2,144,384]{3,2,1,0:T(8,128)(2,1)}), bf16[8,2,144,384]{3,2,1,0:T(8,128)(2,1)S(1)}, u32[]{:S(2)}, u32[]{:S(2)}) %all-to-all-start.5) | async-done | bytes 1769504 | tf_op jit(solution)/shard_map/all_to_all | solution.py:1155
  526.7 4.0 unpack_heads.1
  537.5 10.6 %project_qkv_back.1 = (bf16[288,3072]{1,0:T(8,128)(2,1)}, f32[144,2176]{1,0:T(8,128)S(1)}, bf16[144,2176]{1,0:T(8,128)(2,1)S(1)}) custom-call(s32[8]{0:T(128)S(1)} %copy-done.58, f32[288,1024]{1,0:T(8,128)S(1)} %copy-done.17, f32[288,1024]{1,0:T(8,128)S(1)} %copy-done.18, bf16[288,1024]{1,0:T(8,128)(2,1)S(1)} %copy-done.35, f32[288,3072]{1,0:T(8,128)} %copy-done, ...), custom_call_target="tpu_custom_call" | custom-call | flops 3623878656 | bytes 22000000 | tf_op jit(solution)/shard_map/project_qkv_back/pallas_call | solution.py:640
  554.7 15.8 %all_to_all.47 = bf16[8,32,768]{2,1,0:T(8,128)(2,1)S(1)} all-to-all(bf16[8,32,768]{2,1,0:T(8,128)(2,1)S(1)} %late_gradients.1), channel_id=1, replica_groups=mesh['yl'=2,'x'=4,'z'=4,'yh'=2,'c'=2] {'yl','x'}, dimensions={0} | all-to-all | bytes 786432 | tf_op jit(solution)/shard_map/all_to_all | solution.py:1178
  570.5 27.5 %all_to_all.48 = bf16[8,32,768]{2,1,0:T(8,128)(2,1)S(1)} all-to-all(bf16[8,32,768]{2,1,0:T(8,128)(2,1)S(1)} %broadcast_in_dim.46), channel_id=1, replica_groups=mesh['yl'=2,'x'=4,'z'=4,'yh'=2,'c'=2] {'z','yh'}, dimensions={0} | all-to-all | bytes 786432 | tf_op jit(solution)/shard_map/all_to_all | solution.py:1087
  600.1 5.7 all-to-all-start.8
  605.9 2.3 copy-done.5
  608.2 8.9 %early_outputs.1 = (f32[8,2,16,8192]{3,2,1,0:T(8,128)}, f32[8,16,8192]{2,1,0:T(8,128)}, f32[8,5,16,2048]{3,2,1,0:T(8,128)S(1)}) custom-call(s32[8]{0:T(128)S(1)} %copy-done.58, bf16[8,8,16,2176]{3,2,1,0:T(8,128)(2,1)S(1)} %bitcast.67, bf16[8,8,16,2176]{3,2,1,0:T(8,128)(2,1)} %collective-permute-done.34.refs_1_), custom_call_target="tpu_custom_call" | custom-call | bytes 8912896 | tf_op jit(solution)/shard_map/early_outputs/pallas_call | solution.py:970
  617.1 2.4 copy-done.2
  619.5 8.3 %all-to-all-done.8 = bf16[8,128,768]{2,1,0:T(8,128)(2,1)S(1)} async-done(((bf16[8,128,768]{2,1,0:T(8,128)(2,1)}), bf16[8,128,768]{2,1,0:T(8,128)(2,1)S(1)}, u32[]{:S(2)}, u32[]{:S(2)}) %all-to-all-start.8) | async-done | bytes 1572896 | tf_op jit(solution)/shard_map/all_to_all | solution.py:1087
  628.7 3.0 collective-permute-done.35
  631.8 2.5 copy-done.3
  634.2 6.1 late_outputs.1
  (270 shorter events, 107.2 us)
Async XLA Ops:
  7.2 144.9 %all-gather.7.cloned.1.call-start = ((), (), s32[]{:S(2)}) async-start(), calls=%async_computation.10 | async-start | bytes 8912896 | tf_op jit(solution)/shard_map/all_gather | solution.py:677
  10.4 161.2 %copy-start.56 = (s32[8]{0:T(128)}, s32[8]{0:T(128)S(1)}, u32[]{:S(2)}) copy-start(s32[8]{0:T(128)S(1)} %stack.141.core.me) | copy-start | bytes 100
  11.4 2.7 collective-permute-start.1
  15.7 12.1 %collective-permute-start.2 = (bf16[256,1024]{1,0:T(8,128)(2,1)S(1)}, bf16[256,1024]{1,0:T(8,128)(2,1)S(1)}, u32[]{:S(2)}, u32[]{:S(2)}) collective-permute-start(bf16[256,1024]{1,0:T(8,128)(2,1)S(1)} %get-tuple-element.110.refs_0_), channel_id=1, source_target_pairs={{0,4},{1,13},{2,6},{3,15},{4,8},{5,1},{6,10},{7,3},{8,12},{9,5},{1... | collective-permute-start | bytes 1572872 | tf_op jit(solution)/shard_map/ppermute | solution.py:71
  19.6 8.2 %collective-permute-start.4 = (bf16[256,512]{1,0:T(8,128)(2,1)S(1)}, bf16[256,512]{1,0:T(8,128)(2,1)S(1)}, u32[]{:S(2)}, u32[]{:S(2)}) collective-permute-start(bf16[256,512]{1,0:T(8,128)(2,1)S(1)} %get-tuple-element.113), channel_id=1, source_target_pairs={{0,66},{1,67},{2,64},{3,65},{4,70},{5,71},{6,68},{7,69},{8,74},{9,... | collective-permute-start | bytes 786440 | tf_op jit(solution)/shard_map/ppermute | solution.py:71
  28.7 325.8 %all-gather.5.cloned.1.call-start = ((), (), s32[]{:S(2)}) async-start(), calls=%async_computation.9 | async-start | bytes 35651584 | tf_op jit(solution)/shard_map/all_gather | solution.py:677
  32.1 12.2 %collective-permute-start = (bf16[128,8192]{1,0:T(8,128)(2,1)S(1)}, bf16[128,8192]{1,0:T(8,128)(2,1)S(1)}, u32[]{:S(2)}, u32[]{:S(2)}) collective-permute-start(bf16[128,8192]{1,0:T(8,128)(2,1)S(1)} %get-tuple-element.106), channel_id=1, source_target_pairs={{0,1},{1,0},{2,3},{3,2},{4,5},{5,4},{6,7},{7,6},{8,9},{9,8},{10,11... | collective-permute-start | bytes 6291464 | tf_op jit(solution)/shard_map/ppermute | solution.py:61
  32.2 8.6 %collective-permute-start.3 = (bf16[256,1024]{1,0:T(8,128)(2,1)S(1)}, bf16[256,1024]{1,0:T(8,128)(2,1)S(1)}, u32[]{:S(2)}, u32[]{:S(2)}) collective-permute-start(bf16[256,1024]{1,0:T(8,128)(2,1)S(1)} %collective-permute-done.2.refs_1_), channel_id=1, source_target_pairs={{0,4},{1,13},{2,6},{3,15},{4,8},{5,1},{6,10},{7,3},{8,12},{9,5},{1... | collective-permute-start | bytes 1572872 | tf_op jit(solution)/shard_map/ppermute | solution.py:71
  40.8 15.1 %collective-permute-start.6 = (bf16[256,1024]{1,0:T(8,128)(2,1)S(1)}, bf16[256,1024]{1,0:T(8,128)(2,1)S(1)}, u32[]{:S(2)}, u32[]{:S(2)}) collective-permute-start(bf16[256,1024]{1,0:T(8,128)(2,1)S(1)} %collective-permute-done.3.refs_2_), channel_id=1, source_target_pairs={{0,4},{1,13},{2,6},{3,15},{4,8},{5,1},{6,10},{7,3},{8,12},{9,5},{1... | collective-permute-start | bytes 1572872 | tf_op jit(solution)/shard_map/ppermute | solution.py:71
  48.1 27.0 %collective-permute-start.5 = (bf16[256,2048]{1,0:T(8,128)(2,1)S(1)}, bf16[256,2048]{1,0:T(8,128)(2,1)S(1)}, u32[]{:S(2)}, u32[]{:S(2)}) collective-permute-start(bf16[256,2048]{1,0:T(8,128)(2,1)S(1)} %get-tuple-element.114), channel_id=1, source_target_pairs={{0,66},{1,67},{2,64},{3,65},{4,70},{5,71},{6,68},{7,69},{8,74},{9,... | collective-permute-start | bytes 3145736 | tf_op jit(solution)/shard_map/ppermute | solution.py:71
  56.7 27.7 %collective-permute-start.7 = (bf16[512,1024]{1,0:T(8,128)(2,1)S(1)}, bf16[512,1024]{1,0:T(8,128)(2,1)S(1)}, u32[]{:S(2)}, u32[]{:S(2)}) collective-permute-start(bf16[512,1024]{1,0:T(8,128)(2,1)S(1)} %get-tuple-element.116.refs_1_), channel_id=1, source_target_pairs={{0,64},{1,67},{2,66},{3,65},{4,68},{5,71},{6,70},{7,69},{8,72},{9,... | collective-permute-start | bytes 3145736 | tf_op jit(solution)/shard_map/ppermute | solution.py:71
  60.3 35.3 %collective-permute-start.8 = (bf16[512,1024]{1,0:T(8,128)(2,1)S(1)}, bf16[512,1024]{1,0:T(8,128)(2,1)S(1)}, u32[]{:S(2)}, u32[]{:S(2)}) collective-permute-start(bf16[512,1024]{1,0:T(8,128)(2,1)S(1)} %get-tuple-element.117.refs_5_), channel_id=1, source_target_pairs={{0,64},{1,67},{2,66},{3,65},{4,68},{5,71},{6,70},{7,69},{8,72},{9,... | collective-permute-start | bytes 3145736 | tf_op jit(solution)/shard_map/ppermute | solution.py:71
  84.4 15.7 %copy-start.27 = (bf16[512,1024]{1,0:T(8,128)(2,1)}, bf16[512,1024]{1,0:T(8,128)(2,1)S(1)}, u32[]{:S(2)}) copy-start(bf16[512,1024]{1,0:T(8,128)(2,1)S(1)} %collective-permute-done.7.refs_2_) | copy-start | bytes 3145732
  98.2 16.4 %copy-start.79 = (s32[1,2]{1,0:T(1,128)S(1)}, s32[1,2]{1,0:T(1,128)}, u32[]{:S(2)}) copy-start(s32[1,2]{1,0:T(1,128)} %param.31) | copy-start | bytes 28
  98.2 17.4 %copy-start.8 = (bf16[1,144,2048]{2,1,0:T(8,128)(2,1)S(1)}, bf16[1,144,2048]{2,1,0:T(8,128)(2,1)}, u32[]{:S(2)}) copy-start(bf16[1,144,2048]{2,1,0:T(8,128)(2,1)} %param.16) | copy-start | bytes 1769476
  98.3 14.1 %collective-permute-start.9 = (bf16[256,2048]{1,0:T(8,128)(2,1)S(1)}, bf16[256,2048]{1,0:T(8,128)(2,1)}, u32[]{:S(2)}, u32[]{:S(2)}) collective-permute-start(bf16[256,2048]{1,0:T(8,128)(2,1)S(1)} %get-tuple-element.120.refs_0_), channel_id=1, source_target_pairs={{0,4},{1,13},{2,6},{3,15},{4,8},{5,1},{6,10},{7,3},{8,12},{9,5},{1... | collective-permute-start | bytes 3145736 | tf_op jit(solution)/shard_map/ppermute | solution.py:71
  100.1 16.8 %collective-permute-start.12 = (bf16[512,1024]{1,0:T(8,128)(2,1)S(1)}, bf16[512,1024]{1,0:T(8,128)(2,1)}, u32[]{:S(2)}, u32[]{:S(2)}) collective-permute-start(bf16[512,1024]{1,0:T(8,128)(2,1)S(1)} %collective-permute-done.7.refs_2_), channel_id=1, source_target_pairs={{0,64},{1,67},{2,66},{3,65},{4,68},{5,71},{6,70},{7,69},{8,72},{9,... | collective-permute-start | bytes 3145736 | tf_op jit(solution)/shard_map/ppermute | solution.py:71
  103.6 23.1 %collective-permute-start.14 = (bf16[512,1024]{1,0:T(8,128)(2,1)}, bf16[512,1024]{1,0:T(8,128)(2,1)}, u32[]{:S(2)}, u32[]{:S(2)}) collective-permute-start(bf16[512,1024]{1,0:T(8,128)(2,1)} %copy-done.73), channel_id=1, source_target_pairs={{0,64},{1,67},{2,66},{3,65},{4,68},{5,71},{6,70},{7,69},{8,72},{9,... | collective-permute-start | bytes 3145736 | tf_op jit(solution)/shard_map/ppermute | solution.py:71
  112.4 28.4 %collective-permute-start.10 = (bf16[256,2048]{1,0:T(8,128)(2,1)}, bf16[256,2048]{1,0:T(8,128)(2,1)}, u32[]{:S(2)}, u32[]{:S(2)}) collective-permute-start(bf16[256,2048]{1,0:T(8,128)(2,1)} %collective-permute-done.9.refs_1_), channel_id=1, source_target_pairs={{0,4},{1,13},{2,6},{3,15},{4,8},{5,1},{6,10},{7,3},{8,12},{9,5},{1... | collective-permute-start | bytes 3145736 | tf_op jit(solution)/shard_map/ppermute | solution.py:71
  114.7 1.7 collective-permute-start.18
  115.6 34.4 %collective-permute-start.17 = (bf16[144,2048]{1,0:T(8,128)(2,1)S(1)}, bf16[144,2048]{1,0:T(8,128)(2,1)}, u32[]{:S(2)}, u32[]{:S(2)}) collective-permute-start(bf16[144,2048]{1,0:T(8,128)(2,1)S(1)} %bitcast.71), channel_id=1, source_target_pairs={{0,1},{1,0},{2,3},{3,2},{4,5},{5,4},{6,7},{7,6},{8,9},{9,8},{10,11... | collective-permute-start | bytes 1769480 | tf_op jit(solution)/shard_map/ppermute | solution.py:61
  116.0 36.1 %copy-start.62 = (s32[3,4]{1,0:T(4,128)}, s32[3,4]{1,0:T(4,128)S(1)}, u32[]{:S(2)}) copy-start(s32[3,4]{1,0:T(4,128)S(1)} %pad_add_fusion.places) | copy-start | bytes 148
  116.8 35.2 %collective-permute-start.13 = (bf16[512,1024]{1,0:T(8,128)(2,1)}, bf16[512,1024]{1,0:T(8,128)(2,1)}, u32[]{:S(2)}, u32[]{:S(2)}) collective-permute-start(bf16[512,1024]{1,0:T(8,128)(2,1)} %collective-permute-done.12.refs_3_), channel_id=1, source_target_pairs={{0,64},{1,67},{2,66},{3,65},{4,68},{5,71},{6,70},{7,69},{8,72},{9,... | collective-permute-start | bytes 3145736 | tf_op jit(solution)/shard_map/ppermute | solution.py:71
  126.7 25.3 %collective-permute-start.15 = (bf16[512,1024]{1,0:T(8,128)(2,1)}, bf16[512,1024]{1,0:T(8,128)(2,1)}, u32[]{:S(2)}, u32[]{:S(2)}) collective-permute-start(bf16[512,1024]{1,0:T(8,128)(2,1)} %collective-permute-done.14.refs_7_), channel_id=1, source_target_pairs={{0,64},{1,67},{2,66},{3,65},{4,68},{5,71},{6,70},{7,69},{8,72},{9,... | collective-permute-start | bytes 3145736 | tf_op jit(solution)/shard_map/ppermute | solution.py:71
  140.8 30.9 %collective-permute-start.11 = (bf16[256,2048]{1,0:T(8,128)(2,1)}, bf16[256,2048]{1,0:T(8,128)(2,1)}, u32[]{:S(2)}, u32[]{:S(2)}) collective-permute-start(bf16[256,2048]{1,0:T(8,128)(2,1)} %collective-permute-done.10.refs_2_), channel_id=1, source_target_pairs={{0,4},{1,13},{2,6},{3,15},{4,8},{5,1},{6,10},{7,3},{8,12},{9,5},{1... | collective-permute-start | bytes 3145736 | tf_op jit(solution)/shard_map/ppermute | solution.py:71
  152.0 27.5 %copy-start.51 = (bf16[288,96]{1,0:T(8,128)(2,1)}, bf16[288,96]{1,0:T(8,128)(2,1)S(1)}, u32[]{:S(2)}) copy-start(bf16[288,96]{1,0:T(8,128)(2,1)S(1)} %fusion.1.low.refs_1_) | copy-start | bytes 165892
  176.0 71.4 %collective-permute-start.20 = (bf16[512,2048]{1,0:T(8,128)(2,1)}, bf16[512,2048]{1,0:T(8,128)(2,1)}, u32[]{:S(2)}, u32[]{:S(2)}) collective-permute-start(bf16[512,2048]{1,0:T(8,128)(2,1)} %get-tuple-element.137.refs_5_), channel_id=1, source_target_pairs={{0,64},{1,67},{2,66},{3,65},{4,68},{5,71},{6,70},{7,69},{8,72},{9,... | collective-permute-start | bytes 6291464 | tf_op jit(solution)/shard_map/ppermute | solution.py:71
  179.4 67.9 %collective-permute-start.16 = (bf16[512,2048]{1,0:T(8,128)(2,1)}, bf16[512,2048]{1,0:T(8,128)(2,1)}, u32[]{:S(2)}, u32[]{:S(2)}) collective-permute-start(bf16[512,2048]{1,0:T(8,128)(2,1)} %get-tuple-element.131.refs_1_), channel_id=1, source_target_pairs={{0,64},{1,67},{2,66},{3,65},{4,68},{5,71},{6,70},{7,69},{8,72},{9,... | collective-permute-start | bytes 6291464 | tf_op jit(solution)/shard_map/ppermute | solution.py:71
  194.9 3.0 collective-permute-start.19
  247.3 54.4 %copy-start.10 = (bf16[8,288,384]{2,1,0:T(8,128)(2,1)}, bf16[8,288,384]{2,1,0:T(8,128)(2,1)S(1)}, u32[]{:S(2)}) copy-start(bf16[8,288,384]{2,1,0:T(8,128)(2,1)S(1)} %all_to_all.45) | copy-start | bytes 5308420
  247.4 54.4 %copy-start.53 = (bf16[32,1024]{1,0:T(8,128)(2,1)S(1)}, bf16[32,1024]{1,0:T(8,128)(2,1)}, u32[]{:S(2)}) copy-start(bf16[32,1024]{1,0:T(8,128)(2,1)} %get-tuple-element.143.down) | copy-start | bytes 196612
  247.4 54.4 %copy-start.57 = (s32[8]{0:T(128)S(1)}, s32[8]{0:T(128)}, u32[]{:S(2)}) copy-start(s32[8]{0:T(128)} %copy-done.56) | copy-start | bytes 100
  247.4 59.3 %collective-permute-start.23 = (bf16[512,2048]{1,0:T(8,128)(2,1)}, bf16[512,2048]{1,0:T(8,128)(2,1)S(1)}, u32[]{:S(2)}, u32[]{:S(2)}) collective-permute-start(bf16[512,2048]{1,0:T(8,128)(2,1)} %collective-permute-done.20.refs_6_), channel_id=1, source_target_pairs={{0,64},{1,67},{2,66},{3,65},{4,68},{5,71},{6,70},{7,69},{8,72},{9,... | collective-permute-start | bytes 6291464 | tf_op jit(solution)/shard_map/ppermute | solution.py:71
  250.6 56.1 %collective-permute-start.21 = (bf16[512,2048]{1,0:T(8,128)(2,1)}, bf16[512,2048]{1,0:T(8,128)(2,1)S(1)}, u32[]{:S(2)}, u32[]{:S(2)}) collective-permute-start(bf16[512,2048]{1,0:T(8,128)(2,1)} %collective-permute-done.16.refs_2_), channel_id=1, source_target_pairs={{0,64},{1,67},{2,66},{3,65},{4,68},{5,71},{6,70},{7,69},{8,72},{9,... | collective-permute-start | bytes 6291464 | tf_op jit(solution)/shard_map/ppermute | solution.py:71
  258.5 43.2 %copy-start.64 = (f32[2,1152,128]{2,1,0:T(8,128)}, f32[2,1152,128]{2,1,0:T(8,128)S(1)}, u32[]{:S(2)}) copy-start(f32[2,1152,128]{2,1,0:T(8,128)S(1)} %get-tuple-element.181.exact) | copy-start | bytes 3538948
  306.7 11.4 %copy-start.69 = (bf16[512,2048]{1,0:T(8,128)(2,1)}, bf16[512,2048]{1,0:T(8,128)(2,1)S(1)}, u32[]{:S(2)}) copy-start(bf16[512,2048]{1,0:T(8,128)(2,1)S(1)} %collective-permute-done.23.refs_7_) | copy-start | bytes 6291460
  306.7 25.4 %copy-start.70 = (bf16[512,2048]{1,0:T(8,128)(2,1)}, bf16[512,2048]{1,0:T(8,128)(2,1)S(1)}, u32[]{:S(2)}) copy-start(bf16[512,2048]{1,0:T(8,128)(2,1)S(1)} %collective-permute-done.21.refs_3_) | copy-start | bytes 6291460
  306.7 25.4 %collective-permute-start.22 = (bf16[512,2048]{1,0:T(8,128)(2,1)S(1)}, bf16[512,2048]{1,0:T(8,128)(2,1)S(1)}, u32[]{:S(2)}, u32[]{:S(2)}) collective-permute-start(bf16[512,2048]{1,0:T(8,128)(2,1)S(1)} %collective-permute-done.21.refs_3_), channel_id=1, source_target_pairs={{0,64},{1,67},{2,66},{3,65},{4,68},{5,71},{6,70},{7,69},{8,72},{9,... | collective-permute-start | bytes 6291464 | tf_op jit(solution)/shard_map/ppermute | solution.py:71
  307.9 46.6 %collective-permute-start.24 = (bf16[512,2048]{1,0:T(8,128)(2,1)S(1)}, bf16[512,2048]{1,0:T(8,128)(2,1)}, u32[]{:S(2)}, u32[]{:S(2)}) collective-permute-start(bf16[512,2048]{1,0:T(8,128)(2,1)S(1)} %collective-permute-done.23.refs_7_), channel_id=1, source_target_pairs={{0,64},{1,67},{2,66},{3,65},{4,68},{5,71},{6,70},{7,69},{8,72},{9,... | collective-permute-start | bytes 6291464 | tf_op jit(solution)/shard_map/ppermute | solution.py:71
  310.2 2.5 collective-permute-start.25
  315.7 2.4 collective-permute-start.26
  318.1 13.9 %copy-start.78 = (bf16[144,2176]{1,0:T(8,128)(2,1)}, bf16[144,2176]{1,0:T(8,128)(2,1)S(1)}, u32[]{:S(2)}) copy-start(bf16[144,2176]{1,0:T(8,128)(2,1)S(1)} %collective-permute-done.26.refs_10_) | copy-start | bytes 1880068
  354.5 32.7 %copy-start.7 = (bf16[1,144,2048]{2,1,0:T(8,128)(2,1)S(1)}, bf16[1,144,2048]{2,1,0:T(8,128)(2,1)}, u32[]{:S(2)}) copy-start(bf16[1,144,2048]{2,1,0:T(8,128)(2,1)} %param.17) | copy-start | bytes 1769476
  354.5 32.7 %copy-start.31 = (f32[4,2048]{1,0:T(4,128)S(1)}, f32[4,2048]{1,0:T(4,128)}, u32[]{:S(2)}) copy-start(f32[4,2048]{1,0:T(4,128)} %gains.9) | copy-start | bytes 98308
  354.5 32.7 %copy-start.44 = (bf16[32,2048]{1,0:T(8,128)(2,1)S(1)}, bf16[32,2048]{1,0:T(8,128)(2,1)}, u32[]{:S(2)}) copy-start(bf16[32,2048]{1,0:T(8,128)(2,1)} %get-tuple-element.162.up.refs_11_) | copy-start | bytes 393220
  381.1 6.1 collective-permute-start.27
  392.8 2.1 collective-permute-start.28
  395.7 29.4 %copy-start.60 = (bf16[288,64]{1,0:T(8,128)(2,1)S(1)}, bf16[288,64]{1,0:T(8,128)(2,1)}, u32[]{:S(2)}) copy-start(bf16[288,64]{1,0:T(8,128)(2,1)} %get-tuple-element.170.refs_0_) | copy-start | bytes 110596
  424.6 9.2 %collective-permute-start.29 = (bf16[144,2176]{1,0:T(8,128)(2,1)}, bf16[144,2176]{1,0:T(8,128)(2,1)S(1)}, u32[]{:S(2)}, u32[]{:S(2)}) collective-permute-start(bf16[144,2176]{1,0:T(8,128)(2,1)} %get-tuple-element.167), channel_id=1, source_target_pairs={{0,1},{1,0},{2,3},{3,2},{4,5},{5,4},{6,7},{7,6},{8,9},{9,8},{10,11... | collective-permute-start | bytes 1880072 | tf_op jit(solution)/shard_map/ppermute | solution.py:61
  436.9 16.7 %all-to-all-start.3 = ((bf16[8,32,1664]{2,1,0:T(8,128)(2,1)}), bf16[8,32,1664]{2,1,0:T(8,128)(2,1)}, u32[]{:S(2)}, u32[]{:S(2)}) async-start(bf16[8,32,1664]{2,1,0:T(8,128)(2,1)} %early_gradients.1), calls=%async_computation.3 | async-start | bytes 1703936 | tf_op jit(solution)/shard_map/all_to_all | solution.py:1143
  441.3 2.4 collective-permute-start.30
  453.6 17.3 %all-to-all-start.2 = ((bf16[8,416,128]{2,1,0:T(8,128)(2,1)}), bf16[8,416,128]{2,1,0:T(8,128)(2,1)}, u32[]{:S(2)}, u32[]{:S(2)}) async-start(bf16[8,416,128]{2,1,0:T(8,128)(2,1)} %copy-done.29), calls=%async_computation.2 | async-start | bytes 1703936 | tf_op jit(solution)/shard_map/all_to_all | solution.py:1146
  461.3 20.2 %copy-start.11 = (bf16[8,288,384]{2,1,0:T(8,128)(2,1)S(1)}, bf16[8,288,384]{2,1,0:T(8,128)(2,1)}, u32[]{:S(2)}) copy-start(bf16[8,288,384]{2,1,0:T(8,128)(2,1)} %copy-done.10) | copy-start | bytes 5308420
  477.0 22.4 %all-to-all-start.4 = ((bf16[8,32,2304]{2,1,0:T(8,128)(2,1)}), bf16[8,32,2304]{2,1,0:T(8,128)(2,1)}, u32[]{:S(2)}, u32[]{:S(2)}) async-start(bf16[8,32,2304]{2,1,0:T(8,128)(2,1)} %broadcast_in_dim.44), calls=%async_computation.4 | async-start | bytes 2359296 | tf_op jit(solution)/shard_map/all_to_all | solution.py:1087
  499.4 26.1 %all-to-all-start.5 = ((bf16[8,2,144,384]{3,2,1,0:T(8,128)(2,1)}), bf16[8,2,144,384]{3,2,1,0:T(8,128)(2,1)S(1)}, u32[]{:S(2)}, u32[]{:S(2)}) async-start(bf16[8,2,144,384]{3,2,1,0:T(8,128)(2,1)} %copy-done.12), calls=%async_computation.5 | async-start | bytes 3538944 | tf_op jit(solution)/shard_map/all_to_all | solution.py:1155
  504.4 93.7 %all-gather.9.cloned.1.call-start = ((), (), s32[]{:S(2)}) async-start(), calls=%async_computation.11 | async-start | bytes 5013504 | tf_op jit(solution)/shard_map/all_gather | solution.py:1164
  530.7 2.2 collective-permute-start.31
  537.5 12.7 %copy-start.22 = (f32[144,2048]{1,0:T(8,128)S(1)}, f32[144,2048]{1,0:T(8,128)}, u32[]{:S(2)}) copy-start(f32[144,2048]{1,0:T(8,128)} %copy-done.21) | copy-start | bytes 3538948
  537.5 12.7 %copy-start.50 = (bf16[96,2048]{1,0:T(8,128)(2,1)S(1)}, bf16[96,2048]{1,0:T(8,128)(2,1)}, u32[]{:S(2)}) copy-start(bf16[96,2048]{1,0:T(8,128)(2,1)} %get-tuple-element.132.down) | copy-start | bytes 1179652
  548.1 2.1 collective-permute-start.32
  551.8 1.2 collective-permute-start.33
  598.0 7.9 %collective-permute-start.34 = (bf16[8,8,16,2176]{3,2,1,0:T(8,128)(2,1)}, bf16[8,8,16,2176]{3,2,1,0:T(8,128)(2,1)}, u32[]{:S(2)}, u32[]{:S(2)}) collective-permute-start(bf16[8,8,16,2176]{3,2,1,0:T(8,128)(2,1)} %bitcast.66), channel_id=1, source_target_pairs={{0,1},{1,0},{2,3},{3,2},{4,5},{5,4},{6,7},{7,6},{8,9},{9,8},{10,11... | collective-permute-start | bytes 13369352 | tf_op jit(solution)/shard_map/ppermute | solution.py:61
  600.1 27.7 %all-to-all-start.8 = ((bf16[8,128,768]{2,1,0:T(8,128)(2,1)}), bf16[8,128,768]{2,1,0:T(8,128)(2,1)S(1)}, u32[]{:S(2)}, u32[]{:S(2)}) async-start(bf16[8,128,768]{2,1,0:T(8,128)(2,1)} %broadcast_in_dim.48), calls=%async_computation.8 | async-start | bytes 3145728 | tf_op jit(solution)/shard_map/all_to_all | solution.py:1087
  627.8 4.0 collective-permute-start.35
  (60 other events, 169.8 us)
Sparse Core Ops, SparseCore 0:
  28.8 72.1 all-gather.6
  103.8 237.0 all-gather.4
  530.9 58.9 all-gather.8

commit v4 on v3

--- a/solution.py
+++ b/solution.py
@@ -1152,16 +1152,18 @@
     d_out_heads, own = lax.optimization_barrier((d_out_heads, own))
     groups = spread_over(own, shard).reshape(16, RANK, EARLY + MIDDLE + 128)
     d_heads = attend_back(bounds, heads, d_out_heads, exact, log_total)
+    d_heads, groups = lax.optimization_barrier((d_heads, groups))
     d_heads = lax.all_to_all(d_heads, CTX, 0, 0, tiled=True).reshape(8, 2 * ROWS, 3 * HD)
-    w_q, w_k, d_v, sums = unpack_heads(me, d_heads, qkv, gains, cosine, sine)
 
     def by_slot(groups):
         flat = groups.reshape(16, -1)
         return lax.dot_general(picker, flat, **TN).astype(BF).reshape(8 * RANK, -1)
 
     picker = groups[:, 0, EARLY + MIDDLE : EARLY + MIDDLE + 8]
-    early, w_q = lax.optimization_barrier((by_slot(groups[:, :, : EARLY + MIDDLE]), w_q))
-    early = lax.all_gather(early, CTX)
+    slot_sums = by_slot(groups[:, :, : EARLY + MIDDLE])
+    d_heads = after(d_heads, slot_sums)
+    early = lax.all_gather(slot_sums, CTX)
+    w_q, w_k, d_v, sums = unpack_heads(me, d_heads, qkv, gains, cosine, sine)
     d_qkv, keep, give = project_qkv_back(me, (w_q, w_k), d_v, qkv, squares, (sums, swap(sums)), w_qkv, qkv_up)
     grad_tokens, low = combine_tokens(me, keep, swap(give), d_hidden, qkv_down)
     low = both(low, swap(low)).reshape(2 * ROWS, 128)

time: 658 us -> 662 us (level)
  blocking collectives: 131 us -> 149 us
  waiting for transfers between devices: 170 us -> 157 us
    all_to_all x0 -> x1, blocking collectives: none -> 39.2 us  [on_device(): lax.all_to_all(d_heads, CTX, 0, 0, tiled=True).reshape(8, 2 * ROWS, 3 * HD)]
    all_to_all x1, blocking collectives: 27.5 us -> 10.8 us  [spread_over(): lax.all_to_all(jnp.broadcast_to(value[None], (8,) + value.shape), axes, 0...]
    all_to_all x1 -> x0, waiting for transfers between devices: 13.3 us -> none  [on_device(): lax.all_to_all(d_heads, CTX, 0, 0, tiled=True).reshape(8, 2 * ROWS, 3 * HD)]
    ppermute x16, starting transfers between devices: 13.4 us -> 21.8 us  [swap(): return lax.ppermute(value, ALL, STEPS['core'])]
  transfers between devices with their start and end apart: 44 -> 43, of which waited for: 28 -> 27; matrix products, arithmetic and copies ran while one was open for 3% -> 2% of each run, Pallas kernels for 14% -> 14%
where the time goes in v4:
time: 662 us; the launch traced here: 651 us
  Pallas kernels  160 us (24%)
  waiting for transfers between devices  157 us (24%)
  blocking collectives  149 us (23%)
  starting transfers between devices  87 us (13%)
  local copies, waits for them, and re-layouts  69.6 us (11%)
  between operations  15.2 us (2%)
  other arithmetic  11.6 us (2%)
    ppermute x20, waiting for transfers between devices, send(): self.last = lax.ppermute(value, ALL, STEPS[how])  116 us
    unnamed x166, local copies, waits for them, and re-layouts  61.1 us
    pallas_call x2, Pallas kernels, call(): pl.pallas_call(body, out_shape=outs, in_specs=[_smem()] + [anywhere] * 9...  55.6 us
    ppermute x20, starting transfers between devices, send(): self.last = lax.ppermute(value, ALL, STEPS[how])  45.2 us
    all_to_all x1, blocking collectives, on_device(): lax.all_to_all(packed, CTX, 0, 0, tiled=True).reshape(8, 2, ROWS, 3 * HD)  44.8 us
    all_to_all x1, blocking collectives, on_device(): lax.all_to_all(out_heads, CTX, 0, 0, tiled=True).reshape(8, 2 * ROWS, HD)  43.2 us
    all_to_all x1, blocking collectives, on_device(): lax.all_to_all(d_heads, CTX, 0, 0, tiled=True).reshape(8, 2 * ROWS, 3 * HD)  39.2 us
    pallas_call x14, Pallas kernels, _plain(): pl.pallas_call(body, out_shape=outs, in_specs=[_smem()] * len(scalars) +...  34.4 us
  transfers between devices with their start and end apart: 43, of which 27 were waited for; matrix products, arithmetic and copies ran while one was open for 2% of the time, Pallas kernels for 14%

profile of v4, /device:TPU:7, one launch (start us, length us, event | category | flops | bytes accessed | tf_op | source)
XLA Modules:
  0.0 651.3 jit_solution(10779594773008321127)
XLA Ops:
  15.7 3.8 collective-permute-start.2
  19.6 2.7 collective-permute-start.4
  22.3 5.5 collective-permute-done.4
  28.8 3.4 split_g.1
  34.1 6.7 %collective-permute-done.3.refs_2_ = bf16[256,1024]{1,0:T(8,128)(2,1)S(1)} collective-permute-done((bf16[256,1024]{1,0:T(8,128)(2,1)S(1)}, bf16[256,1024]{1,0:T(8,128)(2,1)S(1)}, u32[]{:S(2)}, u32[]{:S(2)}) %collective-permute-start.3) | collective-permute-done | bytes 524320 | tf_op jit(solution)/shard_map/ppermute | solution.py:71
  40.8 3.5 collective-permute-start.6
  45.6 2.4 parts_m.1
  48.1 3.2 collective-permute-start.5
  51.2 4.7 collective-permute-done.6.refs_3_
  56.7 2.7 collective-permute-start.7
  61.7 13.4 %collective-permute-done.5 = bf16[256,2048]{1,0:T(8,128)(2,1)S(1)} collective-permute-done((bf16[256,2048]{1,0:T(8,128)(2,1)S(1)}, bf16[256,2048]{1,0:T(8,128)(2,1)S(1)}, u32[]{:S(2)}, u32[]{:S(2)}) %collective-permute-start.5) | collective-permute-done | bytes 1048608 | tf_op jit(solution)/shard_map/ppermute | solution.py:71
  75.1 9.3 %collective-permute-done.7.refs_2_ = bf16[512,1024]{1,0:T(8,128)(2,1)S(1)} collective-permute-done((bf16[512,1024]{1,0:T(8,128)(2,1)S(1)}, bf16[512,1024]{1,0:T(8,128)(2,1)S(1)}, u32[]{:S(2)}, u32[]{:S(2)}) %collective-permute-start.7) | collective-permute-done | bytes 1048608 | tf_op jit(solution)/shard_map/ppermute | solution.py:71
  84.4 11.2 %collective-permute-done.8.refs_6_ = bf16[512,1024]{1,0:T(8,128)(2,1)S(1)} collective-permute-done((bf16[512,1024]{1,0:T(8,128)(2,1)S(1)}, bf16[512,1024]{1,0:T(8,128)(2,1)S(1)}, u32[]{:S(2)}, u32[]{:S(2)}) %collective-permute-start.8) | collective-permute-done | bytes 1048608 | tf_op jit(solution)/shard_map/ppermute | solution.py:71
  100.1 3.6 collective-permute-start.12
  103.7 8.7 %collective-permute-done.9.refs_1_ = bf16[256,2048]{1,0:T(8,128)(2,1)} collective-permute-done((bf16[256,2048]{1,0:T(8,128)(2,1)S(1)}, bf16[256,2048]{1,0:T(8,128)(2,1)}, u32[]{:S(2)}, u32[]{:S(2)}) %collective-permute-start.9) | collective-permute-done | bytes 1048608 | tf_op jit(solution)/shard_map/ppermute | solution.py:71
  112.4 2.3 collective-permute-start.10
  116.8 2.7 collective-permute-start.13
  119.5 7.2 %collective-permute-done.14.refs_7_ = bf16[512,1024]{1,0:T(8,128)(2,1)} collective-permute-done((bf16[512,1024]{1,0:T(8,128)(2,1)}, bf16[512,1024]{1,0:T(8,128)(2,1)}, u32[]{:S(2)}, u32[]{:S(2)}) %collective-permute-start.14) | collective-permute-done | bytes 1048608 | tf_op jit(solution)/shard_map/ppermute | solution.py:71
  126.7 3.4 collective-permute-start.15
  130.1 10.7 %collective-permute-done.10.refs_2_ = bf16[256,2048]{1,0:T(8,128)(2,1)} collective-permute-done((bf16[256,2048]{1,0:T(8,128)(2,1)}, bf16[256,2048]{1,0:T(8,128)(2,1)}, u32[]{:S(2)}, u32[]{:S(2)}) %collective-permute-start.10) | collective-permute-done | bytes 1048608 | tf_op jit(solution)/shard_map/ppermute | solution.py:71
  140.8 3.4 collective-permute-start.11
  144.8 3.8 choose_adapters.1
  155.8 12.1 %assemble.1 = (bf16[2048,3072]{1,0:T(8,128)(2,1)}, bf16[1024,2048]{1,0:T(8,128)(2,1)}) custom-call(s32[3,4]{1,0:T(4,128)S(1)} %pad_add_fusion.places, bf16[4,4,2,256,512]{4,3,2,1,0:T(8,128)(2,1)} %bitcast.81, bf16[512,1024]{1,0:T(8,128)(2,1)S(1)} %copy-done.25, bf16[512,1024]{1,0:T(8,128)(2,1)S(1)} %copy-done.29, ...), custom_call_target="tpu_custom_call" | custom-call | bytes 67108864 | tf_op jit(solution)/shard_map/assemble/pallas_call | solution.py:255
  167.9 3.8 collective-permute-done.11.refs_3_
  171.7 4.3 spread_g.1
  176.0 3.4 collective-permute-start.20
  179.5 7.1 %copy-done.1 = bf16[2048,3072]{1,0:T(8,128)(2,1)S(1)} copy-done((bf16[2048,3072]{1,0:T(8,128)(2,1)S(1)}, bf16[2048,3072]{1,0:T(8,128)(2,1)}, u32[]{:S(2)}) %copy-start.1) | copy-done | bytes 12582936
  186.5 6.5 %project_qkv.1 = (f32[288,3072]{1,0:T(8,128)S(1)}, f32[288,128]{1,0:T(8,128)S(1)}) custom-call(bf16[288,2048]{1,0:T(8,128)(2,1)S(1)} %bitcast.62, bf16[2048,3072]{1,0:T(8,128)(2,1)S(1)} %copy-done.1, bf16[288,96]{1,0:T(8,128)(2,1)S(1)} %fusion.1.low.refs_1_, bf16[96,3072]{1,0:T(8,128)(2,1)S(1)} %copy-done.6), custom_call_target="tpu_custom_call" | custom-call | flops 3623878656 | bytes 18000000 | tf_op jit(solution)/shard_map/project_qkv/pallas_call | solution.py:489
  198.6 4.0 pack_heads.1
  202.6 44.8 %all_to_all.45 = bf16[8,288,384]{2,1,0:T(8,128)(2,1)S(1)} all-to-all(bf16[8,288,384]{2,1,0:T(8,128)(2,1)} %pack_heads.1), channel_id=1, replica_groups=mesh['yl'=2,'x'=4,'z'=4,'yh'=2,'c'=2] {'yl','x'}, dimensions={0} | all-to-all | bytes 3538944 | tf_op jit(solution)/shard_map/all_to_all | solution.py:1113
  247.4 3.2 collective-permute-start.23
  250.9 6.6 %attend.1 = (bf16[8,2,144,128]{3,2,1,0:T(8,128)(2,1)S(1)}, f32[2,1152,128]{2,1,0:T(8,128)S(1)}, f32[2,1152,1]{2,1,0:T(8,128)S(1)}) custom-call(s32[2]{0:T(128)S(1)} %get-tuple-element.204.bounds, bf16[8,2,144,384]{3,2,1,0:T(8,128)(2,1)S(1)} %bitcast.72), custom_call_target="tpu_custom_call" | custom-call | flops 900000000 | bytes 5000000 | tf_op jit(solution)/shard_map/attend/pallas_call | solution.py:800
  258.5 43.2 %all_to_all.46 = bf16[8,2,144,128]{3,2,1,0:T(8,128)(2,1)S(1)} all-to-all(bf16[8,2,144,128]{3,2,1,0:T(8,128)(2,1)S(1)} %get-tuple-element.141), channel_id=1, replica_groups=mesh['yl'=2,'x'=4,'z'=4,'yh'=2,'c'=2] {'yl','x'}, dimensions={0} | all-to-all | bytes 1179648 | tf_op jit(solution)/shard_map/all_to_all | solution.py:1117
  301.8 4.1 project_out.1
  307.9 2.2 collective-permute-start.24
  318.1 13.9 %collective-permute-done.22.refs_4_ = bf16[512,2048]{1,0:T(8,128)(2,1)S(1)} collective-permute-done((bf16[512,2048]{1,0:T(8,128)(2,1)S(1)}, bf16[512,2048]{1,0:T(8,128)(2,1)S(1)}, u32[]{:S(2)}, u32[]{:S(2)}) %collective-permute-start.22) | collective-permute-done | bytes 2097184 | tf_op jit(solution)/shard_map/ppermute | solution.py:71
  333.4 21.1 %collective-permute-done.24.refs_8_ = bf16[512,2048]{1,0:T(8,128)(2,1)} collective-permute-done((bf16[512,2048]{1,0:T(8,128)(2,1)S(1)}, bf16[512,2048]{1,0:T(8,128)(2,1)}, u32[]{:S(2)}, u32[]{:S(2)}) %collective-permute-start.24) | collective-permute-done | bytes 2097184 | tf_op jit(solution)/shard_map/ppermute | solution.py:71
  354.5 26.6 %feed_forward.1 = (bf16[288,8192]{1,0:T(8,128)(2,1)}, bf16[288,4096]{1,0:T(8,128)(2,1)}, bf16[288,2176]{1,0:T(8,128)(2,1)}, bf16[288,64]{1,0:T(8,128)(2,1)}, f32...) custom-call(s32[3,4]{1,0:T(4,128)} %copy-done.63, bf16[4,4,2,256,2048]{4,3,2,1,0:T(8,128)(2,1)} %bitcast.79, ...), custom_call_target="tpu_custom_call" | custom-call | flops 14495514624 | bytes 53157888 | tf_op jit(solution)/shard_map/feed_forward/pallas_call | solution.py:358
  381.2 4.2 collective-permute-start.27
  389.8 2.1 combine_output.1
  395.7 29.0 %feed_forward_back.1 = (bf16[288,8192]{1,0:T(8,128)(2,1)}, bf16[288,2176]{1,0:T(8,128)(2,1)}, bf16[288,32]{1,0:T(8,128)(2,1)}, f32[144,2176]{1,0:T(8,128)}, bf16[144,2176]{1,0:T(8,128)(2,1)}) custom-call(s32[3,4]{1,0:T(4,128)} %copy-done.63, bf16[4,4,2,256,2048]{4,3,2,1,0:T(8,128)(2,1)} %bitcast.80, bf16[512,2048]{1,0:T(8,128)(2,1)} %get-tuple-element.131.refs_1_, ...), custom_call_target="tpu_custom_call" | custom-call | flops 14495514624 | bytes 57745408 | tf_op jit(solution)/shard_map/feed_forward_back/pallas_call | solution.py:358
  429.0 4.9 early_gradients.1
  437.0 4.3 all-to-all-start.3
  447.5 5.2 project_out_back.1
  453.6 5.5 all-to-all-start.2
  462.9 8.0 %all-to-all-done.2.grad = bf16[8,416,128]{2,1,0:T(8,128)(2,1)} async-done(((bf16[8,416,128]{2,1,0:T(8,128)(2,1)}), bf16[8,416,128]{2,1,0:T(8,128)(2,1)}, u32[]{:S(2)}, u32[]{:S(2)}) %all-to-all-start.2) | async-done | bytes 852000 | tf_op jit(solution)/shard_map/all_to_all | solution.py:1146
  477.0 4.2 all-to-all-start.4
  484.0 7.6 %attend_back.1 = bf16[8,2,144,384]{3,2,1,0:T(8,128)(2,1)S(1)} custom-call(s32[2]{0:T(128)S(1)} %get-tuple-element.204.bounds, bf16[8,2,144,384]{3,2,1,0:T(8,128)(2,1)S(1)} %bitcast.73, bf16[8,416,128]{2,1,0:T(8,128)(2,1)} %all-to-all-done.2.grad, f32[2,1152,128]{2,1,0:T(8,128)S(1)} %copy-done.66, f32[2,1152,1]{2,1,0:T(8,128)S(1)} %copy-done.68), custom_call_target="tpu_custom_call" | custom-call | flops 2300000000 | bytes 8000000 | tf_op jit(solution)/shard_map/attend_back/pallas_call | solution.py:848
  492.9 6.3 all-to-all-done.4
  504.8 39.2 %all_to_all.47 = bf16[8,2,144,384]{3,2,1,0:T(8,128)(2,1)} all-to-all(bf16[8,2,144,384]{3,2,1,0:T(8,128)(2,1)S(1)} %copy-done.13), channel_id=1, replica_groups=mesh['yl'=2,'x'=4,'z'=4,'yh'=2,'c'=2] {'yl','x'}, dimensions={0} | all-to-all | bytes 3538944 | tf_op jit(solution)/shard_map/all_to_all | solution.py:1156
  544.1 4.1 unpack_heads.1
  548.1 7.0 %collective-permute-start.31 = (f32[288,128]{1,0:T(8,128)}, f32[288,128]{1,0:T(8,128)S(1)}, u32[]{:S(2)}, u32[]{:S(2)}) collective-permute-start(f32[288,128]{1,0:T(8,128)} %get-tuple-element.187.su), channel_id=1, source_target_pairs={{0,1},{1,0},{2,3},{3,2},{4,5},{5,4},{6,7},{7,6},{8,9},{9,8},{10,11... | collective-permute-start | bytes 442376 | tf_op jit(solution)/shard_map/ppermute | solution.py:61
  560.9 10.7 %project_qkv_back.1 = (bf16[288,3072]{1,0:T(8,128)(2,1)}, f32[144,2176]{1,0:T(8,128)S(1)}, bf16[144,2176]{1,0:T(8,128)(2,1)S(1)}) custom-call(s32[8]{0:T(128)S(1)} %copy-done.59, f32[288,1024]{1,0:T(8,128)S(1)} %copy-done.18, f32[288,1024]{1,0:T(8,128)S(1)} %copy-done.19, bf16[288,1024]{1,0:T(8,128)(2,1)S(1)} %copy-done.36, f32[288,3072]{1,0:T(8,128)} %copy-done, ...), custom_call_target="tpu_custom_call" | custom-call | flops 3623878656 | bytes 22000000 | tf_op jit(solution)/shard_map/project_qkv_back/pallas_call | solution.py:640
  578.2 10.6 %all_to_all.48 = bf16[8,32,768]{2,1,0:T(8,128)(2,1)S(1)} all-to-all(bf16[8,32,768]{2,1,0:T(8,128)(2,1)S(1)} %late_gradients.1), channel_id=1, replica_groups=mesh['yl'=2,'x'=4,'z'=4,'yh'=2,'c'=2] {'yl','x'}, dimensions={0} | all-to-all | bytes 786432 | tf_op jit(solution)/shard_map/all_to_all | solution.py:1180
  588.9 10.8 %all_to_all.49 = bf16[8,32,768]{2,1,0:T(8,128)(2,1)S(1)} all-to-all(bf16[8,32,768]{2,1,0:T(8,128)(2,1)S(1)} %broadcast_in_dim.46), channel_id=1, replica_groups=mesh['yl'=2,'x'=4,'z'=4,'yh'=2,'c'=2] {'z','yh'}, dimensions={0} | all-to-all | bytes 786432 | tf_op jit(solution)/shard_map/all_to_all | solution.py:1087
  599.8 2.8 collective-permute-start.34
  604.3 5.7 all-to-all-start.8
  610.1 2.3 copy-done.5
  612.3 8.9 %early_outputs.1 = (f32[8,2,16,8192]{3,2,1,0:T(8,128)}, f32[8,16,8192]{2,1,0:T(8,128)}, f32[8,5,16,2048]{3,2,1,0:T(8,128)S(1)}) custom-call(s32[8]{0:T(128)S(1)} %copy-done.59, bf16[8,8,16,2176]{3,2,1,0:T(8,128)(2,1)S(1)} %bitcast.66, bf16[8,8,16,2176]{3,2,1,0:T(8,128)(2,1)} %collective-permute-done.34.refs_1_), custom_call_target="tpu_custom_call" | custom-call | bytes 8912896 | tf_op jit(solution)/shard_map/early_outputs/pallas_call | solution.py:970
  621.3 2.4 copy-done.2
  623.6 8.5 %all-to-all-done.8 = bf16[8,128,768]{2,1,0:T(8,128)(2,1)S(1)} async-done(((bf16[8,128,768]{2,1,0:T(8,128)(2,1)}), bf16[8,128,768]{2,1,0:T(8,128)(2,1)S(1)}, u32[]{:S(2)}, u32[]{:S(2)}) %all-to-all-start.8) | async-done | bytes 1572896 | tf_op jit(solution)/shard_map/all_to_all | solution.py:1087
  633.0 3.0 collective-permute-done.35
  636.0 2.5 copy-done.3
  638.5 6.1 late_outputs.1
  (269 shorter events, 104.8 us)
Async XLA Ops:
  7.2 144.8 %all-gather.6.cloned.1.call-start = ((), (), s32[]{:S(2)}) async-start(), calls=%async_computation.10 | async-start | bytes 8912896 | tf_op jit(solution)/shard_map/all_gather | solution.py:677
  10.4 161.2 %copy-start.57 = (s32[8]{0:T(128)}, s32[8]{0:T(128)S(1)}, u32[]{:S(2)}) copy-start(s32[8]{0:T(128)S(1)} %stack.141.core.me) | copy-start | bytes 100
  11.4 2.7 collective-permute-start.1
  15.7 12.1 %collective-permute-start.2 = (bf16[256,1024]{1,0:T(8,128)(2,1)S(1)}, bf16[256,1024]{1,0:T(8,128)(2,1)S(1)}, u32[]{:S(2)}, u32[]{:S(2)}) collective-permute-start(bf16[256,1024]{1,0:T(8,128)(2,1)S(1)} %get-tuple-element.110.refs_0_), channel_id=1, source_target_pairs={{0,4},{1,13},{2,6},{3,15},{4,8},{5,1},{6,10},{7,3},{8,12},{9,5},{1... | collective-permute-start | bytes 1572872 | tf_op jit(solution)/shard_map/ppermute | solution.py:71
  19.6 8.2 %collective-permute-start.4 = (bf16[256,512]{1,0:T(8,128)(2,1)S(1)}, bf16[256,512]{1,0:T(8,128)(2,1)S(1)}, u32[]{:S(2)}, u32[]{:S(2)}) collective-permute-start(bf16[256,512]{1,0:T(8,128)(2,1)S(1)} %get-tuple-element.113), channel_id=1, source_target_pairs={{0,66},{1,67},{2,64},{3,65},{4,70},{5,71},{6,68},{7,69},{8,74},{9,... | collective-permute-start | bytes 786440 | tf_op jit(solution)/shard_map/ppermute | solution.py:71
  28.7 325.8 %all-gather.4.cloned.1.call-start = ((), (), s32[]{:S(2)}) async-start(), calls=%async_computation.9 | async-start | bytes 35651584 | tf_op jit(solution)/shard_map/all_gather | solution.py:677
  32.1 12.2 %collective-permute-start = (bf16[128,8192]{1,0:T(8,128)(2,1)S(1)}, bf16[128,8192]{1,0:T(8,128)(2,1)S(1)}, u32[]{:S(2)}, u32[]{:S(2)}) collective-permute-start(bf16[128,8192]{1,0:T(8,128)(2,1)S(1)} %get-tuple-element.106), channel_id=1, source_target_pairs={{0,1},{1,0},{2,3},{3,2},{4,5},{5,4},{6,7},{7,6},{8,9},{9,8},{10,11... | collective-permute-start | bytes 6291464 | tf_op jit(solution)/shard_map/ppermute | solution.py:61
  32.2 8.6 %collective-permute-start.3 = (bf16[256,1024]{1,0:T(8,128)(2,1)S(1)}, bf16[256,1024]{1,0:T(8,128)(2,1)S(1)}, u32[]{:S(2)}, u32[]{:S(2)}) collective-permute-start(bf16[256,1024]{1,0:T(8,128)(2,1)S(1)} %collective-permute-done.2.refs_1_), channel_id=1, source_target_pairs={{0,4},{1,13},{2,6},{3,15},{4,8},{5,1},{6,10},{7,3},{8,12},{9,5},{1... | collective-permute-start | bytes 1572872 | tf_op jit(solution)/shard_map/ppermute | solution.py:71
  40.8 15.1 %collective-permute-start.6 = (bf16[256,1024]{1,0:T(8,128)(2,1)S(1)}, bf16[256,1024]{1,0:T(8,128)(2,1)S(1)}, u32[]{:S(2)}, u32[]{:S(2)}) collective-permute-start(bf16[256,1024]{1,0:T(8,128)(2,1)S(1)} %collective-permute-done.3.refs_2_), channel_id=1, source_target_pairs={{0,4},{1,13},{2,6},{3,15},{4,8},{5,1},{6,10},{7,3},{8,12},{9,5},{1... | collective-permute-start | bytes 1572872 | tf_op jit(solution)/shard_map/ppermute | solution.py:71
  48.1 27.0 %collective-permute-start.5 = (bf16[256,2048]{1,0:T(8,128)(2,1)S(1)}, bf16[256,2048]{1,0:T(8,128)(2,1)S(1)}, u32[]{:S(2)}, u32[]{:S(2)}) collective-permute-start(bf16[256,2048]{1,0:T(8,128)(2,1)S(1)} %get-tuple-element.114), channel_id=1, source_target_pairs={{0,66},{1,67},{2,64},{3,65},{4,70},{5,71},{6,68},{7,69},{8,74},{9,... | collective-permute-start | bytes 3145736 | tf_op jit(solution)/shard_map/ppermute | solution.py:71
  56.7 27.7 %collective-permute-start.7 = (bf16[512,1024]{1,0:T(8,128)(2,1)S(1)}, bf16[512,1024]{1,0:T(8,128)(2,1)S(1)}, u32[]{:S(2)}, u32[]{:S(2)}) collective-permute-start(bf16[512,1024]{1,0:T(8,128)(2,1)S(1)} %get-tuple-element.116.refs_1_), channel_id=1, source_target_pairs={{0,64},{1,67},{2,66},{3,65},{4,68},{5,71},{6,70},{7,69},{8,72},{9,... | collective-permute-start | bytes 3145736 | tf_op jit(solution)/shard_map/ppermute | solution.py:71
  60.3 35.3 %collective-permute-start.8 = (bf16[512,1024]{1,0:T(8,128)(2,1)S(1)}, bf16[512,1024]{1,0:T(8,128)(2,1)S(1)}, u32[]{:S(2)}, u32[]{:S(2)}) collective-permute-start(bf16[512,1024]{1,0:T(8,128)(2,1)S(1)} %get-tuple-element.117.refs_5_), channel_id=1, source_target_pairs={{0,64},{1,67},{2,66},{3,65},{4,68},{5,71},{6,70},{7,69},{8,72},{9,... | collective-permute-start | bytes 3145736 | tf_op jit(solution)/shard_map/ppermute | solution.py:71
  84.4 15.7 %copy-start.28 = (bf16[512,1024]{1,0:T(8,128)(2,1)}, bf16[512,1024]{1,0:T(8,128)(2,1)S(1)}, u32[]{:S(2)}) copy-start(bf16[512,1024]{1,0:T(8,128)(2,1)S(1)} %collective-permute-done.7.refs_2_) | copy-start | bytes 3145732
  98.2 16.4 %copy-start.79 = (s32[1,2]{1,0:T(1,128)S(1)}, s32[1,2]{1,0:T(1,128)}, u32[]{:S(2)}) copy-start(s32[1,2]{1,0:T(1,128)} %param.31) | copy-start | bytes 28
  98.2 17.4 %copy-start.8 = (bf16[1,144,2048]{2,1,0:T(8,128)(2,1)S(1)}, bf16[1,144,2048]{2,1,0:T(8,128)(2,1)}, u32[]{:S(2)}) copy-start(bf16[1,144,2048]{2,1,0:T(8,128)(2,1)} %param.16) | copy-start | bytes 1769476
  98.3 14.1 %collective-permute-start.9 = (bf16[256,2048]{1,0:T(8,128)(2,1)S(1)}, bf16[256,2048]{1,0:T(8,128)(2,1)}, u32[]{:S(2)}, u32[]{:S(2)}) collective-permute-start(bf16[256,2048]{1,0:T(8,128)(2,1)S(1)} %get-tuple-element.120.refs_0_), channel_id=1, source_target_pairs={{0,4},{1,13},{2,6},{3,15},{4,8},{5,1},{6,10},{7,3},{8,12},{9,5},{1... | collective-permute-start | bytes 3145736 | tf_op jit(solution)/shard_map/ppermute | solution.py:71
  100.1 16.8 %collective-permute-start.12 = (bf16[512,1024]{1,0:T(8,128)(2,1)S(1)}, bf16[512,1024]{1,0:T(8,128)(2,1)}, u32[]{:S(2)}, u32[]{:S(2)}) collective-permute-start(bf16[512,1024]{1,0:T(8,128)(2,1)S(1)} %collective-permute-done.7.refs_2_), channel_id=1, source_target_pairs={{0,64},{1,67},{2,66},{3,65},{4,68},{5,71},{6,70},{7,69},{8,72},{9,... | collective-permute-start | bytes 3145736 | tf_op jit(solution)/shard_map/ppermute | solution.py:71
  103.6 23.1 %collective-permute-start.14 = (bf16[512,1024]{1,0:T(8,128)(2,1)}, bf16[512,1024]{1,0:T(8,128)(2,1)}, u32[]{:S(2)}, u32[]{:S(2)}) collective-permute-start(bf16[512,1024]{1,0:T(8,128)(2,1)} %copy-done.73), channel_id=1, source_target_pairs={{0,64},{1,67},{2,66},{3,65},{4,68},{5,71},{6,70},{7,69},{8,72},{9,... | collective-permute-start | bytes 3145736 | tf_op jit(solution)/shard_map/ppermute | solution.py:71
  112.4 28.4 %collective-permute-start.10 = (bf16[256,2048]{1,0:T(8,128)(2,1)}, bf16[256,2048]{1,0:T(8,128)(2,1)}, u32[]{:S(2)}, u32[]{:S(2)}) collective-permute-start(bf16[256,2048]{1,0:T(8,128)(2,1)} %collective-permute-done.9.refs_1_), channel_id=1, source_target_pairs={{0,4},{1,13},{2,6},{3,15},{4,8},{5,1},{6,10},{7,3},{8,12},{9,5},{1... | collective-permute-start | bytes 3145736 | tf_op jit(solution)/shard_map/ppermute | solution.py:71
  114.8 1.7 collective-permute-start.18
  115.6 34.4 %collective-permute-start.17 = (bf16[144,2048]{1,0:T(8,128)(2,1)S(1)}, bf16[144,2048]{1,0:T(8,128)(2,1)}, u32[]{:S(2)}, u32[]{:S(2)}) collective-permute-start(bf16[144,2048]{1,0:T(8,128)(2,1)S(1)} %bitcast.70), channel_id=1, source_target_pairs={{0,1},{1,0},{2,3},{3,2},{4,5},{5,4},{6,7},{7,6},{8,9},{9,8},{10,11... | collective-permute-start | bytes 1769480 | tf_op jit(solution)/shard_map/ppermute | solution.py:61
  116.0 36.0 %copy-start.63 = (s32[3,4]{1,0:T(4,128)}, s32[3,4]{1,0:T(4,128)S(1)}, u32[]{:S(2)}) copy-start(s32[3,4]{1,0:T(4,128)S(1)} %pad_add_fusion.places) | copy-start | bytes 148
  116.8 35.1 %collective-permute-start.13 = (bf16[512,1024]{1,0:T(8,128)(2,1)}, bf16[512,1024]{1,0:T(8,128)(2,1)}, u32[]{:S(2)}, u32[]{:S(2)}) collective-permute-start(bf16[512,1024]{1,0:T(8,128)(2,1)} %collective-permute-done.12.refs_3_), channel_id=1, source_target_pairs={{0,64},{1,67},{2,66},{3,65},{4,68},{5,71},{6,70},{7,69},{8,72},{9,... | collective-permute-start | bytes 3145736 | tf_op jit(solution)/shard_map/ppermute | solution.py:71
  126.7 25.2 %collective-permute-start.15 = (bf16[512,1024]{1,0:T(8,128)(2,1)}, bf16[512,1024]{1,0:T(8,128)(2,1)}, u32[]{:S(2)}, u32[]{:S(2)}) collective-permute-start(bf16[512,1024]{1,0:T(8,128)(2,1)} %collective-permute-done.14.refs_7_), channel_id=1, source_target_pairs={{0,64},{1,67},{2,66},{3,65},{4,68},{5,71},{6,70},{7,69},{8,72},{9,... | collective-permute-start | bytes 3145736 | tf_op jit(solution)/shard_map/ppermute | solution.py:71
  140.8 30.9 %collective-permute-start.11 = (bf16[256,2048]{1,0:T(8,128)(2,1)}, bf16[256,2048]{1,0:T(8,128)(2,1)}, u32[]{:S(2)}, u32[]{:S(2)}) collective-permute-start(bf16[256,2048]{1,0:T(8,128)(2,1)} %collective-permute-done.10.refs_2_), channel_id=1, source_target_pairs={{0,4},{1,13},{2,6},{3,15},{4,8},{5,1},{6,10},{7,3},{8,12},{9,5},{1... | collective-permute-start | bytes 3145736 | tf_op jit(solution)/shard_map/ppermute | solution.py:71
  151.9 27.5 %copy-start.52 = (bf16[288,96]{1,0:T(8,128)(2,1)}, bf16[288,96]{1,0:T(8,128)(2,1)S(1)}, u32[]{:S(2)}) copy-start(bf16[288,96]{1,0:T(8,128)(2,1)S(1)} %fusion.1.low.refs_1_) | copy-start | bytes 165892
  176.0 71.4 %collective-permute-start.20 = (bf16[512,2048]{1,0:T(8,128)(2,1)}, bf16[512,2048]{1,0:T(8,128)(2,1)}, u32[]{:S(2)}, u32[]{:S(2)}) collective-permute-start(bf16[512,2048]{1,0:T(8,128)(2,1)} %get-tuple-element.137.refs_5_), channel_id=1, source_target_pairs={{0,64},{1,67},{2,66},{3,65},{4,68},{5,71},{6,70},{7,69},{8,72},{9,... | collective-permute-start | bytes 6291464 | tf_op jit(solution)/shard_map/ppermute | solution.py:71
  179.4 67.9 %collective-permute-start.16 = (bf16[512,2048]{1,0:T(8,128)(2,1)}, bf16[512,2048]{1,0:T(8,128)(2,1)}, u32[]{:S(2)}, u32[]{:S(2)}) collective-permute-start(bf16[512,2048]{1,0:T(8,128)(2,1)} %get-tuple-element.131.refs_1_), channel_id=1, source_target_pairs={{0,64},{1,67},{2,66},{3,65},{4,68},{5,71},{6,70},{7,69},{8,72},{9,... | collective-permute-start | bytes 6291464 | tf_op jit(solution)/shard_map/ppermute | solution.py:71
  194.9 3.1 collective-permute-start.19
  247.4 54.4 %copy-start.10 = (bf16[8,288,384]{2,1,0:T(8,128)(2,1)}, bf16[8,288,384]{2,1,0:T(8,128)(2,1)S(1)}, u32[]{:S(2)}) copy-start(bf16[8,288,384]{2,1,0:T(8,128)(2,1)S(1)} %all_to_all.45) | copy-start | bytes 5308420
  247.4 54.4 %copy-start.54 = (bf16[32,1024]{1,0:T(8,128)(2,1)S(1)}, bf16[32,1024]{1,0:T(8,128)(2,1)}, u32[]{:S(2)}) copy-start(bf16[32,1024]{1,0:T(8,128)(2,1)} %get-tuple-element.143.down) | copy-start | bytes 196612
  247.4 54.4 %copy-start.58 = (s32[8]{0:T(128)S(1)}, s32[8]{0:T(128)}, u32[]{:S(2)}) copy-start(s32[8]{0:T(128)} %copy-done.57) | copy-start | bytes 100
  247.4 59.3 %collective-permute-start.23 = (bf16[512,2048]{1,0:T(8,128)(2,1)}, bf16[512,2048]{1,0:T(8,128)(2,1)S(1)}, u32[]{:S(2)}, u32[]{:S(2)}) collective-permute-start(bf16[512,2048]{1,0:T(8,128)(2,1)} %collective-permute-done.20.refs_6_), channel_id=1, source_target_pairs={{0,64},{1,67},{2,66},{3,65},{4,68},{5,71},{6,70},{7,69},{8,72},{9,... | collective-permute-start | bytes 6291464 | tf_op jit(solution)/shard_map/ppermute | solution.py:71
  250.6 56.1 %collective-permute-start.21 = (bf16[512,2048]{1,0:T(8,128)(2,1)}, bf16[512,2048]{1,0:T(8,128)(2,1)S(1)}, u32[]{:S(2)}, u32[]{:S(2)}) collective-permute-start(bf16[512,2048]{1,0:T(8,128)(2,1)} %collective-permute-done.16.refs_2_), channel_id=1, source_target_pairs={{0,64},{1,67},{2,66},{3,65},{4,68},{5,71},{6,70},{7,69},{8,72},{9,... | collective-permute-start | bytes 6291464 | tf_op jit(solution)/shard_map/ppermute | solution.py:71
  258.5 43.2 %copy-start.65 = (f32[2,1152,128]{2,1,0:T(8,128)}, f32[2,1152,128]{2,1,0:T(8,128)S(1)}, u32[]{:S(2)}) copy-start(f32[2,1152,128]{2,1,0:T(8,128)S(1)} %get-tuple-element.180.exact) | copy-start | bytes 3538948
  306.7 25.4 %copy-start.70 = (bf16[512,2048]{1,0:T(8,128)(2,1)}, bf16[512,2048]{1,0:T(8,128)(2,1)S(1)}, u32[]{:S(2)}) copy-start(bf16[512,2048]{1,0:T(8,128)(2,1)S(1)} %collective-permute-done.21.refs_3_) | copy-start | bytes 6291460
  306.7 25.4 %collective-permute-start.22 = (bf16[512,2048]{1,0:T(8,128)(2,1)S(1)}, bf16[512,2048]{1,0:T(8,128)(2,1)S(1)}, u32[]{:S(2)}, u32[]{:S(2)}) collective-permute-start(bf16[512,2048]{1,0:T(8,128)(2,1)S(1)} %collective-permute-done.21.refs_3_), channel_id=1, source_target_pairs={{0,64},{1,67},{2,66},{3,65},{4,68},{5,71},{6,70},{7,69},{8,72},{9,... | collective-permute-start | bytes 6291464 | tf_op jit(solution)/shard_map/ppermute | solution.py:71
  307.9 46.6 %collective-permute-start.24 = (bf16[512,2048]{1,0:T(8,128)(2,1)S(1)}, bf16[512,2048]{1,0:T(8,128)(2,1)}, u32[]{:S(2)}, u32[]{:S(2)}) collective-permute-start(bf16[512,2048]{1,0:T(8,128)(2,1)S(1)} %collective-permute-done.23.refs_7_), channel_id=1, source_target_pairs={{0,64},{1,67},{2,66},{3,65},{4,68},{5,71},{6,70},{7,69},{8,72},{9,... | collective-permute-start | bytes 6291464 | tf_op jit(solution)/shard_map/ppermute | solution.py:71
  310.2 2.5 collective-permute-start.25
  315.7 2.4 collective-permute-start.26
  318.1 13.9 %copy-start.78 = (bf16[144,2176]{1,0:T(8,128)(2,1)}, bf16[144,2176]{1,0:T(8,128)(2,1)S(1)}, u32[]{:S(2)}) copy-start(bf16[144,2176]{1,0:T(8,128)(2,1)S(1)} %collective-permute-done.26.refs_10_) | copy-start | bytes 1880068
  354.5 32.7 %copy-start.7 = (bf16[1,144,2048]{2,1,0:T(8,128)(2,1)S(1)}, bf16[1,144,2048]{2,1,0:T(8,128)(2,1)}, u32[]{:S(2)}) copy-start(bf16[1,144,2048]{2,1,0:T(8,128)(2,1)} %param.17) | copy-start | bytes 1769476
  354.5 32.7 %copy-start.32 = (f32[4,2048]{1,0:T(4,128)S(1)}, f32[4,2048]{1,0:T(4,128)}, u32[]{:S(2)}) copy-start(f32[4,2048]{1,0:T(4,128)} %gains.9) | copy-start | bytes 98308
  354.5 32.7 %copy-start.45 = (bf16[32,2048]{1,0:T(8,128)(2,1)S(1)}, bf16[32,2048]{1,0:T(8,128)(2,1)}, u32[]{:S(2)}) copy-start(bf16[32,2048]{1,0:T(8,128)(2,1)} %get-tuple-element.162.up.refs_11_) | copy-start | bytes 393220
  381.2 6.1 collective-permute-start.27
  392.8 2.1 collective-permute-start.28
  395.7 29.4 %copy-start.61 = (bf16[288,64]{1,0:T(8,128)(2,1)S(1)}, bf16[288,64]{1,0:T(8,128)(2,1)}, u32[]{:S(2)}) copy-start(bf16[288,64]{1,0:T(8,128)(2,1)} %get-tuple-element.170.refs_0_) | copy-start | bytes 110596
  424.7 9.2 %collective-permute-start.29 = (bf16[144,2176]{1,0:T(8,128)(2,1)}, bf16[144,2176]{1,0:T(8,128)(2,1)S(1)}, u32[]{:S(2)}, u32[]{:S(2)}) collective-permute-start(bf16[144,2176]{1,0:T(8,128)(2,1)} %get-tuple-element.167), channel_id=1, source_target_pairs={{0,1},{1,0},{2,3},{3,2},{4,5},{5,4},{6,7},{7,6},{8,9},{9,8},{10,11... | collective-permute-start | bytes 1880072 | tf_op jit(solution)/shard_map/ppermute | solution.py:61
  437.0 16.7 %all-to-all-start.3 = ((bf16[8,32,1664]{2,1,0:T(8,128)(2,1)}), bf16[8,32,1664]{2,1,0:T(8,128)(2,1)}, u32[]{:S(2)}, u32[]{:S(2)}) async-start(bf16[8,32,1664]{2,1,0:T(8,128)(2,1)} %early_gradients.1), calls=%async_computation.3 | async-start | bytes 1703936 | tf_op jit(solution)/shard_map/all_to_all | solution.py:1143
  441.3 2.4 collective-permute-start.30
  453.6 17.3 %all-to-all-start.2 = ((bf16[8,416,128]{2,1,0:T(8,128)(2,1)}), bf16[8,416,128]{2,1,0:T(8,128)(2,1)}, u32[]{:S(2)}, u32[]{:S(2)}) async-start(bf16[8,416,128]{2,1,0:T(8,128)(2,1)} %copy-done.30), calls=%async_computation.2 | async-start | bytes 1703936 | tf_op jit(solution)/shard_map/all_to_all | solution.py:1146
  461.3 20.2 %copy-start.11 = (bf16[8,288,384]{2,1,0:T(8,128)(2,1)S(1)}, bf16[8,288,384]{2,1,0:T(8,128)(2,1)}, u32[]{:S(2)}) copy-start(bf16[8,288,384]{2,1,0:T(8,128)(2,1)} %copy-done.10) | copy-start | bytes 5308420
  477.0 22.2 %all-to-all-start.4 = ((bf16[8,32,2304]{2,1,0:T(8,128)(2,1)}), bf16[8,32,2304]{2,1,0:T(8,128)(2,1)}, u32[]{:S(2)}, u32[]{:S(2)}) async-start(bf16[8,32,2304]{2,1,0:T(8,128)(2,1)} %broadcast_in_dim.44), calls=%async_computation.4 | async-start | bytes 2359296 | tf_op jit(solution)/shard_map/all_to_all | solution.py:1087
  481.3 118.5 %all-gather.8.cloned.1.call-start = ((), (), s32[]{:S(2)}) async-start(), calls=%async_computation.11 | async-start | bytes 5013504 | tf_op jit(solution)/shard_map/all_gather | solution.py:1165
  544.1 12.3 %copy-start.40 = (f32[288,128]{1,0:T(8,128)S(1)}, f32[288,128]{1,0:T(8,128)}, u32[]{:S(2)}) copy-start(f32[288,128]{1,0:T(8,128)} %copy-done.39) | copy-start | bytes 442372
  544.1 12.3 %copy-start.59 = (s32[8]{0:T(128)S(1)}, s32[8]{0:T(128)}, u32[]{:S(2)}) copy-start(s32[8]{0:T(128)} %copy-done.57) | copy-start | bytes 100
  548.1 8.2 %collective-permute-start.31 = (f32[288,128]{1,0:T(8,128)}, f32[288,128]{1,0:T(8,128)S(1)}, u32[]{:S(2)}, u32[]{:S(2)}) collective-permute-start(f32[288,128]{1,0:T(8,128)} %get-tuple-element.187.su), channel_id=1, source_target_pairs={{0,1},{1,0},{2,3},{3,2},{4,5},{5,4},{6,7},{7,6},{8,9},{9,8},{10,11... | collective-permute-start | bytes 442376 | tf_op jit(solution)/shard_map/ppermute | solution.py:61
  560.9 12.8 %copy-start.23 = (f32[144,2048]{1,0:T(8,128)S(1)}, f32[144,2048]{1,0:T(8,128)}, u32[]{:S(2)}) copy-start(f32[144,2048]{1,0:T(8,128)} %copy-done.22) | copy-start | bytes 3538948
  560.9 12.8 %copy-start.51 = (bf16[96,2048]{1,0:T(8,128)(2,1)S(1)}, bf16[96,2048]{1,0:T(8,128)(2,1)}, u32[]{:S(2)}) copy-start(bf16[96,2048]{1,0:T(8,128)(2,1)} %get-tuple-element.132.down) | copy-start | bytes 1179652
  571.6 2.1 collective-permute-start.32
  575.4 1.2 collective-permute-start.33
  599.8 10.3 %collective-permute-start.34 = (bf16[8,8,16,2176]{3,2,1,0:T(8,128)(2,1)}, bf16[8,8,16,2176]{3,2,1,0:T(8,128)(2,1)}, u32[]{:S(2)}, u32[]{:S(2)}) collective-permute-start(bf16[8,8,16,2176]{3,2,1,0:T(8,128)(2,1)} %bitcast.65), channel_id=1, source_target_pairs={{0,1},{1,0},{2,3},{3,2},{4,5},{5,4},{6,7},{7,6},{8,9},{9,8},{10,11... | collective-permute-start | bytes 13369352 | tf_op jit(solution)/shard_map/ppermute | solution.py:61
  604.3 27.9 %all-to-all-start.8 = ((bf16[8,128,768]{2,1,0:T(8,128)(2,1)}), bf16[8,128,768]{2,1,0:T(8,128)(2,1)S(1)}, u32[]{:S(2)}, u32[]{:S(2)}) async-start(bf16[8,128,768]{2,1,0:T(8,128)(2,1)} %broadcast_in_dim.48), calls=%async_computation.8 | async-start | bytes 3145728 | tf_op jit(solution)/shard_map/all_to_all | solution.py:1087
  632.2 3.9 collective-permute-start.35
  (59 other events, 176.9 us)
Sparse Core Ops, SparseCore 0:
  28.8 72.1 all-gather.5
  103.8 237.0 all-gather.3
  504.9 68.1 all-gather.7

commit v5 on v3

--- a/solution.py
+++ b/solution.py
@@ -1153,15 +1153,15 @@
     groups = spread_over(own, shard).reshape(16, RANK, EARLY + MIDDLE + 128)
     d_heads = attend_back(bounds, heads, d_out_heads, exact, log_total)
     d_heads = lax.all_to_all(d_heads, CTX, 0, 0, tiled=True).reshape(8, 2 * ROWS, 3 * HD)
-    w_q, w_k, d_v, sums = unpack_heads(me, d_heads, qkv, gains, cosine, sine)
 
     def by_slot(groups):
         flat = groups.reshape(16, -1)
         return lax.dot_general(picker, flat, **TN).astype(BF).reshape(8 * RANK, -1)
 
     picker = groups[:, 0, EARLY + MIDDLE : EARLY + MIDDLE + 8]
-    early, w_q = lax.optimization_barrier((by_slot(groups[:, :, : EARLY + MIDDLE]), w_q))
+    early, d_heads = lax.optimization_barrier((by_slot(groups[:, :, : EARLY + MIDDLE]), d_heads))
     early = lax.all_gather(early, CTX)
+    w_q, w_k, d_v, sums = unpack_heads(me, d_heads, qkv, gains, cosine, sine)
     d_qkv, keep, give = project_qkv_back(me, (w_q, w_k), d_v, qkv, squares, (sums, swap(sums)), w_qkv, qkv_up)
     grad_tokens, low = combine_tokens(me, keep, swap(give), d_hidden, qkv_down)
     low = both(low, swap(low)).reshape(2 * ROWS, 128)

time: 658 us -> 654 us (level)
  transfers between devices with their start and end apart: 44 -> 44, of which waited for: 28 -> 28; matrix products, arithmetic and copies ran while one was open for 3% -> 3% of each run, Pallas kernels for 14% -> 15%
where the time goes in v5:
time: 654 us; the launch traced here: 643 us
  waiting for transfers between devices  170 us (26%)
  Pallas kernels  160 us (24%)
  blocking collectives  127 us (19%)
  starting transfers between devices  83.7 us (13%)
  local copies, waits for them, and re-layouts  73 us (11%)
  between operations  15.2 us (2%)
  other arithmetic  11.7 us (2%)
    ppermute x20, waiting for transfers between devices, send(): self.last = lax.ppermute(value, ALL, STEPS[how])  116 us
    unnamed x166, local copies, waits for them, and re-layouts  63.5 us
    pallas_call x2, Pallas kernels, call(): pl.pallas_call(body, out_shape=outs, in_specs=[_smem()] + [anywhere] * 9...  55.5 us
    ppermute x20, starting transfers between devices, send(): self.last = lax.ppermute(value, ALL, STEPS[how])  45.2 us
    all_to_all x1, blocking collectives, on_device(): lax.all_to_all(packed, CTX, 0, 0, tiled=True).reshape(8, 2, ROWS, 3 * HD)  44.8 us
    all_to_all x1, blocking collectives, on_device(): lax.all_to_all(out_heads, CTX, 0, 0, tiled=True).reshape(8, 2 * ROWS, HD)  43.2 us
    pallas_call x14, Pallas kernels, _plain(): pl.pallas_call(body, out_shape=outs, in_specs=[_smem()] * len(scalars) +...  34.4 us
    all_to_all x1, blocking collectives, spread_over(): lax.all_to_all(jnp.broadcast_to(value[None], (8,) + value.shape), axes, 0...  23.5 us
  transfers between devices with their start and end apart: 44, of which 28 were waited for; matrix products, arithmetic and copies ran while one was open for 3% of the time, Pallas kernels for 15%

profile of v5, /device:TPU:7, one launch (start us, length us, event | category | flops | bytes accessed | tf_op | source)
XLA Modules:
  0.0 643.0 jit_solution(16243420498948520051)
XLA Ops:
  15.7 3.8 collective-permute-start.2
  19.6 2.7 collective-permute-start.4
  22.3 5.5 collective-permute-done.4
  28.8 3.4 split_g.1
  34.1 6.7 %collective-permute-done.3.refs_2_ = bf16[256,1024]{1,0:T(8,128)(2,1)S(1)} collective-permute-done((bf16[256,1024]{1,0:T(8,128)(2,1)S(1)}, bf16[256,1024]{1,0:T(8,128)(2,1)S(1)}, u32[]{:S(2)}, u32[]{:S(2)}) %collective-permute-start.3) | collective-permute-done | bytes 524320 | tf_op jit(solution)/shard_map/ppermute | solution.py:71
  40.8 3.5 collective-permute-start.6
  45.6 2.4 parts_m.1
  48.1 3.2 collective-permute-start.5
  51.2 4.7 collective-permute-done.6.refs_3_
  56.7 2.7 collective-permute-start.7
  61.7 13.4 %collective-permute-done.5 = bf16[256,2048]{1,0:T(8,128)(2,1)S(1)} collective-permute-done((bf16[256,2048]{1,0:T(8,128)(2,1)S(1)}, bf16[256,2048]{1,0:T(8,128)(2,1)S(1)}, u32[]{:S(2)}, u32[]{:S(2)}) %collective-permute-start.5) | collective-permute-done | bytes 1048608 | tf_op jit(solution)/shard_map/ppermute | solution.py:71
  75.1 9.3 %collective-permute-done.7.refs_2_ = bf16[512,1024]{1,0:T(8,128)(2,1)S(1)} collective-permute-done((bf16[512,1024]{1,0:T(8,128)(2,1)S(1)}, bf16[512,1024]{1,0:T(8,128)(2,1)S(1)}, u32[]{:S(2)}, u32[]{:S(2)}) %collective-permute-start.7) | collective-permute-done | bytes 1048608 | tf_op jit(solution)/shard_map/ppermute | solution.py:71
  84.4 11.2 %collective-permute-done.8.refs_6_ = bf16[512,1024]{1,0:T(8,128)(2,1)S(1)} collective-permute-done((bf16[512,1024]{1,0:T(8,128)(2,1)S(1)}, bf16[512,1024]{1,0:T(8,128)(2,1)S(1)}, u32[]{:S(2)}, u32[]{:S(2)}) %collective-permute-start.8) | collective-permute-done | bytes 1048608 | tf_op jit(solution)/shard_map/ppermute | solution.py:71
  100.1 3.6 collective-permute-start.12
  103.7 8.7 %collective-permute-done.9.refs_1_ = bf16[256,2048]{1,0:T(8,128)(2,1)} collective-permute-done((bf16[256,2048]{1,0:T(8,128)(2,1)S(1)}, bf16[256,2048]{1,0:T(8,128)(2,1)}, u32[]{:S(2)}, u32[]{:S(2)}) %collective-permute-start.9) | collective-permute-done | bytes 1048608 | tf_op jit(solution)/shard_map/ppermute | solution.py:71
  112.4 2.3 collective-permute-start.10
  116.8 2.7 collective-permute-start.13
  119.5 7.2 %collective-permute-done.14.refs_7_ = bf16[512,1024]{1,0:T(8,128)(2,1)} collective-permute-done((bf16[512,1024]{1,0:T(8,128)(2,1)}, bf16[512,1024]{1,0:T(8,128)(2,1)}, u32[]{:S(2)}, u32[]{:S(2)}) %collective-permute-start.14) | collective-permute-done | bytes 1048608 | tf_op jit(solution)/shard_map/ppermute | solution.py:71
  126.7 3.4 collective-permute-start.15
  130.1 10.6 %collective-permute-done.10.refs_2_ = bf16[256,2048]{1,0:T(8,128)(2,1)} collective-permute-done((bf16[256,2048]{1,0:T(8,128)(2,1)}, bf16[256,2048]{1,0:T(8,128)(2,1)}, u32[]{:S(2)}, u32[]{:S(2)}) %collective-permute-start.10) | collective-permute-done | bytes 1048608 | tf_op jit(solution)/shard_map/ppermute | solution.py:71
  140.8 3.4 collective-permute-start.11
  144.8 3.8 choose_adapters.1
  155.8 12.1 %assemble.1 = (bf16[2048,3072]{1,0:T(8,128)(2,1)}, bf16[1024,2048]{1,0:T(8,128)(2,1)}) custom-call(s32[3,4]{1,0:T(4,128)S(1)} %pad_add_fusion.places, bf16[4,4,2,256,512]{4,3,2,1,0:T(8,128)(2,1)} %bitcast.82, bf16[512,1024]{1,0:T(8,128)(2,1)S(1)} %copy-done.24, bf16[512,1024]{1,0:T(8,128)(2,1)S(1)} %copy-done.28, ...), custom_call_target="tpu_custom_call" | custom-call | bytes 67108864 | tf_op jit(solution)/shard_map/assemble/pallas_call | solution.py:255
  167.9 3.7 collective-permute-done.11.refs_3_
  171.7 4.3 spread_g.1
  176.0 3.4 collective-permute-start.20
  179.5 7.1 %copy-done.1 = bf16[2048,3072]{1,0:T(8,128)(2,1)S(1)} copy-done((bf16[2048,3072]{1,0:T(8,128)(2,1)S(1)}, bf16[2048,3072]{1,0:T(8,128)(2,1)}, u32[]{:S(2)}) %copy-start.1) | copy-done | bytes 12582936
  186.5 6.5 %project_qkv.1 = (f32[288,3072]{1,0:T(8,128)S(1)}, f32[288,128]{1,0:T(8,128)S(1)}) custom-call(bf16[288,2048]{1,0:T(8,128)(2,1)S(1)} %bitcast.63, bf16[2048,3072]{1,0:T(8,128)(2,1)S(1)} %copy-done.1, bf16[288,96]{1,0:T(8,128)(2,1)S(1)} %fusion.1.low.refs_1_, bf16[96,3072]{1,0:T(8,128)(2,1)S(1)} %copy-done.6), custom_call_target="tpu_custom_call" | custom-call | flops 3623878656 | bytes 18000000 | tf_op jit(solution)/shard_map/project_qkv/pallas_call | solution.py:489
  198.5 4.0 pack_heads.1
  202.6 44.8 %all_to_all.45 = bf16[8,288,384]{2,1,0:T(8,128)(2,1)S(1)} all-to-all(bf16[8,288,384]{2,1,0:T(8,128)(2,1)} %pack_heads.1), channel_id=1, replica_groups=mesh['yl'=2,'x'=4,'z'=4,'yh'=2,'c'=2] {'yl','x'}, dimensions={0} | all-to-all | bytes 3538944 | tf_op jit(solution)/shard_map/all_to_all | solution.py:1113
  247.4 3.2 collective-permute-start.23
  250.9 6.6 %attend.1 = (bf16[8,2,144,128]{3,2,1,0:T(8,128)(2,1)S(1)}, f32[2,1152,128]{2,1,0:T(8,128)S(1)}, f32[2,1152,1]{2,1,0:T(8,128)S(1)}) custom-call(s32[2]{0:T(128)S(1)} %get-tuple-element.204.bounds, bf16[8,2,144,384]{3,2,1,0:T(8,128)(2,1)S(1)} %bitcast.73), custom_call_target="tpu_custom_call" | custom-call | flops 900000000 | bytes 5000000 | tf_op jit(solution)/shard_map/attend/pallas_call | solution.py:800
  258.5 43.2 %all_to_all.46 = bf16[8,2,144,128]{3,2,1,0:T(8,128)(2,1)S(1)} all-to-all(bf16[8,2,144,128]{3,2,1,0:T(8,128)(2,1)S(1)} %get-tuple-element.141), channel_id=1, replica_groups=mesh['yl'=2,'x'=4,'z'=4,'yh'=2,'c'=2] {'yl','x'}, dimensions={0} | all-to-all | bytes 1179648 | tf_op jit(solution)/shard_map/all_to_all | solution.py:1117
  301.8 4.1 project_out.1
  307.9 2.2 collective-permute-start.24
  318.1 13.9 %collective-permute-done.22.refs_4_ = bf16[512,2048]{1,0:T(8,128)(2,1)S(1)} collective-permute-done((bf16[512,2048]{1,0:T(8,128)(2,1)S(1)}, bf16[512,2048]{1,0:T(8,128)(2,1)S(1)}, u32[]{:S(2)}, u32[]{:S(2)}) %collective-permute-start.22) | collective-permute-done | bytes 2097184 | tf_op jit(solution)/shard_map/ppermute | solution.py:71
  333.4 21.1 %collective-permute-done.24.refs_8_ = bf16[512,2048]{1,0:T(8,128)(2,1)} collective-permute-done((bf16[512,2048]{1,0:T(8,128)(2,1)S(1)}, bf16[512,2048]{1,0:T(8,128)(2,1)}, u32[]{:S(2)}, u32[]{:S(2)}) %collective-permute-start.24) | collective-permute-done | bytes 2097184 | tf_op jit(solution)/shard_map/ppermute | solution.py:71
  354.5 26.6 %feed_forward.1 = (bf16[288,8192]{1,0:T(8,128)(2,1)}, bf16[288,4096]{1,0:T(8,128)(2,1)}, bf16[288,2176]{1,0:T(8,128)(2,1)}, bf16[288,64]{1,0:T(8,128)(2,1)}, f32...) custom-call(s32[3,4]{1,0:T(4,128)} %copy-done.62, bf16[4,4,2,256,2048]{4,3,2,1,0:T(8,128)(2,1)} %bitcast.80, ...), custom_call_target="tpu_custom_call" | custom-call | flops 14495514624 | bytes 53157888 | tf_op jit(solution)/shard_map/feed_forward/pallas_call | solution.py:358
  381.1 4.2 collective-permute-start.27
  389.8 2.1 combine_output.1
  395.7 28.9 %feed_forward_back.1 = (bf16[288,8192]{1,0:T(8,128)(2,1)}, bf16[288,2176]{1,0:T(8,128)(2,1)}, bf16[288,32]{1,0:T(8,128)(2,1)}, f32[144,2176]{1,0:T(8,128)}, bf16[144,2176]{1,0:T(8,128)(2,1)}) custom-call(s32[3,4]{1,0:T(4,128)} %copy-done.62, bf16[4,4,2,256,2048]{4,3,2,1,0:T(8,128)(2,1)} %bitcast.81, bf16[512,2048]{1,0:T(8,128)(2,1)} %get-tuple-element.131.refs_1_, ...), custom_call_target="tpu_custom_call" | custom-call | flops 14495514624 | bytes 57745408 | tf_op jit(solution)/shard_map/feed_forward_back/pallas_call | solution.py:358
  428.9 4.9 early_gradients.1
  436.9 4.3 all-to-all-start.3
  447.5 5.2 project_out_back.1
  453.6 5.5 all-to-all-start.2
  463.0 8.0 %all-to-all-done.2.grad = bf16[8,416,128]{2,1,0:T(8,128)(2,1)} async-done(((bf16[8,416,128]{2,1,0:T(8,128)(2,1)}), bf16[8,416,128]{2,1,0:T(8,128)(2,1)}, u32[]{:S(2)}, u32[]{:S(2)}) %all-to-all-start.2) | async-done | bytes 852000 | tf_op jit(solution)/shard_map/all_to_all | solution.py:1146
  477.0 4.4 all-to-all-start.4
  484.0 7.6 %attend_back.1 = bf16[8,2,144,384]{3,2,1,0:T(8,128)(2,1)S(1)} custom-call(s32[2]{0:T(128)S(1)} %get-tuple-element.204.bounds, bf16[8,2,144,384]{3,2,1,0:T(8,128)(2,1)S(1)} %bitcast.74, bf16[8,416,128]{2,1,0:T(8,128)(2,1)} %all-to-all-done.2.grad, f32[2,1152,128]{2,1,0:T(8,128)S(1)} %copy-done.65, f32[2,1152,1]{2,1,0:T(8,128)S(1)} %copy-done.67), custom_call_target="tpu_custom_call" | custom-call | flops 2300000000 | bytes 8000000 | tf_op jit(solution)/shard_map/attend_back/pallas_call | solution.py:848
  492.9 6.5 %all-to-all-done.4 = bf16[8,32,2304]{2,1,0:T(8,128)(2,1)} async-done(((bf16[8,32,2304]{2,1,0:T(8,128)(2,1)}), bf16[8,32,2304]{2,1,0:T(8,128)(2,1)}, u32[]{:S(2)}, u32[]{:S(2)}) %all-to-all-start.4) | async-done | bytes 1179680 | tf_op jit(solution)/shard_map/all_to_all | solution.py:1087
  499.4 5.0 all-to-all-start.5
  505.1 2.3 slice.32
  512.2 13.3 %all-to-all-done.5 = bf16[8,2,144,384]{3,2,1,0:T(8,128)(2,1)S(1)} async-done(((bf16[8,2,144,384]{3,2,1,0:T(8,128)(2,1)}), bf16[8,2,144,384]{3,2,1,0:T(8,128)(2,1)S(1)}, u32[]{:S(2)}, u32[]{:S(2)}) %all-to-all-start.5) | async-done | bytes 1769504 | tf_op jit(solution)/shard_map/all_to_all | solution.py:1155
  526.7 4.1 unpack_heads.1
  537.5 10.7 %project_qkv_back.1 = (bf16[288,3072]{1,0:T(8,128)(2,1)}, f32[144,2176]{1,0:T(8,128)S(1)}, bf16[144,2176]{1,0:T(8,128)(2,1)S(1)}) custom-call(s32[8]{0:T(128)S(1)} %copy-done.58, f32[288,1024]{1,0:T(8,128)S(1)} %copy-done.17, f32[288,1024]{1,0:T(8,128)S(1)} %copy-done.18, bf16[288,1024]{1,0:T(8,128)(2,1)S(1)} %copy-done.35, f32[288,3072]{1,0:T(8,128)} %copy-done, ...), custom_call_target="tpu_custom_call" | custom-call | flops 3623878656 | bytes 22000000 | tf_op jit(solution)/shard_map/project_qkv_back/pallas_call | solution.py:640
  554.8 15.6 %all_to_all.47 = bf16[8,32,768]{2,1,0:T(8,128)(2,1)S(1)} all-to-all(bf16[8,32,768]{2,1,0:T(8,128)(2,1)S(1)} %late_gradients.1), channel_id=1, replica_groups=mesh['yl'=2,'x'=4,'z'=4,'yh'=2,'c'=2] {'yl','x'}, dimensions={0} | all-to-all | bytes 786432 | tf_op jit(solution)/shard_map/all_to_all | solution.py:1178
  570.5 23.5 %all_to_all.48 = bf16[8,32,768]{2,1,0:T(8,128)(2,1)S(1)} all-to-all(bf16[8,32,768]{2,1,0:T(8,128)(2,1)S(1)} %broadcast_in_dim.46), channel_id=1, replica_groups=mesh['yl'=2,'x'=4,'z'=4,'yh'=2,'c'=2] {'z','yh'}, dimensions={0} | all-to-all | bytes 786432 | tf_op jit(solution)/shard_map/all_to_all | solution.py:1087
  596.1 5.7 all-to-all-start.8
  601.9 2.3 copy-done.5
  604.1 8.9 %early_outputs.1 = (f32[8,2,16,8192]{3,2,1,0:T(8,128)}, f32[8,16,8192]{2,1,0:T(8,128)}, f32[8,5,16,2048]{3,2,1,0:T(8,128)S(1)}) custom-call(s32[8]{0:T(128)S(1)} %copy-done.58, bf16[8,8,16,2176]{3,2,1,0:T(8,128)(2,1)S(1)} %bitcast.67, bf16[8,8,16,2176]{3,2,1,0:T(8,128)(2,1)} %collective-permute-done.34.refs_1_), custom_call_target="tpu_custom_call" | custom-call | bytes 8912896 | tf_op jit(solution)/shard_map/early_outputs/pallas_call | solution.py:970
  613.1 2.4 copy-done.2
  615.4 8.3 %all-to-all-done.8 = bf16[8,128,768]{2,1,0:T(8,128)(2,1)S(1)} async-done(((bf16[8,128,768]{2,1,0:T(8,128)(2,1)}), bf16[8,128,768]{2,1,0:T(8,128)(2,1)S(1)}, u32[]{:S(2)}, u32[]{:S(2)}) %all-to-all-start.8) | async-done | bytes 1572896 | tf_op jit(solution)/shard_map/all_to_all | solution.py:1087
  624.7 3.0 collective-permute-done.35
  627.7 2.5 copy-done.3
  630.2 6.1 late_outputs.1
  (270 shorter events, 107.1 us)
Async XLA Ops:
  7.2 144.9 %all-gather.7.cloned.1.call-start = ((), (), s32[]{:S(2)}) async-start(), calls=%async_computation.10 | async-start | bytes 8912896 | tf_op jit(solution)/shard_map/all_gather | solution.py:677
  10.4 161.2 %copy-start.56 = (s32[8]{0:T(128)}, s32[8]{0:T(128)S(1)}, u32[]{:S(2)}) copy-start(s32[8]{0:T(128)S(1)} %stack.141.core.me) | copy-start | bytes 100
  11.4 2.7 collective-permute-start.1
  15.7 12.1 %collective-permute-start.2 = (bf16[256,1024]{1,0:T(8,128)(2,1)S(1)}, bf16[256,1024]{1,0:T(8,128)(2,1)S(1)}, u32[]{:S(2)}, u32[]{:S(2)}) collective-permute-start(bf16[256,1024]{1,0:T(8,128)(2,1)S(1)} %get-tuple-element.110.refs_0_), channel_id=1, source_target_pairs={{0,4},{1,13},{2,6},{3,15},{4,8},{5,1},{6,10},{7,3},{8,12},{9,5},{1... | collective-permute-start | bytes 1572872 | tf_op jit(solution)/shard_map/ppermute | solution.py:71
  19.6 8.2 %collective-permute-start.4 = (bf16[256,512]{1,0:T(8,128)(2,1)S(1)}, bf16[256,512]{1,0:T(8,128)(2,1)S(1)}, u32[]{:S(2)}, u32[]{:S(2)}) collective-permute-start(bf16[256,512]{1,0:T(8,128)(2,1)S(1)} %get-tuple-element.113), channel_id=1, source_target_pairs={{0,66},{1,67},{2,64},{3,65},{4,70},{5,71},{6,68},{7,69},{8,74},{9,... | collective-permute-start | bytes 786440 | tf_op jit(solution)/shard_map/ppermute | solution.py:71
  28.7 325.8 %all-gather.5.cloned.1.call-start = ((), (), s32[]{:S(2)}) async-start(), calls=%async_computation.9 | async-start | bytes 35651584 | tf_op jit(solution)/shard_map/all_gather | solution.py:677
  32.1 12.2 %collective-permute-start = (bf16[128,8192]{1,0:T(8,128)(2,1)S(1)}, bf16[128,8192]{1,0:T(8,128)(2,1)S(1)}, u32[]{:S(2)}, u32[]{:S(2)}) collective-permute-start(bf16[128,8192]{1,0:T(8,128)(2,1)S(1)} %get-tuple-element.106), channel_id=1, source_target_pairs={{0,1},{1,0},{2,3},{3,2},{4,5},{5,4},{6,7},{7,6},{8,9},{9,8},{10,11... | collective-permute-start | bytes 6291464 | tf_op jit(solution)/shard_map/ppermute | solution.py:61
  32.2 8.6 %collective-permute-start.3 = (bf16[256,1024]{1,0:T(8,128)(2,1)S(1)}, bf16[256,1024]{1,0:T(8,128)(2,1)S(1)}, u32[]{:S(2)}, u32[]{:S(2)}) collective-permute-start(bf16[256,1024]{1,0:T(8,128)(2,1)S(1)} %collective-permute-done.2.refs_1_), channel_id=1, source_target_pairs={{0,4},{1,13},{2,6},{3,15},{4,8},{5,1},{6,10},{7,3},{8,12},{9,5},{1... | collective-permute-start | bytes 1572872 | tf_op jit(solution)/shard_map/ppermute | solution.py:71
  40.8 15.1 %collective-permute-start.6 = (bf16[256,1024]{1,0:T(8,128)(2,1)S(1)}, bf16[256,1024]{1,0:T(8,128)(2,1)S(1)}, u32[]{:S(2)}, u32[]{:S(2)}) collective-permute-start(bf16[256,1024]{1,0:T(8,128)(2,1)S(1)} %collective-permute-done.3.refs_2_), channel_id=1, source_target_pairs={{0,4},{1,13},{2,6},{3,15},{4,8},{5,1},{6,10},{7,3},{8,12},{9,5},{1... | collective-permute-start | bytes 1572872 | tf_op jit(solution)/shard_map/ppermute | solution.py:71
  48.1 27.0 %collective-permute-start.5 = (bf16[256,2048]{1,0:T(8,128)(2,1)S(1)}, bf16[256,2048]{1,0:T(8,128)(2,1)S(1)}, u32[]{:S(2)}, u32[]{:S(2)}) collective-permute-start(bf16[256,2048]{1,0:T(8,128)(2,1)S(1)} %get-tuple-element.114), channel_id=1, source_target_pairs={{0,66},{1,67},{2,64},{3,65},{4,70},{5,71},{6,68},{7,69},{8,74},{9,... | collective-permute-start | bytes 3145736 | tf_op jit(solution)/shard_map/ppermute | solution.py:71
  56.7 27.7 %collective-permute-start.7 = (bf16[512,1024]{1,0:T(8,128)(2,1)S(1)}, bf16[512,1024]{1,0:T(8,128)(2,1)S(1)}, u32[]{:S(2)}, u32[]{:S(2)}) collective-permute-start(bf16[512,1024]{1,0:T(8,128)(2,1)S(1)} %get-tuple-element.116.refs_1_), channel_id=1, source_target_pairs={{0,64},{1,67},{2,66},{3,65},{4,68},{5,71},{6,70},{7,69},{8,72},{9,... | collective-permute-start | bytes 3145736 | tf_op jit(solution)/shard_map/ppermute | solution.py:71
  60.3 35.3 %collective-permute-start.8 = (bf16[512,1024]{1,0:T(8,128)(2,1)S(1)}, bf16[512,1024]{1,0:T(8,128)(2,1)S(1)}, u32[]{:S(2)}, u32[]{:S(2)}) collective-permute-start(bf16[512,1024]{1,0:T(8,128)(2,1)S(1)} %get-tuple-element.117.refs_5_), channel_id=1, source_target_pairs={{0,64},{1,67},{2,66},{3,65},{4,68},{5,71},{6,70},{7,69},{8,72},{9,... | collective-permute-start | bytes 3145736 | tf_op jit(solution)/shard_map/ppermute | solution.py:71
  84.4 15.7 %copy-start.27 = (bf16[512,1024]{1,0:T(8,128)(2,1)}, bf16[512,1024]{1,0:T(8,128)(2,1)S(1)}, u32[]{:S(2)}) copy-start(bf16[512,1024]{1,0:T(8,128)(2,1)S(1)} %collective-permute-done.7.refs_2_) | copy-start | bytes 3145732
  98.2 16.4 %copy-start.79 = (s32[1,2]{1,0:T(1,128)S(1)}, s32[1,2]{1,0:T(1,128)}, u32[]{:S(2)}) copy-start(s32[1,2]{1,0:T(1,128)} %param.31) | copy-start | bytes 28
  98.2 17.4 %copy-start.8 = (bf16[1,144,2048]{2,1,0:T(8,128)(2,1)S(1)}, bf16[1,144,2048]{2,1,0:T(8,128)(2,1)}, u32[]{:S(2)}) copy-start(bf16[1,144,2048]{2,1,0:T(8,128)(2,1)} %param.16) | copy-start | bytes 1769476
  98.3 14.1 %collective-permute-start.9 = (bf16[256,2048]{1,0:T(8,128)(2,1)S(1)}, bf16[256,2048]{1,0:T(8,128)(2,1)}, u32[]{:S(2)}, u32[]{:S(2)}) collective-permute-start(bf16[256,2048]{1,0:T(8,128)(2,1)S(1)} %get-tuple-element.120.refs_0_), channel_id=1, source_target_pairs={{0,4},{1,13},{2,6},{3,15},{4,8},{5,1},{6,10},{7,3},{8,12},{9,5},{1... | collective-permute-start | bytes 3145736 | tf_op jit(solution)/shard_map/ppermute | solution.py:71
  100.1 16.8 %collective-permute-start.12 = (bf16[512,1024]{1,0:T(8,128)(2,1)S(1)}, bf16[512,1024]{1,0:T(8,128)(2,1)}, u32[]{:S(2)}, u32[]{:S(2)}) collective-permute-start(bf16[512,1024]{1,0:T(8,128)(2,1)S(1)} %collective-permute-done.7.refs_2_), channel_id=1, source_target_pairs={{0,64},{1,67},{2,66},{3,65},{4,68},{5,71},{6,70},{7,69},{8,72},{9,... | collective-permute-start | bytes 3145736 | tf_op jit(solution)/shard_map/ppermute | solution.py:71
  103.6 23.1 %collective-permute-start.14 = (bf16[512,1024]{1,0:T(8,128)(2,1)}, bf16[512,1024]{1,0:T(8,128)(2,1)}, u32[]{:S(2)}, u32[]{:S(2)}) collective-permute-start(bf16[512,1024]{1,0:T(8,128)(2,1)} %copy-done.73), channel_id=1, source_target_pairs={{0,64},{1,67},{2,66},{3,65},{4,68},{5,71},{6,70},{7,69},{8,72},{9,... | collective-permute-start | bytes 3145736 | tf_op jit(solution)/shard_map/ppermute | solution.py:71
  112.4 28.4 %collective-permute-start.10 = (bf16[256,2048]{1,0:T(8,128)(2,1)}, bf16[256,2048]{1,0:T(8,128)(2,1)}, u32[]{:S(2)}, u32[]{:S(2)}) collective-permute-start(bf16[256,2048]{1,0:T(8,128)(2,1)} %collective-permute-done.9.refs_1_), channel_id=1, source_target_pairs={{0,4},{1,13},{2,6},{3,15},{4,8},{5,1},{6,10},{7,3},{8,12},{9,5},{1... | collective-permute-start | bytes 3145736 | tf_op jit(solution)/shard_map/ppermute | solution.py:71
  114.7 1.7 collective-permute-start.18
  115.6 34.4 %collective-permute-start.17 = (bf16[144,2048]{1,0:T(8,128)(2,1)S(1)}, bf16[144,2048]{1,0:T(8,128)(2,1)}, u32[]{:S(2)}, u32[]{:S(2)}) collective-permute-start(bf16[144,2048]{1,0:T(8,128)(2,1)S(1)} %bitcast.71), channel_id=1, source_target_pairs={{0,1},{1,0},{2,3},{3,2},{4,5},{5,4},{6,7},{7,6},{8,9},{9,8},{10,11... | collective-permute-start | bytes 1769480 | tf_op jit(solution)/shard_map/ppermute | solution.py:61
  116.0 36.1 %copy-start.62 = (s32[3,4]{1,0:T(4,128)}, s32[3,4]{1,0:T(4,128)S(1)}, u32[]{:S(2)}) copy-start(s32[3,4]{1,0:T(4,128)S(1)} %pad_add_fusion.places) | copy-start | bytes 148
  116.8 35.2 %collective-permute-start.13 = (bf16[512,1024]{1,0:T(8,128)(2,1)}, bf16[512,1024]{1,0:T(8,128)(2,1)}, u32[]{:S(2)}, u32[]{:S(2)}) collective-permute-start(bf16[512,1024]{1,0:T(8,128)(2,1)} %collective-permute-done.12.refs_3_), channel_id=1, source_target_pairs={{0,64},{1,67},{2,66},{3,65},{4,68},{5,71},{6,70},{7,69},{8,72},{9,... | collective-permute-start | bytes 3145736 | tf_op jit(solution)/shard_map/ppermute | solution.py:71
  126.7 25.3 %collective-permute-start.15 = (bf16[512,1024]{1,0:T(8,128)(2,1)}, bf16[512,1024]{1,0:T(8,128)(2,1)}, u32[]{:S(2)}, u32[]{:S(2)}) collective-permute-start(bf16[512,1024]{1,0:T(8,128)(2,1)} %collective-permute-done.14.refs_7_), channel_id=1, source_target_pairs={{0,64},{1,67},{2,66},{3,65},{4,68},{5,71},{6,70},{7,69},{8,72},{9,... | collective-permute-start | bytes 3145736 | tf_op jit(solution)/shard_map/ppermute | solution.py:71
  140.8 30.9 %collective-permute-start.11 = (bf16[256,2048]{1,0:T(8,128)(2,1)}, bf16[256,2048]{1,0:T(8,128)(2,1)}, u32[]{:S(2)}, u32[]{:S(2)}) collective-permute-start(bf16[256,2048]{1,0:T(8,128)(2,1)} %collective-permute-done.10.refs_2_), channel_id=1, source_target_pairs={{0,4},{1,13},{2,6},{3,15},{4,8},{5,1},{6,10},{7,3},{8,12},{9,5},{1... | collective-permute-start | bytes 3145736 | tf_op jit(solution)/shard_map/ppermute | solution.py:71
  152.0 27.5 %copy-start.51 = (bf16[288,96]{1,0:T(8,128)(2,1)}, bf16[288,96]{1,0:T(8,128)(2,1)S(1)}, u32[]{:S(2)}) copy-start(bf16[288,96]{1,0:T(8,128)(2,1)S(1)} %fusion.1.low.refs_1_) | copy-start | bytes 165892
  176.0 71.4 %collective-permute-start.20 = (bf16[512,2048]{1,0:T(8,128)(2,1)}, bf16[512,2048]{1,0:T(8,128)(2,1)}, u32[]{:S(2)}, u32[]{:S(2)}) collective-permute-start(bf16[512,2048]{1,0:T(8,128)(2,1)} %get-tuple-element.137.refs_5_), channel_id=1, source_target_pairs={{0,64},{1,67},{2,66},{3,65},{4,68},{5,71},{6,70},{7,69},{8,72},{9,... | collective-permute-start | bytes 6291464 | tf_op jit(solution)/shard_map/ppermute | solution.py:71
  179.4 67.9 %collective-permute-start.16 = (bf16[512,2048]{1,0:T(8,128)(2,1)}, bf16[512,2048]{1,0:T(8,128)(2,1)}, u32[]{:S(2)}, u32[]{:S(2)}) collective-permute-start(bf16[512,2048]{1,0:T(8,128)(2,1)} %get-tuple-element.131.refs_1_), channel_id=1, source_target_pairs={{0,64},{1,67},{2,66},{3,65},{4,68},{5,71},{6,70},{7,69},{8,72},{9,... | collective-permute-start | bytes 6291464 | tf_op jit(solution)/shard_map/ppermute | solution.py:71
  194.9 3.0 collective-permute-start.19
  247.3 54.4 %copy-start.10 = (bf16[8,288,384]{2,1,0:T(8,128)(2,1)}, bf16[8,288,384]{2,1,0:T(8,128)(2,1)S(1)}, u32[]{:S(2)}) copy-start(bf16[8,288,384]{2,1,0:T(8,128)(2,1)S(1)} %all_to_all.45) | copy-start | bytes 5308420
  247.4 54.4 %copy-start.53 = (bf16[32,1024]{1,0:T(8,128)(2,1)S(1)}, bf16[32,1024]{1,0:T(8,128)(2,1)}, u32[]{:S(2)}) copy-start(bf16[32,1024]{1,0:T(8,128)(2,1)} %get-tuple-element.143.down) | copy-start | bytes 196612
  247.4 54.4 %copy-start.57 = (s32[8]{0:T(128)S(1)}, s32[8]{0:T(128)}, u32[]{:S(2)}) copy-start(s32[8]{0:T(128)} %copy-done.56) | copy-start | bytes 100
  247.4 59.3 %collective-permute-start.23 = (bf16[512,2048]{1,0:T(8,128)(2,1)}, bf16[512,2048]{1,0:T(8,128)(2,1)S(1)}, u32[]{:S(2)}, u32[]{:S(2)}) collective-permute-start(bf16[512,2048]{1,0:T(8,128)(2,1)} %collective-permute-done.20.refs_6_), channel_id=1, source_target_pairs={{0,64},{1,67},{2,66},{3,65},{4,68},{5,71},{6,70},{7,69},{8,72},{9,... | collective-permute-start | bytes 6291464 | tf_op jit(solution)/shard_map/ppermute | solution.py:71
  250.6 56.1 %collective-permute-start.21 = (bf16[512,2048]{1,0:T(8,128)(2,1)}, bf16[512,2048]{1,0:T(8,128)(2,1)S(1)}, u32[]{:S(2)}, u32[]{:S(2)}) collective-permute-start(bf16[512,2048]{1,0:T(8,128)(2,1)} %collective-permute-done.16.refs_2_), channel_id=1, source_target_pairs={{0,64},{1,67},{2,66},{3,65},{4,68},{5,71},{6,70},{7,69},{8,72},{9,... | collective-permute-start | bytes 6291464 | tf_op jit(solution)/shard_map/ppermute | solution.py:71
  258.5 43.2 %copy-start.64 = (f32[2,1152,128]{2,1,0:T(8,128)}, f32[2,1152,128]{2,1,0:T(8,128)S(1)}, u32[]{:S(2)}) copy-start(f32[2,1152,128]{2,1,0:T(8,128)S(1)} %get-tuple-element.181.exact) | copy-start | bytes 3538948
  306.7 11.4 %copy-start.69 = (bf16[512,2048]{1,0:T(8,128)(2,1)}, bf16[512,2048]{1,0:T(8,128)(2,1)S(1)}, u32[]{:S(2)}) copy-start(bf16[512,2048]{1,0:T(8,128)(2,1)S(1)} %collective-permute-done.23.refs_7_) | copy-start | bytes 6291460
  306.7 25.4 %copy-start.70 = (bf16[512,2048]{1,0:T(8,128)(2,1)}, bf16[512,2048]{1,0:T(8,128)(2,1)S(1)}, u32[]{:S(2)}) copy-start(bf16[512,2048]{1,0:T(8,128)(2,1)S(1)} %collective-permute-done.21.refs_3_) | copy-start | bytes 6291460
  306.7 25.4 %collective-permute-start.22 = (bf16[512,2048]{1,0:T(8,128)(2,1)S(1)}, bf16[512,2048]{1,0:T(8,128)(2,1)S(1)}, u32[]{:S(2)}, u32[]{:S(2)}) collective-permute-start(bf16[512,2048]{1,0:T(8,128)(2,1)S(1)} %collective-permute-done.21.refs_3_), channel_id=1, source_target_pairs={{0,64},{1,67},{2,66},{3,65},{4,68},{5,71},{6,70},{7,69},{8,72},{9,... | collective-permute-start | bytes 6291464 | tf_op jit(solution)/shard_map/ppermute | solution.py:71
  307.9 46.6 %collective-permute-start.24 = (bf16[512,2048]{1,0:T(8,128)(2,1)S(1)}, bf16[512,2048]{1,0:T(8,128)(2,1)}, u32[]{:S(2)}, u32[]{:S(2)}) collective-permute-start(bf16[512,2048]{1,0:T(8,128)(2,1)S(1)} %collective-permute-done.23.refs_7_), channel_id=1, source_target_pairs={{0,64},{1,67},{2,66},{3,65},{4,68},{5,71},{6,70},{7,69},{8,72},{9,... | collective-permute-start | bytes 6291464 | tf_op jit(solution)/shard_map/ppermute | solution.py:71
  310.2 2.5 collective-permute-start.25
  315.7 2.4 collective-permute-start.26
  318.1 13.9 %copy-start.78 = (bf16[144,2176]{1,0:T(8,128)(2,1)}, bf16[144,2176]{1,0:T(8,128)(2,1)S(1)}, u32[]{:S(2)}) copy-start(bf16[144,2176]{1,0:T(8,128)(2,1)S(1)} %collective-permute-done.26.refs_10_) | copy-start | bytes 1880068
  354.5 32.7 %copy-start.7 = (bf16[1,144,2048]{2,1,0:T(8,128)(2,1)S(1)}, bf16[1,144,2048]{2,1,0:T(8,128)(2,1)}, u32[]{:S(2)}) copy-start(bf16[1,144,2048]{2,1,0:T(8,128)(2,1)} %param.17) | copy-start | bytes 1769476
  354.5 32.7 %copy-start.31 = (f32[4,2048]{1,0:T(4,128)S(1)}, f32[4,2048]{1,0:T(4,128)}, u32[]{:S(2)}) copy-start(f32[4,2048]{1,0:T(4,128)} %gains.9) | copy-start | bytes 98308
  354.5 32.7 %copy-start.44 = (bf16[32,2048]{1,0:T(8,128)(2,1)S(1)}, bf16[32,2048]{1,0:T(8,128)(2,1)}, u32[]{:S(2)}) copy-start(bf16[32,2048]{1,0:T(8,128)(2,1)} %get-tuple-element.162.up.refs_11_) | copy-start | bytes 393220
  381.1 6.1 collective-permute-start.27
  392.8 2.1 collective-permute-start.28
  395.7 29.4 %copy-start.60 = (bf16[288,64]{1,0:T(8,128)(2,1)S(1)}, bf16[288,64]{1,0:T(8,128)(2,1)}, u32[]{:S(2)}) copy-start(bf16[288,64]{1,0:T(8,128)(2,1)} %get-tuple-element.170.refs_0_) | copy-start | bytes 110596
  424.6 9.2 %collective-permute-start.29 = (bf16[144,2176]{1,0:T(8,128)(2,1)}, bf16[144,2176]{1,0:T(8,128)(2,1)S(1)}, u32[]{:S(2)}, u32[]{:S(2)}) collective-permute-start(bf16[144,2176]{1,0:T(8,128)(2,1)} %get-tuple-element.167), channel_id=1, source_target_pairs={{0,1},{1,0},{2,3},{3,2},{4,5},{5,4},{6,7},{7,6},{8,9},{9,8},{10,11... | collective-permute-start | bytes 1880072 | tf_op jit(solution)/shard_map/ppermute | solution.py:61
  436.9 16.7 %all-to-all-start.3 = ((bf16[8,32,1664]{2,1,0:T(8,128)(2,1)}), bf16[8,32,1664]{2,1,0:T(8,128)(2,1)}, u32[]{:S(2)}, u32[]{:S(2)}) async-start(bf16[8,32,1664]{2,1,0:T(8,128)(2,1)} %early_gradients.1), calls=%async_computation.3 | async-start | bytes 1703936 | tf_op jit(solution)/shard_map/all_to_all | solution.py:1143
  441.3 2.4 collective-permute-start.30
  453.6 17.3 %all-to-all-start.2 = ((bf16[8,416,128]{2,1,0:T(8,128)(2,1)}), bf16[8,416,128]{2,1,0:T(8,128)(2,1)}, u32[]{:S(2)}, u32[]{:S(2)}) async-start(bf16[8,416,128]{2,1,0:T(8,128)(2,1)} %copy-done.29), calls=%async_computation.2 | async-start | bytes 1703936 | tf_op jit(solution)/shard_map/all_to_all | solution.py:1146
  461.3 20.2 %copy-start.11 = (bf16[8,288,384]{2,1,0:T(8,128)(2,1)S(1)}, bf16[8,288,384]{2,1,0:T(8,128)(2,1)}, u32[]{:S(2)}) copy-start(bf16[8,288,384]{2,1,0:T(8,128)(2,1)} %copy-done.10) | copy-start | bytes 5308420
  477.0 22.4 %all-to-all-start.4 = ((bf16[8,32,2304]{2,1,0:T(8,128)(2,1)}), bf16[8,32,2304]{2,1,0:T(8,128)(2,1)}, u32[]{:S(2)}, u32[]{:S(2)}) async-start(bf16[8,32,2304]{2,1,0:T(8,128)(2,1)} %broadcast_in_dim.44), calls=%async_computation.4 | async-start | bytes 2359296 | tf_op jit(solution)/shard_map/all_to_all | solution.py:1087
  499.4 26.1 %all-to-all-start.5 = ((bf16[8,2,144,384]{3,2,1,0:T(8,128)(2,1)}), bf16[8,2,144,384]{3,2,1,0:T(8,128)(2,1)S(1)}, u32[]{:S(2)}, u32[]{:S(2)}) async-start(bf16[8,2,144,384]{3,2,1,0:T(8,128)(2,1)} %copy-done.12), calls=%async_computation.5 | async-start | bytes 3538944 | tf_op jit(solution)/shard_map/all_to_all | solution.py:1155
  504.4 89.6 %all-gather.9.cloned.1.call-start = ((), (), s32[]{:S(2)}) async-start(), calls=%async_computation.11 | async-start | bytes 5013504 | tf_op jit(solution)/shard_map/all_gather | solution.py:1163
  530.8 2.2 collective-permute-start.31
  537.5 12.8 %copy-start.22 = (f32[144,2048]{1,0:T(8,128)S(1)}, f32[144,2048]{1,0:T(8,128)}, u32[]{:S(2)}) copy-start(f32[144,2048]{1,0:T(8,128)} %copy-done.21) | copy-start | bytes 3538948
  537.5 12.8 %copy-start.50 = (bf16[96,2048]{1,0:T(8,128)(2,1)S(1)}, bf16[96,2048]{1,0:T(8,128)(2,1)}, u32[]{:S(2)}) copy-start(bf16[96,2048]{1,0:T(8,128)(2,1)} %get-tuple-element.132.down) | copy-start | bytes 1179652
  548.3 2.1 collective-permute-start.32
  552.0 1.2 collective-permute-start.33
  594.0 7.9 %collective-permute-start.34 = (bf16[8,8,16,2176]{3,2,1,0:T(8,128)(2,1)}, bf16[8,8,16,2176]{3,2,1,0:T(8,128)(2,1)}, u32[]{:S(2)}, u32[]{:S(2)}) collective-permute-start(bf16[8,8,16,2176]{3,2,1,0:T(8,128)(2,1)} %bitcast.66), channel_id=1, source_target_pairs={{0,1},{1,0},{2,3},{3,2},{4,5},{5,4},{6,7},{7,6},{8,9},{9,8},{10,11... | collective-permute-start | bytes 13369352 | tf_op jit(solution)/shard_map/ppermute | solution.py:61
  596.1 27.6 %all-to-all-start.8 = ((bf16[8,128,768]{2,1,0:T(8,128)(2,1)}), bf16[8,128,768]{2,1,0:T(8,128)(2,1)S(1)}, u32[]{:S(2)}, u32[]{:S(2)}) async-start(bf16[8,128,768]{2,1,0:T(8,128)(2,1)} %broadcast_in_dim.48), calls=%async_computation.8 | async-start | bytes 3145728 | tf_op jit(solution)/shard_map/all_to_all | solution.py:1087
  623.8 4.0 collective-permute-start.35
  (60 other events, 169.9 us)
Sparse Core Ops, SparseCore 0:
  28.8 72.1 all-gather.6
  103.8 237.0 all-gather.4
  526.8 58.9 all-gather.8

commit v6 on v5

--- a/solution.py
+++ b/solution.py
@@ -492,7 +492,7 @@
         out_shape=[_f32(rows, 3 * HALF), _f32(rows, 128)],
         in_specs=[whole(x), column(D), whole(low), column(maps_up.shape[0])],
         out_specs=[column(rows), pl.BlockSpec((rows, 128), lambda i: (0, 0))],
-        compiler_params=pltpu.CompilerParams(vmem_limit_bytes=32 * 2**20),
+        compiler_params=pltpu.CompilerParams(vmem_limit_bytes=60 * 2**20),
         cost_estimate=pl.CostEstimate(flops=2 * rows * D * 3 * HALF, bytes_accessed=18_000_000, transcendentals=0),
         name="project_qkv",
     )(x, w, low, maps_up)
@@ -974,7 +974,7 @@
         in_specs=[_smem()] + [pl.BlockSpec((8, 1) + v.shape[2:], lambda i: (0, i, 0, 0)) for v in arrays]
         + [pl.BlockSpec((1,) + v.shape[1:], lambda i: (i, 0, 0, 0)) for v in done],
         out_specs=[pl.BlockSpec((1,) + s[1:], lambda i, n=len(s): (i,) + (0,) * (n - 1)) for s in shapes],
-        compiler_params=pltpu.CompilerParams(vmem_limit_bytes=40 * 2**20),
+        compiler_params=pltpu.CompilerParams(vmem_limit_bytes=60 * 2**20),
         cost_estimate=pl.CostEstimate(flops=0, bytes_accessed=size, transcendentals=0),
         name=name,
     )(core, *arrays, *done)

time: 654 us -> 645 us (0.986)
  local copies, waits for them, and re-layouts: 73 us -> 46.7 us
  Pallas kernels: 160 us -> 173 us
  waiting for transfers between devices: 170 us -> 177 us
    unnamed x166 -> x164, local copies, waits for them, and re-layouts: 63.5 us -> 39.3 us
  transfers between devices with their start and end apart: 44 -> 44, of which waited for: 28 -> 29; matrix products, arithmetic and copies ran while one was open for 3% -> 3% of each run, Pallas kernels for 15% -> 16%
where the time goes in v6:
time: 645 us; the launch traced here: 635 us
  waiting for transfers between devices  177 us (27%)
  Pallas kernels  173 us (27%)
  blocking collectives  124 us (19%)
  starting transfers between devices  89.1 us (14%)
  local copies, waits for them, and re-layouts  46.7 us (7%)
  between operations  15.2 us (2%)
  other arithmetic  7.7 us (1%)
    ppermute x20, waiting for transfers between devices, send(): self.last = lax.ppermute(value, ALL, STEPS[how])  115 us
    pallas_call x2, Pallas kernels, call(): pl.pallas_call(body, out_shape=outs, in_specs=[_smem()] + [anywhere] * 9...  55.8 us
    ppermute x20, starting transfers between devices, send(): self.last = lax.ppermute(value, ALL, STEPS[how])  46.4 us
    all_to_all x1, blocking collectives, on_device(): lax.all_to_all(packed, CTX, 0, 0, tiled=True).reshape(8, 2, ROWS, 3 * HD)  44.5 us
    all_to_all x1, blocking collectives, on_device(): lax.all_to_all(out_heads, CTX, 0, 0, tiled=True).reshape(8, 2 * ROWS, HD)  42.8 us
    unnamed x164, local copies, waits for them, and re-layouts  39.3 us
    pallas_call x14, Pallas kernels, _plain(): pl.pallas_call(body, out_shape=outs, in_specs=[_smem()] * len(scalars) +...  35.3 us
    all_to_all x1, blocking collectives, spread_over(): lax.all_to_all(jnp.broadcast_to(value[None], (8,) + value.shape), axes, 0...  21.5 us
  transfers between devices with their start and end apart: 44, of which 29 were waited for; matrix products, arithmetic and copies ran while one was open for 3% of the time, Pallas kernels for 16%

profile of v6, /device:TPU:7, one launch (start us, length us, event | category | flops | bytes accessed | tf_op | source)
XLA Modules:
  0.0 634.7 jit_solution(5076202595482067174)
XLA Ops:
  12.2 1.9 collective-permute-done.1.got
  15.7 3.8 collective-permute-start.2
  19.6 2.7 collective-permute-start.4
  22.3 5.5 collective-permute-done.4
  28.8 3.4 split_g.1
  34.1 6.8 %collective-permute-done.3.refs_2_ = bf16[256,1024]{1,0:T(8,128)(2,1)S(1)} collective-permute-done((bf16[256,1024]{1,0:T(8,128)(2,1)S(1)}, bf16[256,1024]{1,0:T(8,128)(2,1)S(1)}, u32[]{:S(2)}, u32[]{:S(2)}) %collective-permute-start.3) | collective-permute-done | bytes 524320 | tf_op jit(solution)/shard_map/ppermute | solution.py:71
  40.9 3.5 collective-permute-start.6
  45.8 2.4 parts_m.1
  48.2 3.2 collective-permute-start.5
  51.4 4.5 collective-permute-done.6.refs_3_
  56.7 2.7 collective-permute-start.7
  61.7 13.5 %collective-permute-done.5 = bf16[256,2048]{1,0:T(8,128)(2,1)S(1)} collective-permute-done((bf16[256,2048]{1,0:T(8,128)(2,1)S(1)}, bf16[256,2048]{1,0:T(8,128)(2,1)S(1)}, u32[]{:S(2)}, u32[]{:S(2)}) %collective-permute-start.5) | collective-permute-done | bytes 1048608 | tf_op jit(solution)/shard_map/ppermute | solution.py:71
  75.2 9.2 %collective-permute-done.7.refs_2_ = bf16[512,1024]{1,0:T(8,128)(2,1)S(1)} collective-permute-done((bf16[512,1024]{1,0:T(8,128)(2,1)S(1)}, bf16[512,1024]{1,0:T(8,128)(2,1)S(1)}, u32[]{:S(2)}, u32[]{:S(2)}) %collective-permute-start.7) | collective-permute-done | bytes 1048608 | tf_op jit(solution)/shard_map/ppermute | solution.py:71
  84.4 11.2 %collective-permute-done.8.refs_6_ = bf16[512,1024]{1,0:T(8,128)(2,1)S(1)} collective-permute-done((bf16[512,1024]{1,0:T(8,128)(2,1)S(1)}, bf16[512,1024]{1,0:T(8,128)(2,1)S(1)}, u32[]{:S(2)}, u32[]{:S(2)}) %collective-permute-start.8) | collective-permute-done | bytes 1048608 | tf_op jit(solution)/shard_map/ppermute | solution.py:71
  100.2 3.6 collective-permute-start.12
  103.9 8.5 %collective-permute-done.9.refs_1_ = bf16[256,2048]{1,0:T(8,128)(2,1)} collective-permute-done((bf16[256,2048]{1,0:T(8,128)(2,1)S(1)}, bf16[256,2048]{1,0:T(8,128)(2,1)}, u32[]{:S(2)}, u32[]{:S(2)}) %collective-permute-start.9) | collective-permute-done | bytes 1048608 | tf_op jit(solution)/shard_map/ppermute | solution.py:71
  112.4 2.4 collective-permute-start.10
  116.9 2.8 collective-permute-start.13
  119.7 7.2 %collective-permute-done.14.refs_7_ = bf16[512,1024]{1,0:T(8,128)(2,1)} collective-permute-done((bf16[512,1024]{1,0:T(8,128)(2,1)}, bf16[512,1024]{1,0:T(8,128)(2,1)}, u32[]{:S(2)}, u32[]{:S(2)}) %collective-permute-start.14) | collective-permute-done | bytes 1048608 | tf_op jit(solution)/shard_map/ppermute | solution.py:71
  126.9 3.4 collective-permute-start.15
  130.3 11.0 %collective-permute-done.10.refs_2_ = bf16[256,2048]{1,0:T(8,128)(2,1)} collective-permute-done((bf16[256,2048]{1,0:T(8,128)(2,1)}, bf16[256,2048]{1,0:T(8,128)(2,1)}, u32[]{:S(2)}, u32[]{:S(2)}) %collective-permute-start.10) | collective-permute-done | bytes 1048608 | tf_op jit(solution)/shard_map/ppermute | solution.py:71
  141.3 3.4 collective-permute-start.11
  145.4 3.8 choose_adapters.1
  155.7 12.1 %assemble.1 = (bf16[2048,3072]{1,0:T(8,128)(2,1)}, bf16[1024,2048]{1,0:T(8,128)(2,1)}) custom-call(s32[3,4]{1,0:T(4,128)S(1)} %pad_add_fusion.places, bf16[4,4,2,256,512]{4,3,2,1,0:T(8,128)(2,1)} %bitcast.78, bf16[512,1024]{1,0:T(8,128)(2,1)S(1)} %copy-done.20, bf16[512,1024]{1,0:T(8,128)(2,1)S(1)} %copy-done.24, ...), custom_call_target="tpu_custom_call" | custom-call | bytes 67108864 | tf_op jit(solution)/shard_map/assemble/pallas_call | solution.py:255
  167.9 4.0 collective-permute-done.11.refs_3_
  171.8 4.3 spread_g.1
  176.1 3.3 collective-permute-start.20
  179.4 11.7 %project_qkv.1 = (f32[288,3072]{1,0:T(8,128)}, f32[288,128]{1,0:T(8,128)}) custom-call(bf16[288,2048]{1,0:T(8,128)(2,1)} %bitcast.63, bf16[2048,3072]{1,0:T(8,128)(2,1)} %get-tuple-element.128.w, bf16[288,96]{1,0:T(8,128)(2,1)} %fusion.1.low.refs_1_, bf16[96,3072]{1,0:T(8,128)(2,1)} %get-tuple-element.133.up), custom_call_target="tpu_custom_call" | custom-call | flops 3623878656 | bytes 18000000 | tf_op jit(solution)/shard_map/project_qkv/pallas_call | solution.py:489
  191.2 2.4 collective-permute-start.19
  195.7 4.0 pack_heads.1
  199.8 44.5 %all_to_all.45 = bf16[8,288,384]{2,1,0:T(8,128)(2,1)S(1)} all-to-all(bf16[8,288,384]{2,1,0:T(8,128)(2,1)} %pack_heads.1), channel_id=1, replica_groups=mesh['yl'=2,'x'=4,'z'=4,'yh'=2,'c'=2] {'yl','x'}, dimensions={0} | all-to-all | bytes 3538944 | tf_op jit(solution)/shard_map/all_to_all | solution.py:1113
  244.2 3.6 collective-permute-start.23
  248.2 6.6 %attend.1 = (bf16[8,2,144,128]{3,2,1,0:T(8,128)(2,1)S(1)}, f32[2,1152,128]{2,1,0:T(8,128)S(1)}, f32[2,1152,1]{2,1,0:T(8,128)S(1)}) custom-call(s32[2]{0:T(128)S(1)} %get-tuple-element.204.bounds, bf16[8,2,144,384]{3,2,1,0:T(8,128)(2,1)S(1)} %bitcast.70), custom_call_target="tpu_custom_call" | custom-call | flops 900000000 | bytes 5000000 | tf_op jit(solution)/shard_map/attend/pallas_call | solution.py:800
  255.8 42.8 %all_to_all.46 = bf16[8,2,144,128]{3,2,1,0:T(8,128)(2,1)S(1)} all-to-all(bf16[8,2,144,128]{3,2,1,0:T(8,128)(2,1)S(1)} %get-tuple-element.141), channel_id=1, replica_groups=mesh['yl'=2,'x'=4,'z'=4,'yh'=2,'c'=2] {'yl','x'}, dimensions={0} | all-to-all | bytes 1179648 | tf_op jit(solution)/shard_map/all_to_all | solution.py:1117
  298.6 4.2 project_out.1
  305.3 2.3 collective-permute-start.24
  307.6 2.1 collective-permute-start.25
  316.8 12.2 %collective-permute-done.22.refs_4_ = bf16[512,2048]{1,0:T(8,128)(2,1)S(1)} collective-permute-done((bf16[512,2048]{1,0:T(8,128)(2,1)S(1)}, bf16[512,2048]{1,0:T(8,128)(2,1)S(1)}, u32[]{:S(2)}, u32[]{:S(2)}) %collective-permute-start.22) | collective-permute-done | bytes 2097184 | tf_op jit(solution)/shard_map/ppermute | solution.py:71
  330.4 21.1 %collective-permute-done.24.refs_8_ = bf16[512,2048]{1,0:T(8,128)(2,1)} collective-permute-done((bf16[512,2048]{1,0:T(8,128)(2,1)S(1)}, bf16[512,2048]{1,0:T(8,128)(2,1)}, u32[]{:S(2)}, u32[]{:S(2)}) %collective-permute-start.24) | collective-permute-done | bytes 2097184 | tf_op jit(solution)/shard_map/ppermute | solution.py:71
  351.5 26.7 %feed_forward.1 = (bf16[288,8192]{1,0:T(8,128)(2,1)}, bf16[288,4096]{1,0:T(8,128)(2,1)}, bf16[288,2176]{1,0:T(8,128)(2,1)}, bf16[288,64]{1,0:T(8,128)(2,1)}, f32...) custom-call(s32[3,4]{1,0:T(4,128)} %copy-done.55, bf16[4,4,2,256,2048]{4,3,2,1,0:T(8,128)(2,1)} %bitcast.76, ...), custom_call_target="tpu_custom_call" | custom-call | flops 14495514624 | bytes 53157888 | tf_op jit(solution)/shard_map/feed_forward/pallas_call | solution.py:358
  378.2 5.5 collective-permute-start.27
  383.7 1.9 collective-permute-done.27.got
  386.9 2.1 combine_output.1
  392.0 29.1 %feed_forward_back.1 = (bf16[288,8192]{1,0:T(8,128)(2,1)}, bf16[288,2176]{1,0:T(8,128)(2,1)}, bf16[288,32]{1,0:T(8,128)(2,1)}, f32[144,2176]{1,0:T(8,128)}, bf16[144,2176]{1,0:T(8,128)(2,1)}) custom-call(s32[3,4]{1,0:T(4,128)} %copy-done.55, bf16[4,4,2,256,2048]{4,3,2,1,0:T(8,128)(2,1)} %bitcast.77, bf16[512,2048]{1,0:T(8,128)(2,1)} %get-tuple-element.131.refs_1_, ...), custom_call_target="tpu_custom_call" | custom-call | flops 14495514624 | bytes 57745408 | tf_op jit(solution)/shard_map/feed_forward_back/pallas_call | solution.py:358
  425.3 4.9 early_gradients.1
  432.5 5.0 all-to-all-start.3
  442.3 6.0 project_out_back.1
  449.2 5.6 all-to-all-start.2
  456.7 9.7 %all-to-all-done.2.grad = bf16[8,416,128]{2,1,0:T(8,128)(2,1)S(1)} async-done(((bf16[8,416,128]{2,1,0:T(8,128)(2,1)}), bf16[8,416,128]{2,1,0:T(8,128)(2,1)S(1)}, u32[]{:S(2)}, u32[]{:S(2)}) %all-to-all-start.2) | async-done | bytes 852000 | tf_op jit(solution)/shard_map/all_to_all | solution.py:1146
  467.7 4.4 all-to-all-start.4
  474.7 8.0 %attend_back.1 = bf16[8,2,144,384]{3,2,1,0:T(8,128)(2,1)} custom-call(s32[2]{0:T(128)S(1)} %copy-done.57, bf16[8,2,144,384]{3,2,1,0:T(8,128)(2,1)S(1)} %bitcast.71, bf16[8,416,128]{2,1,0:T(8,128)(2,1)S(1)} %all-to-all-done.2.grad, f32[2,1152,128]{2,1,0:T(8,128)S(1)} %copy-done.60, f32[2,1152,1]{2,1,0:T(8,128)S(1)} %copy-done.62), custom_call_target="tpu_custom_call" | custom-call | flops 2300000000 | bytes 8000000 | tf_op jit(solution)/shard_map/attend_back/pallas_call | solution.py:848
  482.7 7.6 %all-to-all-done.4 = bf16[8,32,2304]{2,1,0:T(8,128)(2,1)} async-done(((bf16[8,32,2304]{2,1,0:T(8,128)(2,1)}), bf16[8,32,2304]{2,1,0:T(8,128)(2,1)}, u32[]{:S(2)}, u32[]{:S(2)}) %all-to-all-start.4) | async-done | bytes 1179680 | tf_op jit(solution)/shard_map/all_to_all | solution.py:1087
  490.3 5.3 all-to-all-start.5
  496.3 2.3 slice.32
  501.5 15.5 %all-to-all-done.5 = bf16[8,2,144,384]{3,2,1,0:T(8,128)(2,1)S(1)} async-done(((bf16[8,2,144,384]{3,2,1,0:T(8,128)(2,1)}), bf16[8,2,144,384]{3,2,1,0:T(8,128)(2,1)S(1)}, u32[]{:S(2)}, u32[]{:S(2)}) %all-to-all-start.5) | async-done | bytes 1769504 | tf_op jit(solution)/shard_map/all_to_all | solution.py:1155
  518.3 4.1 unpack_heads.1
  528.8 10.7 %project_qkv_back.1 = (bf16[288,3072]{1,0:T(8,128)(2,1)}, f32[144,2176]{1,0:T(8,128)S(1)}, bf16[144,2176]{1,0:T(8,128)(2,1)S(1)}) custom-call(s32[8]{0:T(128)S(1)} %copy-done.51, f32[288,1024]{1,0:T(8,128)S(1)} %copy-done.13, f32[288,1024]{1,0:T(8,128)S(1)} %copy-done.14, bf16[288,1024]{1,0:T(8,128)(2,1)S(1)} %copy-done.28, ...), custom_call_target="tpu_custom_call" | custom-call | flops 3623878656 | bytes 22000000 | tf_op jit(solution)/shard_map/project_qkv_back/pallas_call | solution.py:640
  546.1 15.6 %all_to_all.47 = bf16[8,32,768]{2,1,0:T(8,128)(2,1)S(1)} all-to-all(bf16[8,32,768]{2,1,0:T(8,128)(2,1)S(1)} %late_gradients.1), channel_id=1, replica_groups=mesh['yl'=2,'x'=4,'z'=4,'yh'=2,'c'=2] {'yl','x'}, dimensions={0} | all-to-all | bytes 786432 | tf_op jit(solution)/shard_map/all_to_all | solution.py:1178
  561.9 21.5 %all_to_all.48 = bf16[8,32,768]{2,1,0:T(8,128)(2,1)S(1)} all-to-all(bf16[8,32,768]{2,1,0:T(8,128)(2,1)S(1)} %broadcast_in_dim.46), channel_id=1, replica_groups=mesh['yl'=2,'x'=4,'z'=4,'yh'=2,'c'=2] {'z','yh'}, dimensions={0} | all-to-all | bytes 786432 | tf_op jit(solution)/shard_map/all_to_all | solution.py:1087
  585.5 5.7 all-to-all-start.8
  591.2 11.0 %early_outputs.1 = (f32[8,2,16,8192]{3,2,1,0:T(8,128)}, f32[8,16,8192]{2,1,0:T(8,128)}, f32[8,5,16,2048]{3,2,1,0:T(8,128)}) custom-call(s32[8]{0:T(128)} %copy-done.47, bf16[8,8,16,2176]{3,2,1,0:T(8,128)(2,1)} %bitcast.83, bf16[8,8,16,2176]{3,2,1,0:T(8,128)(2,1)} %collective-permute-done.34.refs_1_), custom_call_target="tpu_custom_call" | custom-call | bytes 8912896 | tf_op jit(solution)/shard_map/early_outputs/pallas_call | solution.py:970
  602.2 10.9 %all-to-all-done.8 = bf16[8,128,768]{2,1,0:T(8,128)(2,1)S(1)} async-done(((bf16[8,128,768]{2,1,0:T(8,128)(2,1)}), bf16[8,128,768]{2,1,0:T(8,128)(2,1)S(1)}, u32[]{:S(2)}, u32[]{:S(2)}) %all-to-all-start.8) | async-done | bytes 1572896 | tf_op jit(solution)/shard_map/all_to_all | solution.py:1087
  614.0 3.0 collective-permute-done.35
  618.2 9.8 %late_outputs.1 = (f32[8,6,16,2048]{3,2,1,0:T(8,128)}, f32[8,5,16,2048]{3,2,1,0:T(8,128)}) custom-call(s32[8]{0:T(128)} %copy-done.47, bf16[8,8,16,768]{3,2,1,0:T(8,128)(2,1)} %bitcast.80, bf16[8,8,16,768]{3,2,1,0:T(8,128)(2,1)} %bitcast.85, f32[8,5,16,2048]{3,2,1,0:T(8,128)} %get-tuple-element.199.refs_2_), custom_call_target="tpu_custom_call" | custom-call | bytes 3145728 | tf_op jit(solution)/shard_map/late_outputs/pallas_call | solution.py:970
  (268 shorter events, 85.8 us)
Async XLA Ops:
  7.2 144.8 %all-gather.7.cloned.1.call-start = ((), (), s32[]{:S(2)}) async-start(), calls=%async_computation.10 | async-start | bytes 8912896 | tf_op jit(solution)/shard_map/all_gather | solution.py:677
  10.4 161.4 %copy-start.47 = (s32[8]{0:T(128)}, s32[8]{0:T(128)S(1)}, u32[]{:S(2)}) copy-start(s32[8]{0:T(128)S(1)} %stack.141.core.me) | copy-start | bytes 100
  11.4 2.7 collective-permute-start.1
  15.7 12.1 %collective-permute-start.2 = (bf16[256,1024]{1,0:T(8,128)(2,1)S(1)}, bf16[256,1024]{1,0:T(8,128)(2,1)S(1)}, u32[]{:S(2)}, u32[]{:S(2)}) collective-permute-start(bf16[256,1024]{1,0:T(8,128)(2,1)S(1)} %get-tuple-element.110.refs_0_), channel_id=1, source_target_pairs={{0,4},{1,13},{2,6},{3,15},{4,8},{5,1},{6,10},{7,3},{8,12},{9,5},{1... | collective-permute-start | bytes 1572872 | tf_op jit(solution)/shard_map/ppermute | solution.py:71
  19.6 8.2 %collective-permute-start.4 = (bf16[256,512]{1,0:T(8,128)(2,1)S(1)}, bf16[256,512]{1,0:T(8,128)(2,1)S(1)}, u32[]{:S(2)}, u32[]{:S(2)}) collective-permute-start(bf16[256,512]{1,0:T(8,128)(2,1)S(1)} %get-tuple-element.113), channel_id=1, source_target_pairs={{0,66},{1,67},{2,64},{3,65},{4,70},{5,71},{6,68},{7,69},{8,74},{9,... | collective-permute-start | bytes 786440 | tf_op jit(solution)/shard_map/ppermute | solution.py:71
  28.7 322.8 %all-gather.5.cloned.1.call-start = ((), (), s32[]{:S(2)}) async-start(), calls=%async_computation.9 | async-start | bytes 35651584 | tf_op jit(solution)/shard_map/all_gather | solution.py:677
  32.1 12.3 %collective-permute-start = (bf16[128,8192]{1,0:T(8,128)(2,1)S(1)}, bf16[128,8192]{1,0:T(8,128)(2,1)S(1)}, u32[]{:S(2)}, u32[]{:S(2)}) collective-permute-start(bf16[128,8192]{1,0:T(8,128)(2,1)S(1)} %get-tuple-element.106), channel_id=1, source_target_pairs={{0,1},{1,0},{2,3},{3,2},{4,5},{5,4},{6,7},{7,6},{8,9},{9,8},{10,11... | collective-permute-start | bytes 6291464 | tf_op jit(solution)/shard_map/ppermute | solution.py:61
  32.2 8.7 %collective-permute-start.3 = (bf16[256,1024]{1,0:T(8,128)(2,1)S(1)}, bf16[256,1024]{1,0:T(8,128)(2,1)S(1)}, u32[]{:S(2)}, u32[]{:S(2)}) collective-permute-start(bf16[256,1024]{1,0:T(8,128)(2,1)S(1)} %collective-permute-done.2.refs_1_), channel_id=1, source_target_pairs={{0,4},{1,13},{2,6},{3,15},{4,8},{5,1},{6,10},{7,3},{8,12},{9,5},{1... | collective-permute-start | bytes 1572872 | tf_op jit(solution)/shard_map/ppermute | solution.py:71
  40.9 15.0 %collective-permute-start.6 = (bf16[256,1024]{1,0:T(8,128)(2,1)S(1)}, bf16[256,1024]{1,0:T(8,128)(2,1)S(1)}, u32[]{:S(2)}, u32[]{:S(2)}) collective-permute-start(bf16[256,1024]{1,0:T(8,128)(2,1)S(1)} %collective-permute-done.3.refs_2_), channel_id=1, source_target_pairs={{0,4},{1,13},{2,6},{3,15},{4,8},{5,1},{6,10},{7,3},{8,12},{9,5},{1... | collective-permute-start | bytes 1572872 | tf_op jit(solution)/shard_map/ppermute | solution.py:71
  48.2 27.0 %collective-permute-start.5 = (bf16[256,2048]{1,0:T(8,128)(2,1)S(1)}, bf16[256,2048]{1,0:T(8,128)(2,1)S(1)}, u32[]{:S(2)}, u32[]{:S(2)}) collective-permute-start(bf16[256,2048]{1,0:T(8,128)(2,1)S(1)} %get-tuple-element.114), channel_id=1, source_target_pairs={{0,66},{1,67},{2,64},{3,65},{4,70},{5,71},{6,68},{7,69},{8,74},{9,... | collective-permute-start | bytes 3145736 | tf_op jit(solution)/shard_map/ppermute | solution.py:71
  56.7 27.8 %collective-permute-start.7 = (bf16[512,1024]{1,0:T(8,128)(2,1)S(1)}, bf16[512,1024]{1,0:T(8,128)(2,1)S(1)}, u32[]{:S(2)}, u32[]{:S(2)}) collective-permute-start(bf16[512,1024]{1,0:T(8,128)(2,1)S(1)} %get-tuple-element.116.refs_1_), channel_id=1, source_target_pairs={{0,64},{1,67},{2,66},{3,65},{4,68},{5,71},{6,70},{7,69},{8,72},{9,... | collective-permute-start | bytes 3145736 | tf_op jit(solution)/shard_map/ppermute | solution.py:71
  60.3 35.3 %collective-permute-start.8 = (bf16[512,1024]{1,0:T(8,128)(2,1)S(1)}, bf16[512,1024]{1,0:T(8,128)(2,1)S(1)}, u32[]{:S(2)}, u32[]{:S(2)}) collective-permute-start(bf16[512,1024]{1,0:T(8,128)(2,1)S(1)} %get-tuple-element.117.refs_5_), channel_id=1, source_target_pairs={{0,64},{1,67},{2,66},{3,65},{4,68},{5,71},{6,70},{7,69},{8,72},{9,... | collective-permute-start | bytes 3145736 | tf_op jit(solution)/shard_map/ppermute | solution.py:71
  84.4 15.8 %copy-start.23 = (bf16[512,1024]{1,0:T(8,128)(2,1)}, bf16[512,1024]{1,0:T(8,128)(2,1)S(1)}, u32[]{:S(2)}) copy-start(bf16[512,1024]{1,0:T(8,128)(2,1)S(1)} %collective-permute-done.7.refs_2_) | copy-start | bytes 3145732
  98.3 16.5 %copy-start.78 = (s32[1,2]{1,0:T(1,128)S(1)}, s32[1,2]{1,0:T(1,128)}, u32[]{:S(2)}) copy-start(s32[1,2]{1,0:T(1,128)} %param.31) | copy-start | bytes 28
  98.3 17.4 %copy-start.5 = (bf16[1,144,2048]{2,1,0:T(8,128)(2,1)S(1)}, bf16[1,144,2048]{2,1,0:T(8,128)(2,1)}, u32[]{:S(2)}) copy-start(bf16[1,144,2048]{2,1,0:T(8,128)(2,1)} %param.16) | copy-start | bytes 1769476
  98.3 14.1 %collective-permute-start.9 = (bf16[256,2048]{1,0:T(8,128)(2,1)S(1)}, bf16[256,2048]{1,0:T(8,128)(2,1)}, u32[]{:S(2)}, u32[]{:S(2)}) collective-permute-start(bf16[256,2048]{1,0:T(8,128)(2,1)S(1)} %get-tuple-element.120.refs_0_), channel_id=1, source_target_pairs={{0,4},{1,13},{2,6},{3,15},{4,8},{5,1},{6,10},{7,3},{8,12},{9,5},{1... | collective-permute-start | bytes 3145736 | tf_op jit(solution)/shard_map/ppermute | solution.py:71
  100.2 16.7 %collective-permute-start.12 = (bf16[512,1024]{1,0:T(8,128)(2,1)S(1)}, bf16[512,1024]{1,0:T(8,128)(2,1)}, u32[]{:S(2)}, u32[]{:S(2)}) collective-permute-start(bf16[512,1024]{1,0:T(8,128)(2,1)S(1)} %collective-permute-done.7.refs_2_), channel_id=1, source_target_pairs={{0,64},{1,67},{2,66},{3,65},{4,68},{5,71},{6,70},{7,69},{8,72},{9,... | collective-permute-start | bytes 3145736 | tf_op jit(solution)/shard_map/ppermute | solution.py:71
  103.8 23.1 %collective-permute-start.14 = (bf16[512,1024]{1,0:T(8,128)(2,1)}, bf16[512,1024]{1,0:T(8,128)(2,1)}, u32[]{:S(2)}, u32[]{:S(2)}) collective-permute-start(bf16[512,1024]{1,0:T(8,128)(2,1)} %copy-done.70), channel_id=1, source_target_pairs={{0,64},{1,67},{2,66},{3,65},{4,68},{5,71},{6,70},{7,69},{8,72},{9,... | collective-permute-start | bytes 3145736 | tf_op jit(solution)/shard_map/ppermute | solution.py:71
  112.4 28.9 %collective-permute-start.10 = (bf16[256,2048]{1,0:T(8,128)(2,1)}, bf16[256,2048]{1,0:T(8,128)(2,1)}, u32[]{:S(2)}, u32[]{:S(2)}) collective-permute-start(bf16[256,2048]{1,0:T(8,128)(2,1)} %collective-permute-done.9.refs_1_), channel_id=1, source_target_pairs={{0,4},{1,13},{2,6},{3,15},{4,8},{5,1},{6,10},{7,3},{8,12},{9,5},{1... | collective-permute-start | bytes 3145736 | tf_op jit(solution)/shard_map/ppermute | solution.py:71
  114.9 1.6 collective-permute-start.18
  115.7 35.0 %collective-permute-start.17 = (bf16[144,2048]{1,0:T(8,128)(2,1)S(1)}, bf16[144,2048]{1,0:T(8,128)(2,1)S(1)}, u32[]{:S(2)}, u32[]{:S(2)}) collective-permute-start(bf16[144,2048]{1,0:T(8,128)(2,1)S(1)} %bitcast.68), channel_id=1, source_target_pairs={{0,1},{1,0},{2,3},{3,2},{4,5},{5,4},{6,7},{7,6},{8,9},{9,8},{10,11... | collective-permute-start | bytes 1769480 | tf_op jit(solution)/shard_map/ppermute | solution.py:61
  116.0 36.0 %copy-start.55 = (s32[3,4]{1,0:T(4,128)}, s32[3,4]{1,0:T(4,128)S(1)}, u32[]{:S(2)}) copy-start(s32[3,4]{1,0:T(4,128)S(1)} %pad_add_fusion.places) | copy-start | bytes 148
  116.7 32.5 %copy-start.75 = (s32[2]{0:T(128)}, s32[2]{0:T(128)S(1)}, u32[]{:S(2)}) copy-start(s32[2]{0:T(128)S(1)} %get-tuple-element.205) | copy-start | bytes 28
  116.7 131.5 %copy-start.56 = (s32[2]{0:T(128)}, s32[2]{0:T(128)S(1)}, u32[]{:S(2)}) copy-start(s32[2]{0:T(128)S(1)} %get-tuple-element.204.bounds) | copy-start | bytes 28
  116.9 35.1 %collective-permute-start.13 = (bf16[512,1024]{1,0:T(8,128)(2,1)}, bf16[512,1024]{1,0:T(8,128)(2,1)}, u32[]{:S(2)}, u32[]{:S(2)}) collective-permute-start(bf16[512,1024]{1,0:T(8,128)(2,1)} %collective-permute-done.12.refs_3_), channel_id=1, source_target_pairs={{0,64},{1,67},{2,66},{3,65},{4,68},{5,71},{6,70},{7,69},{8,72},{9,... | collective-permute-start | bytes 3145736 | tf_op jit(solution)/shard_map/ppermute | solution.py:71
  126.9 25.1 %collective-permute-start.15 = (bf16[512,1024]{1,0:T(8,128)(2,1)}, bf16[512,1024]{1,0:T(8,128)(2,1)}, u32[]{:S(2)}, u32[]{:S(2)}) collective-permute-start(bf16[512,1024]{1,0:T(8,128)(2,1)} %collective-permute-done.14.refs_7_), channel_id=1, source_target_pairs={{0,64},{1,67},{2,66},{3,65},{4,68},{5,71},{6,70},{7,69},{8,72},{9,... | collective-permute-start | bytes 3145736 | tf_op jit(solution)/shard_map/ppermute | solution.py:71
  141.3 30.5 %collective-permute-start.11 = (bf16[256,2048]{1,0:T(8,128)(2,1)}, bf16[256,2048]{1,0:T(8,128)(2,1)}, u32[]{:S(2)}, u32[]{:S(2)}) collective-permute-start(bf16[256,2048]{1,0:T(8,128)(2,1)} %collective-permute-done.10.refs_2_), channel_id=1, source_target_pairs={{0,4},{1,13},{2,6},{3,15},{4,8},{5,1},{6,10},{7,3},{8,12},{9,5},{1... | collective-permute-start | bytes 3145736 | tf_op jit(solution)/shard_map/ppermute | solution.py:71
  150.8 17.0 %copy-start = (bf16[2,144,2048]{2,1,0:T(8,128)(2,1)}, bf16[2,144,2048]{2,1,0:T(8,128)(2,1)S(1)}, u32[]{:S(2)}) copy-start(bf16[2,144,2048]{2,1,0:T(8,128)(2,1)S(1)} %maximum_select_fusion.1) | copy-start | bytes 3538948
  176.1 68.1 %collective-permute-start.20 = (bf16[512,2048]{1,0:T(8,128)(2,1)}, bf16[512,2048]{1,0:T(8,128)(2,1)}, u32[]{:S(2)}, u32[]{:S(2)}) collective-permute-start(bf16[512,2048]{1,0:T(8,128)(2,1)} %get-tuple-element.137.refs_5_), channel_id=1, source_target_pairs={{0,64},{1,67},{2,66},{3,65},{4,68},{5,71},{6,70},{7,69},{8,72},{9,... | collective-permute-start | bytes 6291464 | tf_op jit(solution)/shard_map/ppermute | solution.py:71
  179.4 64.8 %collective-permute-start.16 = (bf16[512,2048]{1,0:T(8,128)(2,1)}, bf16[512,2048]{1,0:T(8,128)(2,1)}, u32[]{:S(2)}, u32[]{:S(2)}) collective-permute-start(bf16[512,2048]{1,0:T(8,128)(2,1)} %get-tuple-element.131.refs_1_), channel_id=1, source_target_pairs={{0,64},{1,67},{2,66},{3,65},{4,68},{5,71},{6,70},{7,69},{8,72},{9,... | collective-permute-start | bytes 6291464 | tf_op jit(solution)/shard_map/ppermute | solution.py:71
  179.4 14.9 %copy-start.73 = (f32[288,64]{1,0:T(8,128)S(1)}, f32[288,64]{1,0:T(8,128)}, u32[]{:S(2)}) copy-start(f32[288,64]{1,0:T(8,128)} %get-tuple-element.207) | copy-start | bytes 221188
  191.2 3.9 collective-permute-start.19
  244.2 54.4 %copy-start.7 = (bf16[8,288,384]{2,1,0:T(8,128)(2,1)}, bf16[8,288,384]{2,1,0:T(8,128)(2,1)S(1)}, u32[]{:S(2)}) copy-start(bf16[8,288,384]{2,1,0:T(8,128)(2,1)S(1)} %all_to_all.45) | copy-start | bytes 5308420
  244.2 54.4 %copy-start.44 = (bf16[32,1024]{1,0:T(8,128)(2,1)S(1)}, bf16[32,1024]{1,0:T(8,128)(2,1)}, u32[]{:S(2)}) copy-start(bf16[32,1024]{1,0:T(8,128)(2,1)} %get-tuple-element.143.down) | copy-start | bytes 196612
  244.2 54.4 %copy-start.48 = (s32[8]{0:T(128)S(1)}, s32[8]{0:T(128)}, u32[]{:S(2)}) copy-start(s32[8]{0:T(128)} %copy-done.47) | copy-start | bytes 100
  244.2 59.4 %collective-permute-start.23 = (bf16[512,2048]{1,0:T(8,128)(2,1)}, bf16[512,2048]{1,0:T(8,128)(2,1)S(1)}, u32[]{:S(2)}, u32[]{:S(2)}) collective-permute-start(bf16[512,2048]{1,0:T(8,128)(2,1)} %collective-permute-done.20.refs_6_), channel_id=1, source_target_pairs={{0,64},{1,67},{2,66},{3,65},{4,68},{5,71},{6,70},{7,69},{8,72},{9,... | collective-permute-start | bytes 6291464 | tf_op jit(solution)/shard_map/ppermute | solution.py:71
  247.9 55.8 %collective-permute-start.21 = (bf16[512,2048]{1,0:T(8,128)(2,1)}, bf16[512,2048]{1,0:T(8,128)(2,1)S(1)}, u32[]{:S(2)}, u32[]{:S(2)}) collective-permute-start(bf16[512,2048]{1,0:T(8,128)(2,1)} %collective-permute-done.16.refs_2_), channel_id=1, source_target_pairs={{0,64},{1,67},{2,66},{3,65},{4,68},{5,71},{6,70},{7,69},{8,72},{9,... | collective-permute-start | bytes 6291464 | tf_op jit(solution)/shard_map/ppermute | solution.py:71
  255.8 42.8 %copy-start.59 = (f32[2,1152,128]{2,1,0:T(8,128)}, f32[2,1152,128]{2,1,0:T(8,128)S(1)}, u32[]{:S(2)}) copy-start(f32[2,1152,128]{2,1,0:T(8,128)S(1)} %get-tuple-element.181.exact) | copy-start | bytes 3538948
  303.7 25.4 %copy-start.66 = (bf16[512,2048]{1,0:T(8,128)(2,1)}, bf16[512,2048]{1,0:T(8,128)(2,1)S(1)}, u32[]{:S(2)}) copy-start(bf16[512,2048]{1,0:T(8,128)(2,1)S(1)} %collective-permute-done.21.refs_3_) | copy-start | bytes 6291460
  303.7 25.4 %collective-permute-start.22 = (bf16[512,2048]{1,0:T(8,128)(2,1)S(1)}, bf16[512,2048]{1,0:T(8,128)(2,1)S(1)}, u32[]{:S(2)}, u32[]{:S(2)}) collective-permute-start(bf16[512,2048]{1,0:T(8,128)(2,1)S(1)} %collective-permute-done.21.refs_3_), channel_id=1, source_target_pairs={{0,64},{1,67},{2,66},{3,65},{4,68},{5,71},{6,70},{7,69},{8,72},{9,... | collective-permute-start | bytes 6291464 | tf_op jit(solution)/shard_map/ppermute | solution.py:71
  305.3 46.2 %collective-permute-start.24 = (bf16[512,2048]{1,0:T(8,128)(2,1)S(1)}, bf16[512,2048]{1,0:T(8,128)(2,1)}, u32[]{:S(2)}, u32[]{:S(2)}) collective-permute-start(bf16[512,2048]{1,0:T(8,128)(2,1)S(1)} %collective-permute-done.23.refs_7_), channel_id=1, source_target_pairs={{0,64},{1,67},{2,66},{3,65},{4,68},{5,71},{6,70},{7,69},{8,72},{9,... | collective-permute-start | bytes 6291464 | tf_op jit(solution)/shard_map/ppermute | solution.py:71
  307.6 3.8 collective-permute-start.25
  314.4 2.4 collective-permute-start.26
  351.5 34.1 %copy-start.4 = (bf16[1,144,2048]{2,1,0:T(8,128)(2,1)S(1)}, bf16[1,144,2048]{2,1,0:T(8,128)(2,1)}, u32[]{:S(2)}) copy-start(bf16[1,144,2048]{2,1,0:T(8,128)(2,1)} %param.17) | copy-start | bytes 1769476
  351.5 34.1 %copy-start.16 = (f32[144,2048]{1,0:T(8,128)S(1)}, f32[144,2048]{1,0:T(8,128)}, u32[]{:S(2)}) copy-start(f32[144,2048]{1,0:T(8,128)} %copy-done.15) | copy-start | bytes 3538948
  351.5 34.1 %copy-start.36 = (bf16[32,2048]{1,0:T(8,128)(2,1)S(1)}, bf16[32,2048]{1,0:T(8,128)(2,1)}, u32[]{:S(2)}) copy-start(bf16[32,2048]{1,0:T(8,128)(2,1)} %get-tuple-element.162.up.refs_11_) | copy-start | bytes 393220
  378.2 7.4 %collective-permute-start.27 = (bf16[144,2176]{1,0:T(8,128)(2,1)}, bf16[144,2176]{1,0:T(8,128)(2,1)S(1)}, u32[]{:S(2)}, u32[]{:S(2)}) collective-permute-start(bf16[144,2176]{1,0:T(8,128)(2,1)} %get-tuple-element.160), channel_id=1, source_target_pairs={{0,1},{1,0},{2,3},{3,2},{4,5},{5,4},{6,7},{7,6},{8,9},{9,8},{10,11... | collective-permute-start | bytes 1880072 | tf_op jit(solution)/shard_map/ppermute | solution.py:61
  389.1 2.1 collective-permute-start.28
  392.0 29.6 %copy-start.6 = (bf16[288,4096]{1,0:T(8,128)(2,1)S(1)}, bf16[288,4096]{1,0:T(8,128)(2,1)}, u32[]{:S(2)}) copy-start(bf16[288,4096]{1,0:T(8,128)(2,1)} %get-tuple-element.174.refs_4_) | copy-start | bytes 7077892
  421.1 9.1 %collective-permute-start.29 = (bf16[144,2176]{1,0:T(8,128)(2,1)}, bf16[144,2176]{1,0:T(8,128)(2,1)S(1)}, u32[]{:S(2)}, u32[]{:S(2)}) collective-permute-start(bf16[144,2176]{1,0:T(8,128)(2,1)} %get-tuple-element.167), channel_id=1, source_target_pairs={{0,1},{1,0},{2,3},{3,2},{4,5},{5,4},{6,7},{7,6},{8,9},{9,8},{10,11... | collective-permute-start | bytes 1880072 | tf_op jit(solution)/shard_map/ppermute | solution.py:61
  432.5 16.7 %all-to-all-start.3 = ((bf16[8,32,1664]{2,1,0:T(8,128)(2,1)}), bf16[8,32,1664]{2,1,0:T(8,128)(2,1)S(1)}, u32[]{:S(2)}, u32[]{:S(2)}) async-start(bf16[8,32,1664]{2,1,0:T(8,128)(2,1)} %early_gradients.1), calls=%async_computation.3 | async-start | bytes 1703936 | tf_op jit(solution)/shard_map/all_to_all | solution.py:1143
  437.5 2.4 collective-permute-start.30
  449.2 17.2 %all-to-all-start.2 = ((bf16[8,416,128]{2,1,0:T(8,128)(2,1)}), bf16[8,416,128]{2,1,0:T(8,128)(2,1)S(1)}, u32[]{:S(2)}, u32[]{:S(2)}) async-start(bf16[8,416,128]{2,1,0:T(8,128)(2,1)} %get-tuple-element.177), calls=%async_computation.2 | async-start | bytes 1703936 | tf_op jit(solution)/shard_map/all_to_all | solution.py:1146
  455.7 16.4 %copy-start.8 = (bf16[8,288,384]{2,1,0:T(8,128)(2,1)S(1)}, bf16[8,288,384]{2,1,0:T(8,128)(2,1)}, u32[]{:S(2)}) copy-start(bf16[8,288,384]{2,1,0:T(8,128)(2,1)} %copy-done.7) | copy-start | bytes 5308420
  455.7 16.4 %copy-start.57 = (s32[2]{0:T(128)S(1)}, s32[2]{0:T(128)}, u32[]{:S(2)}) copy-start(s32[2]{0:T(128)} %copy-done.56) | copy-start | bytes 28
  467.7 22.6 %all-to-all-start.4 = ((bf16[8,32,2304]{2,1,0:T(8,128)(2,1)}), bf16[8,32,2304]{2,1,0:T(8,128)(2,1)}, u32[]{:S(2)}, u32[]{:S(2)}) async-start(bf16[8,32,2304]{2,1,0:T(8,128)(2,1)} %broadcast_in_dim.44), calls=%async_computation.4 | async-start | bytes 2359296 | tf_op jit(solution)/shard_map/all_to_all | solution.py:1087
  490.3 26.8 %all-to-all-start.5 = ((bf16[8,2,144,384]{3,2,1,0:T(8,128)(2,1)}), bf16[8,2,144,384]{3,2,1,0:T(8,128)(2,1)S(1)}, u32[]{:S(2)}, u32[]{:S(2)}) async-start(bf16[8,2,144,384]{3,2,1,0:T(8,128)(2,1)} %attend_back.1), calls=%async_computation.5 | async-start | bytes 3538944 | tf_op jit(solution)/shard_map/all_to_all | solution.py:1155
  495.6 87.8 %all-gather.9.cloned.1.call-start = ((), (), s32[]{:S(2)}) async-start(), calls=%async_computation.11 | async-start | bytes 5013504 | tf_op jit(solution)/shard_map/all_gather | solution.py:1163
  522.4 1.8 collective-permute-start.31
  539.4 2.1 collective-permute-start.32
  543.3 1.2 collective-permute-start.33
  583.3 7.9 %collective-permute-start.34 = (bf16[8,8,16,2176]{3,2,1,0:T(8,128)(2,1)}, bf16[8,8,16,2176]{3,2,1,0:T(8,128)(2,1)}, u32[]{:S(2)}, u32[]{:S(2)}) collective-permute-start(bf16[8,8,16,2176]{3,2,1,0:T(8,128)(2,1)} %bitcast.82), channel_id=1, source_target_pairs={{0,1},{1,0},{2,3},{3,2},{4,5},{5,4},{6,7},{7,6},{8,9},{9,8},{10,11... | collective-permute-start | bytes 13369352 | tf_op jit(solution)/shard_map/ppermute | solution.py:61
  585.5 27.7 %all-to-all-start.8 = ((bf16[8,128,768]{2,1,0:T(8,128)(2,1)}), bf16[8,128,768]{2,1,0:T(8,128)(2,1)S(1)}, u32[]{:S(2)}, u32[]{:S(2)}) async-start(bf16[8,128,768]{2,1,0:T(8,128)(2,1)} %broadcast_in_dim.48), calls=%async_computation.8 | async-start | bytes 3145728 | tf_op jit(solution)/shard_map/all_to_all | solution.py:1087
  613.1 4.0 collective-permute-start.35
  (59 other events, 233.1 us)
Sparse Core Ops, SparseCore 0:
  28.8 72.1 all-gather.6
  103.7 237.0 all-gather.4
  517.2 57.9 all-gather.8
